TPU v7x, 32 devices: a whole 2x2x4 slice. The times are simulated.
32 devices in a mesh: dp: 4 (over y, x), blk: 8 (over z, core).
Axes of the slice: x: 2, y: 2, z: 4, core: 2. Of those that a mesh axis runs over, the one named last changes fastest.
Arguments:
- visual_inputs: bfloat16 [4, 512, 1152], P('dp', 'blk'), may hold values from -0.38301617 to 0.38301617
- sentence_vectors: bfloat16 [4, 2048, 1152], P('dp', 'blk'), may hold values from -0.38301617 to 0.38301617
- paired_picture_index: int32 [4, 2048], P('dp', 'blk'), may hold values from 0 to 511, as said below
- visual_head_linear_map: bfloat16 [1152, 1152], replicated, may hold values from -3 to 3
- score_multiplier: float32 [], replicated, may hold values from 8 to 16
- score_offset: float32 [], replicated, may hold values from -6 to -3
Outputs:
- grad_features: float32 [4, 512, 1152], P('dp', 'blk')
- sentence_vector_adjoint: float32 [4, 2048, 1152], P('dp', 'blk')
- grad_weight: float32 [1152, 1152], replicated
Inputs may be any that keep to these rules, and one draw needn't show every extreme that they name: `paired_picture_index`: within each loss group, every image index appears exactly 4 times among the labels.
All inputs are finite; a program needn't handle non-finite values.
Results may differ from a plain program's by a relative error of at most 0.0032.
Values may be sent and summed in bfloat16 or wider, within the bound.
No kernel may reach another device: no remote copies, remote signals or barrier semaphores. Data moves between devices by JAX's collectives and lax.ppermute only.
A program may use at most 128 MiB of HBM per device.

v0:
```python
import jax
import jax.numpy as jnp
from jax import lax
from jax.sharding import PartitionSpec as P


def pair_signs(sentence_label_signs, picture_indices):
    return jnp.where(sentence_label_signs[None, :] == picture_indices[:, None], 1.0, -1.0).astype(
        jnp.float32
    )


def logit_gradient_rows(
    unitlength_vectors,
    sentence_tile_slice,
    sentence_label_signs,
    picture_indices,
    score_multiplier,
    score_offset,
):
    contract_last = (((1,), (1,)), ((), ()))
    pairwise_scores = (
        score_multiplier
        * lax.dot_general(
            unitlength_vectors,
            sentence_tile_slice,
            contract_last,
            preferred_element_type=jnp.float32,
        )
        + score_offset
    )
    pair_sign = pair_signs(sentence_label_signs, picture_indices)
    return (-pair_sign * jax.nn.sigmoid(-pair_sign * pairwise_scores)).astype(jnp.bfloat16)


def on_device(
    visual_inputs,
    sentence_vectors,
    paired_picture_index,
    visual_head_linear_map,
    score_multiplier,
    score_offset,
):
    picture_tile_slice = visual_inputs[0]
    sentence_tile_slice = sentence_vectors[0]
    sentence_label_signs = paired_picture_index[0]
    own_count = picture_tile_slice.shape[0]
    contract_first = (((0,), (0,)), ((), ()))
    contract_last = (((1,), (1,)), ((), ()))
    embedding = jnp.dot(
        picture_tile_slice, visual_head_linear_map, preferred_element_type=jnp.float32
    )
    inv_norm = lax.rsqrt(jnp.sum(embedding * embedding, axis=1, keepdims=True) + 1e-06)
    unit_f = embedding * inv_norm
    unitlength_brainfloat = unit_f.astype(jnp.bfloat16)
    local_identifiers = lax.axis_index("blk") * own_count + jnp.arange(own_count, dtype=jnp.int32)
    portion_normalized = lax.all_gather(unitlength_brainfloat, "blk", axis=0, tiled=True)
    portion_identifiers = jnp.arange(portion_normalized.shape[0], dtype=jnp.int32)
    score_adjoint = logit_gradient_rows(
        portion_normalized,
        sentence_tile_slice,
        sentence_label_signs,
        portion_identifiers,
        score_multiplier,
        score_offset,
    )
    reduced_entries = score_multiplier * lax.dot_general(
        score_adjoint, portion_normalized, contract_first, preferred_element_type=jnp.float32
    )
    portion_captions = lax.all_gather(sentence_tile_slice, "blk", axis=0, tiled=True)
    portion_targets = lax.all_gather(sentence_label_signs, "blk", axis=0, tiled=True)
    score_adjoint = logit_gradient_rows(
        unitlength_brainfloat,
        portion_captions,
        portion_targets,
        local_identifiers,
        score_multiplier,
        score_offset,
    )
    unitlength_adjoint = score_multiplier * jnp.dot(
        score_adjoint, portion_captions, preferred_element_type=jnp.float32
    )
    radial = jnp.sum(unit_f * unitlength_adjoint, axis=1, keepdims=True)
    grad_embed = ((unitlength_adjoint - unit_f * radial) * inv_norm).astype(jnp.bfloat16)
    grad_features = lax.dot_general(
        grad_embed, visual_head_linear_map, contract_last, preferred_element_type=jnp.float32
    )
    weight_term = lax.dot_general(
        picture_tile_slice, grad_embed, contract_first, preferred_element_type=jnp.float32
    )
    grad_weight = lax.psum(weight_term, ("dp", "blk")) / lax.axis_size("dp")
    return (grad_features[None], reduced_entries[None], grad_weight)


def solution(mesh):
    placed = (P("dp", "blk", None), P("dp", "blk", None), P("dp", "blk"), P(), P(), P())
    return jax.shard_map(
        on_device,
        mesh=mesh,
        in_specs=placed,
        out_specs=(P("dp", "blk", None), P("dp", "blk", None), P()),
        check_vma=False,
    )
```

profile of v0, /device:TPU:0, one launch (start us, length us, event | category | flops | bytes accessed | tf_op | source)
XLA Modules:
  0.0 261.1 jit_solution(35485239776654619)
XLA Ops:
  7.2 0.0 copy-start
  7.2 0.0 copy-start.2
  7.2 0.0 all-gather.7.cloned.1.call-start
  7.2 0.7 all-gather.7.cloned.1.call-update
  7.9 0.0 all-gather.5.cloned.1.call-start
  8.0 0.9 copy-done
  8.9 1.6 multiply_reduce_fusion.1
  10.5 0.8 multiply_convert_fusion.1
  11.3 0.0 all-gather.5.cloned.1.call-update
  11.3 0.0 all-reduce.2.cloned.1.call-start
  12.7 0.0 copy-done.2
  12.7 13.5 %all-gather = s32[1,2048]{1,0:T(1,128)S(1)} all-gather(s32[1,256]{1,0:T(1,128)S(1)} %copy-done.2), channel_id=2, replica_groups=mesh['dp'=4,'blk'=8] {'blk'}, dimensions={1}, use_global_device_ids=true | all-gather | bytes 9216 | tf_op jit(solution)/shard_map/all_gather | solution.py:71
  26.2 37.9 %all-gather.7.cloned.1.call-done = bf16[1,2048,1152]{2,1,0:T(8,128)(2,1)} async-done(((bf16[1,256,1152]{2,1,0:T(8,128)(2,1)}), bf16[1,2048,1152]{2,1,0:T(8,128)(2,1)}) %all-gather.7.cloned.1.call-update) | async-done | bytes 4718608 | tf_op jit(solution)/shard_map/all_gather | solution.py:70
  64.1 0.0 copy-start.1
  64.1 6.3 %multiply_reduce_fusion = (f32[64]{0:T(128)S(1)}, f32[64,1152]{1,0:T(8,128)S(1)}) fusion(f32[64,1152]{1,0:T(8,128)S(1)} %get-tuple-element.7, f32[64]{0:T(128)S(1)} %add_rsqrt_fusion, bf16[1,2048,1152]{2,1,0:T(8,128)(2,1)} %all-gather.7.cloned.1.call-done, f32[]{:T(128)S(6)} %copy.12, f32[]{:T(128)S(6)} %copy.11, s32[2048]{0:T(1024)S(1)} %bitcast.56, ...), kind=kOutput, calls=%fused_computation.36 | convolution fusion | flops 605863872 | bytes 5317384 | tf_op jit(solution)/shard_map/dot_general | solution.py:80
  70.4 0.1 multiply_convert_fusion
  70.6 0.0 copy-done.1
  70.6 3.3 %convolution_bitcast_fusion = f32[1152,1152]{0,1:T(8,128)} fusion(bf16[64,1152]{1,0:T(8,128)(2,1)S(1)} %multiply_convert_fusion, bf16[1,64,1152]{2,1,0:T(8,128)(2,1)S(1)} %copy-done.1), kind=kOutput, calls=%fused_computation | convolution fusion | flops 169869312 | bytes 5603328 | tf_op jit(solution)/shard_map/dot_general | solution.py:88
  73.8 0.0 all-reduce.2.cloned.1.call-update
  73.9 14.0 %all-gather.5.cloned.1.call-done = bf16[512,1152]{1,0:T(8,128)(2,1)} async-done(((bf16[64,1152]{1,0:T(8,128)(2,1)}), bf16[512,1152]{1,0:T(8,128)(2,1)}) %all-gather.5.cloned.1.call-update) | async-done | bytes 1179664 | tf_op jit(solution)/shard_map/all_gather | solution.py:57
  87.8 4.6 %fusion.4 = f32[1,256,1152]{2,1,0:T(8,128)} fusion(bf16[512,1152]{1,0:T(8,128)(2,1)} %all-gather.5.cloned.1.call-done, bf16[1,256,1152]{2,1,0:T(8,128)(2,1)} %param.7, f32[]{:T(128)S(6)} %copy.11, f32[]{:T(128)S(6)} %copy.12, s32[256]{0:T(256)S(1)} %bitcast.57), kind=kOutput, calls=%fused_computation.6 | convolution fusion | flops 605716480 | bytes 2950152 | tf_op jit(solution)/shard_map/dot_general | solution.py:67
  92.4 1.7 convolution_bitcast_fusion.1
  94.1 148.4 %all-reduce.2.cloned.1.call-done = f32[1152,1152]{0,1:T(8,128)} async-done(((f32[1152,1152]{0,1:T(8,128)}), f32[1152,1152]{0,1:T(8,128)}) %all-reduce.2.cloned.1.call-update) | async-done | bytes 5308432 | tf_op jit(solution)/shard_map/psum | solution.py:91
  242.5 5.2 %broadcast_multiply_fusion = f32[1152,1152]{0,1:T(8,128)} fusion(f32[1152,1152]{0,1:T(8,128)} %all-reduce.2.cloned.1.call-done), kind=kLoop, calls=%fused_computation.7 | loop fusion | flops 1327104 | bytes 10616832 | tf_op jit(solution)/shard_map/div | solution.py:91
  247.7 6.9 %copy.9 = f32[1152,1152]{1,0:T(8,128)} copy(f32[1152,1152]{0,1:T(8,128)} %broadcast_multiply_fusion) | data formatting | bytes 10616832
  (2 shorter events, 0.0 us)
Async XLA Ops:
  7.2 1.8 copy-start
  7.2 5.5 %copy-start.2 = (s32[1,256]{1,0:T(1,128)S(1)}, s32[1,256]{1,0:T(1,128)}, u32[]{:S(2)}) copy-start(s32[1,256]{1,0:T(1,128)} %param.8) | copy-start | bytes 3076
  7.2 56.9 %all-gather.7.cloned.1.call-start = ((), (), s32[]{:S(2)}) async-start(), calls=%async_computation.2 | async-start | bytes 5308416 | tf_op jit(solution)/shard_map/all_gather | solution.py:70
  7.9 79.9 %all-gather.5.cloned.1.call-start = ((), (), s32[]{:S(2)}) async-start(), calls=%async_computation | async-start | bytes 1327104 | tf_op jit(solution)/shard_map/all_gather | solution.py:57
  11.3 231.2 %all-reduce.2.cloned.1.call-start = ((), (), s32[]{:S(2)}) async-start(), calls=%async_computation.1 | async-start | bytes 10616832 | tf_op jit(solution)/shard_map/psum | solution.py:91
  64.1 6.4 %copy-start.1 = (bf16[1,64,1152]{2,1,0:T(8,128)(2,1)S(1)}, bf16[1,64,1152]{2,1,0:T(8,128)(2,1)}, u32[]{:S(2)}) copy-start(bf16[1,64,1152]{2,1,0:T(8,128)(2,1)} %param.6) | copy-start | bytes 442372
Sparse Core Ops, SparseCore 0:
  9.7 54.4 all-gather.6
  66.3 21.4 all-gather.4
  94.2 148.2 all-reduce.1
where the time goes:
time: 261 us
  waiting for transfers between devices  201 us (77%)
  matrix products  17.4 us (7%)
  between operations  15.1 us (6%)
  blocking collectives  13.5 us (5%)
  local copies, waits for them, and re-layouts  7.82 us (3%)
  other arithmetic  6.09 us (2%)
    psum x1, waiting for transfers between devices, on_device(): grad_weight = lax.psum(weight_term, ('dp', 'blk')) / lax.axis_size('dp')  148 us
    all_gather x1, waiting for transfers between devices, on_device(): lax.all_gather(sentence_tile_slice, 'blk', axis=0, tiled=True)  37.9 us
    all_gather x1, waiting for transfers between devices, on_device(): lax.all_gather(unitlength_brainfloat, 'blk', axis=0, tiled=True)  14 us
    all_gather x1, blocking collectives, on_device(): lax.all_gather(sentence_label_signs, 'blk', axis=0, tiled=True)  13.5 us
    unnamed x7, local copies, waits for them, and re-layouts  7.82 us
    dot_general x1, matrix products, on_device(): jnp.dot(score_adjoint, portion_captions, preferred_element_type=jnp.float32)  6.31 us
  transfers between devices with their start and end apart: 3, of which 3 were waited for; matrix products, arithmetic and copies ran while one was open for 7% of the time, Pallas kernels for 0%

commit v1 on v0

v1 whole, which is shorter than its diff:
```python
import jax
import jax.numpy as jnp
from jax import lax
from jax.sharding import PartitionSpec as P

FIRST = (((0,), (0,)), ((), ()))
LAST = (((1,), (1,)), ((), ()))
F32 = jnp.float32
BF16 = jnp.bfloat16


def dot(a, b, dims=(((1,), (0,)), ((), ()))):
    return lax.dot_general(a, b, dims, preferred_element_type=F32)


def on_device(x, captions, labels, weight, scale, offset):
    x, captions, labels = x[0], captions[0], labels[0]
    n_img, depth = x.shape
    n_cap = captions.shape[0]
    nd, nb = lax.axis_size("dp"), lax.axis_size("blk")
    nz = nb // 2
    d, b = lax.axis_index("dp"), lax.axis_index("blk")
    z, c = b // 2, b % 2

    def along_z(v, k):
        return lax.ppermute(
            v, "blk", [(i, ((i // 2 + k) % nz) * 2 + i % 2) for i in range(nb)]
        )

    def swap(v):
        return lax.ppermute(v, "blk", [(i, i ^ 1) for i in range(nb)])

    def in_plane(v, kd, kc):
        perm = []
        for i in range(nd):
            for j in range(nb):
                perm.append((i * nb + j, ((i + kd) % nd) * nb + (j ^ kc)))
        return lax.ppermute(v, ("dp", "blk"), perm)

    xs = jnp.concatenate([x] + [along_z(x, k) for k in range(1, nz)])
    caps = jnp.concatenate([captions, swap(captions)])
    labs = jnp.concatenate([labels, swap(labels)])
    ids = jnp.concatenate(
        [
            (((z - k + nz) % nz) * 2 + c) * n_img + jnp.arange(n_img, dtype=jnp.int32)
            for k in range(nz)
        ]
    )
    embed = dot(xs, weight)
    inv_norm = lax.rsqrt(jnp.sum(embed * embed, axis=1, keepdims=True) + 1e-06)
    unit_f = embed * inv_norm
    unit = unit_f.astype(BF16)
    logits = scale * dot(unit, caps, LAST) + offset
    sign = jnp.where(labs[None, :] == ids[:, None], 1.0, -1.0).astype(F32)
    dlogit = (-sign * jax.nn.sigmoid(-sign * logits)).astype(BF16)

    part = scale * dot(dlogit, caps)
    own = part[:n_img]
    for k in range(1, nz):
        back = along_z(part[k * n_img : (k + 1) * n_img].astype(BF16), nz - k)
        own = own + back.astype(F32)

    adjoint = scale * dot(dlogit, unit, FIRST)
    adjoint = adjoint[:n_cap] + swap(adjoint[n_cap:])

    u = unit_f[:n_img]
    radial = jnp.sum(u * own, axis=1, keepdims=True)
    ge = ((own - u * radial) * inv_norm[:n_img]).astype(BF16)
    grad_features = dot(ge, weight, LAST)

    cols = depth // nz
    blocks = []
    for k in range(nz):
        v = lax.dynamic_slice_in_dim(ge, ((z + k) % nz) * cols, cols, 1)
        blocks.append(along_z(v, k) if k else v)
    wpart = dot(xs, jnp.concatenate(blocks), FIRST)
    rows = depth // (nd * 2)
    piece = None
    for kc in range(2):
        for kd in range(nd):
            to = ((d + kd) % nd) * 2 + (c ^ kc)
            v = lax.dynamic_slice_in_dim(wpart, to * rows, rows, 0)
            if kd or kc:
                v = in_plane(v.astype(BF16), kd, kc).astype(F32)
            piece = v if piece is None else piece + v
    piece = (piece / nd).astype(BF16)
    whole = lax.all_gather(piece, ("dp", "blk"), axis=0)
    whole = whole.reshape(nd, nz, 2, rows, cols).transpose(0, 2, 3, 1, 4)
    grad_weight = whole.reshape(depth, depth).astype(F32)
    return (grad_features[None], adjoint[None], grad_weight)


def solution(mesh):
    placed = (P("dp", "blk", None), P("dp", "blk", None), P("dp", "blk"), P(), P(), P())
    return jax.shard_map(
        on_device,
        mesh=mesh,
        in_specs=placed,
        out_specs=(P("dp", "blk", None), P("dp", "blk", None), P()),
        check_vma=False,
    )
```

time: 261 us -> 168 us (0.64)
  waiting for transfers between devices: 201 us -> 88.6 us
  starting transfers between devices: 0.12 us -> 21.9 us
  blocking collectives: 13.5 us -> 0 us
  local copies, waits for them, and re-layouts: 7.82 us -> 21 us
  matrix products: 17.4 us -> 11.4 us
  other arithmetic: 6.09 us -> 8.93 us
    psum x1 -> x0, waiting for transfers between devices: 148 us -> none  [on_device(): grad_weight = lax.psum(weight_term, ('dp', 'blk')) / lax.axis_size('dp')]
    ppermute x0 -> x19, waiting for transfers between devices: none -> 33.2 us  [the longest x9 25.3 us: along_z(): lax.ppermute(v, 'blk', [(i, (i // 2 + k) % nz * 2 + i % 2) for i in range...]
    ppermute x0 -> x19, starting transfers between devices: none -> 21.8 us  [the longest x9 13 us: along_z(): lax.ppermute(v, 'blk', [(i, (i // 2 + k) % nz * 2 + i % 2) for i in range...]
    convert_element_type x0 -> x4, local copies, waits for them, and re-layouts: none -> 17.4 us  [the longest x2 15.5 us: on_device(): grad_weight = whole.reshape(depth, depth).astype(F32)]
    all_gather x1 -> x0, blocking collectives: 13.5 us -> none  [on_device(): lax.all_gather(sentence_label_signs, 'blk', axis=0, tiled=True)]
    dot_general x5 -> x6, matrix products: 17.4 us -> 11.4 us  [dot(): return lax.dot_general(a, b, dims, preferred_element_type=F32)]
    div x1 -> x0, other arithmetic: 5.2 us -> none  [on_device(): grad_weight = lax.psum(weight_term, ('dp', 'blk')) / lax.axis_size('dp')]
    unnamed x7 -> x18, local copies, waits for them, and re-layouts: 7.82 us -> 2.62 us
  transfers between devices with their start and end apart: 3 -> 20, of which waited for: 3 -> 12; matrix products, arithmetic and copies ran while one was open for 7% -> 5% of each run, Pallas kernels for 0% -> 0%
where the time goes in v1:
time: 168 us; the launch traced here: 167 us
  waiting for transfers between devices  88.6 us (53%)
  starting transfers between devices  21.9 us (13%)
  local copies, waits for them, and re-layouts  21 us (12%)
  between operations  15.5 us (9%)
  matrix products  11.4 us (7%)
  other arithmetic  8.93 us (5%)
    all_gather x1, waiting for transfers between devices, on_device(): whole = lax.all_gather(piece, ('dp', 'blk'), axis=0)  55.4 us
    ppermute x9, waiting for transfers between devices, along_z(): lax.ppermute(v, 'blk', [(i, (i // 2 + k) % nz * 2 + i % 2) for i in range...  25.3 us
    convert_element_type x2, local copies, waits for them, and re-layouts, on_device(): grad_weight = whole.reshape(depth, depth).astype(F32)  15.5 us
    ppermute x9, starting transfers between devices, along_z(): lax.ppermute(v, 'blk', [(i, (i // 2 + k) % nz * 2 + i % 2) for i in range...  13 us
    dot_general x6, matrix products, dot(): return lax.dot_general(a, b, dims, preferred_element_type=F32)  11.4 us
    ppermute x7, starting transfers between devices, in_plane(): return lax.ppermute(v, ('dp', 'blk'), perm)  8.1 us
    ppermute x7, waiting for transfers between devices, in_plane(): return lax.ppermute(v, ('dp', 'blk'), perm)  6.89 us
  transfers between devices with their start and end apart: 20, of which 12 were waited for; matrix products, arithmetic and copies ran while one was open for 5% of the time, Pallas kernels for 0%

profile of v1, /device:TPU:0, one launch (start us, length us, event | category | flops | bytes accessed | tf_op | source)
XLA Modules:
  0.0 167.3 jit_solution(13402289324589481050)
XLA Ops:
  7.2 0.0 copy-start
  7.2 0.0 all-gather.3.cloned.1.call-start
  7.2 5.1 %collective-permute-start.3 = (bf16[64,1152]{1,0:T(8,128)(2,1)}, bf16[64,1152]{1,0:T(8,128)(2,1)S(1)}, u32[]{:S(2)}, u32[]{:S(2)}) collective-permute-start(bf16[64,1152]{1,0:T(8,128)(2,1)} %bitcast.22), channel_id=1, source_target_pairs={{0,6},{1,7},{2,0},{3,1},{4,2},{5,3},{6,4},{7,5},{8,14},{9,15},{10,... | collective-permute-start | bytes 442376 | tf_op jit(solution)/shard_map/ppermute | solution.py:26
  12.3 0.0 collective-permute-start.2
  12.3 1.0 collective-permute-start.1
  13.3 0.0 collective-permute-start
  13.3 0.5 collective-permute-start.4
  13.9 0.1 pad_add_fusion.1
  15.2 0.0 collective-permute-done
  15.2 0.7 pad_add_fusion
  15.9 1.0 collective-permute-done.3
  16.9 8.1 %collective-permute-done.2 = bf16[64,1152]{1,0:T(8,128)(2,1)S(1)} collective-permute-done((bf16[64,1152]{1,0:T(8,128)(2,1)}, bf16[64,1152]{1,0:T(8,128)(2,1)S(1)}, u32[]{:S(2)}, u32[]{:S(2)}) %collective-permute-start.2) | collective-permute-done | bytes 147488 | tf_op jit(solution)/shard_map/ppermute | solution.py:26
  25.0 0.0 collective-permute-done.1
  25.0 2.1 %multiply_reduce_fusion = (f32[256]{0:T(256)S(1)}, f32[256,1152]{1,0:T(8,128)S(1)}) fusion(bf16[1152,1152]{1,0:T(8,128)(2,1)S(1)} %copy-done, bf16[64,1152]{1,0:T(8,128)(2,1)S(1)} %collective-permute-done.3, bf16[64,1152]{1,0:T(8,128)(2,1)S(1)} %collective-permute-done.2, bf16[64,1152]{1,0:T(8,128)(2,1)S(1)} %collective-permute-done.1, ...), kind=kOutput, calls=%fused_computation.16 | convolution fusion | flops 682426112 | bytes 4424704 | tf_op jit(solution)/shard_map/dot_general | solution.py:13
  27.2 0.0 copy-start.3
  27.2 0.1 broadcast_multiply_fusion
  27.3 0.0 copy-start.1
  27.4 0.9 copy-done.3
  28.2 1.7 %fusion.7 = bf16[256,512]{1,0:T(8,128)(2,1)S(1)} fusion(bf16[256,1152]{1,0:T(8,128)(2,1)} %collective-permute-done.4, bf16[256,1152]{1,0:T(8,128)(2,1)S(1)} %bitcast.18, f32[256,1152]{1,0:T(8,128)S(1)} %broadcast_multiply_fusion, f32[]{:T(128)S(6)} %copy.16, f32[]{:T(128)S(6)} %copy.15, s32[512]{0:T(512)S(1)} %pad_add_fusion, s32[256]{0:T(256)S(1)} %pad_add_fusion.1), kind=kOutput, calls=%fused_computation.12 | convolution fusion | flops 306085888 | bytes 2624520 | tf_op jit(solution)/shard_map/dot_general | solution.py:13
  30.0 2.6 %fusion.27 = (bf16[256,1152]{1,0:T(8,128)(2,1)S(1)}, f32[256,1152]{1,0:T(8,128)}) fusion(bf16[256,512]{1,0:T(8,128)(2,1)S(1)} %fusion.7, bf16[256,1152]{1,0:T(8,128)(2,1)} %collective-permute-done.4, bf16[256,1152]{1,0:T(8,128)(2,1)S(1)} %bitcast.19, f32[]{:T(128)S(6)} %copy.15), kind=kOutput, calls=%fused_computation.59 | convolution fusion | flops 304939008 | bytes 3211268 | tf_op jit(solution)/shard_map/dot_general | solution.py:13
  32.6 0.7 fusion.26
  33.3 1.4 collective-permute-start.5
  34.8 0.6 collective-permute-start.7
  35.4 2.7 %collective-permute-start.6 = (bf16[64,1152]{1,0:T(8,128)(2,1)S(1)}, bf16[64,1152]{1,0:T(8,128)(2,1)S(1)}, u32[]{:S(2)}, u32[]{:S(2)}) collective-permute-start(bf16[64,1152]{1,0:T(8,128)(2,1)S(1)} %get-tuple-element.12), channel_id=1, source_target_pairs={{0,4},{1,5},{2,6},{3,7},{4,0},{5,1},{6,2},{7,3},{8,12},{9,13},{10,... | collective-permute-start | bytes 442376 | tf_op jit(solution)/shard_map/ppermute | solution.py:26
  38.1 1.8 %collective-permute-done.5 = bf16[64,1152]{1,0:T(8,128)(2,1)S(1)} collective-permute-done((bf16[64,1152]{1,0:T(8,128)(2,1)}, bf16[64,1152]{1,0:T(8,128)(2,1)S(1)}, u32[]{:S(2)}, u32[]{:S(2)}) %collective-permute-start.5) | collective-permute-done | bytes 147488 | tf_op jit(solution)/shard_map/ppermute | solution.py:26
  39.9 5.5 %collective-permute-done.7 = bf16[64,1152]{1,0:T(8,128)(2,1)S(1)} collective-permute-done((bf16[64,1152]{1,0:T(8,128)(2,1)}, bf16[64,1152]{1,0:T(8,128)(2,1)S(1)}, u32[]{:S(2)}, u32[]{:S(2)}) %collective-permute-start.7) | collective-permute-done | bytes 147488 | tf_op jit(solution)/shard_map/ppermute | solution.py:26
  45.4 3.6 %collective-permute-done.6 = bf16[64,1152]{1,0:T(8,128)(2,1)S(1)} collective-permute-done((bf16[64,1152]{1,0:T(8,128)(2,1)S(1)}, bf16[64,1152]{1,0:T(8,128)(2,1)S(1)}, u32[]{:S(2)}, u32[]{:S(2)}) %collective-permute-start.6) | collective-permute-done | bytes 147488 | tf_op jit(solution)/shard_map/ppermute | solution.py:26
  49.0 1.2 multiply_reduce_fusion.1
  50.2 1.2 multiply_convert_fusion.1
  51.4 0.1 constant_dynamic-slice_fusion.3
  51.6 1.4 collective-permute-start.11
  53.0 0.7 collective-permute-start.9
  53.6 3.0 %collective-permute-done.11 = bf16[64,288]{1,0:T(8,128)(2,1)S(1)} collective-permute-done((bf16[64,288]{1,0:T(8,128)(2,1)S(1)}, bf16[64,288]{1,0:T(8,128)(2,1)S(1)}, u32[]{:S(2)}, u32[]{:S(2)}) %collective-permute-start.11) | collective-permute-done | bytes 36896 | tf_op jit(solution)/shard_map/ppermute | solution.py:26
  56.6 2.3 %collective-permute-done.10 = bf16[64,288]{1,0:T(8,128)(2,1)S(1)} collective-permute-done((bf16[64,288]{1,0:T(8,128)(2,1)S(1)}, bf16[64,288]{1,0:T(8,128)(2,1)S(1)}, u32[]{:S(2)}, u32[]{:S(2)}) %collective-permute-start.10) | collective-permute-done | bytes 36896 | tf_op jit(solution)/shard_map/ppermute | solution.py:26
  59.0 0.0 collective-permute-done.9
  59.0 1.5 fusion.13
  60.5 0.0 copy-start.2
  60.5 1.1 copy-done.2
  61.6 1.1 dynamic-slice_convert_fusion.6
  62.7 1.5 collective-permute-start.12
  64.2 2.7 %collective-permute-start.17 = (bf16[144,288]{0,1:T(8,128)(2,1)}, bf16[144,288]{0,1:T(8,128)(2,1)}, u32[]{:S(2)}, u32[]{:S(2)}) collective-permute-start(bf16[144,288]{0,1:T(8,128)(2,1)} %get-tuple-element.5), channel_id=1, source_target_pairs={{0,17},{1,16},{2,19},{3,18},{4,21},{5,20},{6,23},{7,22},{8,25},{9,... | collective-permute-start | bytes 248840 | tf_op jit(solution)/shard_map/ppermute | solution.py:38
  66.9 0.7 collective-permute-start.15
  67.6 1.8 %collective-permute-done.12 = bf16[144,288]{0,1:T(8,128)(2,1)S(1)} collective-permute-done((bf16[144,288]{0,1:T(8,128)(2,1)S(1)}, bf16[144,288]{0,1:T(8,128)(2,1)S(1)}, u32[]{:S(2)}, u32[]{:S(2)}) %collective-permute-start.12) | collective-permute-done | bytes 82976 | tf_op jit(solution)/shard_map/ppermute | solution.py:38
  69.4 1.7 %collective-permute-start.14 = (bf16[144,288]{0,1:T(8,128)(2,1)S(1)}, bf16[144,288]{0,1:T(8,128)(2,1)}, u32[]{:S(2)}, u32[]{:S(2)}) collective-permute-start(bf16[144,288]{0,1:T(8,128)(2,1)S(1)} %get-tuple-element.8), channel_id=1, source_target_pairs={{0,24},{1,25},{2,26},{3,27},{4,28},{5,29},{6,30},{7,31},{8,0},{9,1... | collective-permute-start | bytes 248840 | tf_op jit(solution)/shard_map/ppermute | solution.py:38
  71.0 0.0 collective-permute-done.18
  71.1 0.6 copy-done.5
  71.7 1.5 collective-permute-start.13
  73.3 1.4 collective-permute-done.16
  74.7 0.0 collective-permute-done.15
  74.7 3.7 %collective-permute-done.14 = bf16[144,288]{0,1:T(8,128)(2,1)} collective-permute-done((bf16[144,288]{0,1:T(8,128)(2,1)S(1)}, bf16[144,288]{0,1:T(8,128)(2,1)}, u32[]{:S(2)}, u32[]{:S(2)}) %collective-permute-start.14) | collective-permute-done | bytes 82976 | tf_op jit(solution)/shard_map/ppermute | solution.py:38
  78.4 0.0 collective-permute-done.13
  78.4 1.7 %multiply_convert_fusion = bf16[144,288]{0,1:T(8,128)(2,1)S(1)} fusion(bf16[144,288]{0,1:T(8,128)(2,1)} %copy-done.5, bf16[144,288]{0,1:T(8,128)(2,1)} %collective-permute-done.17, bf16[144,288]{0,1:T(8,128)(2,1)} %collective-permute-done.16, bf16[144,288]{0,1:T(8,128)(2,1)} %collective-permute-done.15, bf16[144,288]{0,1:T(8,128)(2,1)} %collective-permute-done.14, ...), kind=kLoop, calls=%fused_computation.22 | loop fusion | flops 663552 | bytes 829444 | tf_op jit(solution)/shard_map/convert_element_type | solution.py:86
  80.1 0.8 copy.13
  80.9 0.0 all-gather.3.cloned.1.call-update
  80.9 1.8 %convolution_multiply_fusion = f32[512,1152]{1,0:T(8,128)S(1)} fusion(bf16[256,512]{1,0:T(8,128)(2,1)S(1)} %fusion.7, f32[]{:T(128)S(6)} %copy.15, f32[256,1152]{1,0:T(8,128)} %copy-done.1), kind=kOutput, calls=%fused_computation.1 | convolution fusion | flops 302874624 | bytes 3801092 | tf_op jit(solution)/shard_map/dot_general | solution.py:13
  82.7 0.1 slice.42
  82.8 0.3 collective-permute-start.8
  83.1 1.6 convolution_bitcast_fusion
  84.7 1.0 collective-permute-done.8
  85.7 1.1 fusion.8
  86.8 55.4 %all-gather.3.cloned.1.call-done = bf16[4608,288]{1,0:T(8,128)(2,1)} async-done(((bf16[144,288]{1,0:T(8,128)(2,1)}), bf16[4608,288]{1,0:T(8,128)(2,1)}) %all-gather.3.cloned.1.call-update) | async-done | bytes 2654224 | tf_op jit(solution)/shard_map/all_gather | solution.py:87
  142.2 2.7 %convert_bitcast_fusion = f32[4,2,144,4,288]{4,2,1,3,0:T(8,128)S(1)} fusion(bf16[4,4,2,144,288]{4,3,2,1,0:T(8,128)(2,1)} %bitcast.16), kind=kLoop, calls=%fused_computation | loop fusion | flops 1327104 | bytes 7962624 | tf_op jit(solution)/shard_map/convert_element_type | solution.py:89
  145.0 7.4 %copy.14 = f32[4,2,144,4,288]{4,3,2,1,0:T(4,128)} copy(f32[4,2,144,4,288]{4,2,1,3,0:T(8,128)S(1)} %convert_bitcast_fusion) | data formatting | bytes 10616832 | tf_op jit(solution)/shard_map/convert_element_type | solution.py:89
  152.4 8.1 %reshape.32 = f32[1152,1152]{1,0:T(8,128)} reshape(f32[4,2,144,4,288]{4,3,2,1,0:T(4,128)} %copy.14) | data formatting | bytes 10616832 | tf_op jit(solution)/shard_map/convert_element_type | solution.py:89
  (20 shorter events, 0.0 us)
Async XLA Ops:
  7.2 17.9 %copy-start = (bf16[1152,1152]{1,0:T(8,128)(2,1)S(1)}, bf16[1152,1152]{1,0:T(8,128)(2,1)}, u32[]{:S(2)}) copy-start(bf16[1152,1152]{1,0:T(8,128)(2,1)} %param.9) | copy-start | bytes 7962628
  7.2 135.1 %all-gather.3.cloned.1.call-start = ((), (), s32[]{:S(2)}) async-start(), calls=%async_computation | async-start | bytes 3649536 | tf_op jit(solution)/shard_map/all_gather | solution.py:87
  7.2 9.7 %collective-permute-start.3 = (bf16[64,1152]{1,0:T(8,128)(2,1)}, bf16[64,1152]{1,0:T(8,128)(2,1)S(1)}, u32[]{:S(2)}, u32[]{:S(2)}) collective-permute-start(bf16[64,1152]{1,0:T(8,128)(2,1)} %bitcast.22), channel_id=1, source_target_pairs={{0,6},{1,7},{2,0},{3,1},{4,2},{5,3},{6,4},{7,5},{8,14},{9,15},{10,... | collective-permute-start | bytes 442376 | tf_op jit(solution)/shard_map/ppermute | solution.py:26
  12.3 12.7 %collective-permute-start.2 = (bf16[64,1152]{1,0:T(8,128)(2,1)}, bf16[64,1152]{1,0:T(8,128)(2,1)S(1)}, u32[]{:S(2)}, u32[]{:S(2)}) collective-permute-start(bf16[64,1152]{1,0:T(8,128)(2,1)} %bitcast.23), channel_id=1, source_target_pairs={{0,4},{1,5},{2,6},{3,7},{4,0},{5,1},{6,2},{7,3},{8,12},{9,13},{10,... | collective-permute-start | bytes 442376 | tf_op jit(solution)/shard_map/ppermute | solution.py:26
  12.3 12.7 %collective-permute-start.1 = (bf16[64,1152]{1,0:T(8,128)(2,1)}, bf16[64,1152]{1,0:T(8,128)(2,1)S(1)}, u32[]{:S(2)}, u32[]{:S(2)}) collective-permute-start(bf16[64,1152]{1,0:T(8,128)(2,1)} %bitcast.24), channel_id=1, source_target_pairs={{0,2},{1,3},{2,4},{3,5},{4,6},{5,7},{6,0},{7,1},{8,10},{9,11},{10,... | collective-permute-start | bytes 442376 | tf_op jit(solution)/shard_map/ppermute | solution.py:26
  13.3 1.9 %collective-permute-start = (s32[256]{0:T(256)}, s32[256]{0:T(256)S(1)}, u32[]{:S(2)}, u32[]{:S(2)}) collective-permute-start(s32[256]{0:T(256)} %bitcast.20), channel_id=1, source_target_pairs={{0,1},{1,0},{2,3},{3,2},{4,5},{5,4},{6,7},{7,6},{8,9},{9,8},{10,11... | collective-permute-start | bytes 3080 | tf_op jit(solution)/shard_map/ppermute | solution.py:31
  13.3 14.0 %collective-permute-start.4 = (bf16[256,1152]{1,0:T(8,128)(2,1)}, bf16[256,1152]{1,0:T(8,128)(2,1)}, u32[]{:S(2)}, u32[]{:S(2)}) collective-permute-start(bf16[256,1152]{1,0:T(8,128)(2,1)} %bitcast.17), channel_id=1, source_target_pairs={{0,1},{1,0},{2,3},{3,2},{4,5},{5,4},{6,7},{7,6},{8,9},{9,8},{10,11... | collective-permute-start | bytes 1769480 | tf_op jit(solution)/shard_map/ppermute | solution.py:31
  16.9 10.2 %copy-start.6 = (bf16[64,1152]{1,0:T(8,128)(2,1)}, bf16[64,1152]{1,0:T(8,128)(2,1)S(1)}, u32[]{:S(2)}) copy-start(bf16[64,1152]{1,0:T(8,128)(2,1)S(1)} %collective-permute-done.3) | copy-start | bytes 442372
  25.0 2.1 %copy-start.7 = (bf16[64,1152]{1,0:T(8,128)(2,1)}, bf16[64,1152]{1,0:T(8,128)(2,1)S(1)}, u32[]{:S(2)}) copy-start(bf16[64,1152]{1,0:T(8,128)(2,1)S(1)} %collective-permute-done.2) | copy-start | bytes 442372
  25.0 2.1 %copy-start.8 = (bf16[64,1152]{1,0:T(8,128)(2,1)}, bf16[64,1152]{1,0:T(8,128)(2,1)S(1)}, u32[]{:S(2)}) copy-start(bf16[64,1152]{1,0:T(8,128)(2,1)S(1)} %collective-permute-done.1) | copy-start | bytes 442372
  27.2 1.1 copy-start.3
  27.3 2.7 %copy-start.1 = (f32[256,1152]{1,0:T(8,128)}, f32[256,1152]{1,0:T(8,128)S(1)}, u32[]{:S(2)}) copy-start(f32[256,1152]{1,0:T(8,128)S(1)} %broadcast_multiply_fusion) | copy-start | bytes 3538948
  33.3 6.6 %collective-permute-start.5 = (bf16[64,1152]{1,0:T(8,128)(2,1)}, bf16[64,1152]{1,0:T(8,128)(2,1)S(1)}, u32[]{:S(2)}, u32[]{:S(2)}) collective-permute-start(bf16[64,1152]{1,0:T(8,128)(2,1)} %get-tuple-element.10), channel_id=1, source_target_pairs={{0,6},{1,7},{2,0},{3,1},{4,2},{5,3},{6,4},{7,5},{8,14},{9,15},{10,... | collective-permute-start | bytes 442376 | tf_op jit(solution)/shard_map/ppermute | solution.py:26
  34.8 10.7 %collective-permute-start.7 = (bf16[64,1152]{1,0:T(8,128)(2,1)}, bf16[64,1152]{1,0:T(8,128)(2,1)S(1)}, u32[]{:S(2)}, u32[]{:S(2)}) collective-permute-start(bf16[64,1152]{1,0:T(8,128)(2,1)} %get-tuple-element.11), channel_id=1, source_target_pairs={{0,2},{1,3},{2,4},{3,5},{4,6},{5,7},{6,0},{7,1},{8,10},{9,11},{10,... | collective-permute-start | bytes 442376 | tf_op jit(solution)/shard_map/ppermute | solution.py:26
  35.4 13.6 %collective-permute-start.6 = (bf16[64,1152]{1,0:T(8,128)(2,1)S(1)}, bf16[64,1152]{1,0:T(8,128)(2,1)S(1)}, u32[]{:S(2)}, u32[]{:S(2)}) collective-permute-start(bf16[64,1152]{1,0:T(8,128)(2,1)S(1)} %get-tuple-element.12), channel_id=1, source_target_pairs={{0,4},{1,5},{2,6},{3,7},{4,0},{5,1},{6,2},{7,3},{8,12},{9,13},{10,... | collective-permute-start | bytes 442376 | tf_op jit(solution)/shard_map/ppermute | solution.py:26
  51.6 5.1 %collective-permute-start.11 = (bf16[64,288]{1,0:T(8,128)(2,1)S(1)}, bf16[64,288]{1,0:T(8,128)(2,1)S(1)}, u32[]{:S(2)}, u32[]{:S(2)}) collective-permute-start(bf16[64,288]{1,0:T(8,128)(2,1)S(1)} %get-tuple-element.14), channel_id=1, source_target_pairs={{0,6},{1,7},{2,0},{3,1},{4,2},{5,3},{6,4},{7,5},{8,14},{9,15},{10,... | collective-permute-start | bytes 110600 | tf_op jit(solution)/shard_map/ppermute | solution.py:26
  53.0 6.0 %collective-permute-start.10 = (bf16[64,288]{1,0:T(8,128)(2,1)S(1)}, bf16[64,288]{1,0:T(8,128)(2,1)S(1)}, u32[]{:S(2)}, u32[]{:S(2)}) collective-permute-start(bf16[64,288]{1,0:T(8,128)(2,1)S(1)} %get-tuple-element.15), channel_id=1, source_target_pairs={{0,4},{1,5},{2,6},{3,7},{4,0},{5,1},{6,2},{7,3},{8,12},{9,13},{10,... | collective-permute-start | bytes 110600 | tf_op jit(solution)/shard_map/ppermute | solution.py:26
  53.0 6.0 %collective-permute-start.9 = (bf16[64,288]{1,0:T(8,128)(2,1)S(1)}, bf16[64,288]{1,0:T(8,128)(2,1)S(1)}, u32[]{:S(2)}, u32[]{:S(2)}) collective-permute-start(bf16[64,288]{1,0:T(8,128)(2,1)S(1)} %get-tuple-element.16), channel_id=1, source_target_pairs={{0,2},{1,3},{2,4},{3,5},{4,6},{5,7},{6,0},{7,1},{8,10},{9,11},{10,... | collective-permute-start | bytes 110600 | tf_op jit(solution)/shard_map/ppermute | solution.py:26
  60.5 1.1 copy-start.2
  62.7 6.7 %collective-permute-start.12 = (bf16[144,288]{0,1:T(8,128)(2,1)S(1)}, bf16[144,288]{0,1:T(8,128)(2,1)S(1)}, u32[]{:S(2)}, u32[]{:S(2)}) collective-permute-start(bf16[144,288]{0,1:T(8,128)(2,1)S(1)} %get-tuple-element.3), channel_id=1, source_target_pairs={{0,8},{1,9},{2,10},{3,11},{4,12},{5,13},{6,14},{7,15},{8,16},{9,17... | collective-permute-start | bytes 248840 | tf_op jit(solution)/shard_map/ppermute | solution.py:38
  64.2 6.8 %collective-permute-start.18 = (bf16[144,288]{0,1:T(8,128)(2,1)S(1)}, bf16[144,288]{0,1:T(8,128)(2,1)S(1)}, u32[]{:S(2)}, u32[]{:S(2)}) collective-permute-start(bf16[144,288]{0,1:T(8,128)(2,1)S(1)} %get-tuple-element.4), channel_id=1, source_target_pairs={{0,25},{1,24},{2,27},{3,26},{4,29},{5,28},{6,31},{7,30},{8,1},{9,0... | collective-permute-start | bytes 248840 | tf_op jit(solution)/shard_map/ppermute | solution.py:38
  64.2 9.0 %collective-permute-start.17 = (bf16[144,288]{0,1:T(8,128)(2,1)}, bf16[144,288]{0,1:T(8,128)(2,1)}, u32[]{:S(2)}, u32[]{:S(2)}) collective-permute-start(bf16[144,288]{0,1:T(8,128)(2,1)} %get-tuple-element.5), channel_id=1, source_target_pairs={{0,17},{1,16},{2,19},{3,18},{4,21},{5,20},{6,23},{7,22},{8,25},{9,... | collective-permute-start | bytes 248840 | tf_op jit(solution)/shard_map/ppermute | solution.py:38
  66.9 7.8 %collective-permute-start.16 = (bf16[144,288]{0,1:T(8,128)(2,1)}, bf16[144,288]{0,1:T(8,128)(2,1)}, u32[]{:S(2)}, u32[]{:S(2)}) collective-permute-start(bf16[144,288]{0,1:T(8,128)(2,1)} %get-tuple-element.6), channel_id=1, source_target_pairs={{0,9},{1,8},{2,11},{3,10},{4,13},{5,12},{6,15},{7,14},{8,17},{9,16... | collective-permute-start | bytes 248840 | tf_op jit(solution)/shard_map/ppermute | solution.py:38
  66.9 7.8 %collective-permute-start.15 = (bf16[144,288]{0,1:T(8,128)(2,1)S(1)}, bf16[144,288]{0,1:T(8,128)(2,1)}, u32[]{:S(2)}, u32[]{:S(2)}) collective-permute-start(bf16[144,288]{0,1:T(8,128)(2,1)S(1)} %get-tuple-element.7), channel_id=1, source_target_pairs={{0,1},{1,0},{2,3},{3,2},{4,5},{5,4},{6,7},{7,6},{8,9},{9,8},{10,11... | collective-permute-start | bytes 248840 | tf_op jit(solution)/shard_map/ppermute | solution.py:38
  69.4 1.7 %copy-start.4 = (bf16[144,288]{0,1:T(8,128)(2,1)}, bf16[144,288]{0,1:T(8,128)(2,1)S(1)}, u32[]{:S(2)}) copy-start(bf16[144,288]{0,1:T(8,128)(2,1)S(1)} %collective-permute-done.12) | copy-start | bytes 248836
  69.4 9.0 %collective-permute-start.14 = (bf16[144,288]{0,1:T(8,128)(2,1)S(1)}, bf16[144,288]{0,1:T(8,128)(2,1)}, u32[]{:S(2)}, u32[]{:S(2)}) collective-permute-start(bf16[144,288]{0,1:T(8,128)(2,1)S(1)} %get-tuple-element.8), channel_id=1, source_target_pairs={{0,24},{1,25},{2,26},{3,27},{4,28},{5,29},{6,30},{7,31},{8,0},{9,1... | collective-permute-start | bytes 248840 | tf_op jit(solution)/shard_map/ppermute | solution.py:38
  71.1 0.7 copy-start.5
  71.7 6.7 %collective-permute-start.13 = (bf16[144,288]{0,1:T(8,128)(2,1)S(1)}, bf16[144,288]{0,1:T(8,128)(2,1)}, u32[]{:S(2)}, u32[]{:S(2)}) collective-permute-start(bf16[144,288]{0,1:T(8,128)(2,1)S(1)} %get-tuple-element.9), channel_id=1, source_target_pairs={{0,16},{1,17},{2,18},{3,19},{4,20},{5,21},{6,22},{7,23},{8,24},{9,... | collective-permute-start | bytes 248840 | tf_op jit(solution)/shard_map/ppermute | solution.py:38
  82.8 2.9 %collective-permute-start.8 = (f32[256,1152]{1,0:T(8,128)S(1)}, f32[256,1152]{1,0:T(8,128)S(1)}, u32[]{:S(2)}, u32[]{:S(2)}) collective-permute-start(f32[256,1152]{1,0:T(8,128)S(1)} %slice.42), channel_id=1, source_target_pairs={{0,1},{1,0},{2,3},{3,2},{4,5},{5,4},{6,7},{7,6},{8,9},{9,8},{10,11... | collective-permute-start | bytes 3538952 | tf_op jit(solution)/shard_map/ppermute | solution.py:31
Sparse Core Ops, SparseCore 0:
  81.0 61.1 all-gather.2

commit v2 on v1

v2 whole, which is shorter than its diff:
```python
import functools

import jax
import jax.numpy as jnp
from jax import lax
from jax.experimental import pallas as pl
from jax.experimental.pallas import tpu as pltpu
from jax.sharding import PartitionSpec as P

FIRST = (((0,), (0,)), ((), ()))
LAST = (((1,), (1,)), ((), ()))
F32 = jnp.float32
BF16 = jnp.bfloat16


def dot(a, b, dims=(((1,), (0,)), ((), ()))):
    return lax.dot_general(a, b, dims, preferred_element_type=F32)


def weight_kernel(n_x, n_img, lanes, factor, has_acc, *refs):
    out = refs[-1]
    acc = refs[0] if has_acc else None
    refs = refs[has_acc:-1]
    depth, width = out.shape[0], out.shape[1] // 3
    xs, gs = refs[:n_x], refs[n_x:]

    def columns(j, carry):
        tile = pl.ds(pl.multiple_of(j * width, width), width)
        x_t, g = [], []
        for x_ref, g_ref in zip(xs, gs):
            for at in range(x_ref.shape[0] // depth):
                x_t.append(x_ref[at * depth : (at + 1) * depth, lanes])
                g.append(g_ref[at * n_img : (at + 1) * n_img, tile])
        total = dot(jnp.concatenate(x_t, axis=1), jnp.concatenate(g))
        if has_acc:
            total = total + acc[:, tile]
        out[:, tile] = total * factor
        return carry

    lax.fori_loop(0, 3, columns, 0)


def weight_sum(acc, xs, gs, first, n_img, factor):
    depth = gs[0].shape[1]
    images = 2 * sum(g.shape[0] for g in gs)
    if images > 2048:
        for x, g in zip(xs, gs):
            for at in range(g.shape[0] // n_img):
                x_t = x[at * depth : (at + 1) * depth, first : first + n_img]
                term = dot(x_t, g[at * n_img : (at + 1) * n_img])
                acc = term if acc is None else acc + term
        return acc
    has_acc = acc is not None
    operands = ([acc] if has_acc else []) + xs + gs
    return pl.pallas_call(
        functools.partial(
            weight_kernel,
            len(xs),
            n_img,
            slice(first, first + n_img),
            factor,
            int(has_acc),
        ),
        out_shape=jax.ShapeDtypeStruct((depth, depth), F32),
        in_specs=[pl.BlockSpec(memory_space=pltpu.VMEM)] * len(operands),
        out_specs=pl.BlockSpec(memory_space=pltpu.VMEM),
        compiler_params=pltpu.CompilerParams(vmem_limit_bytes=48 * 2**20),
        cost_estimate=pl.CostEstimate(
            flops=2 * images * depth * depth,
            bytes_accessed=4 * images * depth + 4 * depth * depth,
            transcendentals=0,
        ),
    )(*operands)


def on_device(x, captions, labels, weight, scale, offset):
    x, captions, labels = x[0], captions[0], labels[0]
    n_img, depth = x.shape
    n_cap = captions.shape[0]
    nd, nb = lax.axis_size("dp"), lax.axis_size("blk")
    nz = nb // 2
    b = lax.axis_index("blk")
    z, c = b // 2, b % 2

    def along_z(v, k):
        return lax.ppermute(v, "blk", [(i, i ^ (2 * k)) for i in range(nb)])

    def along_d(v, k):
        return lax.ppermute(v, "dp", [(i, i ^ k) for i in range(nd)])

    def swap(v):
        return lax.ppermute(v, "blk", [(i, i ^ 1) for i in range(nb)])

    xs = jnp.concatenate([x] + [along_z(x, k) for k in range(1, nz)])
    caps = jnp.concatenate([captions, swap(captions)])
    labs = jnp.concatenate([labels, swap(labels)])
    ids = jnp.concatenate(
        [
            ((z ^ k) * 2 + c) * n_img + jnp.arange(n_img, dtype=jnp.int32)
            for k in range(nz)
        ]
    )
    bits = nd.bit_length() - 1

    def over_d(v):
        for i in range(bits):
            perm = []
            for j in range(nd):
                for m in range(nb):
                    to = j ^ (1 << ((i + m % 2) % bits))
                    perm.append((j * nb + m, to * nb + m))
            v = jnp.concatenate(v) if i else v[0]
            v = [v, lax.ppermute(v, ("dp", "blk"), perm)]
        return v

    x_t = over_d([xs.T])

    embed = dot(xs, weight)
    inv_norm = lax.rsqrt(jnp.sum(embed * embed, axis=1, keepdims=True) + 1e-06)
    unit_f = embed * inv_norm
    unit = unit_f.astype(BF16)
    logits = scale * dot(unit, caps, LAST) + offset
    sign = jnp.where(labs[None, :] == ids[:, None], 1.0, -1.0).astype(F32)
    dlogit = (-sign * jax.nn.sigmoid(-sign * logits)).astype(BF16)

    part = scale * dot(dlogit, caps)
    own = part[:n_img]
    back = [
        along_z(part[k * n_img : (k + 1) * n_img].astype(BF16), k)
        for k in range(1, nz)
    ]
    back, x_t = lax.optimization_barrier((back, x_t))
    for v in back:
        own = own + v.astype(F32)

    adjoint = scale * dot(dlogit, unit, FIRST)
    adjoint = adjoint[:n_cap] + swap(adjoint[n_cap:])

    u = unit_f[:n_img]
    radial = jnp.sum(u * own, axis=1, keepdims=True)
    ge = ((own - u * radial) * inv_norm[:n_img]).astype(BF16)
    grad_features = dot(ge, weight, LAST)

    near = [ge] + [along_z(ge, k) for k in range(1, nz // 2)]
    far = [along_z(ge, k) for k in range(nz // 2, nz)]
    n_near = n_img * (nz // 2)
    near, far = over_d([jnp.concatenate(near)]), over_d([jnp.concatenate(far)])
    small = nd * nb * n_img <= 2048
    if small:
        x_t, near, far = (v + [swap(p) for p in v] for v in (x_t, near, far))
    grad_weight = weight_sum(None, x_t, near, 0, n_near, 1.0)
    grad_weight = weight_sum(grad_weight, x_t, far, n_near, n_near, 1.0 / nd)
    if not small:
        grad_weight = (grad_weight + swap(grad_weight)) / nd
    return (grad_features[None], adjoint[None], grad_weight)


def solution(mesh):
    placed = (P("dp", "blk", None), P("dp", "blk", None), P("dp", "blk"), P(), P(), P())
    return jax.shard_map(
        on_device,
        mesh=mesh,
        in_specs=placed,
        out_specs=(P("dp", "blk", None), P("dp", "blk", None), P()),
        check_vma=False,
    )
```

time: 168 us -> 116 us (0.69)
  waiting for transfers between devices: 88.6 us -> 60.9 us
  local copies, waits for them, and re-layouts: 21 us -> 2.51 us
  Pallas kernels: 0 us -> 17.2 us
  between operations: 15.5 us -> 2.09 us
  matrix products: 11.4 us -> 5.73 us
  other arithmetic: 8.93 us -> 4.06 us
    all_gather x1 -> x0, waiting for transfers between devices: 55.4 us -> none  [on_device(): whole = lax.all_gather(piece, ('dp', 'blk'), axis=0)]
    ppermute x16 -> x15, waiting for transfers between devices: 32.2 us -> 60.9 us  [the longest x9 40.9 us: along_z(): return lax.ppermute(v, 'blk', [(i, i ^ 2 * k) for i in range(nb)])]
    convert_element_type x4 -> x0, local copies, waits for them, and re-layouts: 17.4 us -> none  [the longest x2 15.5 us: on_device(): grad_weight = whole.reshape(depth, depth).astype(F32)]
    pallas_call x0 -> x2, Pallas kernels: none -> 17.2 us  [weight_sum(): pl.pallas_call(functools.partial(weight_kernel, len(xs), n_img, slice(fir...]
    dot_general x6 -> x5, matrix products: 11.4 us -> 5.73 us  [dot(): return lax.dot_general(a, b, dims, preferred_element_type=F32)]
    convert_element_type x2 -> x0, other arithmetic: 4.48 us -> none  [the longest x1 2.73 us: on_device(): grad_weight = whole.reshape(depth, depth).astype(F32)]
    ppermute x16 -> x15, starting transfers between devices: 21.1 us -> 21.3 us  [the longest x9 13.8 us: along_z(): return lax.ppermute(v, 'blk', [(i, i ^ 2 * k) for i in range(nb)])]
  transfers between devices with their start and end apart: 20 -> 24, of which waited for: 12 -> 10; matrix products, arithmetic and copies ran while one was open for 5% -> 8% of each run, Pallas kernels for 0% -> 7%
where the time goes in v2:
time: 116 us
  waiting for transfers between devices  60.9 us (52%)
  starting transfers between devices  23.4 us (20%)
  Pallas kernels  17.2 us (15%)
  matrix products  5.73 us (5%)
  other arithmetic  4.06 us (3%)
  local copies, waits for them, and re-layouts  2.51 us (2%)
  between operations  2.09 us (2%)
    ppermute x9, waiting for transfers between devices, along_z(): return lax.ppermute(v, 'blk', [(i, i ^ 2 * k) for i in range(nb)])  40.9 us
    ppermute x6, waiting for transfers between devices, over_d(): v = [v, lax.ppermute(v, ('dp', 'blk'), perm)]  20 us
    pallas_call x2, Pallas kernels, weight_sum(): pl.pallas_call(functools.partial(weight_kernel, len(xs), n_img, slice(fir...  17.2 us
    ppermute x9, starting transfers between devices, along_z(): return lax.ppermute(v, 'blk', [(i, i ^ 2 * k) for i in range(nb)])  13.8 us
    ppermute x6, starting transfers between devices, over_d(): v = [v, lax.ppermute(v, ('dp', 'blk'), perm)]  7.54 us
    dot_general x5, matrix products, dot(): return lax.dot_general(a, b, dims, preferred_element_type=F32)  5.73 us
    unnamed x9, local copies, waits for them, and re-layouts  2.36 us
  transfers between devices with their start and end apart: 24, of which 10 were waited for; matrix products, arithmetic and copies ran while one was open for 8% of the time, Pallas kernels for 7%

profile of v2, /device:TPU:0, one launch (start us, length us, event | category | flops | bytes accessed | tf_op | source)
XLA Modules:
  0.0 115.9 jit_solution(12423873550037626886)
XLA Ops:
  0.6 0.0 copy-start
  0.6 1.3 %copy.9 = bf16[1,64,1152]{1,2,0:T(8,128)(2,1)S(1)} copy(bf16[1,64,1152]{2,1,0:T(8,128)(2,1)} %param.6) | data formatting | bytes 294912 | tf_op args[0]
  1.9 5.1 %collective-permute-start.3 = (bf16[64,1152]{0,1:T(8,128)(2,1)S(1)}, bf16[64,1152]{0,1:T(8,128)(2,1)}, u32[]{:S(2)}, u32[]{:S(2)}) collective-permute-start(bf16[64,1152]{0,1:T(8,128)(2,1)S(1)} %bitcast.14), channel_id=1, source_target_pairs={{0,6},{1,7},{2,4},{3,5},{4,2},{5,3},{6,0},{7,1},{8,14},{9,15},{10,... | collective-permute-start | bytes 442376 | tf_op jit(solution)/shard_map/ppermute | solution.py:86
  7.0 0.0 collective-permute-start.2
  7.0 0.6 collective-permute-start.1
  7.7 0.0 collective-permute-start
  7.7 0.5 collective-permute-start.4
  8.2 0.1 pad_add_fusion.1
  9.6 0.0 collective-permute-done
  9.6 0.7 pad_add_fusion
  10.3 4.8 %collective-permute-done.3 = bf16[64,1152]{0,1:T(8,128)(2,1)} collective-permute-done((bf16[64,1152]{0,1:T(8,128)(2,1)S(1)}, bf16[64,1152]{0,1:T(8,128)(2,1)}, u32[]{:S(2)}, u32[]{:S(2)}) %collective-permute-start.3) | collective-permute-done | bytes 147488 | tf_op jit(solution)/shard_map/ppermute | solution.py:86
  15.1 17.1 %collective-permute-done.2 = bf16[64,1152]{0,1:T(8,128)(2,1)} collective-permute-done((bf16[64,1152]{0,1:T(8,128)(2,1)S(1)}, bf16[64,1152]{0,1:T(8,128)(2,1)}, u32[]{:S(2)}, u32[]{:S(2)}) %collective-permute-start.2) | collective-permute-done | bytes 147488 | tf_op jit(solution)/shard_map/ppermute | solution.py:86
  32.3 0.0 collective-permute-done.1
  32.3 1.5 %fusion.15 = bf16[1152,256]{1,0:T(8,128)(2,1)S(1)} fusion(bf16[64,1152]{0,1:T(8,128)(2,1)} %collective-permute-done.3, bf16[64,1152]{0,1:T(8,128)(2,1)} %collective-permute-done.2, bf16[64,1152]{0,1:T(8,128)(2,1)} %collective-permute-done.1, bf16[64,1152]{0,1:T(8,128)(2,1)S(1)} %bitcast.17), kind=kLoop, calls=%fused_computation.41 | loop fusion | flops 2359296 | bytes 1179648 | tf_op jit(solution)/shard_map/transpose | solution.py:116
  33.8 1.6 %collective-permute-start.8 = (bf16[1152,256]{1,0:T(8,128)(2,1)S(1)}, bf16[1152,256]{1,0:T(8,128)(2,1)S(1)}, u32[]{:S(2)}, u32[]{:S(2)}) collective-permute-start(bf16[1152,256]{1,0:T(8,128)(2,1)S(1)} %fusion.15), channel_id=1, source_target_pairs={{0,8},{1,17},{2,10},{3,19},{4,12},{5,21},{6,14},{7,23},{8,0},{9,25... | collective-permute-start | bytes 1769480 | tf_op jit(solution)/shard_map/ppermute | solution.py:113
  35.4 2.3 %multiply_reduce_fusion = (f32[256]{0:T(256)S(1)}, f32[256,1152]{1,0:T(8,128)S(1)}) fusion(bf16[1152,1152]{1,0:T(8,128)(2,1)S(1)} %copy-done, bf16[64,1152]{0,1:T(8,128)(2,1)} %collective-permute-done.3, bf16[64,1152]{0,1:T(8,128)(2,1)} %collective-permute-done.2, bf16[64,1152]{0,1:T(8,128)(2,1)} %collective-permute-done.1, bf16[64,1152]{0,1:T(8,128)(2,1)S(1)} %bitcast.18), kind=kOutput, calls=%fused_computation.16 | convolution fusion | flops 682426112 | bytes 4424704 | tf_op jit(solution)/shard_map/dot_general | solution.py:17
  37.7 0.2 broadcast_multiply_fusion
  37.9 0.0 copy-start.1
  37.9 5.9 %collective-permute-done.8 = bf16[1152,256]{1,0:T(8,128)(2,1)S(1)} collective-permute-done((bf16[1152,256]{1,0:T(8,128)(2,1)S(1)}, bf16[1152,256]{1,0:T(8,128)(2,1)S(1)}, u32[]{:S(2)}, u32[]{:S(2)}) %collective-permute-start.8) | collective-permute-done | bytes 589856 | tf_op jit(solution)/shard_map/ppermute | solution.py:113
  43.7 0.1 pad_maximum_fusion.1.refs_0_.refs_1_
  43.8 1.6 %collective-permute-start.9 = (bf16[2304,256]{1,0:T(8,128)(2,1)S(1)}, bf16[2304,256]{1,0:T(8,128)(2,1)S(1)}, u32[]{:S(2)}, u32[]{:S(2)}) collective-permute-start(bf16[2304,256]{1,0:T(8,128)(2,1)S(1)} %pad_maximum_fusion.1.refs_0_.refs_1_), channel_id=1, source_target_pairs={{0,16},{1,9},{2,18},{3,11},{4,20},{5,13},{6,22},{7,15},{8,24},{9,1... | collective-permute-start | bytes 3538952 | tf_op jit(solution)/shard_map/ppermute | solution.py:113
  45.4 0.0 collective-permute-done.4
  45.4 0.7 fusion.7
  46.1 0.5 fusion.18
  46.7 2.5 %collective-permute-start.7 = (bf16[64,1152]{1,0:T(8,128)(2,1)S(1)}, bf16[64,1152]{1,0:T(8,128)(2,1)S(1)}, u32[]{:S(2)}, u32[]{:S(2)}) collective-permute-start(bf16[64,1152]{1,0:T(8,128)(2,1)S(1)} %get-tuple-element.13), channel_id=1, source_target_pairs={{0,6},{1,7},{2,4},{3,5},{4,2},{5,3},{6,0},{7,1},{8,14},{9,15},{10,... | collective-permute-start | bytes 442376 | tf_op jit(solution)/shard_map/ppermute | solution.py:86
  49.2 0.0 collective-permute-start.6
  49.2 1.9 %collective-permute-start.5 = (bf16[64,1152]{1,0:T(8,128)(2,1)S(1)}, bf16[64,1152]{1,0:T(8,128)(2,1)S(1)}, u32[]{:S(2)}, u32[]{:S(2)}) collective-permute-start(bf16[64,1152]{1,0:T(8,128)(2,1)S(1)} %get-tuple-element.15), channel_id=1, source_target_pairs={{0,2},{1,3},{2,0},{3,1},{4,6},{5,7},{6,4},{7,5},{8,10},{9,11},{10,... | collective-permute-start | bytes 442376 | tf_op jit(solution)/shard_map/ppermute | solution.py:86
  51.1 4.2 %collective-permute-done.7 = bf16[64,1152]{1,0:T(8,128)(2,1)S(1)} collective-permute-done((bf16[64,1152]{1,0:T(8,128)(2,1)S(1)}, bf16[64,1152]{1,0:T(8,128)(2,1)S(1)}, u32[]{:S(2)}, u32[]{:S(2)}) %collective-permute-start.7) | collective-permute-done | bytes 147488 | tf_op jit(solution)/shard_map/ppermute | solution.py:86
  55.3 4.8 %collective-permute-done.6 = bf16[64,1152]{1,0:T(8,128)(2,1)S(1)} collective-permute-done((bf16[64,1152]{1,0:T(8,128)(2,1)S(1)}, bf16[64,1152]{1,0:T(8,128)(2,1)S(1)}, u32[]{:S(2)}, u32[]{:S(2)}) %collective-permute-start.6) | collective-permute-done | bytes 147488 | tf_op jit(solution)/shard_map/ppermute | solution.py:86
  60.2 0.0 collective-permute-done.5
  60.2 0.0 collective-permute-done.9.refs_1_.refs_2_
  60.2 0.2 multiply_reduce_fusion.1
  60.3 0.1 multiply_convert_fusion
  60.5 0.1 collective-permute-start.13
  60.5 2.5 %collective-permute-start.19 = (bf16[64,1152]{1,0:T(8,128)(2,1)S(1)}, bf16[64,1152]{1,0:T(8,128)(2,1)S(1)}, u32[]{:S(2)}, u32[]{:S(2)}) collective-permute-start(bf16[64,1152]{1,0:T(8,128)(2,1)S(1)} %multiply_convert_fusion), channel_id=1, source_target_pairs={{0,6},{1,7},{2,4},{3,5},{4,2},{5,3},{6,0},{7,1},{8,14},{9,15},{10,... | collective-permute-start | bytes 442376 | tf_op jit(solution)/shard_map/ppermute | solution.py:86
  63.0 1.0 collective-permute-start.18
  64.0 3.6 %collective-permute-done.13 = bf16[64,1152]{1,0:T(8,128)(2,1)S(1)} collective-permute-done((bf16[64,1152]{1,0:T(8,128)(2,1)S(1)}, bf16[64,1152]{1,0:T(8,128)(2,1)S(1)}, u32[]{:S(2)}, u32[]{:S(2)}) %collective-permute-start.13) | collective-permute-done | bytes 147488 | tf_op jit(solution)/shard_map/ppermute | solution.py:86
  67.6 0.4 collective-permute-start.14
  68.1 0.6 convolution_multiply_fusion
  68.6 0.1 slice.42
  68.7 0.1 collective-permute-start.10
  68.8 0.5 collective-permute-start.11
  69.3 0.9 collective-permute-done.19
  70.2 0.0 collective-permute-start.12
  70.2 5.3 %collective-permute-done.18 = bf16[64,1152]{1,0:T(8,128)(2,1)S(1)} collective-permute-done((bf16[64,1152]{1,0:T(8,128)(2,1)S(1)}, bf16[64,1152]{1,0:T(8,128)(2,1)S(1)}, u32[]{:S(2)}, u32[]{:S(2)}) %collective-permute-start.18) | collective-permute-done | bytes 147488 | tf_op jit(solution)/shard_map/ppermute | solution.py:86
  75.6 0.3 collective-permute-start.20
  75.9 0.0 collective-permute-done.14
  75.9 1.9 %collective-permute-start.15 = (bf16[256,1152]{1,0:T(8,128)(2,1)S(1)}, bf16[256,1152]{1,0:T(8,128)(2,1)S(1)}, u32[]{:S(2)}, u32[]{:S(2)}) collective-permute-start(bf16[256,1152]{1,0:T(8,128)(2,1)S(1)} %pad_maximum_fusion.5.refs_4_), channel_id=1, source_target_pairs={{0,16},{1,9},{2,18},{3,11},{4,20},{5,13},{6,22},{7,15},{8,24},{9,1... | collective-permute-start | bytes 1769480 | tf_op jit(solution)/shard_map/ppermute | solution.py:113
  77.9 7.6 %collective-permute-done.20 = bf16[128,1152]{1,0:T(8,128)(2,1)S(1)} collective-permute-done((bf16[128,1152]{1,0:T(8,128)(2,1)S(1)}, bf16[128,1152]{1,0:T(8,128)(2,1)S(1)}, u32[]{:S(2)}, u32[]{:S(2)}) %collective-permute-start.20) | collective-permute-done | bytes 294944 | tf_op jit(solution)/shard_map/ppermute | solution.py:113
  85.5 1.8 %collective-permute-start.21 = (bf16[256,1152]{1,0:T(8,128)(2,1)S(1)}, bf16[256,1152]{1,0:T(8,128)(2,1)S(1)}, u32[]{:S(2)}, u32[]{:S(2)}) collective-permute-start(bf16[256,1152]{1,0:T(8,128)(2,1)S(1)} %constant_dynamic-update-slice_fusion.refs_5_), channel_id=1, source_target_pairs={{0,16},{1,9},{2,18},{3,11},{4,20},{5,13},{6,22},{7,15},{8,24},{9,1... | collective-permute-start | bytes 1769480 | tf_op jit(solution)/shard_map/ppermute | solution.py:113
  87.3 0.5 collective-permute-start.17
  87.8 1.1 fusion.8
  89.0 6.5 %collective-permute-done.21.refs_6_ = bf16[256,1152]{1,0:T(8,128)(2,1)S(1)} collective-permute-done((bf16[256,1152]{1,0:T(8,128)(2,1)S(1)}, bf16[256,1152]{1,0:T(8,128)(2,1)S(1)}, u32[]{:S(2)}, u32[]{:S(2)}) %collective-permute-start.21) | collective-permute-done | bytes 589856 | tf_op jit(solution)/shard_map/ppermute | solution.py:113
  95.5 0.0 collective-permute-start.22
  95.5 0.0 collective-permute-done.16.refs_6_
  95.5 0.5 collective-permute-start.23
  96.0 1.7 %convolution_bitcast_fusion = f32[1,64,1152]{2,1,0:T(8,128)} fusion(bf16[64,1152]{1,0:T(8,128)(2,1)S(1)} %multiply_convert_fusion, bf16[1152,1152]{1,0:T(8,128)(2,1)S(1)} %copy-done), kind=kOutput, calls=%fused_computation.2 | convolution fusion | flops 169869312 | bytes 3096576 | tf_op jit(solution)/shard_map/dot_general | solution.py:17
  97.6 0.0 collective-permute-done.11.refs_2_.refs_3_
  97.7 0.0 collective-permute-done.12.refs_3_.refs_4_
  97.7 1.0 copy-done.2
  98.7 0.0 collective-permute-done.17.refs_7_
  98.7 7.8 %shard_map.85.refs_0_ = f32[1152,1152]{1,0:T(8,128)} custom-call(bf16[2304,256]{1,0:T(8,128)(2,1)S(1)} %pad_maximum_fusion.1.refs_0_.refs_1_, bf16[2304,256]{1,0:T(8,128)(2,1)S(1)} %collective-permute-done.9.refs_1_.refs_2_, bf16[2304,256]{1,0:T(8,128)(2,1)S(1)} %collective-permute-done.11.refs_2_.refs_3_, bf16[2304,256]{1,0:T(8,128)(2,1)} %copy-done.2, ...), custom_call_target="tpu_custom_call" | custom-call | flops 5435817984 | bytes 14745600 | tf_op jit(solution)/shard_map/pallas_call | solution.py:55
  106.5 0.0 collective-permute-done.23.refs_8_
  106.5 9.4 %shard_map.86 = f32[1152,1152]{1,0:T(8,128)} custom-call(f32[1152,1152]{1,0:T(8,128)} %shard_map.85.refs_0_, bf16[2304,256]{1,0:T(8,128)(2,1)S(1)} %pad_maximum_fusion.1.refs_0_.refs_1_, bf16[2304,256]{1,0:T(8,128)(2,1)S(1)} %collective-permute-done.9.refs_1_.refs_2_, bf16[2304,256]{1,0:T(8,128)(2,1)S(1)} %collective-permute-done.11.refs_2_.refs_3_, ...), custom_call_target="tpu_custom_call" | custom-call | flops 5435817984 | bytes 14745600 | tf_op jit(solution)/shard_map/pallas_call | solution.py:55
  (18 shorter events, 0.2 us)
Async XLA Ops:
  0.6 34.7 %copy-start = (bf16[1152,1152]{1,0:T(8,128)(2,1)S(1)}, bf16[1152,1152]{1,0:T(8,128)(2,1)}, u32[]{:S(2)}) copy-start(bf16[1152,1152]{1,0:T(8,128)(2,1)} %param.9) | copy-start | bytes 7962628
  1.9 13.2 %collective-permute-start.3 = (bf16[64,1152]{0,1:T(8,128)(2,1)S(1)}, bf16[64,1152]{0,1:T(8,128)(2,1)}, u32[]{:S(2)}, u32[]{:S(2)}) collective-permute-start(bf16[64,1152]{0,1:T(8,128)(2,1)S(1)} %bitcast.14), channel_id=1, source_target_pairs={{0,6},{1,7},{2,4},{3,5},{4,2},{5,3},{6,0},{7,1},{8,14},{9,15},{10,... | collective-permute-start | bytes 442376 | tf_op jit(solution)/shard_map/ppermute | solution.py:86
  7.0 25.2 %collective-permute-start.2 = (bf16[64,1152]{0,1:T(8,128)(2,1)S(1)}, bf16[64,1152]{0,1:T(8,128)(2,1)}, u32[]{:S(2)}, u32[]{:S(2)}) collective-permute-start(bf16[64,1152]{0,1:T(8,128)(2,1)S(1)} %bitcast.15), channel_id=1, source_target_pairs={{0,4},{1,5},{2,6},{3,7},{4,0},{5,1},{6,2},{7,3},{8,12},{9,13},{10,... | collective-permute-start | bytes 442376 | tf_op jit(solution)/shard_map/ppermute | solution.py:86
  7.0 25.2 %collective-permute-start.1 = (bf16[64,1152]{0,1:T(8,128)(2,1)S(1)}, bf16[64,1152]{0,1:T(8,128)(2,1)}, u32[]{:S(2)}, u32[]{:S(2)}) collective-permute-start(bf16[64,1152]{0,1:T(8,128)(2,1)S(1)} %bitcast.16), channel_id=1, source_target_pairs={{0,2},{1,3},{2,0},{3,1},{4,6},{5,7},{6,4},{7,5},{8,10},{9,11},{10,... | collective-permute-start | bytes 442376 | tf_op jit(solution)/shard_map/ppermute | solution.py:86
  7.7 1.9 %collective-permute-start = (s32[256]{0:T(256)}, s32[256]{0:T(256)S(1)}, u32[]{:S(2)}, u32[]{:S(2)}) collective-permute-start(s32[256]{0:T(256)} %bitcast.22), channel_id=1, source_target_pairs={{0,1},{1,0},{2,3},{3,2},{4,5},{5,4},{6,7},{7,6},{8,9},{9,8},{10,11... | collective-permute-start | bytes 3080 | tf_op jit(solution)/shard_map/ppermute | solution.py:92
  7.7 37.7 %collective-permute-start.4 = (bf16[256,1152]{1,0:T(8,128)(2,1)}, bf16[256,1152]{1,0:T(8,128)(2,1)S(1)}, u32[]{:S(2)}, u32[]{:S(2)}) collective-permute-start(bf16[256,1152]{1,0:T(8,128)(2,1)} %bitcast.19), channel_id=1, source_target_pairs={{0,1},{1,0},{2,3},{3,2},{4,5},{5,4},{6,7},{7,6},{8,9},{9,8},{10,11... | collective-permute-start | bytes 1769480 | tf_op jit(solution)/shard_map/ppermute | solution.py:92
  33.8 9.9 %collective-permute-start.8 = (bf16[1152,256]{1,0:T(8,128)(2,1)S(1)}, bf16[1152,256]{1,0:T(8,128)(2,1)S(1)}, u32[]{:S(2)}, u32[]{:S(2)}) collective-permute-start(bf16[1152,256]{1,0:T(8,128)(2,1)S(1)} %fusion.15), channel_id=1, source_target_pairs={{0,8},{1,17},{2,10},{3,19},{4,12},{5,21},{6,14},{7,23},{8,0},{9,25... | collective-permute-start | bytes 1769480 | tf_op jit(solution)/shard_map/ppermute | solution.py:113
  37.9 7.5 %copy-start.1 = (bf16[1,256,1152]{2,1,0:T(8,128)(2,1)S(1)}, bf16[1,256,1152]{2,1,0:T(8,128)(2,1)}, u32[]{:S(2)}) copy-start(bf16[1,256,1152]{2,1,0:T(8,128)(2,1)} %param.7) | copy-start | bytes 1769476
  43.8 16.3 %collective-permute-start.9 = (bf16[2304,256]{1,0:T(8,128)(2,1)S(1)}, bf16[2304,256]{1,0:T(8,128)(2,1)S(1)}, u32[]{:S(2)}, u32[]{:S(2)}) collective-permute-start(bf16[2304,256]{1,0:T(8,128)(2,1)S(1)} %pad_maximum_fusion.1.refs_0_.refs_1_), channel_id=1, source_target_pairs={{0,16},{1,9},{2,18},{3,11},{4,20},{5,13},{6,22},{7,15},{8,24},{9,1... | collective-permute-start | bytes 3538952 | tf_op jit(solution)/shard_map/ppermute | solution.py:113
  46.7 8.7 %collective-permute-start.7 = (bf16[64,1152]{1,0:T(8,128)(2,1)S(1)}, bf16[64,1152]{1,0:T(8,128)(2,1)S(1)}, u32[]{:S(2)}, u32[]{:S(2)}) collective-permute-start(bf16[64,1152]{1,0:T(8,128)(2,1)S(1)} %get-tuple-element.13), channel_id=1, source_target_pairs={{0,6},{1,7},{2,4},{3,5},{4,2},{5,3},{6,0},{7,1},{8,14},{9,15},{10,... | collective-permute-start | bytes 442376 | tf_op jit(solution)/shard_map/ppermute | solution.py:86
  49.2 11.0 %collective-permute-start.6 = (bf16[64,1152]{1,0:T(8,128)(2,1)S(1)}, bf16[64,1152]{1,0:T(8,128)(2,1)S(1)}, u32[]{:S(2)}, u32[]{:S(2)}) collective-permute-start(bf16[64,1152]{1,0:T(8,128)(2,1)S(1)} %get-tuple-element.14), channel_id=1, source_target_pairs={{0,4},{1,5},{2,6},{3,7},{4,0},{5,1},{6,2},{7,3},{8,12},{9,13},{10,... | collective-permute-start | bytes 442376 | tf_op jit(solution)/shard_map/ppermute | solution.py:86
  49.2 11.0 %collective-permute-start.5 = (bf16[64,1152]{1,0:T(8,128)(2,1)S(1)}, bf16[64,1152]{1,0:T(8,128)(2,1)S(1)}, u32[]{:S(2)}, u32[]{:S(2)}) collective-permute-start(bf16[64,1152]{1,0:T(8,128)(2,1)S(1)} %get-tuple-element.15), channel_id=1, source_target_pairs={{0,2},{1,3},{2,0},{3,1},{4,6},{5,7},{6,4},{7,5},{8,10},{9,11},{10,... | collective-permute-start | bytes 442376 | tf_op jit(solution)/shard_map/ppermute | solution.py:86
  60.5 7.2 %collective-permute-start.13 = (bf16[64,1152]{1,0:T(8,128)(2,1)S(1)}, bf16[64,1152]{1,0:T(8,128)(2,1)S(1)}, u32[]{:S(2)}, u32[]{:S(2)}) collective-permute-start(bf16[64,1152]{1,0:T(8,128)(2,1)S(1)} %multiply_convert_fusion), channel_id=1, source_target_pairs={{0,2},{1,3},{2,0},{3,1},{4,6},{5,7},{6,4},{7,5},{8,10},{9,11},{10,... | collective-permute-start | bytes 442376 | tf_op jit(solution)/shard_map/ppermute | solution.py:86
  60.5 9.7 %collective-permute-start.19 = (bf16[64,1152]{1,0:T(8,128)(2,1)S(1)}, bf16[64,1152]{1,0:T(8,128)(2,1)S(1)}, u32[]{:S(2)}, u32[]{:S(2)}) collective-permute-start(bf16[64,1152]{1,0:T(8,128)(2,1)S(1)} %multiply_convert_fusion), channel_id=1, source_target_pairs={{0,6},{1,7},{2,4},{3,5},{4,2},{5,3},{6,0},{7,1},{8,14},{9,15},{10,... | collective-permute-start | bytes 442376 | tf_op jit(solution)/shard_map/ppermute | solution.py:86
  63.0 12.5 %collective-permute-start.18 = (bf16[64,1152]{1,0:T(8,128)(2,1)S(1)}, bf16[64,1152]{1,0:T(8,128)(2,1)S(1)}, u32[]{:S(2)}, u32[]{:S(2)}) collective-permute-start(bf16[64,1152]{1,0:T(8,128)(2,1)S(1)} %multiply_convert_fusion), channel_id=1, source_target_pairs={{0,4},{1,5},{2,6},{3,7},{4,0},{5,1},{6,2},{7,3},{8,12},{9,13},{10,... | collective-permute-start | bytes 442376 | tf_op jit(solution)/shard_map/ppermute | solution.py:86
  67.6 8.3 %collective-permute-start.14 = (bf16[128,1152]{1,0:T(8,128)(2,1)S(1)}, bf16[128,1152]{1,0:T(8,128)(2,1)S(1)}, u32[]{:S(2)}, u32[]{:S(2)}) collective-permute-start(bf16[128,1152]{1,0:T(8,128)(2,1)S(1)} %pad_maximum_fusion.6), channel_id=1, source_target_pairs={{0,8},{1,17},{2,10},{3,19},{4,12},{5,21},{6,14},{7,23},{8,0},{9,25... | collective-permute-start | bytes 884744 | tf_op jit(solution)/shard_map/ppermute | solution.py:113
  68.7 16.8 %collective-permute-start.10 = (f32[256,1152]{1,0:T(8,128)S(1)}, f32[256,1152]{1,0:T(8,128)S(1)}, u32[]{:S(2)}, u32[]{:S(2)}) collective-permute-start(f32[256,1152]{1,0:T(8,128)S(1)} %slice.42), channel_id=1, source_target_pairs={{0,1},{1,0},{2,3},{3,2},{4,5},{5,4},{6,7},{7,6},{8,9},{9,8},{10,11... | collective-permute-start | bytes 3538952 | tf_op jit(solution)/shard_map/ppermute | solution.py:92
  68.8 28.9 %collective-permute-start.11 = (bf16[2304,256]{1,0:T(8,128)(2,1)S(1)}, bf16[2304,256]{1,0:T(8,128)(2,1)S(1)}, u32[]{:S(2)}, u32[]{:S(2)}) collective-permute-start(bf16[2304,256]{1,0:T(8,128)(2,1)S(1)} %pad_maximum_fusion.1.refs_0_.refs_1_), channel_id=1, source_target_pairs={{0,1},{1,0},{2,3},{3,2},{4,5},{5,4},{6,7},{7,6},{8,9},{9,8},{10,11... | collective-permute-start | bytes 3538952 | tf_op jit(solution)/shard_map/ppermute | solution.py:92
  70.2 27.4 %collective-permute-start.12 = (bf16[2304,256]{1,0:T(8,128)(2,1)S(1)}, bf16[2304,256]{1,0:T(8,128)(2,1)S(1)}, u32[]{:S(2)}, u32[]{:S(2)}) collective-permute-start(bf16[2304,256]{1,0:T(8,128)(2,1)S(1)} %collective-permute-done.9.refs_1_.refs_2_), channel_id=1, source_target_pairs={{0,1},{1,0},{2,3},{3,2},{4,5},{5,4},{6,7},{7,6},{8,9},{9,8},{10,11... | collective-permute-start | bytes 3538952 | tf_op jit(solution)/shard_map/ppermute | solution.py:92
  75.6 9.9 %collective-permute-start.20 = (bf16[128,1152]{1,0:T(8,128)(2,1)S(1)}, bf16[128,1152]{1,0:T(8,128)(2,1)S(1)}, u32[]{:S(2)}, u32[]{:S(2)}) collective-permute-start(bf16[128,1152]{1,0:T(8,128)(2,1)S(1)} %pad_maximum_fusion.7), channel_id=1, source_target_pairs={{0,8},{1,17},{2,10},{3,19},{4,12},{5,21},{6,14},{7,23},{8,0},{9,25... | collective-permute-start | bytes 884744 | tf_op jit(solution)/shard_map/ppermute | solution.py:113
  75.9 11.4 %collective-permute-start.15 = (bf16[256,1152]{1,0:T(8,128)(2,1)S(1)}, bf16[256,1152]{1,0:T(8,128)(2,1)S(1)}, u32[]{:S(2)}, u32[]{:S(2)}) collective-permute-start(bf16[256,1152]{1,0:T(8,128)(2,1)S(1)} %pad_maximum_fusion.5.refs_4_), channel_id=1, source_target_pairs={{0,16},{1,9},{2,18},{3,11},{4,20},{5,13},{6,22},{7,15},{8,24},{9,1... | collective-permute-start | bytes 1769480 | tf_op jit(solution)/shard_map/ppermute | solution.py:113
  85.5 10.0 %collective-permute-start.16 = (bf16[256,1152]{1,0:T(8,128)(2,1)S(1)}, bf16[256,1152]{1,0:T(8,128)(2,1)S(1)}, u32[]{:S(2)}, u32[]{:S(2)}) collective-permute-start(bf16[256,1152]{1,0:T(8,128)(2,1)S(1)} %pad_maximum_fusion.5.refs_4_), channel_id=1, source_target_pairs={{0,1},{1,0},{2,3},{3,2},{4,5},{5,4},{6,7},{7,6},{8,9},{9,8},{10,11... | collective-permute-start | bytes 1769480 | tf_op jit(solution)/shard_map/ppermute | solution.py:92
  85.5 9.9 %collective-permute-start.21 = (bf16[256,1152]{1,0:T(8,128)(2,1)S(1)}, bf16[256,1152]{1,0:T(8,128)(2,1)S(1)}, u32[]{:S(2)}, u32[]{:S(2)}) collective-permute-start(bf16[256,1152]{1,0:T(8,128)(2,1)S(1)} %constant_dynamic-update-slice_fusion.refs_5_), channel_id=1, source_target_pairs={{0,16},{1,9},{2,18},{3,11},{4,20},{5,13},{6,22},{7,15},{8,24},{9,1... | collective-permute-start | bytes 1769480 | tf_op jit(solution)/shard_map/ppermute | solution.py:113
  87.3 11.4 %collective-permute-start.17 = (bf16[256,1152]{1,0:T(8,128)(2,1)S(1)}, bf16[256,1152]{1,0:T(8,128)(2,1)S(1)}, u32[]{:S(2)}, u32[]{:S(2)}) collective-permute-start(bf16[256,1152]{1,0:T(8,128)(2,1)S(1)} %collective-permute-done.15.refs_5_), channel_id=1, source_target_pairs={{0,1},{1,0},{2,3},{3,2},{4,5},{5,4},{6,7},{7,6},{8,9},{9,8},{10,11... | collective-permute-start | bytes 1769480 | tf_op jit(solution)/shard_map/ppermute | solution.py:92
  95.5 11.0 %collective-permute-start.22 = (bf16[256,1152]{1,0:T(8,128)(2,1)S(1)}, bf16[256,1152]{1,0:T(8,128)(2,1)S(1)}, u32[]{:S(2)}, u32[]{:S(2)}) collective-permute-start(bf16[256,1152]{1,0:T(8,128)(2,1)S(1)} %constant_dynamic-update-slice_fusion.refs_5_), channel_id=1, source_target_pairs={{0,1},{1,0},{2,3},{3,2},{4,5},{5,4},{6,7},{7,6},{8,9},{9,8},{10,11... | collective-permute-start | bytes 1769480 | tf_op jit(solution)/shard_map/ppermute | solution.py:92
  95.5 11.0 %collective-permute-start.23 = (bf16[256,1152]{1,0:T(8,128)(2,1)S(1)}, bf16[256,1152]{1,0:T(8,128)(2,1)S(1)}, u32[]{:S(2)}, u32[]{:S(2)}) collective-permute-start(bf16[256,1152]{1,0:T(8,128)(2,1)S(1)} %collective-permute-done.21.refs_6_), channel_id=1, source_target_pairs={{0,1},{1,0},{2,3},{3,2},{4,5},{5,4},{6,7},{7,6},{8,9},{9,8},{10,11... | collective-permute-start | bytes 1769480 | tf_op jit(solution)/shard_map/ppermute | solution.py:92
  97.7 1.0 copy-start.2

commit v3 on v1

v3 whole, which is shorter than its diff:
```python
import functools

import jax
import jax.numpy as jnp
from jax import lax
from jax.experimental import pallas as pl
from jax.experimental.pallas import tpu as pltpu
from jax.sharding import PartitionSpec as P

FIRST = (((0,), (0,)), ((), ()))
LAST = (((1,), (1,)), ((), ()))
F32 = jnp.float32
BF16 = jnp.bfloat16


def dot(a, b, dims=(((1,), (0,)), ((), ()))):
    return lax.dot_general(a, b, dims, preferred_element_type=F32)


def turn_kernel(sizes, n_chunk, *refs):
    out, refs = refs[-1], refs[:-1]
    half = len(refs) // 2
    per = n_chunk // half
    step = refs[0].shape[0] // per
    col = 0
    for core in range(2):
        first = 0
        for size in sizes:
            rows = []
            for chunk in range(n_chunk):
                at = (chunk % per) * step + first
                rows.append(refs[core * half + chunk // per][at : at + size, :])
            rows = jnp.concatenate(rows)
            out[:, col : col + rows.shape[0]] = rows.T
            col += rows.shape[0]
            first += size


def turned(xs, sizes, n_chunk):
    images = sum(v.shape[0] for v in xs)
    depth = xs[0].shape[1]
    return pl.pallas_call(
        functools.partial(turn_kernel, sizes, n_chunk),
        out_shape=jax.ShapeDtypeStruct((depth, images), BF16),
        in_specs=[pl.BlockSpec(memory_space=pltpu.VMEM)] * len(xs),
        out_specs=pl.BlockSpec(memory_space=pltpu.VMEM),
        compiler_params=pltpu.CompilerParams(vmem_limit_bytes=24 * 2**20),
        cost_estimate=pl.CostEstimate(
            flops=0, bytes_accessed=4 * images * depth, transcendentals=0
        ),
    )(*xs)


def weight_kernel(factor, x_t, *refs):
    gs, (out, stacked, tiles, sems) = refs[:-4], refs[-4:]
    at = 0
    for g in gs:
        stacked[at : at + g.shape[0], :] = g[...]
        at += g.shape[0]
    n, rows = tiles.shape[:2]
    copies = []
    for i in range(n):
        here = slice(i * rows, (i + 1) * rows)
        tiles[i] = dot(x_t[here, :], stacked[...]) * factor
        copies.append(pltpu.make_async_copy(tiles.at[i], out.at[here, :], sems.at[i]))
        copies[-1].start()
    for copy in copies:
        copy.wait()


def weight_sum(x_t, gs, factor):
    depth, images = x_t.shape
    n = 3
    return pl.pallas_call(
        functools.partial(weight_kernel, factor),
        out_shape=jax.ShapeDtypeStruct((depth, depth), F32),
        in_specs=[pl.BlockSpec(memory_space=pltpu.VMEM)] * (1 + len(gs)),
        out_specs=pl.BlockSpec(memory_space=pl.ANY),
        scratch_shapes=[
            pltpu.VMEM((images, depth), BF16),
            pltpu.VMEM((n, depth // n, depth), F32),
            pltpu.SemaphoreType.DMA((n,)),
        ],
        compiler_params=pltpu.CompilerParams(vmem_limit_bytes=28 * 2**20),
        cost_estimate=pl.CostEstimate(
            flops=2 * images * depth * depth,
            bytes_accessed=4 * images * depth + 4 * depth * depth,
            transcendentals=0,
        ),
    )(x_t, *gs)


def on_device(x, captions, labels, weight, scale, offset):
    x, captions, labels = x[0], captions[0], labels[0]
    n_img, depth = x.shape
    n_cap = captions.shape[0]
    nd, nb = lax.axis_size("dp"), lax.axis_size("blk")
    nz = nb // 2
    b = lax.axis_index("blk")
    z, c = b // 2, b % 2

    def along_z(v, k):
        return lax.ppermute(v, "blk", [(i, i ^ (2 * k)) for i in range(nb)])

    def swap(v):
        return lax.ppermute(v, "blk", [(i, i ^ 1) for i in range(nb)])

    xs = jnp.concatenate([x] + [along_z(x, k) for k in range(1, nz)])
    caps = jnp.concatenate([captions, swap(captions)])
    labs = jnp.concatenate([labels, swap(labels)])
    ids = jnp.concatenate(
        [
            ((z ^ k) * 2 + c) * n_img + jnp.arange(n_img, dtype=jnp.int32)
            for k in range(nz)
        ]
    )
    bits = nd.bit_length() - 1

    def step_d(v, i):
        perm = []
        for j in range(nd):
            for m in range(nb):
                to = j ^ (1 << ((i + m % 2) % bits))
                perm.append((j * nb + m, to * nb + m))
        return lax.ppermute(v, ("dp", "blk"), perm)

    def over_d(v, first=None):
        v = [v]
        for i in range(bits):
            if i:
                v = [jnp.concatenate(v)]
            v.append(step_d(v[0], i) if i or first is None else first)
        return v

    x_first = step_d(xs, 0)
    embed = dot(xs, weight)
    inv_norm = lax.rsqrt(jnp.sum(embed * embed, axis=1, keepdims=True) + 1e-06)
    unit_f = embed * inv_norm
    unit = unit_f.astype(BF16)
    logits = scale * dot(unit, caps, LAST) + offset
    sign = jnp.where(labs[None, :] == ids[:, None], 1.0, -1.0).astype(F32)
    dlogit = (-sign * jax.nn.sigmoid(-sign * logits)).astype(BF16)

    part = scale * dot(dlogit, caps)
    own = part[:n_img]
    sent = [part[k * n_img : (k + 1) * n_img].astype(BF16) for k in range(1, nz)]
    back = [along_z(v, k + 1) for k, v in enumerate(sent)]
    x_first = lax.optimization_barrier((x_first, sent))[0]
    x_own = over_d(xs, x_first)
    back = lax.optimization_barrier((back, x_own[0]))[0]
    for v in back:
        own = own + v.astype(F32)

    dlogit = lax.optimization_barrier((dlogit, sent))[0]
    adjoint = scale * dot(dlogit, unit, FIRST)
    adjoint_other = swap(adjoint[n_cap:])
    adjoint = adjoint[:n_cap] + adjoint_other

    u = unit_f[:n_img]
    radial = jnp.sum(u * own, axis=1, keepdims=True)
    ge = ((own - u * radial) * inv_norm[:n_img]).astype(BF16)
    ge = lax.optimization_barrier((ge, adjoint_other))[0]
    grad_features = dot(ge, weight, LAST)

    half = nz // 2
    blocks = [ge] + [along_z(ge, k) for k in range(1, nz)]
    groups = [blocks[:1], blocks[1:half], blocks[half:]]
    sizes = [n_img * len(g) for g in groups]
    g_own = [over_d(jnp.concatenate(g)) for g in groups]
    if nd * nb * n_img <= 2048:
        for i in range(2):
            g_own[i] = [jnp.concatenate(g_own[i])]
        g_own = [v for g in g_own for v in g]
        x_t = turned(x_own + [swap(v) for v in x_own], sizes, nd)
        g_own[-1] = lax.optimization_barrier((g_own[-1], x_t))[0]
        grad_weight = weight_sum(x_t, g_own + [swap(v) for v in g_own], 1.0 / nd)
    else:
        grad_weight = 0.0
        n_own = nz * n_img
        for i, x_part in enumerate(x_own):
            for at in range(nd // 2):
                g_part = [g[i][at * m : (at + 1) * m] for m, g in zip(sizes, g_own)]
                grad_weight = grad_weight + dot(
                    x_part[at * n_own : (at + 1) * n_own],
                    jnp.concatenate(g_part),
                    FIRST,
                )
        grad_weight = (grad_weight + swap(grad_weight)) / nd
    return (grad_features[None], adjoint[None], grad_weight)


def solution(mesh):
    placed = (P("dp", "blk", None), P("dp", "blk", None), P("dp", "blk"), P(), P(), P())
    return jax.shard_map(
        on_device,
        mesh=mesh,
        in_specs=placed,
        out_specs=(P("dp", "blk", None), P("dp", "blk", None), P()),
        check_vma=False,
    )
```

time: 168 us -> 91.5 us (0.54)
  waiting for transfers between devices: 88.6 us -> 41.6 us
  local copies, waits for them, and re-layouts: 21 us -> 2.94 us
  between operations: 15.5 us -> 2.23 us
  Pallas kernels: 0 us -> 8.92 us
  other arithmetic: 8.93 us -> 3.46 us
  matrix products: 11.4 us -> 6.57 us
  starting transfers between devices: 21.9 us -> 25.5 us
    all_gather x1 -> x0, waiting for transfers between devices: 55.4 us -> none  [on_device(): whole = lax.all_gather(piece, ('dp', 'blk'), axis=0)]
    convert_element_type x4 -> x0, local copies, waits for them, and re-layouts: 17.4 us -> none  [the longest x2 15.5 us: on_device(): grad_weight = whole.reshape(depth, depth).astype(F32)]
    pallas_call x0 -> x2, Pallas kernels: none -> 8.92 us  [the longest x1 7.55 us: weight_sum(): pl.pallas_call(functools.partial(weight_kernel, factor), out_shape=jax.Sh...]
    ppermute x16 -> x17, waiting for transfers between devices: 32.2 us -> 40.7 us  [the longest x9 24.7 us: along_z(): return lax.ppermute(v, 'blk', [(i, i ^ 2 * k) for i in range(nb)])]
    dot_general x6 -> x5, matrix products: 11.4 us -> 6.57 us  [dot(): return lax.dot_general(a, b, dims, preferred_element_type=F32)]
    convert_element_type x2 -> x0, other arithmetic: 4.48 us -> none  [the longest x1 2.73 us: on_device(): grad_weight = whole.reshape(depth, depth).astype(F32)]
    ppermute x16 -> x17, starting transfers between devices: 21.1 us -> 24.1 us  [the longest x9 14.7 us: along_z(): return lax.ppermute(v, 'blk', [(i, i ^ 2 * k) for i in range(nb)])]
  transfers between devices with their start and end apart: 20 -> 26, of which waited for: 12 -> 10; matrix products, arithmetic and copies ran while one was open for 5% -> 13% of each run, Pallas kernels for 0% -> 1%
where the time goes in v3:
time: 91.5 us; the launch traced here: 91.2 us
  waiting for transfers between devices  41.6 us (45%)
  starting transfers between devices  25.5 us (28%)
  Pallas kernels  8.92 us (10%)
  matrix products  6.57 us (7%)
  other arithmetic  3.46 us (4%)
  local copies, waits for them, and re-layouts  2.94 us (3%)
  between operations  2.23 us (2%)
    ppermute x9, waiting for transfers between devices, along_z(): return lax.ppermute(v, 'blk', [(i, i ^ 2 * k) for i in range(nb)])  24.7 us
    ppermute x8, waiting for transfers between devices, step_d(): return lax.ppermute(v, ('dp', 'blk'), perm)  16.1 us
    ppermute x9, starting transfers between devices, along_z(): return lax.ppermute(v, 'blk', [(i, i ^ 2 * k) for i in range(nb)])  14.7 us
    ppermute x8, starting transfers between devices, step_d(): return lax.ppermute(v, ('dp', 'blk'), perm)  9.44 us
    pallas_call x1, Pallas kernels, weight_sum(): pl.pallas_call(functools.partial(weight_kernel, factor), out_shape=jax.Sh...  7.55 us
    dot_general x5, matrix products, dot(): return lax.dot_general(a, b, dims, preferred_element_type=F32)  6.57 us
    unnamed x20, local copies, waits for them, and re-layouts  2.66 us
  transfers between devices with their start and end apart: 26, of which 10 were waited for; matrix products, arithmetic and copies ran while one was open for 13% of the time, Pallas kernels for 1%

profile of v3, /device:TPU:0, one launch (start us, length us, event | category | flops | bytes accessed | tf_op | source)
XLA Modules:
  0.0 91.2 jit_solution(16405866481375685420)
XLA Ops:
  0.6 0.0 copy-start
  0.6 0.0 copy-start.2
  0.7 5.1 %collective-permute-start.3 = (bf16[64,1152]{1,0:T(8,128)(2,1)}, bf16[64,1152]{1,0:T(8,128)(2,1)S(1)}, u32[]{:S(2)}, u32[]{:S(2)}) collective-permute-start(bf16[64,1152]{1,0:T(8,128)(2,1)} %bitcast.13), channel_id=1, source_target_pairs={{0,6},{1,7},{2,4},{3,5},{4,2},{5,3},{6,0},{7,1},{8,14},{9,15},{10,... | collective-permute-start | bytes 442376 | tf_op jit(solution)/shard_map/ppermute | solution.py:103
  5.8 0.0 collective-permute-start.2
  5.8 0.6 collective-permute-start.1
  6.4 0.0 collective-permute-start
  6.4 0.5 collective-permute-start.4
  6.9 1.6 %constant_dynamic-update-slice_fusion.4 = bf16[512,1152]{1,0:T(8,128)(2,1)} fusion(bf16[1,64,1152]{2,1,0:T(8,128)(2,1)} %param.6), kind=kLoop, calls=%fused_computation.32 | loop fusion | bytes 294912
  8.5 0.1 pad_add_fusion.1
  9.9 0.0 copy-start.1
  9.9 0.0 collective-permute-done
  9.9 0.8 pad_add_fusion
  10.7 0.1 collective-permute-done.3
  10.8 7.7 %collective-permute-done.2 = bf16[64,1152]{1,0:T(8,128)(2,1)S(1)} collective-permute-done((bf16[64,1152]{1,0:T(8,128)(2,1)}, bf16[64,1152]{1,0:T(8,128)(2,1)S(1)}, u32[]{:S(2)}, u32[]{:S(2)}) %collective-permute-start.2) | collective-permute-done | bytes 147488 | tf_op jit(solution)/shard_map/ppermute | solution.py:103
  18.5 1.0 %pad_maximum_fusion.3 = bf16[256,1152]{1,0:T(8,128)(2,1)S(1)} fusion(bf16[64,1152]{1,0:T(8,128)(2,1)S(1)} %collective-permute-done.3, bf16[64,1152]{1,0:T(8,128)(2,1)S(1)} %collective-permute-done.2, bf16[64,1152]{1,0:T(8,128)(2,1)S(1)} %collective-permute-done.1, bf16[64,1152]{1,0:T(8,128)(2,1)} %bitcast.16), kind=kLoop, calls=%fused_computation.16 | loop fusion | flops 2359296 | bytes 1179648 | tf_op jit(solution)/shard_map/concatenate | solution.py:108
  19.4 1.6 %collective-permute-start.8 = (bf16[256,1152]{1,0:T(8,128)(2,1)S(1)}, bf16[256,1152]{1,0:T(8,128)(2,1)S(1)}, u32[]{:S(2)}, u32[]{:S(2)}) collective-permute-start(bf16[256,1152]{1,0:T(8,128)(2,1)S(1)} %pad_maximum_fusion.3), channel_id=1, source_target_pairs={{0,8},{1,17},{2,10},{3,19},{4,12},{5,21},{6,14},{7,23},{8,0},{9,25... | collective-permute-start | bytes 1769480 | tf_op jit(solution)/shard_map/ppermute | solution.py:125
  21.0 1.1 %multiply_reduce_fusion = (f32[256]{0:T(256)S(1)}, f32[256,1152]{1,0:T(8,128)S(1)}) fusion(bf16[1152,1152]{1,0:T(8,128)(2,1)S(1)} %copy-done, bf16[64,1152]{1,0:T(8,128)(2,1)S(1)} %collective-permute-done.3, bf16[64,1152]{1,0:T(8,128)(2,1)S(1)} %collective-permute-done.2, bf16[64,1152]{1,0:T(8,128)(2,1)S(1)} %collective-permute-done.1, ...), kind=kOutput, calls=%fused_computation.15 | convolution fusion | flops 682426112 | bytes 4424704 | tf_op jit(solution)/shard_map/dot_general | solution.py:17
  22.1 0.0 copy-start.4
  22.1 0.0 copy-start.3
  22.1 0.1 broadcast_multiply_fusion
  22.3 0.0 collective-permute-done.4
  22.3 0.9 copy-done.3
  23.2 1.7 %fusion.7 = bf16[256,512]{1,0:T(8,128)(2,1)S(1)} fusion(bf16[256,1152]{1,0:T(8,128)(2,1)} %collective-permute-done.4, bf16[256,1152]{1,0:T(8,128)(2,1)S(1)} %bitcast.19, f32[256,1152]{1,0:T(8,128)S(1)} %broadcast_multiply_fusion, f32[]{:T(128)S(6)} %copy.20, f32[]{:T(128)S(6)} %copy.19, s32[512]{0:T(512)S(1)} %pad_add_fusion, s32[256]{0:T(256)S(1)} %pad_add_fusion.1), kind=kOutput, calls=%fused_computation.11 | convolution fusion | flops 306085888 | bytes 2624520 | tf_op jit(solution)/shard_map/dot_general | solution.py:17
  24.9 1.6 %fusion.17 = (bf16[256,1152]{1,0:T(8,128)(2,1)S(1)}, f32[256,1152]{1,0:T(8,128)S(1)}) fusion(bf16[256,512]{1,0:T(8,128)(2,1)S(1)} %fusion.7, bf16[256,1152]{1,0:T(8,128)(2,1)} %collective-permute-done.4, bf16[256,1152]{1,0:T(8,128)(2,1)S(1)} %bitcast.20, f32[]{:T(128)S(6)} %copy.19), kind=kOutput, calls=%fused_computation.53 | convolution fusion | flops 304939008 | bytes 3211268 | tf_op jit(solution)/shard_map/dot_general | solution.py:17
  26.6 0.5 convolution_multiply_fusion
  27.1 0.1 slice.41
  27.2 0.1 collective-permute-start.9
  27.3 0.0 slice-start
  27.3 2.6 %collective-permute-start.7 = (bf16[64,1152]{1,0:T(8,128)(2,1)S(1)}, bf16[64,1152]{1,0:T(8,128)(2,1)S(1)}, u32[]{:S(2)}, u32[]{:S(2)}) collective-permute-start(bf16[64,1152]{1,0:T(8,128)(2,1)S(1)} %get-tuple-element.17), channel_id=1, source_target_pairs={{0,6},{1,7},{2,4},{3,5},{4,2},{5,3},{6,0},{7,1},{8,14},{9,15},{10,... | collective-permute-start | bytes 442376 | tf_op jit(solution)/shard_map/ppermute | solution.py:103
  29.9 1.9 %collective-permute-start.5 = (bf16[64,1152]{1,0:T(8,128)(2,1)S(1)}, bf16[64,1152]{1,0:T(8,128)(2,1)S(1)}, u32[]{:S(2)}, u32[]{:S(2)}) collective-permute-start(bf16[64,1152]{1,0:T(8,128)(2,1)S(1)} %get-tuple-element.19), channel_id=1, source_target_pairs={{0,2},{1,3},{2,0},{3,1},{4,6},{5,7},{6,4},{7,5},{8,10},{9,11},{10,... | collective-permute-start | bytes 442376 | tf_op jit(solution)/shard_map/ppermute | solution.py:103
  31.8 0.1 constant_dynamic-update-slice_fusion.refs_0_
  31.9 0.1 collective-permute-start.11
  31.9 4.0 %collective-permute-done.7 = bf16[64,1152]{1,0:T(8,128)(2,1)S(1)} collective-permute-done((bf16[64,1152]{1,0:T(8,128)(2,1)S(1)}, bf16[64,1152]{1,0:T(8,128)(2,1)S(1)}, u32[]{:S(2)}, u32[]{:S(2)}) %collective-permute-start.7) | collective-permute-done | bytes 147488 | tf_op jit(solution)/shard_map/ppermute | solution.py:103
  36.0 1.5 %collective-permute-start.10 = (bf16[512,1152]{1,0:T(8,128)(2,1)S(1)}, bf16[512,1152]{1,0:T(8,128)(2,1)S(1)}, u32[]{:S(2)}, u32[]{:S(2)}) collective-permute-start(bf16[512,1152]{1,0:T(8,128)(2,1)S(1)} %constant_dynamic-update-slice_fusion.refs_0_), channel_id=1, source_target_pairs={{0,16},{1,9},{2,18},{3,11},{4,20},{5,13},{6,22},{7,15},{8,24},{9,1... | collective-permute-start | bytes 3538952 | tf_op jit(solution)/shard_map/ppermute | solution.py:125
  37.5 4.9 %collective-permute-done.6 = bf16[64,1152]{1,0:T(8,128)(2,1)S(1)} collective-permute-done((bf16[64,1152]{1,0:T(8,128)(2,1)S(1)}, bf16[64,1152]{1,0:T(8,128)(2,1)S(1)}, u32[]{:S(2)}, u32[]{:S(2)}) %collective-permute-start.6) | collective-permute-done | bytes 147488 | tf_op jit(solution)/shard_map/ppermute | solution.py:103
  42.4 0.0 collective-permute-done.5
  42.4 0.2 multiply_reduce_fusion.1
  42.5 0.1 multiply_convert_fusion
  42.7 0.0 collective-permute-done.9
  42.7 2.0 %collective-permute-start.19 = (bf16[64,1152]{1,0:T(8,128)(2,1)S(1)}, bf16[64,1152]{1,0:T(8,128)(2,1)S(1)}, u32[]{:S(2)}, u32[]{:S(2)}) collective-permute-start(bf16[64,1152]{1,0:T(8,128)(2,1)S(1)} %multiply_convert_fusion), channel_id=1, source_target_pairs={{0,6},{1,7},{2,4},{3,5},{4,2},{5,3},{6,0},{7,1},{8,14},{9,15},{10,... | collective-permute-start | bytes 442376 | tf_op jit(solution)/shard_map/ppermute | solution.py:103
  44.7 0.0 collective-permute-start.18
  44.7 2.4 %collective-permute-start.15 = (bf16[64,1152]{1,0:T(8,128)(2,1)S(1)}, bf16[64,1152]{1,0:T(8,128)(2,1)S(1)}, u32[]{:S(2)}, u32[]{:S(2)}) collective-permute-start(bf16[64,1152]{1,0:T(8,128)(2,1)S(1)} %multiply_convert_fusion), channel_id=1, source_target_pairs={{0,2},{1,3},{2,0},{3,1},{4,6},{5,7},{6,4},{7,5},{8,10},{9,11},{10,... | collective-permute-start | bytes 442376 | tf_op jit(solution)/shard_map/ppermute | solution.py:103
  47.1 1.6 %convolution_bitcast_fusion = f32[1,64,1152]{2,1,0:T(8,128)} fusion(bf16[64,1152]{1,0:T(8,128)(2,1)S(1)} %multiply_convert_fusion, bf16[1152,1152]{1,0:T(8,128)(2,1)S(1)} %copy-done), kind=kOutput, calls=%fused_computation.2 | convolution fusion | flops 169869312 | bytes 3096576 | tf_op jit(solution)/shard_map/dot_general | solution.py:17
  48.8 2.6 %collective-permute-done.19 = bf16[64,1152]{1,0:T(8,128)(2,1)S(1)} collective-permute-done((bf16[64,1152]{1,0:T(8,128)(2,1)S(1)}, bf16[64,1152]{1,0:T(8,128)(2,1)S(1)}, u32[]{:S(2)}, u32[]{:S(2)}) %collective-permute-start.19) | collective-permute-done | bytes 147488 | tf_op jit(solution)/shard_map/ppermute | solution.py:103
  51.4 0.5 collective-permute-start.13
  51.9 5.4 %collective-permute-done.18 = bf16[64,1152]{1,0:T(8,128)(2,1)S(1)} collective-permute-done((bf16[64,1152]{1,0:T(8,128)(2,1)S(1)}, bf16[64,1152]{1,0:T(8,128)(2,1)S(1)}, u32[]{:S(2)}, u32[]{:S(2)}) %collective-permute-start.18) | collective-permute-done | bytes 147488 | tf_op jit(solution)/shard_map/ppermute | solution.py:103
  57.3 0.6 collective-permute-start.20
  58.0 1.6 %collective-permute-start.14 = (bf16[128,1152]{1,0:T(8,128)(2,1)S(1)}, bf16[128,1152]{1,0:T(8,128)(2,1)S(1)}, u32[]{:S(2)}, u32[]{:S(2)}) collective-permute-start(bf16[128,1152]{1,0:T(8,128)(2,1)S(1)} %pad_maximum_fusion.4), channel_id=1, source_target_pairs={{0,16},{1,9},{2,18},{3,11},{4,20},{5,13},{6,22},{7,15},{8,24},{9,1... | collective-permute-start | bytes 884744 | tf_op jit(solution)/shard_map/ppermute | solution.py:125
  59.6 0.0 collective-permute-done.15
  59.6 1.5 %collective-permute-start.16 = (bf16[64,1152]{1,0:T(8,128)(2,1)S(1)}, bf16[64,1152]{1,0:T(8,128)(2,1)S(1)}, u32[]{:S(2)}, u32[]{:S(2)}) collective-permute-start(bf16[64,1152]{1,0:T(8,128)(2,1)S(1)} %collective-permute-done.15), channel_id=1, source_target_pairs={{0,8},{1,17},{2,10},{3,19},{4,12},{5,21},{6,14},{7,23},{8,0},{9,25... | collective-permute-start | bytes 442376 | tf_op jit(solution)/shard_map/ppermute | solution.py:125
  61.1 0.0 collective-permute-done.10.refs_1_
  61.1 0.1 collective-permute-start.12
  61.2 7.3 %collective-permute-done.16 = bf16[64,1152]{1,0:T(8,128)(2,1)S(1)} collective-permute-done((bf16[64,1152]{1,0:T(8,128)(2,1)S(1)}, bf16[64,1152]{1,0:T(8,128)(2,1)S(1)}, u32[]{:S(2)}, u32[]{:S(2)}) %collective-permute-start.16) | collective-permute-done | bytes 147488 | tf_op jit(solution)/shard_map/ppermute | solution.py:125
  68.5 0.6 collective-permute-start.17
  69.2 1.6 %collective-permute-start.21 = (bf16[256,1152]{1,0:T(8,128)(2,1)S(1)}, bf16[256,1152]{1,0:T(8,128)(2,1)S(1)}, u32[]{:S(2)}, u32[]{:S(2)}) collective-permute-start(bf16[256,1152]{1,0:T(8,128)(2,1)S(1)} %constant_dynamic-update-slice_fusion.11.refs_2_), channel_id=1, source_target_pairs={{0,16},{1,9},{2,18},{3,11},{4,20},{5,13},{6,22},{7,15},{8,24},{9,1... | collective-permute-start | bytes 1769480 | tf_op jit(solution)/shard_map/ppermute | solution.py:125
  70.8 0.1 collective-permute-start.24
  70.9 4.4 %collective-permute-done.17 = bf16[128,1152]{1,0:T(8,128)(2,1)S(1)} collective-permute-done((bf16[128,1152]{1,0:T(8,128)(2,1)S(1)}, bf16[128,1152]{1,0:T(8,128)(2,1)S(1)}, u32[]{:S(2)}, u32[]{:S(2)}) %collective-permute-start.17) | collective-permute-done | bytes 294944 | tf_op jit(solution)/shard_map/ppermute | solution.py:125
  75.4 0.6 collective-permute-start.23
  75.9 0.0 collective-permute-done.12.refs_3_
  75.9 1.4 %shard_map.85.x_t = bf16[1152,2048]{1,0:T(8,128)(2,1)S(1)} custom-call(bf16[512,1152]{1,0:T(8,128)(2,1)S(1)} %constant_dynamic-update-slice_fusion.refs_0_, bf16[512,1152]{1,0:T(8,128)(2,1)S(1)} %collective-permute-done.10.refs_1_, bf16[512,1152]{1,0:T(8,128)(2,1)S(1)} %collective-permute-done.11.refs_2_, bf16[512,1152]{1,0:T(8,128)(2,1)S(1)} %collective-permute-done.12.refs_3_), custom_call_target="tpu_custom_call" | custom-call | bytes 9437184 | tf_op jit(solution)/shard_map/pallas_call | solution.py:42
  77.3 4.3 %collective-permute-done.21.refs_3_ = bf16[256,1152]{1,0:T(8,128)(2,1)S(1)} collective-permute-done((bf16[256,1152]{1,0:T(8,128)(2,1)S(1)}, bf16[256,1152]{1,0:T(8,128)(2,1)S(1)}, u32[]{:S(2)}, u32[]{:S(2)}) %collective-permute-start.21) | collective-permute-done | bytes 589856 | tf_op jit(solution)/shard_map/ppermute | solution.py:125
  81.6 1.1 %fusion.8 = f32[1,256,1152]{2,1,0:T(8,128)} fusion(f32[256,1152]{1,0:T(8,128)S(1)} %collective-permute-done.9, f32[512,1152]{1,0:T(8,128)S(1)} %convolution_multiply_fusion), kind=kLoop, calls=%fused_computation.13 | loop fusion | flops 294912 | bytes 3538944 | tf_op jit(solution)/shard_map/broadcast_in_dim | solution.py:189
  82.8 0.9 collective-permute-done.25.refs_7_
  83.6 7.6 %shard_map.86 = f32[1152,1152]{1,0:T(8,128)} custom-call(bf16[1152,2048]{1,0:T(8,128)(2,1)S(1)} %shard_map.85.x_t, bf16[256,1152]{1,0:T(8,128)(2,1)S(1)} %constant_dynamic-update-slice_fusion.5.refs_0_, bf16[256,1152]{1,0:T(8,128)(2,1)S(1)} %constant_dynamic-update-slice_fusion.8.refs_1_, bf16[256,1152]{1,0:T(8,128)(2,1)S(1)} %constant_dynamic-update-slice_fusion.11.refs_2_, ...), custom_call_target="tpu_custom_call" | custom-call | flops 5435817984 | bytes 14745600 | tf_op jit(solution)/shard_map/pallas_call | solution.py:74
  (36 shorter events, 0.4 us)
Async XLA Ops:
  0.6 20.4 %copy-start = (bf16[1152,1152]{1,0:T(8,128)(2,1)S(1)}, bf16[1152,1152]{1,0:T(8,128)(2,1)}, u32[]{:S(2)}) copy-start(bf16[1152,1152]{1,0:T(8,128)(2,1)} %param.9) | copy-start | bytes 7962628
  0.6 20.4 %copy-start.2 = (bf16[1,64,1152]{2,1,0:T(8,128)(2,1)S(1)}, bf16[1,64,1152]{2,1,0:T(8,128)(2,1)}, u32[]{:S(2)}) copy-start(bf16[1,64,1152]{2,1,0:T(8,128)(2,1)} %param.6) | copy-start | bytes 442372
  0.7 10.1 %collective-permute-start.3 = (bf16[64,1152]{1,0:T(8,128)(2,1)}, bf16[64,1152]{1,0:T(8,128)(2,1)S(1)}, u32[]{:S(2)}, u32[]{:S(2)}) collective-permute-start(bf16[64,1152]{1,0:T(8,128)(2,1)} %bitcast.13), channel_id=1, source_target_pairs={{0,6},{1,7},{2,4},{3,5},{4,2},{5,3},{6,0},{7,1},{8,14},{9,15},{10,... | collective-permute-start | bytes 442376 | tf_op jit(solution)/shard_map/ppermute | solution.py:103
  5.8 12.7 %collective-permute-start.2 = (bf16[64,1152]{1,0:T(8,128)(2,1)}, bf16[64,1152]{1,0:T(8,128)(2,1)S(1)}, u32[]{:S(2)}, u32[]{:S(2)}) collective-permute-start(bf16[64,1152]{1,0:T(8,128)(2,1)} %bitcast.14), channel_id=1, source_target_pairs={{0,4},{1,5},{2,6},{3,7},{4,0},{5,1},{6,2},{7,3},{8,12},{9,13},{10,... | collective-permute-start | bytes 442376 | tf_op jit(solution)/shard_map/ppermute | solution.py:103
  5.8 12.7 %collective-permute-start.1 = (bf16[64,1152]{1,0:T(8,128)(2,1)}, bf16[64,1152]{1,0:T(8,128)(2,1)S(1)}, u32[]{:S(2)}, u32[]{:S(2)}) collective-permute-start(bf16[64,1152]{1,0:T(8,128)(2,1)} %bitcast.15), channel_id=1, source_target_pairs={{0,2},{1,3},{2,0},{3,1},{4,6},{5,7},{6,4},{7,5},{8,10},{9,11},{10,... | collective-permute-start | bytes 442376 | tf_op jit(solution)/shard_map/ppermute | solution.py:103
  6.4 3.5 %collective-permute-start = (s32[256]{0:T(256)}, s32[256]{0:T(256)S(1)}, u32[]{:S(2)}, u32[]{:S(2)}) collective-permute-start(s32[256]{0:T(256)} %bitcast.21), channel_id=1, source_target_pairs={{0,1},{1,0},{2,3},{3,2},{4,5},{5,4},{6,7},{7,6},{8,9},{9,8},{10,11... | collective-permute-start | bytes 3080 | tf_op jit(solution)/shard_map/ppermute | solution.py:106
  6.4 15.9 %collective-permute-start.4 = (bf16[256,1152]{1,0:T(8,128)(2,1)}, bf16[256,1152]{1,0:T(8,128)(2,1)}, u32[]{:S(2)}, u32[]{:S(2)}) collective-permute-start(bf16[256,1152]{1,0:T(8,128)(2,1)} %bitcast.18), channel_id=1, source_target_pairs={{0,1},{1,0},{2,3},{3,2},{4,5},{5,4},{6,7},{7,6},{8,9},{9,8},{10,11... | collective-permute-start | bytes 1769480 | tf_op jit(solution)/shard_map/ppermute | solution.py:106
  9.9 11.1 %copy-start.1 = (bf16[512,1152]{1,0:T(8,128)(2,1)S(1)}, bf16[512,1152]{1,0:T(8,128)(2,1)}, u32[]{:S(2)}) copy-start(bf16[512,1152]{1,0:T(8,128)(2,1)} %constant_dynamic-update-slice_fusion.4) | copy-start | bytes 3538948
  19.4 12.4 %collective-permute-start.8 = (bf16[256,1152]{1,0:T(8,128)(2,1)S(1)}, bf16[256,1152]{1,0:T(8,128)(2,1)S(1)}, u32[]{:S(2)}, u32[]{:S(2)}) collective-permute-start(bf16[256,1152]{1,0:T(8,128)(2,1)S(1)} %pad_maximum_fusion.3), channel_id=1, source_target_pairs={{0,8},{1,17},{2,10},{3,19},{4,12},{5,21},{6,14},{7,23},{8,0},{9,25... | collective-permute-start | bytes 1769480 | tf_op jit(solution)/shard_map/ppermute | solution.py:125
  22.1 5.2 %copy-start.4 = (f32[256]{0:T(256)}, f32[256]{0:T(256)S(1)}, u32[]{:S(2)}) copy-start(f32[256]{0:T(256)S(1)} %add_rsqrt_fusion) | copy-start | bytes 3076
  22.1 1.1 %copy-start.3 = (bf16[1,256,1152]{2,1,0:T(8,128)(2,1)S(1)}, bf16[1,256,1152]{2,1,0:T(8,128)(2,1)}, u32[]{:S(2)}) copy-start(bf16[1,256,1152]{2,1,0:T(8,128)(2,1)} %param.7) | copy-start | bytes 1769476
  27.2 15.5 %collective-permute-start.9 = (f32[256,1152]{1,0:T(8,128)S(1)}, f32[256,1152]{1,0:T(8,128)S(1)}, u32[]{:S(2)}, u32[]{:S(2)}) collective-permute-start(f32[256,1152]{1,0:T(8,128)S(1)} %slice.41), channel_id=1, source_target_pairs={{0,1},{1,0},{2,3},{3,2},{4,5},{5,4},{6,7},{7,6},{8,9},{9,8},{10,11... | collective-permute-start | bytes 3538952 | tf_op jit(solution)/shard_map/ppermute | solution.py:106
  27.3 15.2 %slice-start = ((f32[256]{0:T(256)}), f32[64]{0:T(128)S(1)}, s32[]{:S(2)}) async-start(f32[256]{0:T(256)} %copy-done.4), calls=%async_computation | async-start | bytes 1024 | tf_op jit(solution)/shard_map/slice | solution.py:161
  27.3 8.7 %collective-permute-start.7 = (bf16[64,1152]{1,0:T(8,128)(2,1)S(1)}, bf16[64,1152]{1,0:T(8,128)(2,1)S(1)}, u32[]{:S(2)}, u32[]{:S(2)}) collective-permute-start(bf16[64,1152]{1,0:T(8,128)(2,1)S(1)} %get-tuple-element.17), channel_id=1, source_target_pairs={{0,6},{1,7},{2,4},{3,5},{4,2},{5,3},{6,0},{7,1},{8,14},{9,15},{10,... | collective-permute-start | bytes 442376 | tf_op jit(solution)/shard_map/ppermute | solution.py:103
  29.9 12.5 %collective-permute-start.6 = (bf16[64,1152]{1,0:T(8,128)(2,1)S(1)}, bf16[64,1152]{1,0:T(8,128)(2,1)S(1)}, u32[]{:S(2)}, u32[]{:S(2)}) collective-permute-start(bf16[64,1152]{1,0:T(8,128)(2,1)S(1)} %get-tuple-element.18), channel_id=1, source_target_pairs={{0,4},{1,5},{2,6},{3,7},{4,0},{5,1},{6,2},{7,3},{8,12},{9,13},{10,... | collective-permute-start | bytes 442376 | tf_op jit(solution)/shard_map/ppermute | solution.py:103
  29.9 12.5 %collective-permute-start.5 = (bf16[64,1152]{1,0:T(8,128)(2,1)S(1)}, bf16[64,1152]{1,0:T(8,128)(2,1)S(1)}, u32[]{:S(2)}, u32[]{:S(2)}) collective-permute-start(bf16[64,1152]{1,0:T(8,128)(2,1)S(1)} %get-tuple-element.19), channel_id=1, source_target_pairs={{0,2},{1,3},{2,0},{3,1},{4,6},{5,7},{6,4},{7,5},{8,10},{9,11},{10,... | collective-permute-start | bytes 442376 | tf_op jit(solution)/shard_map/ppermute | solution.py:103
  31.9 43.5 %collective-permute-start.11 = (bf16[512,1152]{1,0:T(8,128)(2,1)S(1)}, bf16[512,1152]{1,0:T(8,128)(2,1)S(1)}, u32[]{:S(2)}, u32[]{:S(2)}) collective-permute-start(bf16[512,1152]{1,0:T(8,128)(2,1)S(1)} %constant_dynamic-update-slice_fusion.refs_0_), channel_id=1, source_target_pairs={{0,1},{1,0},{2,3},{3,2},{4,5},{5,4},{6,7},{7,6},{8,9},{9,8},{10,11... | collective-permute-start | bytes 3538952 | tf_op jit(solution)/shard_map/ppermute | solution.py:106
  36.0 25.1 %collective-permute-start.10 = (bf16[512,1152]{1,0:T(8,128)(2,1)S(1)}, bf16[512,1152]{1,0:T(8,128)(2,1)S(1)}, u32[]{:S(2)}, u32[]{:S(2)}) collective-permute-start(bf16[512,1152]{1,0:T(8,128)(2,1)S(1)} %constant_dynamic-update-slice_fusion.refs_0_), channel_id=1, source_target_pairs={{0,16},{1,9},{2,18},{3,11},{4,20},{5,13},{6,22},{7,15},{8,24},{9,1... | collective-permute-start | bytes 3538952 | tf_op jit(solution)/shard_map/ppermute | solution.py:125
  42.7 8.7 %collective-permute-start.19 = (bf16[64,1152]{1,0:T(8,128)(2,1)S(1)}, bf16[64,1152]{1,0:T(8,128)(2,1)S(1)}, u32[]{:S(2)}, u32[]{:S(2)}) collective-permute-start(bf16[64,1152]{1,0:T(8,128)(2,1)S(1)} %multiply_convert_fusion), channel_id=1, source_target_pairs={{0,6},{1,7},{2,4},{3,5},{4,2},{5,3},{6,0},{7,1},{8,14},{9,15},{10,... | collective-permute-start | bytes 442376 | tf_op jit(solution)/shard_map/ppermute | solution.py:103
  44.7 12.6 %collective-permute-start.18 = (bf16[64,1152]{1,0:T(8,128)(2,1)S(1)}, bf16[64,1152]{1,0:T(8,128)(2,1)S(1)}, u32[]{:S(2)}, u32[]{:S(2)}) collective-permute-start(bf16[64,1152]{1,0:T(8,128)(2,1)S(1)} %multiply_convert_fusion), channel_id=1, source_target_pairs={{0,4},{1,5},{2,6},{3,7},{4,0},{5,1},{6,2},{7,3},{8,12},{9,13},{10,... | collective-permute-start | bytes 442376 | tf_op jit(solution)/shard_map/ppermute | solution.py:103
  44.7 14.9 %collective-permute-start.15 = (bf16[64,1152]{1,0:T(8,128)(2,1)S(1)}, bf16[64,1152]{1,0:T(8,128)(2,1)S(1)}, u32[]{:S(2)}, u32[]{:S(2)}) collective-permute-start(bf16[64,1152]{1,0:T(8,128)(2,1)S(1)} %multiply_convert_fusion), channel_id=1, source_target_pairs={{0,2},{1,3},{2,0},{3,1},{4,6},{5,7},{6,4},{7,5},{8,10},{9,11},{10,... | collective-permute-start | bytes 442376 | tf_op jit(solution)/shard_map/ppermute | solution.py:103
  51.4 6.6 %collective-permute-start.13 = (bf16[64,1152]{1,0:T(8,128)(2,1)S(1)}, bf16[64,1152]{1,0:T(8,128)(2,1)S(1)}, u32[]{:S(2)}, u32[]{:S(2)}) collective-permute-start(bf16[64,1152]{1,0:T(8,128)(2,1)S(1)} %multiply_convert_fusion), channel_id=1, source_target_pairs={{0,8},{1,17},{2,10},{3,19},{4,12},{5,21},{6,14},{7,23},{8,0},{9,25... | collective-permute-start | bytes 442376 | tf_op jit(solution)/shard_map/ppermute | solution.py:125
  57.3 11.8 %collective-permute-start.20 = (bf16[128,1152]{1,0:T(8,128)(2,1)S(1)}, bf16[128,1152]{1,0:T(8,128)(2,1)S(1)}, u32[]{:S(2)}, u32[]{:S(2)}) collective-permute-start(bf16[128,1152]{1,0:T(8,128)(2,1)S(1)} %pad_maximum_fusion.6), channel_id=1, source_target_pairs={{0,8},{1,17},{2,10},{3,19},{4,12},{5,21},{6,14},{7,23},{8,0},{9,25... | collective-permute-start | bytes 884744 | tf_op jit(solution)/shard_map/ppermute | solution.py:125
  58.0 12.8 %collective-permute-start.14 = (bf16[128,1152]{1,0:T(8,128)(2,1)S(1)}, bf16[128,1152]{1,0:T(8,128)(2,1)S(1)}, u32[]{:S(2)}, u32[]{:S(2)}) collective-permute-start(bf16[128,1152]{1,0:T(8,128)(2,1)S(1)} %pad_maximum_fusion.4), channel_id=1, source_target_pairs={{0,16},{1,9},{2,18},{3,11},{4,20},{5,13},{6,22},{7,15},{8,24},{9,1... | collective-permute-start | bytes 884744 | tf_op jit(solution)/shard_map/ppermute | solution.py:125
  59.6 9.0 %collective-permute-start.16 = (bf16[64,1152]{1,0:T(8,128)(2,1)S(1)}, bf16[64,1152]{1,0:T(8,128)(2,1)S(1)}, u32[]{:S(2)}, u32[]{:S(2)}) collective-permute-start(bf16[64,1152]{1,0:T(8,128)(2,1)S(1)} %collective-permute-done.15), channel_id=1, source_target_pairs={{0,8},{1,17},{2,10},{3,19},{4,12},{5,21},{6,14},{7,23},{8,0},{9,25... | collective-permute-start | bytes 442376 | tf_op jit(solution)/shard_map/ppermute | solution.py:125
  61.1 14.8 %collective-permute-start.12 = (bf16[512,1152]{1,0:T(8,128)(2,1)S(1)}, bf16[512,1152]{1,0:T(8,128)(2,1)S(1)}, u32[]{:S(2)}, u32[]{:S(2)}) collective-permute-start(bf16[512,1152]{1,0:T(8,128)(2,1)S(1)} %collective-permute-done.10.refs_1_), channel_id=1, source_target_pairs={{0,1},{1,0},{2,3},{3,2},{4,5},{5,4},{6,7},{7,6},{8,9},{9,8},{10,11... | collective-permute-start | bytes 3538952 | tf_op jit(solution)/shard_map/ppermute | solution.py:106
  68.5 6.8 %collective-permute-start.17 = (bf16[128,1152]{1,0:T(8,128)(2,1)S(1)}, bf16[128,1152]{1,0:T(8,128)(2,1)S(1)}, u32[]{:S(2)}, u32[]{:S(2)}) collective-permute-start(bf16[128,1152]{1,0:T(8,128)(2,1)S(1)} %pad_maximum_fusion.5), channel_id=1, source_target_pairs={{0,16},{1,9},{2,18},{3,11},{4,20},{5,13},{6,22},{7,15},{8,24},{9,1... | collective-permute-start | bytes 884744 | tf_op jit(solution)/shard_map/ppermute | solution.py:125
  69.2 12.5 %collective-permute-start.21 = (bf16[256,1152]{1,0:T(8,128)(2,1)S(1)}, bf16[256,1152]{1,0:T(8,128)(2,1)S(1)}, u32[]{:S(2)}, u32[]{:S(2)}) collective-permute-start(bf16[256,1152]{1,0:T(8,128)(2,1)S(1)} %constant_dynamic-update-slice_fusion.11.refs_2_), channel_id=1, source_target_pairs={{0,16},{1,9},{2,18},{3,11},{4,20},{5,13},{6,22},{7,15},{8,24},{9,1... | collective-permute-start | bytes 1769480 | tf_op jit(solution)/shard_map/ppermute | solution.py:125
  70.8 12.0 %collective-permute-start.24 = (bf16[256,1152]{1,0:T(8,128)(2,1)S(1)}, bf16[256,1152]{1,0:T(8,128)(2,1)S(1)}, u32[]{:S(2)}, u32[]{:S(2)}) collective-permute-start(bf16[256,1152]{1,0:T(8,128)(2,1)S(1)} %constant_dynamic-update-slice_fusion.11.refs_2_), channel_id=1, source_target_pairs={{0,1},{1,0},{2,3},{3,2},{4,5},{5,4},{6,7},{7,6},{8,9},{9,8},{10,11... | collective-permute-start | bytes 1769480 | tf_op jit(solution)/shard_map/ppermute | solution.py:106
  75.3 7.5 %collective-permute-start.22 = (bf16[256,1152]{1,0:T(8,128)(2,1)S(1)}, bf16[256,1152]{1,0:T(8,128)(2,1)S(1)}, u32[]{:S(2)}, u32[]{:S(2)}) collective-permute-start(bf16[256,1152]{1,0:T(8,128)(2,1)S(1)} %constant_dynamic-update-slice_fusion.5.refs_0_), channel_id=1, source_target_pairs={{0,1},{1,0},{2,3},{3,2},{4,5},{5,4},{6,7},{7,6},{8,9},{9,8},{10,11... | collective-permute-start | bytes 1769480 | tf_op jit(solution)/shard_map/ppermute | solution.py:106
  75.4 7.4 %collective-permute-start.23 = (bf16[256,1152]{1,0:T(8,128)(2,1)S(1)}, bf16[256,1152]{1,0:T(8,128)(2,1)S(1)}, u32[]{:S(2)}, u32[]{:S(2)}) collective-permute-start(bf16[256,1152]{1,0:T(8,128)(2,1)S(1)} %constant_dynamic-update-slice_fusion.8.refs_1_), channel_id=1, source_target_pairs={{0,1},{1,0},{2,3},{3,2},{4,5},{5,4},{6,7},{7,6},{8,9},{9,8},{10,11... | collective-permute-start | bytes 1769480 | tf_op jit(solution)/shard_map/ppermute | solution.py:106
  81.6 2.0 %collective-permute-start.25 = (bf16[256,1152]{1,0:T(8,128)(2,1)S(1)}, bf16[256,1152]{1,0:T(8,128)(2,1)S(1)}, u32[]{:S(2)}, u32[]{:S(2)}) collective-permute-start(bf16[256,1152]{1,0:T(8,128)(2,1)S(1)} %collective-permute-done.21.refs_3_), channel_id=1, source_target_pairs={{0,1},{1,0},{2,3},{3,2},{4,5},{5,4},{6,7},{7,6},{8,9},{9,8},{10,11... | collective-permute-start | bytes 1769480 | tf_op jit(solution)/shard_map/ppermute | solution.py:106

commit v4 on v3

v4 whole, which is shorter than its diff:
```python
import functools

import jax
import jax.numpy as jnp
from jax import lax
from jax.experimental import pallas as pl
from jax.experimental.pallas import tpu as pltpu
from jax.sharding import PartitionSpec as P

FIRST = (((0,), (0,)), ((), ()))
LAST = (((1,), (1,)), ((), ()))
F32 = jnp.float32
BF16 = jnp.bfloat16


def dot(a, b, dims=(((1,), (0,)), ((), ()))):
    return lax.dot_general(a, b, dims, preferred_element_type=F32)


def after(v, *others):
    return lax.optimization_barrier((v, others))[0]


def score_kernel(nz, scale, offset, index, embed, *refs):
    labels, captions, refs = refs[:2], refs[2:4], refs[4:]
    own, unit_own, inv_own, unit, dlogit = refs[:5]
    sent, (caps, sems) = refs[5:-2], refs[-2:]
    n_img, n_cap = embed.shape[0] // nz, captions[0].shape[0]
    copies = []
    for i in range(2):
        here = caps.at[i * n_cap : (i + 1) * n_cap, :]
        copies.append(pltpu.make_async_copy(captions[i], here, sems.at[i]))
        copies[-1].start()
    embed = embed[...]
    inv_norm = lax.rsqrt(jnp.sum(embed * embed, axis=1, keepdims=True) + 1e-06)
    unit_f = embed * inv_norm
    unit_own[...] = unit_f[:n_img]
    inv_own[...] = inv_norm[:n_img]
    u = unit_f.astype(BF16)
    unit[...] = u
    ids = []
    for k in range(nz):
        first = (index[0] ^ (2 * k)) * n_img
        ids.append(first + lax.broadcasted_iota(jnp.int32, (n_img, 1), 0))
    ids = jnp.concatenate(ids)
    labs = jnp.concatenate([v[...] for v in labels], axis=1)
    sign = jnp.where(labs == ids, 1.0, -1.0).astype(F32)
    for copy in copies:
        copy.wait()
    logits = scale[0] * dot(u, caps[...], LAST) + offset[0]
    d = (-sign * jax.nn.sigmoid(-sign * logits)).astype(BF16)
    dlogit[...] = d
    part = scale[0] * dot(d, caps[...])
    own[...] = part[:n_img]
    for k in range(1, nz):
        sent[k - 1][...] = part[k * n_img : (k + 1) * n_img].astype(BF16)


def scores(nz, scale, offset, index, embed, labels, captions):
    images, depth = embed.shape
    n_img, n_cap = images // nz, captions[0].shape[0]
    caps = 2 * n_cap
    smem = pl.BlockSpec(memory_space=pltpu.SMEM)
    vmem = pl.BlockSpec(memory_space=pltpu.VMEM)
    block = jax.ShapeDtypeStruct((n_img, depth), F32)
    outs = [
        block,
        block,
        jax.ShapeDtypeStruct((n_img, 1), F32),
        jax.ShapeDtypeStruct((images, depth), BF16),
        jax.ShapeDtypeStruct((images, caps), BF16),
    ] + [jax.ShapeDtypeStruct((n_img, depth), BF16)] * (nz - 1)
    return pl.pallas_call(
        functools.partial(score_kernel, nz),
        out_shape=outs,
        in_specs=[smem] * 3
        + [vmem] * 3
        + [pl.BlockSpec(memory_space=pl.ANY)] * 2,
        out_specs=[vmem] * len(outs),
        scratch_shapes=[pltpu.VMEM((caps, depth), BF16), pltpu.SemaphoreType.DMA((2,))],
        compiler_params=pltpu.CompilerParams(
            vmem_limit_bytes=12 * 2**20 + 24 * images * depth
        ),
        cost_estimate=pl.CostEstimate(
            flops=4 * images * depth * caps,
            bytes_accessed=2 * depth * (caps + 6 * images),
            transcendentals=images * caps,
        ),
    )(scale, offset, index, embed, *labels, *captions)


def turn_kernel(plan, *refs):
    ins, outs = refs[: -len(plan)], refs[-len(plan) :]
    for out, pieces in zip(outs, plan):
        col = 0
        for runs in pieces:
            rows = [ins[i][at : at + size, :] for i, at, size in runs]
            rows = jnp.concatenate(rows)
            out[:, col : col + rows.shape[0]] = rows.T
            col += rows.shape[0]


def turned(xs, plan):
    depth = xs[0].shape[1]
    images = [sum(size for runs in pieces for _, _, size in runs) for pieces in plan]
    return pl.pallas_call(
        functools.partial(turn_kernel, plan),
        out_shape=[jax.ShapeDtypeStruct((depth, n), BF16) for n in images],
        in_specs=[pl.BlockSpec(memory_space=pltpu.VMEM)] * len(xs),
        out_specs=[pl.BlockSpec(memory_space=pltpu.VMEM)] * len(plan),
        compiler_params=pltpu.CompilerParams(vmem_limit_bytes=16 * 2**20),
        cost_estimate=pl.CostEstimate(
            flops=0, bytes_accessed=4 * sum(images) * depth, transcendentals=0
        ),
    )(*xs)


def weight_kernel(factor, has_acc, x_t, *refs):
    gs, (out, stacked, tiles, sems) = refs[has_acc:-4], refs[-4:]
    n, rows = tiles.shape[:2]
    here = [slice(i * rows, (i + 1) * rows) for i in range(n)]
    held, copies = [], []
    for i in range(n if has_acc else 0):
        held.append(
            pltpu.make_async_copy(refs[0].at[here[i], :], tiles.at[i], sems.at[n + i])
        )
        held[-1].start()
    at = 0
    for g in gs:
        stacked[at : at + g.shape[0], :] = g[...]
        at += g.shape[0]
    for i in range(n):
        total = dot(x_t[here[i], :], stacked[...])
        if has_acc:
            held[i].wait()
            total = tiles[i] + total
        tiles[i] = total * factor
        copies.append(
            pltpu.make_async_copy(tiles.at[i], out.at[here[i], :], sems.at[i])
        )
        copies[-1].start()
    for copy in copies:
        copy.wait()


def weight_sum(acc, x_t, gs, factor):
    depth, images = x_t.shape
    n = 3
    has_acc = acc is not None
    vmem = pl.BlockSpec(memory_space=pltpu.VMEM)
    anywhere = pl.BlockSpec(memory_space=pl.ANY)
    return pl.pallas_call(
        functools.partial(weight_kernel, factor, int(has_acc)),
        out_shape=jax.ShapeDtypeStruct((depth, depth), F32),
        in_specs=[vmem] + [anywhere] * has_acc + [vmem] * len(gs),
        out_specs=anywhere,
        scratch_shapes=[
            pltpu.VMEM((images, depth), BF16),
            pltpu.VMEM((n, depth // n, depth), F32),
            pltpu.SemaphoreType.DMA((2 * n,)),
        ],
        compiler_params=pltpu.CompilerParams(vmem_limit_bytes=20 * 2**20),
        cost_estimate=pl.CostEstimate(
            flops=2 * images * depth * depth,
            bytes_accessed=4 * images * depth + 4 * depth * depth * (1 + has_acc),
            transcendentals=0,
        ),
    )(x_t, *([acc] if has_acc else []), *gs)


def on_device(x, captions, labels, weight, scale, offset):
    x, captions = x[0], captions[0]
    n_img, depth = x.shape
    n_cap = captions.shape[0]
    nd, nb = lax.axis_size("dp"), lax.axis_size("blk")
    nz = nb // 2
    index = lax.axis_index("blk")
    bits = nd.bit_length() - 1

    def along_z(v, k):
        return lax.ppermute(v, "blk", [(i, i ^ (2 * k)) for i in range(nb)])

    def swap(v):
        return lax.ppermute(v, "blk", [(i, i ^ 1) for i in range(nb)])

    def step_d(v, i):
        perm = []
        for j in range(nd):
            for m in range(nb):
                to = j ^ (1 << ((i + m % 2) % bits))
                perm.append((j * nb + m, to * nb + m))
        return lax.ppermute(v, ("dp", "blk"), perm)

    xs = [x] + [along_z(x, k) for k in range(1, nz)]
    embed = dot(jnp.concatenate(xs), weight)
    own, u, inv_norm, unit, dlogit, *sent = scores(
        nz,
        scale.reshape(1),
        offset.reshape(1),
        index.reshape(1),
        embed,
        [labels, swap(labels)],
        [captions, swap(captions)],
    )
    back = [along_z(v, k + 1) for k, v in enumerate(sent)]

    xs, dlogit = after((xs, dlogit), back[0])
    x_own = jnp.concatenate(xs)
    for i in range(bits):
        x_own = [x_own, step_d(x_own, i)]
        if i < bits - 1:
            x_own = jnp.concatenate(x_own)

    adjoint = scale * dot(dlogit, unit, FIRST)
    adjoint_other = swap(adjoint[n_cap:])
    adjoint = adjoint[:n_cap] + adjoint_other

    back = after(back, x_own[0])
    for v in back:
        own = own + v.astype(F32)
    radial = jnp.sum(u * own, axis=1, keepdims=True)
    ge = ((own - u * radial) * inv_norm).astype(BF16)
    grad_features = dot(ge, weight, LAST)
    ge = after(ge, adjoint_other)

    half = nz // 2
    near = [along_z(ge, k) for k in range(1, half)]
    own_first = step_d(ge, 0)
    far = [along_z(ge, k) for k in range(half, nz)]

    def over_d(v, first, *before):
        v = [v, first]
        for i in range(1, bits):
            v = after(jnp.concatenate(v), before)
            v = [v, step_d(v, i)]
        return v

    g_own = over_d(ge, own_first)
    near = after(jnp.concatenate(near), g_own[0])
    near_first = step_d(near, 0)
    g_near = over_d(near, near_first)
    far = after(jnp.concatenate(far), near)
    small = nd * nb * n_img <= 2048
    before = []
    if small:
        g_own = jnp.concatenate(g_own)
        x_other = [swap(after(v, near)) for v in x_own]
        before = x_other + [swap(g_own)]
    g_far = over_d(far, step_d(far, 0), before)
    sizes = [n_img, n_img * (half - 1), n_img * half]
    firsts = [0, n_img, n_img * half]
    n_own = nz * n_img
    per = nd // 2
    if small:
        plan = [[], []]
        for core in range(2):
            for g in range(3):
                runs = [
                    (2 * core + i // per, (i % per) * n_own + firsts[g], sizes[g])
                    for i in range(nd)
                ]
                if g < 2:
                    plan[0].append(runs)
                else:
                    plan[0].append(runs[:per])
                    plan[1].append(runs[per:])
        early = [g_own, jnp.concatenate(g_near), g_far[0]]
        x_early, x_late = turned(x_own + x_other, plan)
        others = [before[2], swap(early[1]), swap(after(early[2], g_near[1]))]
        acc = weight_sum(None, x_early, early + others, 1.0)
        late = after(g_far[1], acc)
        grad_weight = weight_sum(acc, x_late, [late, swap(late)], 1.0 / nd)
    else:
        grad_weight = 0.0
        for i, x_part in enumerate(x_own):
            for at in range(per):
                g_part = [
                    g[i][at * m : (at + 1) * m]
                    for m, g in zip(sizes, (g_own, g_near, g_far))
                ]
                grad_weight = grad_weight + dot(
                    x_part[at * n_own : (at + 1) * n_own],
                    jnp.concatenate(g_part),
                    FIRST,
                )
        grad_weight = (grad_weight + swap(grad_weight)) / nd
    return (grad_features[None], adjoint[None], grad_weight)


def solution(mesh):
    placed = (P("dp", "blk", None), P("dp", "blk", None), P("dp", "blk"), P(), P(), P())
    return jax.shard_map(
        on_device,
        mesh=mesh,
        in_specs=placed,
        out_specs=(P("dp", "blk", None), P("dp", "blk", None), P()),
        check_vma=False,
    )
```

time: 91.5 us -> 97.6 us (1.067)
  waiting for transfers between devices: 41.6 us -> 32.8 us
  Pallas kernels: 8.92 us -> 17.4 us
  local copies, waits for them, and re-layouts: 2.94 us -> 8.5 us
  other arithmetic: 3.46 us -> 6.2 us
  matrix products: 6.57 us -> 4.24 us
    ppermute x9, waiting for transfers between devices: 24.7 us -> 14.8 us  [along_z(): return lax.ppermute(v, 'blk', [(i, i ^ 2 * k) for i in range(nb)])]
    pallas_call x2 -> x4, Pallas kernels: 8.92 us -> 17.4 us  [the longest x2 12.3 us: weight_sum(): pl.pallas_call(functools.partial(weight_kernel, factor, int(has_acc)), ou...]
    unnamed x20 -> x26, local copies, waits for them, and re-layouts: 2.66 us -> 6.47 us
    dot_general x5 -> x3, matrix products: 6.57 us -> 4.24 us  [dot(): return lax.dot_general(a, b, dims, preferred_element_type=F32)]
    ppermute x8, waiting for transfers between devices: 16.1 us -> 18 us  [step_d(): return lax.ppermute(v, ('dp', 'blk'), perm)]
    ppermute x9, starting transfers between devices: 14.7 us -> 13.3 us  [along_z(): return lax.ppermute(v, 'blk', [(i, i ^ 2 * k) for i in range(nb)])]
    broadcast_in_dim x1, other arithmetic: 1.13 us -> 2.45 us  [on_device(): return (grad_features[None], adjoint[None], grad_weight)]
    ppermute x8, starting transfers between devices: 9.44 us -> 10.7 us  [step_d(): return lax.ppermute(v, ('dp', 'blk'), perm)]
  transfers between devices with their start and end apart: 26 -> 26, of which waited for: 10 -> 9; matrix products, arithmetic and copies ran while one was open for 13% -> 18% of each run, Pallas kernels for 1% -> 10%
where the time goes in v4:
time: 97.6 us; the launch traced here: 97.2 us
  waiting for transfers between devices  32.8 us (34%)
  starting transfers between devices  25.8 us (26%)
  Pallas kernels  17.4 us (18%)
  local copies, waits for them, and re-layouts  8.5 us (9%)
  other arithmetic  6.2 us (6%)
  matrix products  4.24 us (4%)
  between operations  2.19 us (2%)
    ppermute x8, waiting for transfers between devices, step_d(): return lax.ppermute(v, ('dp', 'blk'), perm)  18 us
    ppermute x9, waiting for transfers between devices, along_z(): return lax.ppermute(v, 'blk', [(i, i ^ 2 * k) for i in range(nb)])  14.8 us
    ppermute x9, starting transfers between devices, along_z(): return lax.ppermute(v, 'blk', [(i, i ^ 2 * k) for i in range(nb)])  13.3 us
    pallas_call x2, Pallas kernels, weight_sum(): pl.pallas_call(functools.partial(weight_kernel, factor, int(has_acc)), ou...  12.3 us
    ppermute x8, starting transfers between devices, step_d(): return lax.ppermute(v, ('dp', 'blk'), perm)  10.7 us
    unnamed x26, local copies, waits for them, and re-layouts  6.47 us
    dot_general x3, matrix products, dot(): return lax.dot_general(a, b, dims, preferred_element_type=F32)  4.24 us
    pallas_call x1, Pallas kernels, turned(): pl.pallas_call(functools.partial(turn_kernel, plan), out_shape=[jax.Shape...  2.89 us
  transfers between devices with their start and end apart: 26, of which 9 were waited for; matrix products, arithmetic and copies ran while one was open for 18% of the time, Pallas kernels for 10%

profile of v4, /device:TPU:0, one launch (start us, length us, event | category | flops | bytes accessed | tf_op | source)
XLA Modules:
  0.0 97.2 jit_solution(16170573228166713761)
XLA Ops:
  0.6 0.0 copy-start
  0.6 0.5 collective-permute-start.4
  1.2 4.7 %collective-permute-start.2 = (bf16[64,1152]{1,0:T(8,128)(2,1)}, bf16[64,1152]{1,0:T(8,128)(2,1)S(1)}, u32[]{:S(2)}, u32[]{:S(2)}) collective-permute-start(bf16[64,1152]{1,0:T(8,128)(2,1)} %bitcast.18), channel_id=1, source_target_pairs={{0,6},{1,7},{2,4},{3,5},{4,2},{5,3},{6,0},{7,1},{8,14},{9,15},{10,... | collective-permute-start | bytes 442376 | tf_op jit(solution)/shard_map/ppermute | solution.py:181
  5.8 0.6 collective-permute-start
  7.8 3.1 %collective-permute-done.2 = bf16[64,1152]{1,0:T(8,128)(2,1)S(1)} collective-permute-done((bf16[64,1152]{1,0:T(8,128)(2,1)}, bf16[64,1152]{1,0:T(8,128)(2,1)S(1)}, u32[]{:S(2)}, u32[]{:S(2)}) %collective-permute-start.2) | collective-permute-done | bytes 147488 | tf_op jit(solution)/shard_map/ppermute | solution.py:181
  10.9 8.4 %collective-permute-done.1 = bf16[64,1152]{1,0:T(8,128)(2,1)} collective-permute-done((bf16[64,1152]{1,0:T(8,128)(2,1)}, bf16[64,1152]{1,0:T(8,128)(2,1)}, u32[]{:S(2)}, u32[]{:S(2)}) %collective-permute-start.1) | collective-permute-done | bytes 147488 | tf_op jit(solution)/shard_map/ppermute | solution.py:181
  19.3 2.0 %fusion.1.embed = f32[256,1152]{1,0:T(8,128)S(1)} fusion(bf16[1152,1152]{1,0:T(8,128)(2,1)S(1)} %copy-done, bf16[64,1152]{1,0:T(8,128)(2,1)S(1)} %collective-permute-done.2, bf16[64,1152]{1,0:T(8,128)(2,1)} %collective-permute-done.1, bf16[64,1152]{1,0:T(8,128)(2,1)} %collective-permute-done, bf16[64,1152]{1,0:T(8,128)(2,1)} %bitcast.21), kind=kOutput, calls=%fused_computation.4 | convolution fusion | flops 681836544 | bytes 4423680 | tf_op jit(solution)/shard_map/dot_general | solution.py:17
  21.3 0.0 copy-start.2
  21.3 0.8 copy-done.2
  22.2 1.1 %copy-done.3 = bf16[256,1152]{1,0:T(8,128)(2,1)S(1)} copy-done((bf16[256,1152]{1,0:T(8,128)(2,1)S(1)}, bf16[256,1152]{1,0:T(8,128)(2,1)}, u32[]{:S(2)}) %copy-start.3) | copy-done | bytes 589848
  23.2 2.2 %shard_map.85 = (f32[64,1152]{1,0:T(8,128)S(1)}, f32[64,1152]{1,0:T(8,128)S(1)}, f32[64,1]{1,0:T(8,128)S(1)}, bf16[256,1152]{1,0:T(8,128)(2,1)S(1)}, bf16[256,51...) custom-call(f32[1]{0:T(128)} %bitcast.14.scale, ...), custom_call_target="tpu_custom_call" | custom-call | flops 603979776 | bytes 4718592 | tf_op jit(solution)/shard_map/pallas_call | solution.py:73
  25.5 0.1 collective-permute-start.5
  25.5 3.0 %collective-permute-start.6 = (bf16[64,1152]{1,0:T(8,128)(2,1)}, bf16[64,1152]{1,0:T(8,128)(2,1)}, u32[]{:S(2)}, u32[]{:S(2)}) collective-permute-start(bf16[64,1152]{1,0:T(8,128)(2,1)} %get-tuple-element.31), channel_id=1, source_target_pairs={{0,4},{1,5},{2,6},{3,7},{4,0},{5,1},{6,2},{7,3},{8,12},{9,13},{10,... | collective-permute-start | bytes 442376 | tf_op jit(solution)/shard_map/ppermute | solution.py:181
  28.6 1.3 %collective-permute-start.7 = (bf16[64,1152]{1,0:T(8,128)(2,1)S(1)}, bf16[64,1152]{1,0:T(8,128)(2,1)}, u32[]{:S(2)}, u32[]{:S(2)}) collective-permute-start(bf16[64,1152]{1,0:T(8,128)(2,1)S(1)} %get-tuple-element.32), channel_id=1, source_target_pairs={{0,6},{1,7},{2,4},{3,5},{4,2},{5,3},{6,0},{7,1},{8,14},{9,15},{10,... | collective-permute-start | bytes 442376 | tf_op jit(solution)/shard_map/ppermute | solution.py:181
  29.9 3.3 %collective-permute-done.5 = bf16[64,1152]{1,0:T(8,128)(2,1)S(1)} collective-permute-done((bf16[64,1152]{1,0:T(8,128)(2,1)S(1)}, bf16[64,1152]{1,0:T(8,128)(2,1)S(1)}, u32[]{:S(2)}, u32[]{:S(2)}) %collective-permute-start.5) | collective-permute-done | bytes 147488 | tf_op jit(solution)/shard_map/ppermute | solution.py:181
  33.2 0.7 constant_dynamic-update-slice_fusion.4
  33.9 1.0 %pad_maximum_fusion = bf16[256,1152]{1,0:T(8,128)(2,1)S(1)} fusion(bf16[64,1152]{1,0:T(8,128)(2,1)S(1)} %copy-done.9, bf16[64,1152]{1,0:T(8,128)(2,1)} %collective-permute-done.1, bf16[64,1152]{1,0:T(8,128)(2,1)} %collective-permute-done, bf16[64,1152]{1,0:T(8,128)(2,1)S(1)} %bitcast.23), kind=kLoop, calls=%fused_computation.12 | loop fusion | flops 2359296 | bytes 1179648 | tf_op jit(solution)/shard_map/concatenate | solution.py:208
  35.0 1.6 %collective-permute-start.8 = (bf16[256,1152]{1,0:T(8,128)(2,1)S(1)}, bf16[256,1152]{1,0:T(8,128)(2,1)S(1)}, u32[]{:S(2)}, u32[]{:S(2)}) collective-permute-start(bf16[256,1152]{1,0:T(8,128)(2,1)S(1)} %pad_maximum_fusion), channel_id=1, source_target_pairs={{0,8},{1,17},{2,10},{3,19},{4,12},{5,21},{6,14},{7,23},{8,0},{9,25... | collective-permute-start | bytes 1769480 | tf_op jit(solution)/shard_map/ppermute | solution.py:192
  36.5 0.5 convolution_multiply_fusion
  37.1 0.0 copy-start.5
  37.1 1.2 %slice.9 = f32[256,1152]{1,0:T(8,128)} slice(f32[512,1152]{1,0:T(8,128)S(1)} %convolution_multiply_fusion), slice={[256:512], [0:1152]} | slice | bytes 2359296 | tf_op jit(solution)/shard_map/slice | solution.py:215
  38.2 0.0 collective-permute-start.9
  38.2 1.6 %constant_dynamic-update-slice_fusion.3 = bf16[512,1152]{1,0:T(8,128)(2,1)} fusion(bf16[512,1152]{1,0:T(8,128)(2,1)} %constant_dynamic-update-slice_fusion.4, bf16[64,1152]{1,0:T(8,128)(2,1)} %collective-permute-done), kind=kLoop, calls=%fused_computation.25 | loop fusion | bytes 294912
  39.8 1.6 %constant_dynamic-update-slice_fusion.2 = bf16[512,1152]{1,0:T(8,128)(2,1)} fusion(bf16[512,1152]{1,0:T(8,128)(2,1)} %constant_dynamic-update-slice_fusion.3, bf16[64,1152]{1,0:T(8,128)(2,1)} %collective-permute-done.1), kind=kLoop, calls=%fused_computation.24 | loop fusion | bytes 294912
  41.4 0.7 constant_dynamic-update-slice_fusion.1
  42.1 2.8 %collective-permute-done.8 = bf16[256,1152]{1,0:T(8,128)(2,1)S(1)} collective-permute-done((bf16[256,1152]{1,0:T(8,128)(2,1)S(1)}, bf16[256,1152]{1,0:T(8,128)(2,1)S(1)}, u32[]{:S(2)}, u32[]{:S(2)}) %collective-permute-start.8) | collective-permute-done | bytes 589856 | tf_op jit(solution)/shard_map/ppermute | solution.py:192
  44.9 0.9 constant_dynamic-update-slice_fusion.refs_0_
  45.8 1.5 %collective-permute-start.10 = (bf16[512,1152]{1,0:T(8,128)(2,1)}, bf16[512,1152]{1,0:T(8,128)(2,1)}, u32[]{:S(2)}, u32[]{:S(2)}) collective-permute-start(bf16[512,1152]{1,0:T(8,128)(2,1)} %constant_dynamic-update-slice_fusion.refs_0_), channel_id=1, source_target_pairs={{0,16},{1,9},{2,18},{3,11},{4,20},{5,13},{6,22},{7,15},{8,24},{9,1... | collective-permute-start | bytes 3538952 | tf_op jit(solution)/shard_map/ppermute | solution.py:192
  47.3 0.1 reduce
  47.4 0.0 collective-permute-done.7
  47.5 1.2 %multiply_reduce_fusion = f32[64]{0:T(128)S(1)} fusion(f32[64,1152]{1,0:T(8,128)S(1)} %get-tuple-element.41, bf16[64,1152]{1,0:T(8,128)(2,1)} %collective-permute-done.7, bf16[64,1152]{1,0:T(8,128)(2,1)} %collective-permute-done.6, f32[64,1152]{1,0:T(8,128)S(1)} %get-tuple-element.29, bf16[64,1152]{1,0:T(8,128)(2,1)} %copy-done.10), kind=kLoop, calls=%fused_computation.20 | loop fusion | flops 589760 | bytes 1032448 | tf_op jit(solution)/shard_map/reduce_sum | solution.py:221
  48.7 1.2 %multiply_convert_fusion = bf16[64,1152]{1,0:T(8,128)(2,1)S(1)} fusion(f32[64,1152]{1,0:T(8,128)S(1)} %get-tuple-element.41, f32[64]{0:T(128)S(1)} %reduce, f32[64]{0:T(128)S(1)} %multiply_reduce_fusion, bf16[64,1152]{1,0:T(8,128)(2,1)} %collective-permute-done.7, bf16[64,1152]{1,0:T(8,128)(2,1)} %collective-permute-done.6, ...), kind=kLoop, calls=%fused_computation.19 | loop fusion | flops 737280 | bytes 1180160 | tf_op jit(solution)/shard_map/convert_element_type | solution.py:222
  49.9 1.5 %collective-permute-start.12 = (bf16[64,1152]{1,0:T(8,128)(2,1)S(1)}, bf16[64,1152]{1,0:T(8,128)(2,1)S(1)}, u32[]{:S(2)}, u32[]{:S(2)}) collective-permute-start(bf16[64,1152]{1,0:T(8,128)(2,1)S(1)} %multiply_convert_fusion), channel_id=1, source_target_pairs={{0,8},{1,17},{2,10},{3,19},{4,12},{5,21},{6,14},{7,23},{8,0},{9,25... | collective-permute-start | bytes 442376 | tf_op jit(solution)/shard_map/ppermute | solution.py:192
  51.4 1.8 %collective-permute-start.19 = (bf16[64,1152]{1,0:T(8,128)(2,1)S(1)}, bf16[64,1152]{1,0:T(8,128)(2,1)S(1)}, u32[]{:S(2)}, u32[]{:S(2)}) collective-permute-start(bf16[64,1152]{1,0:T(8,128)(2,1)S(1)} %multiply_convert_fusion), channel_id=1, source_target_pairs={{0,6},{1,7},{2,4},{3,5},{4,2},{5,3},{6,0},{7,1},{8,14},{9,15},{10,... | collective-permute-start | bytes 442376 | tf_op jit(solution)/shard_map/ppermute | solution.py:181
  53.2 1.7 %collective-permute-start.18 = (bf16[64,1152]{1,0:T(8,128)(2,1)S(1)}, bf16[64,1152]{1,0:T(8,128)(2,1)S(1)}, u32[]{:S(2)}, u32[]{:S(2)}) collective-permute-start(bf16[64,1152]{1,0:T(8,128)(2,1)S(1)} %multiply_convert_fusion), channel_id=1, source_target_pairs={{0,4},{1,5},{2,6},{3,7},{4,0},{5,1},{6,2},{7,3},{8,12},{9,13},{10,... | collective-permute-start | bytes 442376 | tf_op jit(solution)/shard_map/ppermute | solution.py:181
  54.9 1.8 %collective-permute-done.12 = bf16[64,1152]{1,0:T(8,128)(2,1)S(1)} collective-permute-done((bf16[64,1152]{1,0:T(8,128)(2,1)S(1)}, bf16[64,1152]{1,0:T(8,128)(2,1)S(1)}, u32[]{:S(2)}, u32[]{:S(2)}) %collective-permute-start.12) | collective-permute-done | bytes 147488 | tf_op jit(solution)/shard_map/ppermute | solution.py:192
  56.7 0.6 collective-permute-start.15
  57.3 0.0 collective-permute-done.11
  57.3 1.5 %collective-permute-start.16 = (bf16[64,1152]{1,0:T(8,128)(2,1)S(1)}, bf16[64,1152]{1,0:T(8,128)(2,1)S(1)}, u32[]{:S(2)}, u32[]{:S(2)}) collective-permute-start(bf16[64,1152]{1,0:T(8,128)(2,1)S(1)} %collective-permute-done.11), channel_id=1, source_target_pairs={{0,8},{1,17},{2,10},{3,19},{4,12},{5,21},{6,14},{7,23},{8,0},{9,25... | collective-permute-start | bytes 442376 | tf_op jit(solution)/shard_map/ppermute | solution.py:192
  58.8 6.7 %collective-permute-done.10.refs_1_ = bf16[512,1152]{1,0:T(8,128)(2,1)} collective-permute-done((bf16[512,1152]{1,0:T(8,128)(2,1)}, bf16[512,1152]{1,0:T(8,128)(2,1)}, u32[]{:S(2)}, u32[]{:S(2)}) %collective-permute-start.10) | collective-permute-done | bytes 1179680 | tf_op jit(solution)/shard_map/ppermute | solution.py:192
  65.5 0.0 collective-permute-start.13
  65.5 0.0 collective-permute-done.19
  65.5 0.5 collective-permute-start.14
  66.0 0.0 collective-permute-done.18
  66.0 0.9 collective-permute-start.20
  66.9 1.6 %collective-permute-done.15 = bf16[128,1152]{1,0:T(8,128)(2,1)S(1)} collective-permute-done((bf16[128,1152]{1,0:T(8,128)(2,1)S(1)}, bf16[128,1152]{1,0:T(8,128)(2,1)S(1)}, u32[]{:S(2)}, u32[]{:S(2)}) %collective-permute-start.15) | collective-permute-done | bytes 294944 | tf_op jit(solution)/shard_map/ppermute | solution.py:192
  68.6 0.1 collective-permute-start.21
  68.7 0.0 collective-permute-done.16
  68.7 1.6 %collective-permute-start.17 = (bf16[128,1152]{1,0:T(8,128)(2,1)S(1)}, bf16[128,1152]{1,0:T(8,128)(2,1)S(1)}, u32[]{:S(2)}, u32[]{:S(2)}) collective-permute-start(bf16[128,1152]{1,0:T(8,128)(2,1)S(1)} %pad_maximum_fusion.5), channel_id=1, source_target_pairs={{0,16},{1,9},{2,18},{3,11},{4,20},{5,13},{6,22},{7,15},{8,24},{9,1... | collective-permute-start | bytes 884744 | tf_op jit(solution)/shard_map/ppermute | solution.py:192
  70.3 3.4 %collective-permute-done.20 = bf16[128,1152]{1,0:T(8,128)(2,1)S(1)} collective-permute-done((bf16[128,1152]{1,0:T(8,128)(2,1)S(1)}, bf16[128,1152]{1,0:T(8,128)(2,1)S(1)}, u32[]{:S(2)}, u32[]{:S(2)}) %collective-permute-start.20) | collective-permute-done | bytes 294944 | tf_op jit(solution)/shard_map/ppermute | solution.py:192
  73.8 1.7 %collective-permute-done.17 = bf16[128,1152]{1,0:T(8,128)(2,1)S(1)} collective-permute-done((bf16[128,1152]{1,0:T(8,128)(2,1)S(1)}, bf16[128,1152]{1,0:T(8,128)(2,1)S(1)}, u32[]{:S(2)}, u32[]{:S(2)}) %collective-permute-start.17) | collective-permute-done | bytes 294944 | tf_op jit(solution)/shard_map/ppermute | solution.py:192
  75.5 0.4 collective-permute-start.22
  75.9 0.0 collective-permute-done.21.refs_3_
  75.9 0.0 collective-permute-done.13.refs_2_
  75.9 0.0 collective-permute-done.14.refs_3_
  75.9 0.3 collective-permute-start.23
  76.2 1.5 %collective-permute-start.24 = (bf16[256,1152]{1,0:T(8,128)(2,1)S(1)}, bf16[256,1152]{1,0:T(8,128)(2,1)S(1)}, u32[]{:S(2)}, u32[]{:S(2)}) collective-permute-start(bf16[256,1152]{1,0:T(8,128)(2,1)S(1)} %pad_maximum_fusion.3.refs_2_), channel_id=1, source_target_pairs={{0,16},{1,9},{2,18},{3,11},{4,20},{5,13},{6,22},{7,15},{8,24},{9,1... | collective-permute-start | bytes 1769480 | tf_op jit(solution)/shard_map/ppermute | solution.py:192
  77.7 1.7 %convolution_bitcast_fusion = f32[1,64,1152]{2,1,0:T(8,128)} fusion(bf16[64,1152]{1,0:T(8,128)(2,1)S(1)} %multiply_convert_fusion, bf16[1152,1152]{1,0:T(8,128)(2,1)S(1)} %copy-done), kind=kOutput, calls=%fused_computation.1 | convolution fusion | flops 169869312 | bytes 3096576 | tf_op jit(solution)/shard_map/dot_general | solution.py:17
  79.4 2.9 %shard_map.86 = (bf16[1152,1536]{1,0:T(8,128)(2,1)S(1)}, bf16[1152,512]{1,0:T(8,128)(2,1)S(1)}) custom-call(bf16[512,1152]{1,0:T(8,128)(2,1)} %constant_dynamic-update-slice_fusion.refs_0_, bf16[512,1152]{1,0:T(8,128)(2,1)} %collective-permute-done.10.refs_1_, bf16[512,1152]{1,0:T(8,128)(2,1)S(1)} %collective-permute-done.13.refs_2_, ...), custom_call_target="tpu_custom_call" | custom-call | bytes 9437184 | tf_op jit(solution)/shard_map/pallas_call | solution.py:106
  82.3 0.0 copy-start.6
  82.3 6.9 %shard_map.87.refs_0_ = f32[1152,1152]{1,0:T(8,128)S(1)} custom-call(bf16[1152,1536]{1,0:T(8,128)(2,1)S(1)} %get-tuple-element.50.x_t, bf16[256,1152]{1,0:T(8,128)(2,1)S(1)} %pad_maximum_fusion.1.refs_0_, bf16[256,1152]{1,0:T(8,128)(2,1)S(1)} %pad_maximum_fusion.2.refs_1_, bf16[256,1152]{1,0:T(8,128)(2,1)S(1)} %pad_maximum_fusion.3.refs_2_, ...), custom_call_target="tpu_custom_call" | custom-call | flops 4076863488 | bytes 12386304 | tf_op jit(solution)/shard_map/pallas_call | solution.py:152
  89.3 0.1 collective-permute-start.25
  89.4 2.5 %fusion = f32[1,256,1152]{2,1,0:T(8,128)} fusion(f32[256,1152]{1,0:T(8,128)} %collective-permute-done.9, f32[512,1152]{1,0:T(8,128)S(1)} %copy-done.6), kind=kLoop, calls=%fused_computation.3 | loop fusion | flops 294912 | bytes 3538944 | tf_op jit(solution)/shard_map/broadcast_in_dim | solution.py:287
  91.8 5.4 %shard_map.88 = f32[1152,1152]{1,0:T(8,128)} custom-call(bf16[1152,512]{1,0:T(8,128)(2,1)S(1)} %get-tuple-element.49.x_t, f32[1152,1152]{1,0:T(8,128)S(1)} %shard_map.87.refs_0_, bf16[256,1152]{1,0:T(8,128)(2,1)S(1)} %collective-permute-done.24.refs_1_, bf16[256,1152]{1,0:T(8,128)(2,1)S(1)} %collective-permute-done.25.refs_2_), custom_call_target="tpu_custom_call" | custom-call | flops 1358954496 | bytes 12976128 | tf_op jit(solution)/shard_map/pallas_call | solution.py:152
  (34 shorter events, 0.3 us)
Async XLA Ops:
  0.6 18.6 %copy-start = (bf16[1152,1152]{1,0:T(8,128)(2,1)S(1)}, bf16[1152,1152]{1,0:T(8,128)(2,1)}, u32[]{:S(2)}) copy-start(bf16[1152,1152]{1,0:T(8,128)(2,1)} %param.9) | copy-start | bytes 7962628
  0.6 20.7 %collective-permute-start.4 = (bf16[256,1152]{1,0:T(8,128)(2,1)}, bf16[256,1152]{1,0:T(8,128)(2,1)S(1)}, u32[]{:S(2)}, u32[]{:S(2)}) collective-permute-start(bf16[256,1152]{1,0:T(8,128)(2,1)} %bitcast.16), channel_id=1, source_target_pairs={{0,1},{1,0},{2,3},{3,2},{4,5},{5,4},{6,7},{7,6},{8,9},{9,8},{10,11... | collective-permute-start | bytes 1769480 | tf_op jit(solution)/shard_map/ppermute | solution.py:184
  1.2 9.7 %collective-permute-start.2 = (bf16[64,1152]{1,0:T(8,128)(2,1)}, bf16[64,1152]{1,0:T(8,128)(2,1)S(1)}, u32[]{:S(2)}, u32[]{:S(2)}) collective-permute-start(bf16[64,1152]{1,0:T(8,128)(2,1)} %bitcast.18), channel_id=1, source_target_pairs={{0,6},{1,7},{2,4},{3,5},{4,2},{5,3},{6,0},{7,1},{8,14},{9,15},{10,... | collective-permute-start | bytes 442376 | tf_op jit(solution)/shard_map/ppermute | solution.py:181
  5.8 13.4 %collective-permute-start.1 = (bf16[64,1152]{1,0:T(8,128)(2,1)}, bf16[64,1152]{1,0:T(8,128)(2,1)}, u32[]{:S(2)}, u32[]{:S(2)}) collective-permute-start(bf16[64,1152]{1,0:T(8,128)(2,1)} %bitcast.19), channel_id=1, source_target_pairs={{0,4},{1,5},{2,6},{3,7},{4,0},{5,1},{6,2},{7,3},{8,12},{9,13},{10,... | collective-permute-start | bytes 442376 | tf_op jit(solution)/shard_map/ppermute | solution.py:181
  5.8 13.4 %collective-permute-start = (bf16[64,1152]{1,0:T(8,128)(2,1)}, bf16[64,1152]{1,0:T(8,128)(2,1)}, u32[]{:S(2)}, u32[]{:S(2)}) collective-permute-start(bf16[64,1152]{1,0:T(8,128)(2,1)} %bitcast.20), channel_id=1, source_target_pairs={{0,2},{1,3},{2,0},{3,1},{4,6},{5,7},{6,4},{7,5},{8,10},{9,11},{10,... | collective-permute-start | bytes 442376 | tf_op jit(solution)/shard_map/ppermute | solution.py:181
  6.5 14.8 %collective-permute-start.3 = (s32[1,256]{1,0:T(1,128)}, s32[1,256]{1,0:T(1,128)S(1)}, u32[]{:S(2)}, u32[]{:S(2)}) collective-permute-start(s32[1,256]{1,0:T(1,128)} %refs_0_.1), channel_id=1, source_target_pairs={{0,1},{1,0},{2,3},{3,2},{4,5},{5,4},{6,7},{7,6},{8,9},{9,8},{10,11... | collective-permute-start | bytes 3080 | tf_op jit(solution)/shard_map/ppermute | solution.py:184
  7.8 14.4 %copy-start.1 = (bf16[1,256,1152]{2,1,0:T(8,128)(2,1)S(1)}, bf16[1,256,1152]{2,1,0:T(8,128)(2,1)}, u32[]{:S(2)}) copy-start(bf16[1,256,1152]{2,1,0:T(8,128)(2,1)} %param.7) | copy-start | bytes 1769476
  7.8 14.4 %copy-start.4 = (s32[1,256]{1,0:T(1,128)S(1)}, s32[1,256]{1,0:T(1,128)}, u32[]{:S(2)}) copy-start(s32[1,256]{1,0:T(1,128)} %refs_0_.1) | copy-start | bytes 3076
  10.9 10.4 %copy-start.8 = (bf16[64,1152]{1,0:T(8,128)(2,1)}, bf16[64,1152]{1,0:T(8,128)(2,1)S(1)}, u32[]{:S(2)}) copy-start(bf16[64,1152]{1,0:T(8,128)(2,1)S(1)} %collective-permute-done.2) | copy-start | bytes 442372
  21.3 0.8 copy-start.2
  22.2 1.1 %copy-start.3 = (bf16[256,1152]{1,0:T(8,128)(2,1)S(1)}, bf16[256,1152]{1,0:T(8,128)(2,1)}, u32[]{:S(2)}) copy-start(bf16[256,1152]{1,0:T(8,128)(2,1)} %copy-done.2) | copy-start | bytes 1769476
  23.2 10.0 %copy-start.7 = (bf16[1,64,1152]{2,1,0:T(8,128)(2,1)S(1)}, bf16[1,64,1152]{2,1,0:T(8,128)(2,1)}, u32[]{:S(2)}) copy-start(bf16[1,64,1152]{2,1,0:T(8,128)(2,1)} %param.6) | copy-start | bytes 442372
  23.2 10.7 %copy-start.9 = (bf16[64,1152]{1,0:T(8,128)(2,1)S(1)}, bf16[64,1152]{1,0:T(8,128)(2,1)}, u32[]{:S(2)}) copy-start(bf16[64,1152]{1,0:T(8,128)(2,1)} %copy-done.8) | copy-start | bytes 442372
  25.5 7.8 %collective-permute-start.5 = (bf16[64,1152]{1,0:T(8,128)(2,1)S(1)}, bf16[64,1152]{1,0:T(8,128)(2,1)S(1)}, u32[]{:S(2)}, u32[]{:S(2)}) collective-permute-start(bf16[64,1152]{1,0:T(8,128)(2,1)S(1)} %get-tuple-element.30), channel_id=1, source_target_pairs={{0,2},{1,3},{2,0},{3,1},{4,6},{5,7},{6,4},{7,5},{8,10},{9,11},{10,... | collective-permute-start | bytes 442376 | tf_op jit(solution)/shard_map/ppermute | solution.py:181
  25.5 21.9 %collective-permute-start.6 = (bf16[64,1152]{1,0:T(8,128)(2,1)}, bf16[64,1152]{1,0:T(8,128)(2,1)}, u32[]{:S(2)}, u32[]{:S(2)}) collective-permute-start(bf16[64,1152]{1,0:T(8,128)(2,1)} %get-tuple-element.31), channel_id=1, source_target_pairs={{0,4},{1,5},{2,6},{3,7},{4,0},{5,1},{6,2},{7,3},{8,12},{9,13},{10,... | collective-permute-start | bytes 442376 | tf_op jit(solution)/shard_map/ppermute | solution.py:181
  28.6 18.9 %collective-permute-start.7 = (bf16[64,1152]{1,0:T(8,128)(2,1)S(1)}, bf16[64,1152]{1,0:T(8,128)(2,1)}, u32[]{:S(2)}, u32[]{:S(2)}) collective-permute-start(bf16[64,1152]{1,0:T(8,128)(2,1)S(1)} %get-tuple-element.32), channel_id=1, source_target_pairs={{0,6},{1,7},{2,4},{3,5},{4,2},{5,3},{6,0},{7,1},{8,14},{9,15},{10,... | collective-permute-start | bytes 442376 | tf_op jit(solution)/shard_map/ppermute | solution.py:181
  33.2 6.6 %copy-start.10 = (bf16[64,1152]{1,0:T(8,128)(2,1)}, bf16[64,1152]{1,0:T(8,128)(2,1)S(1)}, u32[]{:S(2)}) copy-start(bf16[64,1152]{1,0:T(8,128)(2,1)S(1)} %collective-permute-done.5) | copy-start | bytes 442372
  35.0 9.9 %collective-permute-start.8 = (bf16[256,1152]{1,0:T(8,128)(2,1)S(1)}, bf16[256,1152]{1,0:T(8,128)(2,1)S(1)}, u32[]{:S(2)}, u32[]{:S(2)}) collective-permute-start(bf16[256,1152]{1,0:T(8,128)(2,1)S(1)} %pad_maximum_fusion), channel_id=1, source_target_pairs={{0,8},{1,17},{2,10},{3,19},{4,12},{5,21},{6,14},{7,23},{8,0},{9,25... | collective-permute-start | bytes 1769480 | tf_op jit(solution)/shard_map/ppermute | solution.py:192
  37.1 2.8 %copy-start.5 = (f32[512,1152]{1,0:T(8,128)}, f32[512,1152]{1,0:T(8,128)S(1)}, u32[]{:S(2)}) copy-start(f32[512,1152]{1,0:T(8,128)S(1)} %convolution_multiply_fusion) | copy-start | bytes 7077892
  38.2 11.6 %collective-permute-start.9 = (f32[256,1152]{1,0:T(8,128)}, f32[256,1152]{1,0:T(8,128)}, u32[]{:S(2)}, u32[]{:S(2)}) collective-permute-start(f32[256,1152]{1,0:T(8,128)} %slice.9), channel_id=1, source_target_pairs={{0,1},{1,0},{2,3},{3,2},{4,5},{5,4},{6,7},{7,6},{8,9},{9,8},{10,11... | collective-permute-start | bytes 3538952 | tf_op jit(solution)/shard_map/ppermute | solution.py:184
  45.8 19.7 %collective-permute-start.10 = (bf16[512,1152]{1,0:T(8,128)(2,1)}, bf16[512,1152]{1,0:T(8,128)(2,1)}, u32[]{:S(2)}, u32[]{:S(2)}) collective-permute-start(bf16[512,1152]{1,0:T(8,128)(2,1)} %constant_dynamic-update-slice_fusion.refs_0_), channel_id=1, source_target_pairs={{0,16},{1,9},{2,18},{3,11},{4,20},{5,13},{6,22},{7,15},{8,24},{9,1... | collective-permute-start | bytes 3538952 | tf_op jit(solution)/shard_map/ppermute | solution.py:192
  49.9 6.9 %collective-permute-start.12 = (bf16[64,1152]{1,0:T(8,128)(2,1)S(1)}, bf16[64,1152]{1,0:T(8,128)(2,1)S(1)}, u32[]{:S(2)}, u32[]{:S(2)}) collective-permute-start(bf16[64,1152]{1,0:T(8,128)(2,1)S(1)} %multiply_convert_fusion), channel_id=1, source_target_pairs={{0,8},{1,17},{2,10},{3,19},{4,12},{5,21},{6,14},{7,23},{8,0},{9,25... | collective-permute-start | bytes 442376 | tf_op jit(solution)/shard_map/ppermute | solution.py:192
  51.4 5.9 %collective-permute-start.11 = (bf16[64,1152]{1,0:T(8,128)(2,1)S(1)}, bf16[64,1152]{1,0:T(8,128)(2,1)S(1)}, u32[]{:S(2)}, u32[]{:S(2)}) collective-permute-start(bf16[64,1152]{1,0:T(8,128)(2,1)S(1)} %multiply_convert_fusion), channel_id=1, source_target_pairs={{0,2},{1,3},{2,0},{3,1},{4,6},{5,7},{6,4},{7,5},{8,10},{9,11},{10,... | collective-permute-start | bytes 442376 | tf_op jit(solution)/shard_map/ppermute | solution.py:181
  51.4 14.1 %collective-permute-start.19 = (bf16[64,1152]{1,0:T(8,128)(2,1)S(1)}, bf16[64,1152]{1,0:T(8,128)(2,1)S(1)}, u32[]{:S(2)}, u32[]{:S(2)}) collective-permute-start(bf16[64,1152]{1,0:T(8,128)(2,1)S(1)} %multiply_convert_fusion), channel_id=1, source_target_pairs={{0,6},{1,7},{2,4},{3,5},{4,2},{5,3},{6,0},{7,1},{8,14},{9,15},{10,... | collective-permute-start | bytes 442376 | tf_op jit(solution)/shard_map/ppermute | solution.py:181
  53.2 12.7 %collective-permute-start.18 = (bf16[64,1152]{1,0:T(8,128)(2,1)S(1)}, bf16[64,1152]{1,0:T(8,128)(2,1)S(1)}, u32[]{:S(2)}, u32[]{:S(2)}) collective-permute-start(bf16[64,1152]{1,0:T(8,128)(2,1)S(1)} %multiply_convert_fusion), channel_id=1, source_target_pairs={{0,4},{1,5},{2,6},{3,7},{4,0},{5,1},{6,2},{7,3},{8,12},{9,13},{10,... | collective-permute-start | bytes 442376 | tf_op jit(solution)/shard_map/ppermute | solution.py:181
  56.7 11.8 %collective-permute-start.15 = (bf16[128,1152]{1,0:T(8,128)(2,1)S(1)}, bf16[128,1152]{1,0:T(8,128)(2,1)S(1)}, u32[]{:S(2)}, u32[]{:S(2)}) collective-permute-start(bf16[128,1152]{1,0:T(8,128)(2,1)S(1)} %pad_maximum_fusion.4), channel_id=1, source_target_pairs={{0,16},{1,9},{2,18},{3,11},{4,20},{5,13},{6,22},{7,15},{8,24},{9,1... | collective-permute-start | bytes 884744 | tf_op jit(solution)/shard_map/ppermute | solution.py:192
  57.3 11.3 %collective-permute-start.16 = (bf16[64,1152]{1,0:T(8,128)(2,1)S(1)}, bf16[64,1152]{1,0:T(8,128)(2,1)S(1)}, u32[]{:S(2)}, u32[]{:S(2)}) collective-permute-start(bf16[64,1152]{1,0:T(8,128)(2,1)S(1)} %collective-permute-done.11), channel_id=1, source_target_pairs={{0,8},{1,17},{2,10},{3,19},{4,12},{5,21},{6,14},{7,23},{8,0},{9,25... | collective-permute-start | bytes 442376 | tf_op jit(solution)/shard_map/ppermute | solution.py:192
  65.5 10.4 %collective-permute-start.13 = (bf16[512,1152]{1,0:T(8,128)(2,1)}, bf16[512,1152]{1,0:T(8,128)(2,1)S(1)}, u32[]{:S(2)}, u32[]{:S(2)}) collective-permute-start(bf16[512,1152]{1,0:T(8,128)(2,1)} %constant_dynamic-update-slice_fusion.refs_0_), channel_id=1, source_target_pairs={{0,1},{1,0},{2,3},{3,2},{4,5},{5,4},{6,7},{7,6},{8,9},{9,8},{10,11... | collective-permute-start | bytes 3538952 | tf_op jit(solution)/shard_map/ppermute | solution.py:184
  65.5 10.4 %collective-permute-start.14 = (bf16[512,1152]{1,0:T(8,128)(2,1)}, bf16[512,1152]{1,0:T(8,128)(2,1)S(1)}, u32[]{:S(2)}, u32[]{:S(2)}) collective-permute-start(bf16[512,1152]{1,0:T(8,128)(2,1)} %collective-permute-done.10.refs_1_), channel_id=1, source_target_pairs={{0,1},{1,0},{2,3},{3,2},{4,5},{5,4},{6,7},{7,6},{8,9},{9,8},{10,11... | collective-permute-start | bytes 3538952 | tf_op jit(solution)/shard_map/ppermute | solution.py:184
  66.0 7.7 %collective-permute-start.20 = (bf16[128,1152]{1,0:T(8,128)(2,1)S(1)}, bf16[128,1152]{1,0:T(8,128)(2,1)S(1)}, u32[]{:S(2)}, u32[]{:S(2)}) collective-permute-start(bf16[128,1152]{1,0:T(8,128)(2,1)S(1)} %pad_maximum_fusion.6), channel_id=1, source_target_pairs={{0,8},{1,17},{2,10},{3,19},{4,12},{5,21},{6,14},{7,23},{8,0},{9,25... | collective-permute-start | bytes 884744 | tf_op jit(solution)/shard_map/ppermute | solution.py:192
  68.6 7.3 %collective-permute-start.21 = (bf16[256,1152]{1,0:T(8,128)(2,1)S(1)}, bf16[256,1152]{1,0:T(8,128)(2,1)S(1)}, u32[]{:S(2)}, u32[]{:S(2)}) collective-permute-start(bf16[256,1152]{1,0:T(8,128)(2,1)S(1)} %pad_maximum_fusion.1.refs_0_), channel_id=1, source_target_pairs={{0,1},{1,0},{2,3},{3,2},{4,5},{5,4},{6,7},{7,6},{8,9},{9,8},{10,11... | collective-permute-start | bytes 1769480 | tf_op jit(solution)/shard_map/ppermute | solution.py:184
  68.7 6.8 %collective-permute-start.17 = (bf16[128,1152]{1,0:T(8,128)(2,1)S(1)}, bf16[128,1152]{1,0:T(8,128)(2,1)S(1)}, u32[]{:S(2)}, u32[]{:S(2)}) collective-permute-start(bf16[128,1152]{1,0:T(8,128)(2,1)S(1)} %pad_maximum_fusion.5), channel_id=1, source_target_pairs={{0,16},{1,9},{2,18},{3,11},{4,20},{5,13},{6,22},{7,15},{8,24},{9,1... | collective-permute-start | bytes 884744 | tf_op jit(solution)/shard_map/ppermute | solution.py:192
  75.5 6.7 %collective-permute-start.22 = (bf16[256,1152]{1,0:T(8,128)(2,1)S(1)}, bf16[256,1152]{1,0:T(8,128)(2,1)S(1)}, u32[]{:S(2)}, u32[]{:S(2)}) collective-permute-start(bf16[256,1152]{1,0:T(8,128)(2,1)S(1)} %pad_maximum_fusion.2.refs_1_), channel_id=1, source_target_pairs={{0,1},{1,0},{2,3},{3,2},{4,5},{5,4},{6,7},{7,6},{8,9},{9,8},{10,11... | collective-permute-start | bytes 1769480 | tf_op jit(solution)/shard_map/ppermute | solution.py:184
  75.9 6.4 %collective-permute-start.23 = (bf16[256,1152]{1,0:T(8,128)(2,1)S(1)}, bf16[256,1152]{1,0:T(8,128)(2,1)S(1)}, u32[]{:S(2)}, u32[]{:S(2)}) collective-permute-start(bf16[256,1152]{1,0:T(8,128)(2,1)S(1)} %pad_maximum_fusion.3.refs_2_), channel_id=1, source_target_pairs={{0,1},{1,0},{2,3},{3,2},{4,5},{5,4},{6,7},{7,6},{8,9},{9,8},{10,11... | collective-permute-start | bytes 1769480 | tf_op jit(solution)/shard_map/ppermute | solution.py:184
  76.2 13.1 %collective-permute-start.24 = (bf16[256,1152]{1,0:T(8,128)(2,1)S(1)}, bf16[256,1152]{1,0:T(8,128)(2,1)S(1)}, u32[]{:S(2)}, u32[]{:S(2)}) collective-permute-start(bf16[256,1152]{1,0:T(8,128)(2,1)S(1)} %pad_maximum_fusion.3.refs_2_), channel_id=1, source_target_pairs={{0,16},{1,9},{2,18},{3,11},{4,20},{5,13},{6,22},{7,15},{8,24},{9,1... | collective-permute-start | bytes 1769480 | tf_op jit(solution)/shard_map/ppermute | solution.py:192
  82.3 7.1 %copy-start.6 = (f32[512,1152]{1,0:T(8,128)S(1)}, f32[512,1152]{1,0:T(8,128)}, u32[]{:S(2)}) copy-start(f32[512,1152]{1,0:T(8,128)} %copy-done.5) | copy-start | bytes 7077892
  89.3 2.5 %collective-permute-start.25 = (bf16[256,1152]{1,0:T(8,128)(2,1)S(1)}, bf16[256,1152]{1,0:T(8,128)(2,1)S(1)}, u32[]{:S(2)}, u32[]{:S(2)}) collective-permute-start(bf16[256,1152]{1,0:T(8,128)(2,1)S(1)} %collective-permute-done.24.refs_1_), channel_id=1, source_target_pairs={{0,1},{1,0},{2,3},{3,2},{4,5},{5,4},{6,7},{7,6},{8,9},{9,8},{10,11... | collective-permute-start | bytes 1769480 | tf_op jit(solution)/shard_map/ppermute | solution.py:184

commit v5 on v4

v5 whole, which is shorter than its diff:
```python
import functools

import jax
import jax.numpy as jnp
from jax import lax
from jax.experimental import pallas as pl
from jax.experimental.pallas import tpu as pltpu
from jax.sharding import PartitionSpec as P

FIRST = (((0,), (0,)), ((), ()))
LAST = (((1,), (1,)), ((), ()))
F32 = jnp.float32
BF16 = jnp.bfloat16


def dot(a, b, dims=(((1,), (0,)), ((), ()))):
    return lax.dot_general(a, b, dims, preferred_element_type=F32)


def after(v, *others):
    return lax.optimization_barrier((v, others))[0]


def score_kernel(nz, both, embed, *refs):
    scale, offset = both[0:1, 0:1], both[8:9, 0:1]
    labels, captions, refs = refs[:2], refs[2:4], refs[4:]
    own, unit_own, inv_own, unit, dlogit = refs[:5]
    sent, (caps, sems) = refs[5:-2], refs[-2:]
    n_img, n_cap = embed.shape[0] // nz, captions[0].shape[0]
    copies = []
    for i in range(2):
        here = caps.at[i * n_cap : (i + 1) * n_cap, :]
        copies.append(pltpu.make_async_copy(captions[i], here, sems.at[i]))
        copies[-1].start()
    embed = embed[...]
    inv_norm = lax.rsqrt(jnp.sum(embed * embed, axis=1, keepdims=True) + 1e-06)
    unit_f = embed * inv_norm
    unit_own[...] = unit_f[:n_img]
    inv_own[...] = jnp.broadcast_to(inv_norm[:n_img], inv_own.shape)
    u = unit_f.astype(BF16)
    unit[...] = u
    index = lax.axis_index("blk")
    ids = []
    for k in range(nz):
        first = (index ^ (2 * k)) * n_img
        ids.append(first + lax.broadcasted_iota(jnp.int32, (n_img, 1), 0))
    ids = jnp.concatenate(ids)
    labs = jnp.concatenate([v[...] for v in labels], axis=1)
    sign = jnp.where(labs == ids, 1.0, -1.0).astype(F32)
    for copy in copies:
        copy.wait()
    logits = scale * dot(u, caps[...], LAST) + offset
    d = (-sign * jax.nn.sigmoid(-sign * logits)).astype(BF16)
    dlogit[...] = d
    part = scale * dot(d, caps[...])
    own[...] = part[:n_img]
    for k in range(1, nz):
        sent[k - 1][...] = part[k * n_img : (k + 1) * n_img].astype(BF16)


def scores(nz, both, embed, labels, captions):
    images, depth = embed.shape
    n_img, n_cap = images // nz, captions[0].shape[0]
    caps = 2 * n_cap
    vmem = pl.BlockSpec(memory_space=pltpu.VMEM)
    block = jax.ShapeDtypeStruct((n_img, depth), F32)
    outs = [
        block,
        block,
        jax.ShapeDtypeStruct((n_img, 128), F32),
        jax.ShapeDtypeStruct((images, depth), BF16),
        jax.ShapeDtypeStruct((images, caps), BF16),
    ] + [jax.ShapeDtypeStruct((n_img, depth), BF16)] * (nz - 1)
    return pl.pallas_call(
        functools.partial(score_kernel, nz),
        out_shape=outs,
        in_specs=[vmem] * 4
        + [pl.BlockSpec(memory_space=pl.ANY)] * 2,
        out_specs=[vmem] * len(outs),
        scratch_shapes=[pltpu.VMEM((caps, depth), BF16), pltpu.SemaphoreType.DMA((2,))],
        compiler_params=pltpu.CompilerParams(
            vmem_limit_bytes=12 * 2**20 + 24 * images * depth
        ),
        cost_estimate=pl.CostEstimate(
            flops=4 * images * depth * caps,
            bytes_accessed=2 * depth * (caps + 6 * images),
            transcendentals=images * caps,
        ),
    )(both, embed, *labels, *captions)


def caption_kernel(both, dlogit, unit, own, other):
    scale = both[0:1, 0:1]
    n_cap = own.shape[0]
    own[...] = scale * dot(dlogit[:, :n_cap], unit[...], FIRST)
    other[...] = scale * dot(dlogit[:, n_cap:], unit[...], FIRST)


def caption_sums(both, dlogit, unit):
    images, caps = dlogit.shape
    depth = unit.shape[1]
    vmem = pl.BlockSpec(memory_space=pltpu.VMEM)
    return pl.pallas_call(
        caption_kernel,
        out_shape=[jax.ShapeDtypeStruct((caps // 2, depth), F32)] * 2,
        in_specs=[vmem] * 3,
        out_specs=[vmem] * 2,
        compiler_params=pltpu.CompilerParams(
            vmem_limit_bytes=10 * 2**20 + 8 * images * depth
        ),
        cost_estimate=pl.CostEstimate(
            flops=2 * images * caps * depth,
            bytes_accessed=4 * caps * depth + 2 * images * (depth + caps),
            transcendentals=0,
        ),
    )(both, dlogit, unit)


def embed_grad_kernel(own, unit, inv_norm, *refs):
    back, out = refs[:-1], refs[-1]
    total = own[...]
    for v in back:
        total = total + v[...].astype(F32)
    u = unit[...]
    radial = jnp.sum(u * total, axis=1, keepdims=True)
    out[...] = ((total - u * radial) * inv_norm[:, :1]).astype(BF16)


def embed_grad(own, unit, inv_norm, back):
    vmem = pl.BlockSpec(memory_space=pltpu.VMEM)
    return pl.pallas_call(
        embed_grad_kernel,
        out_shape=jax.ShapeDtypeStruct(own.shape, BF16),
        in_specs=[vmem] * (3 + len(back)),
        out_specs=vmem,
        compiler_params=pltpu.CompilerParams(vmem_limit_bytes=8 * 2**20),
        cost_estimate=pl.CostEstimate(
            flops=8 * own.size, bytes_accessed=12 * own.size, transcendentals=0
        ),
    )(own, unit, inv_norm, *back)


def turn_kernel(plan, *refs):
    ins, outs = refs[: -len(plan)], refs[-len(plan) :]
    for out, pieces in zip(outs, plan):
        col = 0
        for runs in pieces:
            rows = [ins[i][at : at + size, :] for i, at, size in runs]
            rows = jnp.concatenate(rows)
            out[:, col : col + rows.shape[0]] = rows.T
            col += rows.shape[0]


def turned(xs, plan):
    depth = xs[0].shape[1]
    images = [sum(size for runs in pieces for _, _, size in runs) for pieces in plan]
    return pl.pallas_call(
        functools.partial(turn_kernel, plan),
        out_shape=[jax.ShapeDtypeStruct((depth, n), BF16) for n in images],
        in_specs=[pl.BlockSpec(memory_space=pltpu.VMEM)] * len(xs),
        out_specs=[pl.BlockSpec(memory_space=pltpu.VMEM)] * len(plan),
        compiler_params=pltpu.CompilerParams(vmem_limit_bytes=16 * 2**20),
        cost_estimate=pl.CostEstimate(
            flops=0, bytes_accessed=4 * sum(images) * depth, transcendentals=0
        ),
    )(*xs)


def stack(stacked, gs):
    at = 0
    for g in gs:
        stacked[at : at + g.shape[0], :] = g[...]
        at += g.shape[0]


def early_kernel(n, x_t, *refs):
    gs, (out, stacked) = refs[:-2], refs[-2:]
    stack(stacked, gs)
    rows = out.shape[0] // n
    for i in range(n):
        here = slice(i * rows, (i + 1) * rows)
        out[here, :] = dot(x_t[here, :], stacked[...])


def late_kernel(factor, x_t, acc, *refs):
    gs, (out, stacked, tiles, sems) = refs[:-4], refs[-4:]
    stack(stacked, gs)
    n, rows = tiles.shape[:2]
    copies = []
    for i in range(n):
        here = slice(i * rows, (i + 1) * rows)
        tiles[i] = (acc[here, :] + dot(x_t[here, :], stacked[...])) * factor
        copies.append(pltpu.make_async_copy(tiles.at[i], out.at[here, :], sems.at[i]))
        copies[-1].start()
    for copy in copies:
        copy.wait()


def weight_sum(acc, x_t, gs, factor):
    depth, images = x_t.shape
    n = 3
    early = acc is None
    vmem = pl.BlockSpec(memory_space=pltpu.VMEM)
    scratch = [pltpu.VMEM((images, depth), BF16)]
    if early:
        kernel = functools.partial(early_kernel, n)
    else:
        kernel = functools.partial(late_kernel, factor)
        scratch.append(pltpu.VMEM((n, depth // n, depth), F32))
        scratch.append(pltpu.SemaphoreType.DMA((n,)))
    operands = [x_t] + ([] if early else [acc]) + gs
    return pl.pallas_call(
        kernel,
        out_shape=jax.ShapeDtypeStruct((depth, depth), F32),
        in_specs=[vmem] * len(operands),
        out_specs=vmem if early else pl.BlockSpec(memory_space=pl.ANY),
        scratch_shapes=scratch,
        compiler_params=pltpu.CompilerParams(vmem_limit_bytes=24 * 2**20),
        cost_estimate=pl.CostEstimate(
            flops=2 * images * depth * depth,
            bytes_accessed=4 * images * depth + 4 * depth * depth * (2 - early),
            transcendentals=0,
        ),
    )(*operands)


def on_device(x, captions, labels, weight, scale, offset):
    x, captions = x[0], captions[0]
    n_img, depth = x.shape
    n_cap = captions.shape[0]
    nd, nb = lax.axis_size("dp"), lax.axis_size("blk")
    nz = nb // 2
    bits = nd.bit_length() - 1

    def along_z(v, k):
        return lax.ppermute(v, "blk", [(i, i ^ (2 * k)) for i in range(nb)])

    def swap(v):
        return lax.ppermute(v, "blk", [(i, i ^ 1) for i in range(nb)])

    def step_d(v, i):
        perm = []
        for j in range(nd):
            for m in range(nb):
                to = j ^ (1 << ((i + m % 2) % bits))
                perm.append((j * nb + m, to * nb + m))
        return lax.ppermute(v, ("dp", "blk"), perm)

    xs = [x] + [along_z(x, k) for k in range(1, nz)]
    x_own = jnp.concatenate(xs)
    x_first = step_d(x_own, 0)
    embed = dot(jnp.concatenate(xs), weight)
    row = lax.broadcasted_iota(jnp.int32, (16, 128), 0)
    both = jnp.where(row < 8, scale, offset)
    own, u, inv_norm, unit, dlogit, *sent = scores(
        nz,
        both,
        embed,
        [labels, swap(labels)],
        [captions, swap(captions)],
    )
    back = [along_z(v, k + 1) for k, v in enumerate(sent)]

    x_first = after(x_first, back)
    x_own = [x_own, x_first]
    for i in range(1, bits):
        x_own = jnp.concatenate(x_own)
        x_own = [x_own, step_d(x_own, i)]
    small = nd * nb * n_img <= 2048

    adjoint, adjoint_other = caption_sums(both, after(dlogit, x_first), unit)

    ge = embed_grad(own, u, inv_norm, back)
    grad_features = dot(ge, weight, LAST)

    half = nz // 2
    near = [along_z(ge, k) for k in range(1, half)]
    own_first = step_d(ge, 0)
    far = [along_z(ge, k) for k in range(half, nz)]

    def over_d(v, first, *before):
        v = [v, first]
        for i in range(1, bits):
            v = after(jnp.concatenate(v), before)
            v = [v, step_d(v, i)]
        return v

    g_own = over_d(ge, own_first)
    near = after(jnp.concatenate(near), g_own[0])
    near_first = step_d(near, 0)
    g_near = over_d(near, near_first)
    far = after(jnp.concatenate(far), near_first, g_own[1])
    far_first = step_d(far, 0)
    adjoint = adjoint + swap(after(adjoint_other, far_first))
    sizes = [n_img, n_img * (half - 1), n_img * half]
    firsts = [0, n_img, n_img * half]
    n_own = nz * n_img
    per = nd // 2
    if small:
        plan = [[], []]
        for core in range(2):
            for g in range(3):
                runs = [(core, i * n_own + firsts[g], sizes[g]) for i in range(nd)]
                if g < 2:
                    plan[0].append(runs)
                else:
                    plan[0].append(runs[:per])
                    plan[1].append(runs[per:])
        x_own = jnp.concatenate(x_own)
        x_early, x_late = turned([x_own, swap(after(x_own, far))], plan)
        g_own = jnp.concatenate(g_own)
        own_swapped = swap(g_own)
        g_far = over_d(far, far_first, own_swapped, g_near[1])
        early = [g_own, jnp.concatenate(g_near), g_far[0]]
        others = [own_swapped, swap(early[1]), swap(after(early[2], g_near[1]))]
        acc = weight_sum(None, x_early, early + others, 1.0)
        late = after(g_far[1], acc)
        grad_weight = weight_sum(acc, x_late, [late, swap(late)], 1.0 / nd)
    else:
        g_far = over_d(far, far_first)
        grad_weight = 0.0
        for i, x_part in enumerate(x_own):
            for at in range(per):
                g_part = [
                    g[i][at * m : (at + 1) * m]
                    for m, g in zip(sizes, (g_own, g_near, g_far))
                ]
                grad_weight = grad_weight + dot(
                    x_part[at * n_own : (at + 1) * n_own],
                    jnp.concatenate(g_part),
                    FIRST,
                )
        grad_weight = (grad_weight + swap(grad_weight)) / nd
    return (grad_features[None], adjoint[None], grad_weight)


def solution(mesh):
    placed = (P("dp", "blk", None), P("dp", "blk", None), P("dp", "blk"), P(), P(), P())
    return jax.shard_map(
        on_device,
        mesh=mesh,
        in_specs=placed,
        out_specs=(P("dp", "blk", None), P("dp", "blk", None), P()),
        check_vma=False,
    )
```

time: 97.6 us -> 87.9 us (0.901)
  Pallas kernels: 17.4 us -> 11.4 us
  waiting for transfers between devices: 32.8 us -> 38.7 us
  local copies, waits for them, and re-layouts: 8.5 us -> 3.99 us
  other arithmetic: 6.2 us -> 2.45 us
  starting transfers between devices: 25.8 us -> 24.6 us
    ppermute x9, waiting for transfers between devices: 14.8 us -> 24 us  [along_z(): return lax.ppermute(v, 'blk', [(i, i ^ 2 * k) for i in range(nb)])]
    ppermute x8, waiting for transfers between devices: 18 us -> 13.8 us  [step_d(): return lax.ppermute(v, ('dp', 'blk'), perm)]
    pallas_call x2 -> x4, Pallas kernels: 12.3 us -> 8.59 us  [the longest x2 7.85 us: weight_sum(): pl.pallas_call(kernel, out_shape=jax.ShapeDtypeStruct((depth, depth), F32...]
    ppermute x8, starting transfers between devices: 10.7 us -> 7.69 us  [step_d(): return lax.ppermute(v, ('dp', 'blk'), perm)]
    unnamed x26 -> x16, local copies, waits for them, and re-layouts: 6.47 us -> 3.6 us
    pallas_call x1, Pallas kernels: 2.89 us -> 1.26 us  [turned(): pl.pallas_call(functools.partial(turn_kernel, plan), out_shape=[jax.Shape...]
    ppermute x9, starting transfers between devices: 13.3 us -> 14.6 us  [along_z(): return lax.ppermute(v, 'blk', [(i, i ^ 2 * k) for i in range(nb)])]
    broadcast_in_dim x1, other arithmetic: 2.45 us -> 1.13 us  [on_device(): return (grad_features[None], adjoint[None], grad_weight)]
  transfers between devices with their start and end apart: 26 -> 25, of which waited for: 9 -> 13; matrix products, arithmetic and copies ran while one was open for 18% -> 11% of each run, Pallas kernels for 10% -> 10%
where the time goes in v5:
time: 87.9 us; the launch traced here: 86.9 us
  waiting for transfers between devices  38.7 us (44%)
  starting transfers between devices  24.6 us (28%)
  Pallas kernels  11.4 us (13%)
  local copies, waits for them, and re-layouts  3.99 us (5%)
  matrix products  3.64 us (4%)
  other arithmetic  2.45 us (3%)
  between operations  2.17 us (2%)
    ppermute x9, waiting for transfers between devices, along_z(): return lax.ppermute(v, 'blk', [(i, i ^ 2 * k) for i in range(nb)])  24 us
    ppermute x9, starting transfers between devices, along_z(): return lax.ppermute(v, 'blk', [(i, i ^ 2 * k) for i in range(nb)])  14.6 us
    ppermute x8, waiting for transfers between devices, step_d(): return lax.ppermute(v, ('dp', 'blk'), perm)  13.8 us
    pallas_call x2, Pallas kernels, weight_sum(): pl.pallas_call(kernel, out_shape=jax.ShapeDtypeStruct((depth, depth), F32...  7.85 us
    ppermute x8, starting transfers between devices, step_d(): return lax.ppermute(v, ('dp', 'blk'), perm)  7.69 us
    dot_general x2, matrix products, dot(): return lax.dot_general(a, b, dims, preferred_element_type=F32)  3.64 us
    unnamed x16, local copies, waits for them, and re-layouts  3.6 us
    ppermute x8, starting transfers between devices, swap(): return lax.ppermute(v, 'blk', [(i, i ^ 1) for i in range(nb)])  2.29 us
  transfers between devices with their start and end apart: 25, of which 13 were waited for; matrix products, arithmetic and copies ran while one was open for 11% of the time, Pallas kernels for 10%

profile of v5, /device:TPU:0, one launch (start us, length us, event | category | flops | bytes accessed | tf_op | source)
XLA Modules:
  0.0 86.9 jit_solution(3278361320218858569)
XLA Ops:
  0.6 0.0 copy-start
  0.6 0.0 copy-start.4
  0.7 5.1 %collective-permute-start.2 = (bf16[64,1152]{1,0:T(8,128)(2,1)}, bf16[64,1152]{1,0:T(8,128)(2,1)S(1)}, u32[]{:S(2)}, u32[]{:S(2)}) collective-permute-start(bf16[64,1152]{1,0:T(8,128)(2,1)} %bitcast.13), channel_id=1, source_target_pairs={{0,6},{1,7},{2,4},{3,5},{4,2},{5,3},{6,0},{7,1},{8,14},{9,15},{10,... | collective-permute-start | bytes 442376 | tf_op jit(solution)/shard_map/ppermute | solution.py:236
  5.8 0.6 collective-permute-start
  6.4 0.0 collective-permute-start.3
  6.4 0.5 collective-permute-start.4
  6.9 1.6 %constant_dynamic-update-slice_fusion.4 = (bf16[512,1152]{1,0:T(8,128)(2,1)}, bf16[1024,1152]{1,0:T(8,128)(2,1)}) fusion(bf16[1,64,1152]{2,1,0:T(8,128)(2,1)} %param.6), kind=kLoop, calls=%fused_computation.13 | loop fusion | bytes 442368
  9.9 0.9 %collective-permute-done.2 = bf16[64,1152]{1,0:T(8,128)(2,1)S(1)} collective-permute-done((bf16[64,1152]{1,0:T(8,128)(2,1)}, bf16[64,1152]{1,0:T(8,128)(2,1)S(1)}, u32[]{:S(2)}, u32[]{:S(2)}) %collective-permute-start.2) | collective-permute-done | bytes 147488 | tf_op jit(solution)/shard_map/ppermute | solution.py:236
  10.8 7.8 %collective-permute-done.1 = bf16[64,1152]{1,0:T(8,128)(2,1)} collective-permute-done((bf16[64,1152]{1,0:T(8,128)(2,1)}, bf16[64,1152]{1,0:T(8,128)(2,1)}, u32[]{:S(2)}, u32[]{:S(2)}) %collective-permute-start.1) | collective-permute-done | bytes 147488 | tf_op jit(solution)/shard_map/ppermute | solution.py:236
  18.6 1.1 %pad_maximum_fusion = bf16[256,1152]{1,0:T(8,128)(2,1)S(1)} fusion(bf16[64,1152]{1,0:T(8,128)(2,1)S(1)} %collective-permute-done.2, bf16[64,1152]{1,0:T(8,128)(2,1)} %collective-permute-done.1, bf16[64,1152]{1,0:T(8,128)(2,1)} %collective-permute-done, bf16[64,1152]{1,0:T(8,128)(2,1)} %bitcast.16), kind=kLoop, calls=%fused_computation.2 | loop fusion | flops 2359296 | bytes 1179648 | tf_op jit(solution)/shard_map/concatenate | solution.py:252
  19.7 0.0 copy-start.1
  19.7 0.0 copy-start.5
  19.7 0.0 copy-start.2
  19.7 0.0 copy-start.3
  19.7 1.6 %collective-permute-start.8 = (bf16[256,1152]{1,0:T(8,128)(2,1)S(1)}, bf16[256,1152]{1,0:T(8,128)(2,1)S(1)}, u32[]{:S(2)}, u32[]{:S(2)}) collective-permute-start(bf16[256,1152]{1,0:T(8,128)(2,1)S(1)} %pad_maximum_fusion), channel_id=1, source_target_pairs={{0,8},{1,17},{2,10},{3,19},{4,12},{5,21},{6,14},{7,23},{8,0},{9,25... | collective-permute-start | bytes 1769480 | tf_op jit(solution)/shard_map/ppermute | solution.py:247
  21.3 2.0 %fusion.embed = f32[256,1152]{1,0:T(8,128)S(1)} fusion(bf16[1152,1152]{1,0:T(8,128)(2,1)S(1)} %copy-done, bf16[64,1152]{1,0:T(8,128)(2,1)S(1)} %collective-permute-done.2, bf16[64,1152]{1,0:T(8,128)(2,1)} %collective-permute-done.1, bf16[64,1152]{1,0:T(8,128)(2,1)} %collective-permute-done, bf16[64,1152]{1,0:T(8,128)(2,1)S(1)} %bitcast.17), kind=kOutput, calls=%fused_computation.21 | convolution fusion | flops 681836544 | bytes 4423680 | tf_op jit(solution)/shard_map/dot_general | solution.py:17
  23.3 0.9 %constant_dynamic-update-slice_fusion.3 = (bf16[512,1152]{1,0:T(8,128)(2,1)S(1)}, bf16[1024,1152]{1,0:T(8,128)(2,1)S(1)}) fusion(bf16[512,1152]{1,0:T(8,128)(2,1)S(1)} %copy-done.5, bf16[64,1152]{1,0:T(8,128)(2,1)} %collective-permute-done, bf16[1024,1152]{1,0:T(8,128)(2,1)S(1)} %copy-done.1), kind=kLoop, calls=%fused_computation.12 | loop fusion | bytes 442368
  24.2 0.9 %constant_dynamic-update-slice_fusion.2 = (bf16[512,1152]{1,0:T(8,128)(2,1)S(1)}, bf16[1024,1152]{1,0:T(8,128)(2,1)S(1)}) fusion(bf16[512,1152]{1,0:T(8,128)(2,1)S(1)} %get-tuple-element.51, bf16[64,1152]{1,0:T(8,128)(2,1)} %collective-permute-done.1, bf16[1024,1152]{1,0:T(8,128)(2,1)S(1)} %get-tuple-element.52), kind=kLoop, calls=%fused_computation.11 | loop fusion | bytes 442368
  25.2 0.0 collective-permute-done.3.refs_1_
  25.2 0.0 collective-permute-done.4.refs_3_
  25.2 0.1 iota.7.both
  25.3 1.6 %shard_map.85 = (f32[64,1152]{1,0:T(8,128)S(1)}, f32[64,1152]{1,0:T(8,128)S(1)}, f32[64,128]{1,0:T(8,128)S(1)}, bf16[256,1152]{1,0:T(8,128)(2,1)S(1)}, bf16[256,...) custom-call(f32[16,128]{1,0:T(8,128)S(1)} %iota.7.both, ...), custom_call_target="tpu_custom_call" | custom-call | flops 603979776 | bytes 4718592 | tf_op jit(solution)/shard_map/pallas_call | solution.py:74
  26.9 0.1 collective-permute-start.5
  26.9 3.1 %collective-permute-start.6 = (bf16[64,1152]{1,0:T(8,128)(2,1)S(1)}, bf16[64,1152]{1,0:T(8,128)(2,1)S(1)}, u32[]{:S(2)}, u32[]{:S(2)}) collective-permute-start(bf16[64,1152]{1,0:T(8,128)(2,1)S(1)} %get-tuple-element.28), channel_id=1, source_target_pairs={{0,4},{1,5},{2,6},{3,7},{4,0},{5,1},{6,2},{7,3},{8,12},{9,13},{10,... | collective-permute-start | bytes 442376 | tf_op jit(solution)/shard_map/ppermute | solution.py:236
  30.0 1.3 %collective-permute-start.7 = (bf16[64,1152]{1,0:T(8,128)(2,1)S(1)}, bf16[64,1152]{1,0:T(8,128)(2,1)S(1)}, u32[]{:S(2)}, u32[]{:S(2)}) collective-permute-start(bf16[64,1152]{1,0:T(8,128)(2,1)S(1)} %get-tuple-element.29), channel_id=1, source_target_pairs={{0,6},{1,7},{2,4},{3,5},{4,2},{5,3},{6,0},{7,1},{8,14},{9,15},{10,... | collective-permute-start | bytes 442376 | tf_op jit(solution)/shard_map/ppermute | solution.py:236
  31.3 3.0 %collective-permute-done.5.refs_0_ = bf16[64,1152]{1,0:T(8,128)(2,1)S(1)} collective-permute-done((bf16[64,1152]{1,0:T(8,128)(2,1)S(1)}, bf16[64,1152]{1,0:T(8,128)(2,1)S(1)}, u32[]{:S(2)}, u32[]{:S(2)}) %collective-permute-start.5) | collective-permute-done | bytes 147488 | tf_op jit(solution)/shard_map/ppermute | solution.py:236
  34.3 6.1 %collective-permute-done.6.refs_1_ = bf16[64,1152]{1,0:T(8,128)(2,1)S(1)} collective-permute-done((bf16[64,1152]{1,0:T(8,128)(2,1)S(1)}, bf16[64,1152]{1,0:T(8,128)(2,1)S(1)}, u32[]{:S(2)}, u32[]{:S(2)}) %collective-permute-start.6) | collective-permute-done | bytes 147488 | tf_op jit(solution)/shard_map/ppermute | solution.py:236
  40.4 0.0 collective-permute-done.7.refs_2_
  40.4 0.0 collective-permute-done.8
  40.4 0.2 constant_dynamic-update-slice_fusion
  40.5 0.8 collective-permute-start.17
  41.3 0.2 shard_map.86
  41.5 1.5 %collective-permute-start.12 = (bf16[64,1152]{1,0:T(8,128)(2,1)S(1)}, bf16[64,1152]{1,0:T(8,128)(2,1)S(1)}, u32[]{:S(2)}, u32[]{:S(2)}) collective-permute-start(bf16[64,1152]{1,0:T(8,128)(2,1)S(1)} %shard_map.86), channel_id=1, source_target_pairs={{0,8},{1,17},{2,10},{3,19},{4,12},{5,21},{6,14},{7,23},{8,0},{9,25... | collective-permute-start | bytes 442376 | tf_op jit(solution)/shard_map/ppermute | solution.py:247
  43.0 2.5 %collective-permute-start.10 = (bf16[64,1152]{1,0:T(8,128)(2,1)S(1)}, bf16[64,1152]{1,0:T(8,128)(2,1)S(1)}, u32[]{:S(2)}, u32[]{:S(2)}) collective-permute-start(bf16[64,1152]{1,0:T(8,128)(2,1)S(1)} %shard_map.86), channel_id=1, source_target_pairs={{0,6},{1,7},{2,4},{3,5},{4,2},{5,3},{6,0},{7,1},{8,14},{9,15},{10,... | collective-permute-start | bytes 442376 | tf_op jit(solution)/shard_map/ppermute | solution.py:236
  45.5 1.3 %collective-permute-start.9 = (bf16[64,1152]{1,0:T(8,128)(2,1)S(1)}, bf16[64,1152]{1,0:T(8,128)(2,1)S(1)}, u32[]{:S(2)}, u32[]{:S(2)}) collective-permute-start(bf16[64,1152]{1,0:T(8,128)(2,1)S(1)} %shard_map.86), channel_id=1, source_target_pairs={{0,4},{1,5},{2,6},{3,7},{4,0},{5,1},{6,2},{7,3},{8,12},{9,13},{10,... | collective-permute-start | bytes 442376 | tf_op jit(solution)/shard_map/ppermute | solution.py:236
  46.8 0.7 collective-permute-start.11
  47.4 0.9 %collective-permute-done.12 = bf16[64,1152]{1,0:T(8,128)(2,1)S(1)} collective-permute-done((bf16[64,1152]{1,0:T(8,128)(2,1)S(1)}, bf16[64,1152]{1,0:T(8,128)(2,1)S(1)}, u32[]{:S(2)}, u32[]{:S(2)}) %collective-permute-start.12) | collective-permute-done | bytes 147488 | tf_op jit(solution)/shard_map/ppermute | solution.py:247
  48.4 1.4 %collective-permute-start.14 = (bf16[128,1152]{1,0:T(8,128)(2,1)S(1)}, bf16[128,1152]{1,0:T(8,128)(2,1)S(1)}, u32[]{:S(2)}, u32[]{:S(2)}) collective-permute-start(bf16[128,1152]{1,0:T(8,128)(2,1)S(1)} %pad_maximum_fusion.5), channel_id=1, source_target_pairs={{0,16},{1,9},{2,18},{3,11},{4,20},{5,13},{6,22},{7,15},{8,24},{9,1... | collective-permute-start | bytes 884744 | tf_op jit(solution)/shard_map/ppermute | solution.py:247
  49.8 3.3 %collective-permute-done.11 = bf16[64,1152]{1,0:T(8,128)(2,1)S(1)} collective-permute-done((bf16[64,1152]{1,0:T(8,128)(2,1)S(1)}, bf16[64,1152]{1,0:T(8,128)(2,1)S(1)}, u32[]{:S(2)}, u32[]{:S(2)}) %collective-permute-start.11) | collective-permute-done | bytes 147488 | tf_op jit(solution)/shard_map/ppermute | solution.py:236
  53.1 0.4 collective-permute-start.13
  53.5 3.0 %collective-permute-done.9 = bf16[64,1152]{1,0:T(8,128)(2,1)S(1)} collective-permute-done((bf16[64,1152]{1,0:T(8,128)(2,1)S(1)}, bf16[64,1152]{1,0:T(8,128)(2,1)S(1)}, u32[]{:S(2)}, u32[]{:S(2)}) %collective-permute-start.9) | collective-permute-done | bytes 147488 | tf_op jit(solution)/shard_map/ppermute | solution.py:236
  56.5 2.3 %collective-permute-done.13 = bf16[64,1152]{1,0:T(8,128)(2,1)S(1)} collective-permute-done((bf16[64,1152]{1,0:T(8,128)(2,1)S(1)}, bf16[64,1152]{1,0:T(8,128)(2,1)S(1)}, u32[]{:S(2)}, u32[]{:S(2)}) %collective-permute-start.13) | collective-permute-done | bytes 147488 | tf_op jit(solution)/shard_map/ppermute | solution.py:247
  58.8 2.8 %collective-permute-done.14 = bf16[128,1152]{1,0:T(8,128)(2,1)S(1)} collective-permute-done((bf16[128,1152]{1,0:T(8,128)(2,1)S(1)}, bf16[128,1152]{1,0:T(8,128)(2,1)S(1)}, u32[]{:S(2)}, u32[]{:S(2)}) %collective-permute-start.14) | collective-permute-done | bytes 294944 | tf_op jit(solution)/shard_map/ppermute | solution.py:247
  61.6 0.0 collective-permute-done.17
  61.6 0.2 constant_dynamic-update-slice_fusion.5.refs_0_
  61.7 0.1 collective-permute-start.18
  61.8 0.8 collective-permute-start.19
  62.7 1.1 %collective-permute-start.20 = (bf16[256,1152]{1,0:T(8,128)(2,1)S(1)}, bf16[256,1152]{1,0:T(8,128)(2,1)S(1)}, u32[]{:S(2)}, u32[]{:S(2)}) collective-permute-start(bf16[256,1152]{1,0:T(8,128)(2,1)S(1)} %pad_maximum_fusion.1.refs_0_), channel_id=1, source_target_pairs={{0,1},{1,0},{2,3},{3,2},{4,5},{5,4},{6,7},{7,6},{8,9},{9,8},{10,11... | collective-permute-start | bytes 1769480 | tf_op jit(solution)/shard_map/ppermute | solution.py:239
  63.7 0.5 collective-permute-start.15
  64.3 0.5 shard_map.87
  64.8 6.0 %collective-permute-done.19 = bf16[128,1152]{1,0:T(8,128)(2,1)S(1)} collective-permute-done((bf16[128,1152]{1,0:T(8,128)(2,1)S(1)}, bf16[128,1152]{1,0:T(8,128)(2,1)S(1)}, u32[]{:S(2)}, u32[]{:S(2)}) %collective-permute-start.19) | collective-permute-done | bytes 294944 | tf_op jit(solution)/shard_map/ppermute | solution.py:247
  70.9 0.1 collective-permute-start.21
  71.0 0.3 collective-permute-done.15
  71.3 0.3 collective-permute-start.16
  71.7 0.3 collective-permute-start.22
  71.9 0.7 collective-permute-start.23
  72.7 1.7 %convolution_bitcast_fusion = f32[1,64,1152]{2,1,0:T(8,128)} fusion(bf16[64,1152]{1,0:T(8,128)(2,1)S(1)} %shard_map.86, bf16[1152,1152]{1,0:T(8,128)(2,1)S(1)} %copy-done), kind=kOutput, calls=%fused_computation | convolution fusion | flops 169869312 | bytes 3096576 | tf_op jit(solution)/shard_map/dot_general | solution.py:17
  74.3 1.3 %shard_map.88 = (bf16[1152,1536]{1,0:T(8,128)(2,1)S(1)}, bf16[1152,512]{1,0:T(8,128)(2,1)S(1)}) custom-call(bf16[1024,1152]{1,0:T(8,128)(2,1)S(1)} %constant_dynamic-update-slice_fusion.5.refs_0_, bf16[1024,1152]{1,0:T(8,128)(2,1)S(1)} %collective-permute-done.18.refs_1_), custom_call_target="tpu_custom_call" | custom-call | bytes 9437184 | tf_op jit(solution)/shard_map/pallas_call | solution.py:157
  75.6 0.0 collective-permute-done.21.refs_4_
  75.6 4.8 %shard_map.89.acc = f32[1152,1152]{1,0:T(8,128)S(1)} custom-call(bf16[1152,1536]{1,0:T(8,128)(2,1)S(1)} %get-tuple-element.41.x_t, bf16[256,1152]{1,0:T(8,128)(2,1)S(1)} %pad_maximum_fusion.1.refs_0_, bf16[256,1152]{1,0:T(8,128)(2,1)S(1)} %pad_maximum_fusion.2.refs_1_, bf16[256,1152]{1,0:T(8,128)(2,1)S(1)} %pad_maximum_fusion.3.refs_2_, ...), custom_call_target="tpu_custom_call" | custom-call | flops 4076863488 | bytes 12386304 | tf_op jit(solution)/shard_map/pallas_call | solution.py:212
  80.4 1.4 %collective-permute-done.23.refs_0_ = bf16[256,1152]{1,0:T(8,128)(2,1)S(1)} collective-permute-done((bf16[256,1152]{1,0:T(8,128)(2,1)S(1)}, bf16[256,1152]{1,0:T(8,128)(2,1)S(1)}, u32[]{:S(2)}, u32[]{:S(2)}) %collective-permute-start.23) | collective-permute-done | bytes 589856 | tf_op jit(solution)/shard_map/ppermute | solution.py:247
  81.8 1.1 %add_bitcast_fusion = f32[1,256,1152]{2,1,0:T(8,128)} fusion(f32[256,1152]{1,0:T(8,128)S(1)} %get-tuple-element.34, f32[256,1152]{1,0:T(8,128)S(1)} %collective-permute-done.16), kind=kLoop, calls=%fused_computation.1 | loop fusion | flops 294912 | bytes 3538944 | tf_op jit(solution)/shard_map/broadcast_in_dim | solution.py:334
  83.0 0.9 collective-permute-done.24.refs_1_
  83.8 3.1 %shard_map.90 = f32[1152,1152]{1,0:T(8,128)} custom-call(bf16[1152,512]{1,0:T(8,128)(2,1)S(1)} %get-tuple-element.40.x_t, f32[1152,1152]{1,0:T(8,128)S(1)} %shard_map.89.acc, bf16[256,1152]{1,0:T(8,128)(2,1)S(1)} %collective-permute-done.23.refs_0_, bf16[256,1152]{1,0:T(8,128)(2,1)S(1)} %collective-permute-done.24.refs_1_), custom_call_target="tpu_custom_call" | custom-call | flops 1358954496 | bytes 12976128 | tf_op jit(solution)/shard_map/pallas_call | solution.py:212
  (22 shorter events, 0.3 us)
Async XLA Ops:
  0.6 20.6 %copy-start = (bf16[1152,1152]{1,0:T(8,128)(2,1)S(1)}, bf16[1152,1152]{1,0:T(8,128)(2,1)}, u32[]{:S(2)}) copy-start(bf16[1152,1152]{1,0:T(8,128)(2,1)} %param.9) | copy-start | bytes 7962628
  0.6 20.6 %copy-start.4 = (bf16[1,64,1152]{2,1,0:T(8,128)(2,1)S(1)}, bf16[1,64,1152]{2,1,0:T(8,128)(2,1)}, u32[]{:S(2)}) copy-start(bf16[1,64,1152]{2,1,0:T(8,128)(2,1)} %param.6) | copy-start | bytes 442372
  0.7 10.1 %collective-permute-start.2 = (bf16[64,1152]{1,0:T(8,128)(2,1)}, bf16[64,1152]{1,0:T(8,128)(2,1)S(1)}, u32[]{:S(2)}, u32[]{:S(2)}) collective-permute-start(bf16[64,1152]{1,0:T(8,128)(2,1)} %bitcast.13), channel_id=1, source_target_pairs={{0,6},{1,7},{2,4},{3,5},{4,2},{5,3},{6,0},{7,1},{8,14},{9,15},{10,... | collective-permute-start | bytes 442376 | tf_op jit(solution)/shard_map/ppermute | solution.py:236
  5.8 12.8 %collective-permute-start.1 = (bf16[64,1152]{1,0:T(8,128)(2,1)}, bf16[64,1152]{1,0:T(8,128)(2,1)}, u32[]{:S(2)}, u32[]{:S(2)}) collective-permute-start(bf16[64,1152]{1,0:T(8,128)(2,1)} %bitcast.14), channel_id=1, source_target_pairs={{0,4},{1,5},{2,6},{3,7},{4,0},{5,1},{6,2},{7,3},{8,12},{9,13},{10,... | collective-permute-start | bytes 442376 | tf_op jit(solution)/shard_map/ppermute | solution.py:236
  5.8 12.8 %collective-permute-start = (bf16[64,1152]{1,0:T(8,128)(2,1)}, bf16[64,1152]{1,0:T(8,128)(2,1)}, u32[]{:S(2)}, u32[]{:S(2)}) collective-permute-start(bf16[64,1152]{1,0:T(8,128)(2,1)} %bitcast.15), channel_id=1, source_target_pairs={{0,2},{1,3},{2,0},{3,1},{4,6},{5,7},{6,4},{7,5},{8,10},{9,11},{10,... | collective-permute-start | bytes 442376 | tf_op jit(solution)/shard_map/ppermute | solution.py:236
  6.4 18.8 %collective-permute-start.3 = (s32[1,256]{1,0:T(1,128)}, s32[1,256]{1,0:T(1,128)S(1)}, u32[]{:S(2)}, u32[]{:S(2)}) collective-permute-start(s32[1,256]{1,0:T(1,128)} %refs_0_.1), channel_id=1, source_target_pairs={{0,1},{1,0},{2,3},{3,2},{4,5},{5,4},{6,7},{7,6},{8,9},{9,8},{10,11... | collective-permute-start | bytes 3080 | tf_op jit(solution)/shard_map/ppermute | solution.py:239
  6.4 18.8 %collective-permute-start.4 = (bf16[256,1152]{1,0:T(8,128)(2,1)}, bf16[256,1152]{1,0:T(8,128)(2,1)S(1)}, u32[]{:S(2)}, u32[]{:S(2)}) collective-permute-start(bf16[256,1152]{1,0:T(8,128)(2,1)} %bitcast.11), channel_id=1, source_target_pairs={{0,1},{1,0},{2,3},{3,2},{4,5},{5,4},{6,7},{7,6},{8,9},{9,8},{10,11... | collective-permute-start | bytes 1769480 | tf_op jit(solution)/shard_map/ppermute | solution.py:239
  19.7 3.6 %copy-start.1 = (bf16[1024,1152]{1,0:T(8,128)(2,1)S(1)}, bf16[1024,1152]{1,0:T(8,128)(2,1)}, u32[]{:S(2)}) copy-start(bf16[1024,1152]{1,0:T(8,128)(2,1)} %get-tuple-element.54) | copy-start | bytes 7077892
  19.7 3.6 %copy-start.5 = (bf16[512,1152]{1,0:T(8,128)(2,1)S(1)}, bf16[512,1152]{1,0:T(8,128)(2,1)}, u32[]{:S(2)}) copy-start(bf16[512,1152]{1,0:T(8,128)(2,1)} %get-tuple-element.53) | copy-start | bytes 3538948
  19.7 5.6 %copy-start.2 = (bf16[1,256,1152]{2,1,0:T(8,128)(2,1)S(1)}, bf16[1,256,1152]{2,1,0:T(8,128)(2,1)}, u32[]{:S(2)}) copy-start(bf16[1,256,1152]{2,1,0:T(8,128)(2,1)} %param.7) | copy-start | bytes 1769476
  19.7 5.6 %copy-start.3 = (s32[1,256]{1,0:T(1,128)S(1)}, s32[1,256]{1,0:T(1,128)}, u32[]{:S(2)}) copy-start(s32[1,256]{1,0:T(1,128)} %refs_0_.1) | copy-start | bytes 3076
  19.7 20.7 %collective-permute-start.8 = (bf16[256,1152]{1,0:T(8,128)(2,1)S(1)}, bf16[256,1152]{1,0:T(8,128)(2,1)S(1)}, u32[]{:S(2)}, u32[]{:S(2)}) collective-permute-start(bf16[256,1152]{1,0:T(8,128)(2,1)S(1)} %pad_maximum_fusion), channel_id=1, source_target_pairs={{0,8},{1,17},{2,10},{3,19},{4,12},{5,21},{6,14},{7,23},{8,0},{9,25... | collective-permute-start | bytes 1769480 | tf_op jit(solution)/shard_map/ppermute | solution.py:247
  26.9 7.4 %collective-permute-start.5 = (bf16[64,1152]{1,0:T(8,128)(2,1)S(1)}, bf16[64,1152]{1,0:T(8,128)(2,1)S(1)}, u32[]{:S(2)}, u32[]{:S(2)}) collective-permute-start(bf16[64,1152]{1,0:T(8,128)(2,1)S(1)} %get-tuple-element.27), channel_id=1, source_target_pairs={{0,2},{1,3},{2,0},{3,1},{4,6},{5,7},{6,4},{7,5},{8,10},{9,11},{10,... | collective-permute-start | bytes 442376 | tf_op jit(solution)/shard_map/ppermute | solution.py:236
  26.9 13.4 %collective-permute-start.6 = (bf16[64,1152]{1,0:T(8,128)(2,1)S(1)}, bf16[64,1152]{1,0:T(8,128)(2,1)S(1)}, u32[]{:S(2)}, u32[]{:S(2)}) collective-permute-start(bf16[64,1152]{1,0:T(8,128)(2,1)S(1)} %get-tuple-element.28), channel_id=1, source_target_pairs={{0,4},{1,5},{2,6},{3,7},{4,0},{5,1},{6,2},{7,3},{8,12},{9,13},{10,... | collective-permute-start | bytes 442376 | tf_op jit(solution)/shard_map/ppermute | solution.py:236
  30.0 10.4 %collective-permute-start.7 = (bf16[64,1152]{1,0:T(8,128)(2,1)S(1)}, bf16[64,1152]{1,0:T(8,128)(2,1)S(1)}, u32[]{:S(2)}, u32[]{:S(2)}) collective-permute-start(bf16[64,1152]{1,0:T(8,128)(2,1)S(1)} %get-tuple-element.29), channel_id=1, source_target_pairs={{0,6},{1,7},{2,4},{3,5},{4,2},{5,3},{6,0},{7,1},{8,14},{9,15},{10,... | collective-permute-start | bytes 442376 | tf_op jit(solution)/shard_map/ppermute | solution.py:236
  40.5 21.0 %collective-permute-start.17 = (bf16[512,1152]{1,0:T(8,128)(2,1)S(1)}, bf16[512,1152]{1,0:T(8,128)(2,1)S(1)}, u32[]{:S(2)}, u32[]{:S(2)}) collective-permute-start(bf16[512,1152]{1,0:T(8,128)(2,1)S(1)} %get-tuple-element.45), channel_id=1, source_target_pairs={{0,16},{1,9},{2,18},{3,11},{4,20},{5,13},{6,22},{7,15},{8,24},{9,1... | collective-permute-start | bytes 3538952 | tf_op jit(solution)/shard_map/ppermute | solution.py:247
  41.5 6.8 %collective-permute-start.12 = (bf16[64,1152]{1,0:T(8,128)(2,1)S(1)}, bf16[64,1152]{1,0:T(8,128)(2,1)S(1)}, u32[]{:S(2)}, u32[]{:S(2)}) collective-permute-start(bf16[64,1152]{1,0:T(8,128)(2,1)S(1)} %shard_map.86), channel_id=1, source_target_pairs={{0,8},{1,17},{2,10},{3,19},{4,12},{5,21},{6,14},{7,23},{8,0},{9,25... | collective-permute-start | bytes 442376 | tf_op jit(solution)/shard_map/ppermute | solution.py:247
  43.0 10.5 %collective-permute-start.10 = (bf16[64,1152]{1,0:T(8,128)(2,1)S(1)}, bf16[64,1152]{1,0:T(8,128)(2,1)S(1)}, u32[]{:S(2)}, u32[]{:S(2)}) collective-permute-start(bf16[64,1152]{1,0:T(8,128)(2,1)S(1)} %shard_map.86), channel_id=1, source_target_pairs={{0,6},{1,7},{2,4},{3,5},{4,2},{5,3},{6,0},{7,1},{8,14},{9,15},{10,... | collective-permute-start | bytes 442376 | tf_op jit(solution)/shard_map/ppermute | solution.py:236
  45.5 11.0 %collective-permute-start.9 = (bf16[64,1152]{1,0:T(8,128)(2,1)S(1)}, bf16[64,1152]{1,0:T(8,128)(2,1)S(1)}, u32[]{:S(2)}, u32[]{:S(2)}) collective-permute-start(bf16[64,1152]{1,0:T(8,128)(2,1)S(1)} %shard_map.86), channel_id=1, source_target_pairs={{0,4},{1,5},{2,6},{3,7},{4,0},{5,1},{6,2},{7,3},{8,12},{9,13},{10,... | collective-permute-start | bytes 442376 | tf_op jit(solution)/shard_map/ppermute | solution.py:236
  46.8 6.3 %collective-permute-start.11 = (bf16[64,1152]{1,0:T(8,128)(2,1)S(1)}, bf16[64,1152]{1,0:T(8,128)(2,1)S(1)}, u32[]{:S(2)}, u32[]{:S(2)}) collective-permute-start(bf16[64,1152]{1,0:T(8,128)(2,1)S(1)} %shard_map.86), channel_id=1, source_target_pairs={{0,2},{1,3},{2,0},{3,1},{4,6},{5,7},{6,4},{7,5},{8,10},{9,11},{10,... | collective-permute-start | bytes 442376 | tf_op jit(solution)/shard_map/ppermute | solution.py:236
  48.4 13.1 %collective-permute-start.14 = (bf16[128,1152]{1,0:T(8,128)(2,1)S(1)}, bf16[128,1152]{1,0:T(8,128)(2,1)S(1)}, u32[]{:S(2)}, u32[]{:S(2)}) collective-permute-start(bf16[128,1152]{1,0:T(8,128)(2,1)S(1)} %pad_maximum_fusion.5), channel_id=1, source_target_pairs={{0,16},{1,9},{2,18},{3,11},{4,20},{5,13},{6,22},{7,15},{8,24},{9,1... | collective-permute-start | bytes 884744 | tf_op jit(solution)/shard_map/ppermute | solution.py:247
  53.1 5.7 %collective-permute-start.13 = (bf16[64,1152]{1,0:T(8,128)(2,1)S(1)}, bf16[64,1152]{1,0:T(8,128)(2,1)S(1)}, u32[]{:S(2)}, u32[]{:S(2)}) collective-permute-start(bf16[64,1152]{1,0:T(8,128)(2,1)S(1)} %collective-permute-done.11), channel_id=1, source_target_pairs={{0,8},{1,17},{2,10},{3,19},{4,12},{5,21},{6,14},{7,23},{8,0},{9,25... | collective-permute-start | bytes 442376 | tf_op jit(solution)/shard_map/ppermute | solution.py:247
  61.7 12.6 %collective-permute-start.18 = (bf16[1024,1152]{1,0:T(8,128)(2,1)S(1)}, bf16[1024,1152]{1,0:T(8,128)(2,1)S(1)}, u32[]{:S(2)}, u32[]{:S(2)}) collective-permute-start(bf16[1024,1152]{1,0:T(8,128)(2,1)S(1)} %constant_dynamic-update-slice_fusion.5.refs_0_), channel_id=1, source_target_pairs={{0,1},{1,0},{2,3},{3,2},{4,5},{5,4},{6,7},{7,6},{8,9},{9,8},{10,11... | collective-permute-start | bytes 7077896 | tf_op jit(solution)/shard_map/ppermute | solution.py:239
  61.8 9.0 %collective-permute-start.19 = (bf16[128,1152]{1,0:T(8,128)(2,1)S(1)}, bf16[128,1152]{1,0:T(8,128)(2,1)S(1)}, u32[]{:S(2)}, u32[]{:S(2)}) collective-permute-start(bf16[128,1152]{1,0:T(8,128)(2,1)S(1)} %pad_maximum_fusion.6), channel_id=1, source_target_pairs={{0,16},{1,9},{2,18},{3,11},{4,20},{5,13},{6,22},{7,15},{8,24},{9,1... | collective-permute-start | bytes 884744 | tf_op jit(solution)/shard_map/ppermute | solution.py:247
  62.7 9.0 %collective-permute-start.20 = (bf16[256,1152]{1,0:T(8,128)(2,1)S(1)}, bf16[256,1152]{1,0:T(8,128)(2,1)S(1)}, u32[]{:S(2)}, u32[]{:S(2)}) collective-permute-start(bf16[256,1152]{1,0:T(8,128)(2,1)S(1)} %pad_maximum_fusion.1.refs_0_), channel_id=1, source_target_pairs={{0,1},{1,0},{2,3},{3,2},{4,5},{5,4},{6,7},{7,6},{8,9},{9,8},{10,11... | collective-permute-start | bytes 1769480 | tf_op jit(solution)/shard_map/ppermute | solution.py:239
  63.7 7.6 %collective-permute-start.15 = (bf16[128,1152]{1,0:T(8,128)(2,1)S(1)}, bf16[128,1152]{1,0:T(8,128)(2,1)S(1)}, u32[]{:S(2)}, u32[]{:S(2)}) collective-permute-start(bf16[128,1152]{1,0:T(8,128)(2,1)S(1)} %pad_maximum_fusion.4), channel_id=1, source_target_pairs={{0,8},{1,17},{2,10},{3,19},{4,12},{5,21},{6,14},{7,23},{8,0},{9,25... | collective-permute-start | bytes 884744 | tf_op jit(solution)/shard_map/ppermute | solution.py:247
  70.9 4.7 %collective-permute-start.21 = (bf16[256,1152]{1,0:T(8,128)(2,1)S(1)}, bf16[256,1152]{1,0:T(8,128)(2,1)S(1)}, u32[]{:S(2)}, u32[]{:S(2)}) collective-permute-start(bf16[256,1152]{1,0:T(8,128)(2,1)S(1)} %pad_maximum_fusion.2.refs_1_), channel_id=1, source_target_pairs={{0,1},{1,0},{2,3},{3,2},{4,5},{5,4},{6,7},{7,6},{8,9},{9,8},{10,11... | collective-permute-start | bytes 1769480 | tf_op jit(solution)/shard_map/ppermute | solution.py:239
  71.3 10.5 %collective-permute-start.16 = (f32[256,1152]{1,0:T(8,128)S(1)}, f32[256,1152]{1,0:T(8,128)S(1)}, u32[]{:S(2)}, u32[]{:S(2)}) collective-permute-start(f32[256,1152]{1,0:T(8,128)S(1)} %get-tuple-element.38), channel_id=1, source_target_pairs={{0,1},{1,0},{2,3},{3,2},{4,5},{5,4},{6,7},{7,6},{8,9},{9,8},{10,11... | collective-permute-start | bytes 3538952 | tf_op jit(solution)/shard_map/ppermute | solution.py:239
  71.7 3.9 %collective-permute-start.22 = (bf16[256,1152]{1,0:T(8,128)(2,1)S(1)}, bf16[256,1152]{1,0:T(8,128)(2,1)S(1)}, u32[]{:S(2)}, u32[]{:S(2)}) collective-permute-start(bf16[256,1152]{1,0:T(8,128)(2,1)S(1)} %pad_maximum_fusion.3.refs_2_), channel_id=1, source_target_pairs={{0,1},{1,0},{2,3},{3,2},{4,5},{5,4},{6,7},{7,6},{8,9},{9,8},{10,11... | collective-permute-start | bytes 1769480 | tf_op jit(solution)/shard_map/ppermute | solution.py:239
  71.9 9.9 %collective-permute-start.23 = (bf16[256,1152]{1,0:T(8,128)(2,1)S(1)}, bf16[256,1152]{1,0:T(8,128)(2,1)S(1)}, u32[]{:S(2)}, u32[]{:S(2)}) collective-permute-start(bf16[256,1152]{1,0:T(8,128)(2,1)S(1)} %pad_maximum_fusion.3.refs_2_), channel_id=1, source_target_pairs={{0,16},{1,9},{2,18},{3,11},{4,20},{5,13},{6,22},{7,15},{8,24},{9,1... | collective-permute-start | bytes 1769480 | tf_op jit(solution)/shard_map/ppermute | solution.py:247
  81.8 2.0 %collective-permute-start.24 = (bf16[256,1152]{1,0:T(8,128)(2,1)S(1)}, bf16[256,1152]{1,0:T(8,128)(2,1)S(1)}, u32[]{:S(2)}, u32[]{:S(2)}) collective-permute-start(bf16[256,1152]{1,0:T(8,128)(2,1)S(1)} %collective-permute-done.23.refs_0_), channel_id=1, source_target_pairs={{0,1},{1,0},{2,3},{3,2},{4,5},{5,4},{6,7},{7,6},{8,9},{9,8},{10,11... | collective-permute-start | bytes 1769480 | tf_op jit(solution)/shard_map/ppermute | solution.py:239

commit v6 on v5

--- a/solution.py
+++ b/solution.py
@@ -89,6 +89,29 @@
     )(both, embed, *labels, *captions)
 
 
+def join_kernel(*refs):
+    at = 0
+    for v in refs[:-1]:
+        refs[-1][at : at + v.shape[0], :] = v[...]
+        at += v.shape[0]
+
+
+def joined(vs):
+    rows = sum(v.shape[0] for v in vs)
+    depth = vs[0].shape[1]
+    vmem = pl.BlockSpec(memory_space=pltpu.VMEM)
+    return pl.pallas_call(
+        join_kernel,
+        out_shape=jax.ShapeDtypeStruct((rows, depth), vs[0].dtype),
+        in_specs=[vmem] * len(vs),
+        out_specs=vmem,
+        compiler_params=pltpu.CompilerParams(vmem_limit_bytes=12 * 2**20),
+        cost_estimate=pl.CostEstimate(
+            flops=0, bytes_accessed=4 * rows * depth, transcendentals=0
+        ),
+    )(*vs)
+
+
 def caption_kernel(both, dlogit, unit, own, other):
     scale = both[0:1, 0:1]
     n_cap = own.shape[0]
@@ -142,18 +165,16 @@
 
 def turn_kernel(plan, *refs):
     ins, outs = refs[: -len(plan)], refs[-len(plan) :]
-    for out, pieces in zip(outs, plan):
+    for out, runs in zip(outs, plan):
         col = 0
-        for runs in pieces:
-            rows = [ins[i][at : at + size, :] for i, at, size in runs]
-            rows = jnp.concatenate(rows)
-            out[:, col : col + rows.shape[0]] = rows.T
-            col += rows.shape[0]
+        for i, at, size in runs:
+            out[:, col : col + size] = ins[i][at : at + size, :].T
+            col += size
 
 
 def turned(xs, plan):
     depth = xs[0].shape[1]
-    images = [sum(size for runs in pieces for _, _, size in runs) for pieces in plan]
+    images = [sum(size for _, _, size in runs) for runs in plan]
     return pl.pallas_call(
         functools.partial(turn_kernel, plan),
         out_shape=[jax.ShapeDtypeStruct((depth, n), BF16) for n in images],
@@ -246,9 +267,19 @@
                 perm.append((j * nb + m, to * nb + m))
         return lax.ppermute(v, ("dp", "blk"), perm)
 
+    def over_d(v, first, *before):
+        v = [v, first]
+        for i in range(1, bits):
+            v = after(jnp.concatenate(v), before)
+            v = [v, step_d(v, i)]
+        return v
+
+    half = nz // 2
     xs = [x] + [along_z(x, k) for k in range(1, nz)]
-    x_own = jnp.concatenate(xs)
-    x_first = step_d(x_own, 0)
+    x_near, x_far = jnp.concatenate(xs[1:half]), jnp.concatenate(xs[half:])
+    x_own = over_d(x, step_d(x, 0))
+    x_near_first = step_d(x_near, 0)
+    x_far_first = step_d(x_far, 0)
     embed = dot(jnp.concatenate(xs), weight)
     row = lax.broadcasted_iota(jnp.int32, (16, 128), 0)
     both = jnp.where(row < 8, scale, offset)
@@ -259,58 +290,40 @@
         [labels, swap(labels)],
         [captions, swap(captions)],
     )
+    sent = after(sent, x_own)
     back = [along_z(v, k + 1) for k, v in enumerate(sent)]
 
-    x_first = after(x_first, back)
-    x_own = [x_own, x_first]
-    for i in range(1, bits):
-        x_own = jnp.concatenate(x_own)
-        x_own = [x_own, step_d(x_own, i)]
-    small = nd * nb * n_img <= 2048
-
-    adjoint, adjoint_other = caption_sums(both, after(dlogit, x_first), unit)
-
+    x_near = over_d(x_near, after(x_near_first, sent))
+    x_far = over_d(x_far, after(x_far_first, sent))
+    back = after(back, x_far, x_near)
     ge = embed_grad(own, u, inv_norm, back)
     grad_features = dot(ge, weight, LAST)
 
-    half = nz // 2
     near = [along_z(ge, k) for k in range(1, half)]
     own_first = step_d(ge, 0)
     far = [along_z(ge, k) for k in range(half, nz)]
-
-    def over_d(v, first, *before):
-        v = [v, first]
-        for i in range(1, bits):
-            v = after(jnp.concatenate(v), before)
-            v = [v, step_d(v, i)]
-        return v
 
     g_own = over_d(ge, own_first)
     near = after(jnp.concatenate(near), g_own[0])
     near_first = step_d(near, 0)
     g_near = over_d(near, near_first)
-    far = after(jnp.concatenate(far), near_first, g_own[1])
+    far = after(jnp.concatenate(far), near)
     far_first = step_d(far, 0)
-    adjoint = adjoint + swap(after(adjoint_other, far_first))
-    sizes = [n_img, n_img * (half - 1), n_img * half]
-    firsts = [0, n_img, n_img * half]
-    n_own = nz * n_img
-    per = nd // 2
-    if small:
+    dlogit = after(dlogit, far_first)
+    adjoint, adjoint_other = caption_sums(both, dlogit, unit)
+    adjoint = adjoint + swap(adjoint_other)
+    if nd * nb * n_img <= 2048:
+        x_all = [joined(x_own + x_near), joined(x_far)]
+        x_all += [swap(after(v, near)) for v in x_all]
+        n = n_img * nd
         plan = [[], []]
-        for core in range(2):
-            for g in range(3):
-                runs = [(core, i * n_own + firsts[g], sizes[g]) for i in range(nd)]
-                if g < 2:
-                    plan[0].append(runs)
-                else:
-                    plan[0].append(runs[:per])
-                    plan[1].append(runs[per:])
-        x_own = jnp.concatenate(x_own)
-        x_early, x_late = turned([x_own, swap(after(x_own, far))], plan)
+        for core in (0, 2):
+            plan[0] += [(core, 0, n), (core, n, n), (core + 1, 0, n)]
+            plan[1] += [(core + 1, n, n)]
+        x_early, x_late = turned(x_all, plan)
         g_own = jnp.concatenate(g_own)
         own_swapped = swap(g_own)
-        g_far = over_d(far, far_first, own_swapped, g_near[1])
+        g_far = over_d(far, far_first, own_swapped)
         early = [g_own, jnp.concatenate(g_near), g_far[0]]
         others = [own_swapped, swap(early[1]), swap(after(early[2], g_near[1]))]
         acc = weight_sum(None, x_early, early + others, 1.0)
@@ -319,17 +332,8 @@
     else:
         g_far = over_d(far, far_first)
         grad_weight = 0.0
-        for i, x_part in enumerate(x_own):
-            for at in range(per):
-                g_part = [
-                    g[i][at * m : (at + 1) * m]
-                    for m, g in zip(sizes, (g_own, g_near, g_far))
-                ]
-                grad_weight = grad_weight + dot(
-                    x_part[at * n_own : (at + 1) * n_own],
-                    jnp.concatenate(g_part),
-                    FIRST,
-                )
+        for v, g in zip(x_own + x_near + x_far, g_own + g_near + g_far):
+            grad_weight = grad_weight + dot(v, g, FIRST)
         grad_weight = (grad_weight + swap(grad_weight)) / nd
     return (grad_features[None], adjoint[None], grad_weight)
 

time: 87.9 us -> 87.4 us (level)
  starting transfers between devices: 24.6 us -> 33.1 us
  waiting for transfers between devices: 38.7 us -> 33 us
  local copies, waits for them, and re-layouts: 3.99 us -> 0.1 us
  other arithmetic: 2.45 us -> 3.37 us
    ppermute x8 -> x12, starting transfers between devices: 7.69 us -> 17.8 us  [step_d(): return lax.ppermute(v, ('dp', 'blk'), perm)]
    ppermute x8 -> x12, waiting for transfers between devices: 13.8 us -> 8.21 us  [step_d(): return lax.ppermute(v, ('dp', 'blk'), perm)]
    unnamed x16 -> x8, local copies, waits for them, and re-layouts: 3.6 us -> 0.03 us
    concatenate x3 -> x6, other arithmetic: 0.1 us -> 2.09 us  [over_d(): v = after(jnp.concatenate(v), before)]
    ppermute x9, starting transfers between devices: 14.6 us -> 13.4 us  [along_z(): return lax.ppermute(v, 'blk', [(i, i ^ 2 * k) for i in range(nb)])]
    concatenate x2, other arithmetic: 1.12 us -> 0.05 us  [the longest x1 0.02 us: on_device(): x_near, x_far = (jnp.concatenate(xs[1:half]), jnp.concatenate(xs[half:]))]
    ppermute x8 -> x9, starting transfers between devices: 2.29 us -> 1.87 us  [swap(): return lax.ppermute(v, 'blk', [(i, i ^ 1) for i in range(nb)])]
  transfers between devices with their start and end apart: 25 -> 30, of which waited for: 13 -> 9; matrix products, arithmetic and copies ran while one was open for 11% -> 8% of each run, Pallas kernels for 10% -> 10%
where the time goes in v6:
time: 87.4 us; the launch traced here: 86.9 us
  starting transfers between devices  33.1 us (38%)
  waiting for transfers between devices  33 us (38%)
  Pallas kernels  11.6 us (13%)
  matrix products  3.59 us (4%)
  other arithmetic  3.37 us (4%)
  between operations  2.16 us (2%)
    ppermute x9, waiting for transfers between devices, along_z(): return lax.ppermute(v, 'blk', [(i, i ^ 2 * k) for i in range(nb)])  23.9 us
    ppermute x12, starting transfers between devices, step_d(): return lax.ppermute(v, ('dp', 'blk'), perm)  17.8 us
    ppermute x9, starting transfers between devices, along_z(): return lax.ppermute(v, 'blk', [(i, i ^ 2 * k) for i in range(nb)])  13.4 us
    ppermute x12, waiting for transfers between devices, step_d(): return lax.ppermute(v, ('dp', 'blk'), perm)  8.21 us
    pallas_call x2, Pallas kernels, weight_sum(): pl.pallas_call(kernel, out_shape=jax.ShapeDtypeStruct((depth, depth), F32...  7.84 us
    dot_general x2, matrix products, dot(): return lax.dot_general(a, b, dims, preferred_element_type=F32)  3.59 us
    concatenate x6, other arithmetic, over_d(): v = after(jnp.concatenate(v), before)  2.09 us
    ppermute x9, starting transfers between devices, swap(): return lax.ppermute(v, 'blk', [(i, i ^ 1) for i in range(nb)])  1.87 us
  transfers between devices with their start and end apart: 30, of which 9 were waited for; matrix products, arithmetic and copies ran while one was open for 8% of the time, Pallas kernels for 10%

profile of v6, /device:TPU:0, one launch (start us, length us, event | category | flops | bytes accessed | tf_op | source)
XLA Modules:
  0.0 86.9 jit_solution(10546643961925592563)
XLA Ops:
  0.6 0.0 copy-start
  0.6 3.0 %collective-permute-start.5 = (bf16[64,1152]{1,0:T(8,128)(2,1)}, bf16[64,1152]{1,0:T(8,128)(2,1)}, u32[]{:S(2)}, u32[]{:S(2)}) collective-permute-start(bf16[64,1152]{1,0:T(8,128)(2,1)} %bitcast.11), channel_id=1, source_target_pairs={{0,8},{1,17},{2,10},{3,19},{4,12},{5,21},{6,14},{7,23},{8,0},{9,25... | collective-permute-start | bytes 442376 | tf_op jit(solution)/shard_map/ppermute | solution.py:268
  3.6 1.6 %collective-permute-start = (bf16[64,1152]{1,0:T(8,128)(2,1)}, bf16[64,1152]{1,0:T(8,128)(2,1)}, u32[]{:S(2)}, u32[]{:S(2)}) collective-permute-start(bf16[64,1152]{1,0:T(8,128)(2,1)} %bitcast.12), channel_id=1, source_target_pairs={{0,2},{1,3},{2,0},{3,1},{4,6},{5,7},{6,4},{7,5},{8,10},{9,11},{10,... | collective-permute-start | bytes 442376 | tf_op jit(solution)/shard_map/ppermute | solution.py:257
  5.2 2.6 %collective-permute-start.1 = (bf16[64,1152]{1,0:T(8,128)(2,1)}, bf16[64,1152]{1,0:T(8,128)(2,1)S(1)}, u32[]{:S(2)}, u32[]{:S(2)}) collective-permute-start(bf16[64,1152]{1,0:T(8,128)(2,1)} %bitcast.13), channel_id=1, source_target_pairs={{0,4},{1,5},{2,6},{3,7},{4,0},{5,1},{6,2},{7,3},{8,12},{9,13},{10,... | collective-permute-start | bytes 442376 | tf_op jit(solution)/shard_map/ppermute | solution.py:257
  7.8 0.2 collective-permute-start.2
  8.0 0.0 collective-permute-start.4
  9.3 0.0 copy-start.3
  9.4 0.0 collective-permute-done.5
  9.4 0.6 collective-permute-start.3
  9.9 1.0 %pad_maximum_fusion.4.refs_0_ = bf16[128,1152]{1,0:T(8,128)(2,1)S(1)} fusion(bf16[64,1152]{1,0:T(8,128)(2,1)} %collective-permute-done.5, bf16[64,1152]{1,0:T(8,128)(2,1)} %bitcast.15), kind=kLoop, calls=%fused_computation.14 | loop fusion | flops 589824 | bytes 589824 | tf_op jit(solution)/shard_map/concatenate | solution.py:273
  11.0 8.4 %collective-permute-done.1 = bf16[64,1152]{1,0:T(8,128)(2,1)S(1)} collective-permute-done((bf16[64,1152]{1,0:T(8,128)(2,1)}, bf16[64,1152]{1,0:T(8,128)(2,1)S(1)}, u32[]{:S(2)}, u32[]{:S(2)}) %collective-permute-start.1) | collective-permute-done | bytes 147488 | tf_op jit(solution)/shard_map/ppermute | solution.py:257
  19.4 0.5 collective-permute-start.6
  19.8 0.0 copy-start.1
  19.9 0.0 copy-start.2
  19.9 1.6 %collective-permute-start.10 = (bf16[128,1152]{1,0:T(8,128)(2,1)S(1)}, bf16[128,1152]{1,0:T(8,128)(2,1)S(1)}, u32[]{:S(2)}, u32[]{:S(2)}) collective-permute-start(bf16[128,1152]{1,0:T(8,128)(2,1)S(1)} %pad_maximum_fusion.5), channel_id=1, source_target_pairs={{0,8},{1,17},{2,10},{3,19},{4,12},{5,21},{6,14},{7,23},{8,0},{9,25... | collective-permute-start | bytes 884744 | tf_op jit(solution)/shard_map/ppermute | solution.py:268
  21.5 0.0 collective-permute-done
  21.5 0.5 collective-permute-start.12
  22.0 1.9 %fusion.embed = f32[256,1152]{1,0:T(8,128)S(1)} fusion(bf16[1152,1152]{1,0:T(8,128)(2,1)S(1)} %copy-done, bf16[64,1152]{1,0:T(8,128)(2,1)S(1)} %collective-permute-done.2, bf16[64,1152]{1,0:T(8,128)(2,1)S(1)} %collective-permute-done.1, bf16[64,1152]{1,0:T(8,128)(2,1)} %collective-permute-done, bf16[64,1152]{1,0:T(8,128)(2,1)S(1)} %bitcast.16), kind=kOutput, calls=%fused_computation.2 | convolution fusion | flops 681836544 | bytes 4423680 | tf_op jit(solution)/shard_map/dot_general | solution.py:17
  23.9 0.1 iota.7.both
  24.0 1.6 %shard_map.85 = (f32[64,1152]{1,0:T(8,128)S(1)}, f32[64,1152]{1,0:T(8,128)S(1)}, f32[64,128]{1,0:T(8,128)S(1)}, bf16[256,1152]{1,0:T(8,128)(2,1)S(1)}, bf16[256,...) custom-call(f32[16,128]{1,0:T(8,128)S(1)} %iota.7.both, ...), custom_call_target="tpu_custom_call" | custom-call | flops 603979776 | bytes 4718592 | tf_op jit(solution)/shard_map/pallas_call | solution.py:74
  25.6 1.3 %collective-permute-done.6.refs_1_ = bf16[128,1152]{1,0:T(8,128)(2,1)S(1)} collective-permute-done((bf16[128,1152]{1,0:T(8,128)(2,1)S(1)}, bf16[128,1152]{1,0:T(8,128)(2,1)S(1)}, u32[]{:S(2)}, u32[]{:S(2)}) %collective-permute-start.6) | collective-permute-done | bytes 294944 | tf_op jit(solution)/shard_map/ppermute | solution.py:268
  26.9 0.0 collective-permute-done.10
  26.9 3.1 %collective-permute-start.11 = (bf16[256,1152]{1,0:T(8,128)(2,1)S(1)}, bf16[256,1152]{1,0:T(8,128)(2,1)S(1)}, u32[]{:S(2)}, u32[]{:S(2)}) collective-permute-start(bf16[256,1152]{1,0:T(8,128)(2,1)S(1)} %pad_maximum_fusion.refs_0_), channel_id=1, source_target_pairs={{0,16},{1,9},{2,18},{3,11},{4,20},{5,13},{6,22},{7,15},{8,24},{9,1... | collective-permute-start | bytes 1769480 | tf_op jit(solution)/shard_map/ppermute | solution.py:268
  30.0 0.0 collective-permute-done.12
  30.0 0.9 %pad_maximum_fusion.6.refs_2_ = bf16[128,1152]{1,0:T(8,128)(2,1)S(1)} fusion(bf16[64,1152]{1,0:T(8,128)(2,1)S(1)} %collective-permute-done.12, bf16[64,1152]{1,0:T(8,128)(2,1)} %collective-permute-done), kind=kLoop, calls=%fused_computation.16 | loop fusion | flops 589824 | bytes 589824 | tf_op jit(solution)/shard_map/concatenate | solution.py:273
  30.9 3.1 %collective-permute-start.13 = (bf16[128,1152]{1,0:T(8,128)(2,1)S(1)}, bf16[128,1152]{1,0:T(8,128)(2,1)S(1)}, u32[]{:S(2)}, u32[]{:S(2)}) collective-permute-start(bf16[128,1152]{1,0:T(8,128)(2,1)S(1)} %pad_maximum_fusion.6.refs_2_), channel_id=1, source_target_pairs={{0,16},{1,9},{2,18},{3,11},{4,20},{5,13},{6,22},{7,15},{8,24},{9,1... | collective-permute-start | bytes 884744 | tf_op jit(solution)/shard_map/ppermute | solution.py:268
  34.0 0.0 collective-permute-start.7
  34.0 1.2 %collective-permute-start.8 = (bf16[64,1152]{1,0:T(8,128)(2,1)S(1)}, bf16[64,1152]{1,0:T(8,128)(2,1)S(1)}, u32[]{:S(2)}, u32[]{:S(2)}) collective-permute-start(bf16[64,1152]{1,0:T(8,128)(2,1)S(1)} %get-tuple-element.38), channel_id=1, source_target_pairs={{0,4},{1,5},{2,6},{3,7},{4,0},{5,1},{6,2},{7,3},{8,12},{9,13},{10,... | collective-permute-start | bytes 442376 | tf_op jit(solution)/shard_map/ppermute | solution.py:257
  35.2 3.2 %collective-permute-start.9 = (bf16[64,1152]{1,0:T(8,128)(2,1)S(1)}, bf16[64,1152]{1,0:T(8,128)(2,1)S(1)}, u32[]{:S(2)}, u32[]{:S(2)}) collective-permute-start(bf16[64,1152]{1,0:T(8,128)(2,1)S(1)} %get-tuple-element.39), channel_id=1, source_target_pairs={{0,6},{1,7},{2,4},{3,5},{4,2},{5,3},{6,0},{7,1},{8,14},{9,15},{10,... | collective-permute-start | bytes 442376 | tf_op jit(solution)/shard_map/ppermute | solution.py:257
  38.4 3.2 %collective-permute-done.7.refs_0_ = bf16[64,1152]{1,0:T(8,128)(2,1)S(1)} collective-permute-done((bf16[64,1152]{1,0:T(8,128)(2,1)S(1)}, bf16[64,1152]{1,0:T(8,128)(2,1)S(1)}, u32[]{:S(2)}, u32[]{:S(2)}) %collective-permute-start.7) | collective-permute-done | bytes 147488 | tf_op jit(solution)/shard_map/ppermute | solution.py:257
  41.6 4.4 %collective-permute-done.8.refs_1_ = bf16[64,1152]{1,0:T(8,128)(2,1)S(1)} collective-permute-done((bf16[64,1152]{1,0:T(8,128)(2,1)S(1)}, bf16[64,1152]{1,0:T(8,128)(2,1)S(1)}, u32[]{:S(2)}, u32[]{:S(2)}) %collective-permute-start.8) | collective-permute-done | bytes 147488 | tf_op jit(solution)/shard_map/ppermute | solution.py:257
  46.1 0.2 shard_map.86
  46.3 1.1 %collective-permute-start.17 = (bf16[64,1152]{1,0:T(8,128)(2,1)S(1)}, bf16[64,1152]{1,0:T(8,128)(2,1)S(1)}, u32[]{:S(2)}, u32[]{:S(2)}) collective-permute-start(bf16[64,1152]{1,0:T(8,128)(2,1)S(1)} %shard_map.86), channel_id=1, source_target_pairs={{0,8},{1,17},{2,10},{3,19},{4,12},{5,21},{6,14},{7,23},{8,0},{9,25... | collective-permute-start | bytes 442376 | tf_op jit(solution)/shard_map/ppermute | solution.py:268
  47.3 2.2 %collective-permute-start.16 = (bf16[64,1152]{1,0:T(8,128)(2,1)S(1)}, bf16[64,1152]{1,0:T(8,128)(2,1)S(1)}, u32[]{:S(2)}, u32[]{:S(2)}) collective-permute-start(bf16[64,1152]{1,0:T(8,128)(2,1)S(1)} %shard_map.86), channel_id=1, source_target_pairs={{0,2},{1,3},{2,0},{3,1},{4,6},{5,7},{6,4},{7,5},{8,10},{9,11},{10,... | collective-permute-start | bytes 442376 | tf_op jit(solution)/shard_map/ppermute | solution.py:257
  49.6 0.5 collective-permute-start.14
  50.1 1.9 %collective-permute-start.15 = (bf16[64,1152]{1,0:T(8,128)(2,1)S(1)}, bf16[64,1152]{1,0:T(8,128)(2,1)S(1)}, u32[]{:S(2)}, u32[]{:S(2)}) collective-permute-start(bf16[64,1152]{1,0:T(8,128)(2,1)S(1)} %shard_map.86), channel_id=1, source_target_pairs={{0,6},{1,7},{2,4},{3,5},{4,2},{5,3},{6,0},{7,1},{8,14},{9,15},{10,... | collective-permute-start | bytes 442376 | tf_op jit(solution)/shard_map/ppermute | solution.py:257
  51.9 0.0 collective-permute-done.17
  52.0 0.7 collective-permute-start.22
  52.7 0.1 shard_map.88.refs_0_
  52.8 0.1 shard_map.89.refs_1_
  52.9 1.1 %collective-permute-done.16 = bf16[64,1152]{1,0:T(8,128)(2,1)S(1)} collective-permute-done((bf16[64,1152]{1,0:T(8,128)(2,1)S(1)}, bf16[64,1152]{1,0:T(8,128)(2,1)S(1)}, u32[]{:S(2)}, u32[]{:S(2)}) %collective-permute-start.16) | collective-permute-done | bytes 147488 | tf_op jit(solution)/shard_map/ppermute | solution.py:257
  53.9 1.1 %collective-permute-start.23 = (bf16[64,1152]{1,0:T(8,128)(2,1)S(1)}, bf16[64,1152]{1,0:T(8,128)(2,1)S(1)}, u32[]{:S(2)}, u32[]{:S(2)}) collective-permute-start(bf16[64,1152]{1,0:T(8,128)(2,1)S(1)} %collective-permute-done.16), channel_id=1, source_target_pairs={{0,8},{1,17},{2,10},{3,19},{4,12},{5,21},{6,14},{7,23},{8,0},{9,25... | collective-permute-start | bytes 442376 | tf_op jit(solution)/shard_map/ppermute | solution.py:268
  55.0 6.8 %collective-permute-done.14 = bf16[64,1152]{1,0:T(8,128)(2,1)S(1)} collective-permute-done((bf16[64,1152]{1,0:T(8,128)(2,1)S(1)}, bf16[64,1152]{1,0:T(8,128)(2,1)S(1)}, u32[]{:S(2)}, u32[]{:S(2)}) %collective-permute-start.14) | collective-permute-done | bytes 147488 | tf_op jit(solution)/shard_map/ppermute | solution.py:257
  61.8 0.0 collective-permute-done.15
  61.9 1.0 %collective-permute-start.18 = (bf16[128,1152]{1,0:T(8,128)(2,1)S(1)}, bf16[128,1152]{1,0:T(8,128)(2,1)S(1)}, u32[]{:S(2)}, u32[]{:S(2)}) collective-permute-start(bf16[128,1152]{1,0:T(8,128)(2,1)S(1)} %pad_maximum_fusion.7), channel_id=1, source_target_pairs={{0,8},{1,17},{2,10},{3,19},{4,12},{5,21},{6,14},{7,23},{8,0},{9,25... | collective-permute-start | bytes 884744 | tf_op jit(solution)/shard_map/ppermute | solution.py:268
  62.9 0.5 collective-permute-start.20
  63.4 0.0 collective-permute-done.22
  63.5 0.1 collective-permute-start.25
  63.6 1.4 %collective-permute-start.24 = (bf16[128,1152]{1,0:T(8,128)(2,1)S(1)}, bf16[128,1152]{1,0:T(8,128)(2,1)S(1)}, u32[]{:S(2)}, u32[]{:S(2)}) collective-permute-start(bf16[128,1152]{1,0:T(8,128)(2,1)S(1)} %pad_maximum_fusion.9), channel_id=1, source_target_pairs={{0,16},{1,9},{2,18},{3,11},{4,20},{5,13},{6,22},{7,15},{8,24},{9,1... | collective-permute-start | bytes 884744 | tf_op jit(solution)/shard_map/ppermute | solution.py:268
  65.0 5.5 %collective-permute-done.18 = bf16[128,1152]{1,0:T(8,128)(2,1)S(1)} collective-permute-done((bf16[128,1152]{1,0:T(8,128)(2,1)S(1)}, bf16[128,1152]{1,0:T(8,128)(2,1)S(1)}, u32[]{:S(2)}, u32[]{:S(2)}) %collective-permute-start.18) | collective-permute-done | bytes 294944 | tf_op jit(solution)/shard_map/ppermute | solution.py:268
  70.5 0.5 shard_map.87
  71.1 0.1 collective-permute-start.19
  71.2 0.0 collective-permute-done.24
  71.3 0.6 collective-permute-start.26
  71.8 0.1 collective-permute-start.27
  71.9 0.8 collective-permute-start.28
  72.7 1.7 %convolution_bitcast_fusion = f32[1,64,1152]{2,1,0:T(8,128)} fusion(bf16[64,1152]{1,0:T(8,128)(2,1)S(1)} %shard_map.86, bf16[1152,1152]{1,0:T(8,128)(2,1)S(1)} %copy-done), kind=kOutput, calls=%fused_computation | convolution fusion | flops 169869312 | bytes 3096576 | tf_op jit(solution)/shard_map/dot_general | solution.py:17
  74.4 1.3 %shard_map.90 = (bf16[1152,1536]{1,0:T(8,128)(2,1)S(1)}, bf16[1152,512]{1,0:T(8,128)(2,1)S(1)}) custom-call(bf16[512,1152]{1,0:T(8,128)(2,1)S(1)} %shard_map.88.refs_0_, bf16[512,1152]{1,0:T(8,128)(2,1)S(1)} %shard_map.89.refs_1_, bf16[512,1152]{1,0:T(8,128)(2,1)S(1)} %collective-permute-done.20.refs_2_, bf16[512,1152]{1,0:T(8,128)(2,1)S(1)} %collective-permute-done.21.refs_3_), custom_call_target="tpu_custom_call" | custom-call | bytes 9437184 | tf_op jit(solution)/shard_map/pallas_call | solution.py:178
  75.7 0.0 collective-permute-done.27.refs_5_
  75.7 4.8 %shard_map.91.acc = f32[1152,1152]{1,0:T(8,128)S(1)} custom-call(bf16[1152,1536]{1,0:T(8,128)(2,1)S(1)} %get-tuple-element.55.x_t, bf16[256,1152]{1,0:T(8,128)(2,1)S(1)} %pad_maximum_fusion.1.refs_0_, bf16[256,1152]{1,0:T(8,128)(2,1)S(1)} %pad_maximum_fusion.2.refs_1_, bf16[256,1152]{1,0:T(8,128)(2,1)S(1)} %pad_maximum_fusion.3.refs_2_, ...), custom_call_target="tpu_custom_call" | custom-call | flops 4076863488 | bytes 12386304 | tf_op jit(solution)/shard_map/pallas_call | solution.py:233
  80.5 1.4 %collective-permute-done.28.refs_0_ = bf16[256,1152]{1,0:T(8,128)(2,1)S(1)} collective-permute-done((bf16[256,1152]{1,0:T(8,128)(2,1)S(1)}, bf16[256,1152]{1,0:T(8,128)(2,1)S(1)}, u32[]{:S(2)}, u32[]{:S(2)}) %collective-permute-start.28) | collective-permute-done | bytes 589856 | tf_op jit(solution)/shard_map/ppermute | solution.py:268
  81.8 1.1 %add_bitcast_fusion = f32[1,256,1152]{2,1,0:T(8,128)} fusion(f32[256,1152]{1,0:T(8,128)S(1)} %get-tuple-element.50, f32[256,1152]{1,0:T(8,128)S(1)} %collective-permute-done.19), kind=kLoop, calls=%fused_computation.1 | loop fusion | flops 294912 | bytes 3538944 | tf_op jit(solution)/shard_map/broadcast_in_dim | solution.py:338
  83.0 0.9 collective-permute-done.29.refs_1_
  83.8 3.1 %shard_map.92 = f32[1152,1152]{1,0:T(8,128)} custom-call(bf16[1152,512]{1,0:T(8,128)(2,1)S(1)} %get-tuple-element.54.x_t, f32[1152,1152]{1,0:T(8,128)S(1)} %shard_map.91.acc, bf16[256,1152]{1,0:T(8,128)(2,1)S(1)} %collective-permute-done.28.refs_0_, bf16[256,1152]{1,0:T(8,128)(2,1)S(1)} %collective-permute-done.29.refs_1_), custom_call_target="tpu_custom_call" | custom-call | flops 1358954496 | bytes 12976128 | tf_op jit(solution)/shard_map/pallas_call | solution.py:233
  (27 shorter events, 0.3 us)
Async XLA Ops:
  0.6 21.3 %copy-start = (bf16[1152,1152]{1,0:T(8,128)(2,1)S(1)}, bf16[1152,1152]{1,0:T(8,128)(2,1)}, u32[]{:S(2)}) copy-start(bf16[1152,1152]{1,0:T(8,128)(2,1)} %param.9) | copy-start | bytes 7962628
  0.6 8.7 %collective-permute-start.5 = (bf16[64,1152]{1,0:T(8,128)(2,1)}, bf16[64,1152]{1,0:T(8,128)(2,1)}, u32[]{:S(2)}, u32[]{:S(2)}) collective-permute-start(bf16[64,1152]{1,0:T(8,128)(2,1)} %bitcast.11), channel_id=1, source_target_pairs={{0,8},{1,17},{2,10},{3,19},{4,12},{5,21},{6,14},{7,23},{8,0},{9,25... | collective-permute-start | bytes 442376 | tf_op jit(solution)/shard_map/ppermute | solution.py:268
  3.6 17.8 %collective-permute-start = (bf16[64,1152]{1,0:T(8,128)(2,1)}, bf16[64,1152]{1,0:T(8,128)(2,1)}, u32[]{:S(2)}, u32[]{:S(2)}) collective-permute-start(bf16[64,1152]{1,0:T(8,128)(2,1)} %bitcast.12), channel_id=1, source_target_pairs={{0,2},{1,3},{2,0},{3,1},{4,6},{5,7},{6,4},{7,5},{8,10},{9,11},{10,... | collective-permute-start | bytes 442376 | tf_op jit(solution)/shard_map/ppermute | solution.py:257
  5.2 14.1 %collective-permute-start.1 = (bf16[64,1152]{1,0:T(8,128)(2,1)}, bf16[64,1152]{1,0:T(8,128)(2,1)S(1)}, u32[]{:S(2)}, u32[]{:S(2)}) collective-permute-start(bf16[64,1152]{1,0:T(8,128)(2,1)} %bitcast.13), channel_id=1, source_target_pairs={{0,4},{1,5},{2,6},{3,7},{4,0},{5,1},{6,2},{7,3},{8,12},{9,13},{10,... | collective-permute-start | bytes 442376 | tf_op jit(solution)/shard_map/ppermute | solution.py:257
  7.8 12.0 %collective-permute-start.2 = (bf16[64,1152]{1,0:T(8,128)(2,1)}, bf16[64,1152]{1,0:T(8,128)(2,1)S(1)}, u32[]{:S(2)}, u32[]{:S(2)}) collective-permute-start(bf16[64,1152]{1,0:T(8,128)(2,1)} %bitcast.14), channel_id=1, source_target_pairs={{0,6},{1,7},{2,4},{3,5},{4,2},{5,3},{6,0},{7,1},{8,14},{9,15},{10,... | collective-permute-start | bytes 442376 | tf_op jit(solution)/shard_map/ppermute | solution.py:257
  8.0 15.9 %collective-permute-start.4 = (bf16[256,1152]{1,0:T(8,128)(2,1)}, bf16[256,1152]{1,0:T(8,128)(2,1)S(1)}, u32[]{:S(2)}, u32[]{:S(2)}) collective-permute-start(bf16[256,1152]{1,0:T(8,128)(2,1)} %bitcast.9), channel_id=1, source_target_pairs={{0,1},{1,0},{2,3},{3,2},{4,5},{5,4},{6,7},{7,6},{8,9},{9,8},{10,11... | collective-permute-start | bytes 1769480 | tf_op jit(solution)/shard_map/ppermute | solution.py:260
  9.3 12.6 %copy-start.3 = (bf16[1,64,1152]{2,1,0:T(8,128)(2,1)S(1)}, bf16[1,64,1152]{2,1,0:T(8,128)(2,1)}, u32[]{:S(2)}) copy-start(bf16[1,64,1152]{2,1,0:T(8,128)(2,1)} %param.6) | copy-start | bytes 442372
  9.4 14.5 %collective-permute-start.3 = (s32[1,256]{1,0:T(1,128)}, s32[1,256]{1,0:T(1,128)S(1)}, u32[]{:S(2)}, u32[]{:S(2)}) collective-permute-start(s32[1,256]{1,0:T(1,128)} %refs_0_.1), channel_id=1, source_target_pairs={{0,1},{1,0},{2,3},{3,2},{4,5},{5,4},{6,7},{7,6},{8,9},{9,8},{10,11... | collective-permute-start | bytes 3080 | tf_op jit(solution)/shard_map/ppermute | solution.py:260
  19.4 7.5 %collective-permute-start.6 = (bf16[128,1152]{1,0:T(8,128)(2,1)S(1)}, bf16[128,1152]{1,0:T(8,128)(2,1)S(1)}, u32[]{:S(2)}, u32[]{:S(2)}) collective-permute-start(bf16[128,1152]{1,0:T(8,128)(2,1)S(1)} %pad_maximum_fusion.4.refs_0_), channel_id=1, source_target_pairs={{0,16},{1,9},{2,18},{3,11},{4,20},{5,13},{6,22},{7,15},{8,24},{9,1... | collective-permute-start | bytes 884744 | tf_op jit(solution)/shard_map/ppermute | solution.py:268
  19.8 4.2 %copy-start.1 = (bf16[1,256,1152]{2,1,0:T(8,128)(2,1)S(1)}, bf16[1,256,1152]{2,1,0:T(8,128)(2,1)}, u32[]{:S(2)}) copy-start(bf16[1,256,1152]{2,1,0:T(8,128)(2,1)} %param.7) | copy-start | bytes 1769476
  19.9 4.1 %copy-start.2 = (s32[1,256]{1,0:T(1,128)S(1)}, s32[1,256]{1,0:T(1,128)}, u32[]{:S(2)}) copy-start(s32[1,256]{1,0:T(1,128)} %refs_0_.1) | copy-start | bytes 3076
  19.9 7.0 %collective-permute-start.10 = (bf16[128,1152]{1,0:T(8,128)(2,1)S(1)}, bf16[128,1152]{1,0:T(8,128)(2,1)S(1)}, u32[]{:S(2)}, u32[]{:S(2)}) collective-permute-start(bf16[128,1152]{1,0:T(8,128)(2,1)S(1)} %pad_maximum_fusion.5), channel_id=1, source_target_pairs={{0,8},{1,17},{2,10},{3,19},{4,12},{5,21},{6,14},{7,23},{8,0},{9,25... | collective-permute-start | bytes 884744 | tf_op jit(solution)/shard_map/ppermute | solution.py:268
  21.5 8.5 %collective-permute-start.12 = (bf16[64,1152]{1,0:T(8,128)(2,1)}, bf16[64,1152]{1,0:T(8,128)(2,1)S(1)}, u32[]{:S(2)}, u32[]{:S(2)}) collective-permute-start(bf16[64,1152]{1,0:T(8,128)(2,1)} %collective-permute-done), channel_id=1, source_target_pairs={{0,8},{1,17},{2,10},{3,19},{4,12},{5,21},{6,14},{7,23},{8,0},{9,25... | collective-permute-start | bytes 442376 | tf_op jit(solution)/shard_map/ppermute | solution.py:268
  26.9 19.1 %collective-permute-start.11 = (bf16[256,1152]{1,0:T(8,128)(2,1)S(1)}, bf16[256,1152]{1,0:T(8,128)(2,1)S(1)}, u32[]{:S(2)}, u32[]{:S(2)}) collective-permute-start(bf16[256,1152]{1,0:T(8,128)(2,1)S(1)} %pad_maximum_fusion.refs_0_), channel_id=1, source_target_pairs={{0,16},{1,9},{2,18},{3,11},{4,20},{5,13},{6,22},{7,15},{8,24},{9,1... | collective-permute-start | bytes 1769480 | tf_op jit(solution)/shard_map/ppermute | solution.py:268
  30.9 15.1 %collective-permute-start.13 = (bf16[128,1152]{1,0:T(8,128)(2,1)S(1)}, bf16[128,1152]{1,0:T(8,128)(2,1)S(1)}, u32[]{:S(2)}, u32[]{:S(2)}) collective-permute-start(bf16[128,1152]{1,0:T(8,128)(2,1)S(1)} %pad_maximum_fusion.6.refs_2_), channel_id=1, source_target_pairs={{0,16},{1,9},{2,18},{3,11},{4,20},{5,13},{6,22},{7,15},{8,24},{9,1... | collective-permute-start | bytes 884744 | tf_op jit(solution)/shard_map/ppermute | solution.py:268
  34.0 7.6 %collective-permute-start.7 = (bf16[64,1152]{1,0:T(8,128)(2,1)S(1)}, bf16[64,1152]{1,0:T(8,128)(2,1)S(1)}, u32[]{:S(2)}, u32[]{:S(2)}) collective-permute-start(bf16[64,1152]{1,0:T(8,128)(2,1)S(1)} %get-tuple-element.37), channel_id=1, source_target_pairs={{0,2},{1,3},{2,0},{3,1},{4,6},{5,7},{6,4},{7,5},{8,10},{9,11},{10,... | collective-permute-start | bytes 442376 | tf_op jit(solution)/shard_map/ppermute | solution.py:257
  34.0 12.0 %collective-permute-start.8 = (bf16[64,1152]{1,0:T(8,128)(2,1)S(1)}, bf16[64,1152]{1,0:T(8,128)(2,1)S(1)}, u32[]{:S(2)}, u32[]{:S(2)}) collective-permute-start(bf16[64,1152]{1,0:T(8,128)(2,1)S(1)} %get-tuple-element.38), channel_id=1, source_target_pairs={{0,4},{1,5},{2,6},{3,7},{4,0},{5,1},{6,2},{7,3},{8,12},{9,13},{10,... | collective-permute-start | bytes 442376 | tf_op jit(solution)/shard_map/ppermute | solution.py:257
  35.2 10.8 %collective-permute-start.9 = (bf16[64,1152]{1,0:T(8,128)(2,1)S(1)}, bf16[64,1152]{1,0:T(8,128)(2,1)S(1)}, u32[]{:S(2)}, u32[]{:S(2)}) collective-permute-start(bf16[64,1152]{1,0:T(8,128)(2,1)S(1)} %get-tuple-element.39), channel_id=1, source_target_pairs={{0,6},{1,7},{2,4},{3,5},{4,2},{5,3},{6,0},{7,1},{8,14},{9,15},{10,... | collective-permute-start | bytes 442376 | tf_op jit(solution)/shard_map/ppermute | solution.py:257
  46.3 5.7 %collective-permute-start.17 = (bf16[64,1152]{1,0:T(8,128)(2,1)S(1)}, bf16[64,1152]{1,0:T(8,128)(2,1)S(1)}, u32[]{:S(2)}, u32[]{:S(2)}) collective-permute-start(bf16[64,1152]{1,0:T(8,128)(2,1)S(1)} %shard_map.86), channel_id=1, source_target_pairs={{0,8},{1,17},{2,10},{3,19},{4,12},{5,21},{6,14},{7,23},{8,0},{9,25... | collective-permute-start | bytes 442376 | tf_op jit(solution)/shard_map/ppermute | solution.py:268
  47.3 6.6 %collective-permute-start.16 = (bf16[64,1152]{1,0:T(8,128)(2,1)S(1)}, bf16[64,1152]{1,0:T(8,128)(2,1)S(1)}, u32[]{:S(2)}, u32[]{:S(2)}) collective-permute-start(bf16[64,1152]{1,0:T(8,128)(2,1)S(1)} %shard_map.86), channel_id=1, source_target_pairs={{0,2},{1,3},{2,0},{3,1},{4,6},{5,7},{6,4},{7,5},{8,10},{9,11},{10,... | collective-permute-start | bytes 442376 | tf_op jit(solution)/shard_map/ppermute | solution.py:257
  49.6 12.3 %collective-permute-start.14 = (bf16[64,1152]{1,0:T(8,128)(2,1)S(1)}, bf16[64,1152]{1,0:T(8,128)(2,1)S(1)}, u32[]{:S(2)}, u32[]{:S(2)}) collective-permute-start(bf16[64,1152]{1,0:T(8,128)(2,1)S(1)} %shard_map.86), channel_id=1, source_target_pairs={{0,4},{1,5},{2,6},{3,7},{4,0},{5,1},{6,2},{7,3},{8,12},{9,13},{10,... | collective-permute-start | bytes 442376 | tf_op jit(solution)/shard_map/ppermute | solution.py:257
  50.1 11.8 %collective-permute-start.15 = (bf16[64,1152]{1,0:T(8,128)(2,1)S(1)}, bf16[64,1152]{1,0:T(8,128)(2,1)S(1)}, u32[]{:S(2)}, u32[]{:S(2)}) collective-permute-start(bf16[64,1152]{1,0:T(8,128)(2,1)S(1)} %shard_map.86), channel_id=1, source_target_pairs={{0,6},{1,7},{2,4},{3,5},{4,2},{5,3},{6,0},{7,1},{8,14},{9,15},{10,... | collective-permute-start | bytes 442376 | tf_op jit(solution)/shard_map/ppermute | solution.py:257
  52.0 11.5 %collective-permute-start.22 = (bf16[128,1152]{1,0:T(8,128)(2,1)S(1)}, bf16[128,1152]{1,0:T(8,128)(2,1)S(1)}, u32[]{:S(2)}, u32[]{:S(2)}) collective-permute-start(bf16[128,1152]{1,0:T(8,128)(2,1)S(1)} %pad_maximum_fusion.8), channel_id=1, source_target_pairs={{0,16},{1,9},{2,18},{3,11},{4,20},{5,13},{6,22},{7,15},{8,24},{9,1... | collective-permute-start | bytes 884744 | tf_op jit(solution)/shard_map/ppermute | solution.py:268
  53.9 9.6 %collective-permute-start.23 = (bf16[64,1152]{1,0:T(8,128)(2,1)S(1)}, bf16[64,1152]{1,0:T(8,128)(2,1)S(1)}, u32[]{:S(2)}, u32[]{:S(2)}) collective-permute-start(bf16[64,1152]{1,0:T(8,128)(2,1)S(1)} %collective-permute-done.16), channel_id=1, source_target_pairs={{0,8},{1,17},{2,10},{3,19},{4,12},{5,21},{6,14},{7,23},{8,0},{9,25... | collective-permute-start | bytes 442376 | tf_op jit(solution)/shard_map/ppermute | solution.py:268
  61.9 8.7 %collective-permute-start.18 = (bf16[128,1152]{1,0:T(8,128)(2,1)S(1)}, bf16[128,1152]{1,0:T(8,128)(2,1)S(1)}, u32[]{:S(2)}, u32[]{:S(2)}) collective-permute-start(bf16[128,1152]{1,0:T(8,128)(2,1)S(1)} %pad_maximum_fusion.7), channel_id=1, source_target_pairs={{0,8},{1,17},{2,10},{3,19},{4,12},{5,21},{6,14},{7,23},{8,0},{9,25... | collective-permute-start | bytes 884744 | tf_op jit(solution)/shard_map/ppermute | solution.py:268
  62.9 9.0 %collective-permute-start.21 = (bf16[512,1152]{1,0:T(8,128)(2,1)S(1)}, bf16[512,1152]{1,0:T(8,128)(2,1)S(1)}, u32[]{:S(2)}, u32[]{:S(2)}) collective-permute-start(bf16[512,1152]{1,0:T(8,128)(2,1)S(1)} %shard_map.89.refs_1_), channel_id=1, source_target_pairs={{0,1},{1,0},{2,3},{3,2},{4,5},{5,4},{6,7},{7,6},{8,9},{9,8},{10,11... | collective-permute-start | bytes 3538952 | tf_op jit(solution)/shard_map/ppermute | solution.py:260
  62.9 11.4 %collective-permute-start.20 = (bf16[512,1152]{1,0:T(8,128)(2,1)S(1)}, bf16[512,1152]{1,0:T(8,128)(2,1)S(1)}, u32[]{:S(2)}, u32[]{:S(2)}) collective-permute-start(bf16[512,1152]{1,0:T(8,128)(2,1)S(1)} %shard_map.88.refs_0_), channel_id=1, source_target_pairs={{0,1},{1,0},{2,3},{3,2},{4,5},{5,4},{6,7},{7,6},{8,9},{9,8},{10,11... | collective-permute-start | bytes 3538952 | tf_op jit(solution)/shard_map/ppermute | solution.py:260
  63.5 8.4 %collective-permute-start.25 = (bf16[256,1152]{1,0:T(8,128)(2,1)S(1)}, bf16[256,1152]{1,0:T(8,128)(2,1)S(1)}, u32[]{:S(2)}, u32[]{:S(2)}) collective-permute-start(bf16[256,1152]{1,0:T(8,128)(2,1)S(1)} %pad_maximum_fusion.1.refs_0_), channel_id=1, source_target_pairs={{0,1},{1,0},{2,3},{3,2},{4,5},{5,4},{6,7},{7,6},{8,9},{9,8},{10,11... | collective-permute-start | bytes 1769480 | tf_op jit(solution)/shard_map/ppermute | solution.py:260
  63.6 7.6 %collective-permute-start.24 = (bf16[128,1152]{1,0:T(8,128)(2,1)S(1)}, bf16[128,1152]{1,0:T(8,128)(2,1)S(1)}, u32[]{:S(2)}, u32[]{:S(2)}) collective-permute-start(bf16[128,1152]{1,0:T(8,128)(2,1)S(1)} %pad_maximum_fusion.9), channel_id=1, source_target_pairs={{0,16},{1,9},{2,18},{3,11},{4,20},{5,13},{6,22},{7,15},{8,24},{9,1... | collective-permute-start | bytes 884744 | tf_op jit(solution)/shard_map/ppermute | solution.py:268
  71.1 10.7 %collective-permute-start.19 = (f32[256,1152]{1,0:T(8,128)S(1)}, f32[256,1152]{1,0:T(8,128)S(1)}, u32[]{:S(2)}, u32[]{:S(2)}) collective-permute-start(f32[256,1152]{1,0:T(8,128)S(1)} %get-tuple-element.51), channel_id=1, source_target_pairs={{0,1},{1,0},{2,3},{3,2},{4,5},{5,4},{6,7},{7,6},{8,9},{9,8},{10,11... | collective-permute-start | bytes 3538952 | tf_op jit(solution)/shard_map/ppermute | solution.py:260
  71.3 4.4 %collective-permute-start.26 = (bf16[256,1152]{1,0:T(8,128)(2,1)S(1)}, bf16[256,1152]{1,0:T(8,128)(2,1)S(1)}, u32[]{:S(2)}, u32[]{:S(2)}) collective-permute-start(bf16[256,1152]{1,0:T(8,128)(2,1)S(1)} %pad_maximum_fusion.2.refs_1_), channel_id=1, source_target_pairs={{0,1},{1,0},{2,3},{3,2},{4,5},{5,4},{6,7},{7,6},{8,9},{9,8},{10,11... | collective-permute-start | bytes 1769480 | tf_op jit(solution)/shard_map/ppermute | solution.py:260
  71.8 3.8 %collective-permute-start.27 = (bf16[256,1152]{1,0:T(8,128)(2,1)S(1)}, bf16[256,1152]{1,0:T(8,128)(2,1)S(1)}, u32[]{:S(2)}, u32[]{:S(2)}) collective-permute-start(bf16[256,1152]{1,0:T(8,128)(2,1)S(1)} %pad_maximum_fusion.3.refs_2_), channel_id=1, source_target_pairs={{0,1},{1,0},{2,3},{3,2},{4,5},{5,4},{6,7},{7,6},{8,9},{9,8},{10,11... | collective-permute-start | bytes 1769480 | tf_op jit(solution)/shard_map/ppermute | solution.py:260
  71.9 9.9 %collective-permute-start.28 = (bf16[256,1152]{1,0:T(8,128)(2,1)S(1)}, bf16[256,1152]{1,0:T(8,128)(2,1)S(1)}, u32[]{:S(2)}, u32[]{:S(2)}) collective-permute-start(bf16[256,1152]{1,0:T(8,128)(2,1)S(1)} %pad_maximum_fusion.3.refs_2_), channel_id=1, source_target_pairs={{0,16},{1,9},{2,18},{3,11},{4,20},{5,13},{6,22},{7,15},{8,24},{9,1... | collective-permute-start | bytes 1769480 | tf_op jit(solution)/shard_map/ppermute | solution.py:268
  81.8 2.0 %collective-permute-start.29 = (bf16[256,1152]{1,0:T(8,128)(2,1)S(1)}, bf16[256,1152]{1,0:T(8,128)(2,1)S(1)}, u32[]{:S(2)}, u32[]{:S(2)}) collective-permute-start(bf16[256,1152]{1,0:T(8,128)(2,1)S(1)} %collective-permute-done.28.refs_0_), channel_id=1, source_target_pairs={{0,1},{1,0},{2,3},{3,2},{4,5},{5,4},{6,7},{7,6},{8,9},{9,8},{10,11... | collective-permute-start | bytes 1769480 | tf_op jit(solution)/shard_map/ppermute | solution.py:260

commit v7 on v6

--- a/solution.py
+++ b/solution.py
@@ -25,7 +25,7 @@
     scale, offset = both[0:1, 0:1], both[8:9, 0:1]
     labels, captions, refs = refs[:2], refs[2:4], refs[4:]
     own, unit_own, inv_own, unit, dlogit = refs[:5]
-    sent, (caps, sems) = refs[5:-2], refs[-2:]
+    sent, caps, sems = refs[5:]
     n_img, n_cap = embed.shape[0] // nz, captions[0].shape[0]
     copies = []
     for i in range(2):
@@ -54,8 +54,10 @@
     dlogit[...] = d
     part = scale * dot(d, caps[...])
     own[...] = part[:n_img]
-    for k in range(1, nz):
-        sent[k - 1][...] = part[k * n_img : (k + 1) * n_img].astype(BF16)
+    for k in range(nz):
+        row = pl.multiple_of(((index // 2) ^ k) * n_img, n_img)
+        block = part[k * n_img : (k + 1) * n_img]
+        sent[pl.ds(row, n_img), :] = block.astype(BF16)
 
 
 def scores(nz, both, embed, labels, captions):
@@ -70,7 +72,8 @@
         jax.ShapeDtypeStruct((n_img, 128), F32),
         jax.ShapeDtypeStruct((images, depth), BF16),
         jax.ShapeDtypeStruct((images, caps), BF16),
-    ] + [jax.ShapeDtypeStruct((n_img, depth), BF16)] * (nz - 1)
+        jax.ShapeDtypeStruct((images, depth), BF16),
+    ]
     return pl.pallas_call(
         functools.partial(score_kernel, nz),
         out_shape=outs,
@@ -139,11 +142,14 @@
     )(both, dlogit, unit)
 
 
-def embed_grad_kernel(own, unit, inv_norm, *refs):
-    back, out = refs[:-1], refs[-1]
+def embed_grad_kernel(own, unit, inv_norm, back, out):
+    n_img = own.shape[0]
+    nz = back.shape[0] // n_img
+    z = lax.axis_index("blk") // 2
     total = own[...]
-    for v in back:
-        total = total + v[...].astype(F32)
+    for k in range(1, nz):
+        row = pl.multiple_of((z ^ k) * n_img, n_img)
+        total = total + back[pl.ds(row, n_img), :].astype(F32)
     u = unit[...]
     radial = jnp.sum(u * total, axis=1, keepdims=True)
     out[...] = ((total - u * radial) * inv_norm[:, :1]).astype(BF16)
@@ -154,27 +160,29 @@
     return pl.pallas_call(
         embed_grad_kernel,
         out_shape=jax.ShapeDtypeStruct(own.shape, BF16),
-        in_specs=[vmem] * (3 + len(back)),
+        in_specs=[vmem] * 4,
         out_specs=vmem,
-        compiler_params=pltpu.CompilerParams(vmem_limit_bytes=8 * 2**20),
+        compiler_params=pltpu.CompilerParams(vmem_limit_bytes=12 * 2**20),
         cost_estimate=pl.CostEstimate(
             flops=8 * own.size, bytes_accessed=12 * own.size, transcendentals=0
         ),
-    )(own, unit, inv_norm, *back)
+    )(own, unit, inv_norm, back)
 
 
 def turn_kernel(plan, *refs):
     ins, outs = refs[: -len(plan)], refs[-len(plan) :]
-    for out, runs in zip(outs, plan):
+    for out, pieces in zip(outs, plan):
         col = 0
-        for i, at, size in runs:
-            out[:, col : col + size] = ins[i][at : at + size, :].T
-            col += size
+        for runs in pieces:
+            rows = [ins[i][at : at + size, :] for i, at, size in runs]
+            rows = jnp.concatenate(rows)
+            out[:, col : col + rows.shape[0]] = rows.T
+            col += rows.shape[0]
 
 
 def turned(xs, plan):
     depth = xs[0].shape[1]
-    images = [sum(size for _, _, size in runs) for runs in plan]
+    images = [sum(size for runs in pieces for _, _, size in runs) for pieces in plan]
     return pl.pallas_call(
         functools.partial(turn_kernel, plan),
         out_shape=[jax.ShapeDtypeStruct((depth, n), BF16) for n in images],
@@ -194,13 +202,14 @@
         at += g.shape[0]
 
 
-def early_kernel(n, x_t, *refs):
-    gs, (out, stacked) = refs[:-2], refs[-2:]
+def early_kernel(n, has_acc, x_t, *refs):
+    gs, (out, stacked) = refs[has_acc:-2], refs[-2:]
     stack(stacked, gs)
     rows = out.shape[0] // n
     for i in range(n):
         here = slice(i * rows, (i + 1) * rows)
-        out[here, :] = dot(x_t[here, :], stacked[...])
+        total = dot(x_t[here, :], stacked[...])
+        out[here, :] = refs[0][here, :] + total if has_acc else total
 
 
 def late_kernel(factor, x_t, acc, *refs):
@@ -217,19 +226,19 @@
         copy.wait()
 
 
-def weight_sum(acc, x_t, gs, factor):
+def weight_sum(acc, x_t, gs, factor=None):
     depth, images = x_t.shape
     n = 3
-    early = acc is None
+    early, has_acc = factor is None, int(acc is not None)
     vmem = pl.BlockSpec(memory_space=pltpu.VMEM)
     scratch = [pltpu.VMEM((images, depth), BF16)]
     if early:
-        kernel = functools.partial(early_kernel, n)
+        kernel = functools.partial(early_kernel, n, has_acc)
     else:
         kernel = functools.partial(late_kernel, factor)
         scratch.append(pltpu.VMEM((n, depth // n, depth), F32))
         scratch.append(pltpu.SemaphoreType.DMA((n,)))
-    operands = [x_t] + ([] if early else [acc]) + gs
+    operands = [x_t] + [acc] * has_acc + gs
     return pl.pallas_call(
         kernel,
         out_shape=jax.ShapeDtypeStruct((depth, depth), F32),
@@ -239,7 +248,7 @@
         compiler_params=pltpu.CompilerParams(vmem_limit_bytes=24 * 2**20),
         cost_estimate=pl.CostEstimate(
             flops=2 * images * depth * depth,
-            bytes_accessed=4 * images * depth + 4 * depth * depth * (2 - early),
+            bytes_accessed=4 * images * depth + 4 * depth * depth * (1 + has_acc),
             transcendentals=0,
         ),
     )(*operands)
@@ -276,64 +285,79 @@
 
     half = nz // 2
     xs = [x] + [along_z(x, k) for k in range(1, nz)]
-    x_near, x_far = jnp.concatenate(xs[1:half]), jnp.concatenate(xs[half:])
-    x_own = over_d(x, step_d(x, 0))
-    x_near_first = step_d(x_near, 0)
-    x_far_first = step_d(x_far, 0)
-    embed = dot(jnp.concatenate(xs), weight)
+    x_own = over_d(x, step_d(after(x, xs[1]), 0))
+    x_rest = jnp.concatenate(xs[1:])
+    x_rest_first = step_d(x_rest, 0)
+    embed = dot(joined(xs), weight)
     row = lax.broadcasted_iota(jnp.int32, (16, 128), 0)
     both = jnp.where(row < 8, scale, offset)
-    own, u, inv_norm, unit, dlogit, *sent = scores(
+    own, u, inv_norm, unit, dlogit, sent = scores(
         nz,
         both,
         embed,
         [labels, swap(labels)],
         [captions, swap(captions)],
     )
-    sent = after(sent, x_own)
-    back = [along_z(v, k + 1) for k, v in enumerate(sent)]
-
-    x_near = over_d(x_near, after(x_near_first, sent))
-    x_far = over_d(x_far, after(x_far_first, sent))
-    back = after(back, x_far, x_near)
+    x_rest = over_d(x_rest, after(x_rest_first, sent))
+    adjoint, adjoint_other = caption_sums(both, after(dlogit, sent), unit)
+    adjoint_other = swap(adjoint_other)
+    adjoint = adjoint + adjoint_other
+    chips = [list(range(c, nb, 2)) for c in range(2)]
+    sent = after(sent, x_own, x_rest[0])
+    back = lax.all_to_all(sent, "blk", 0, 0, axis_index_groups=chips, tiled=True)
+    back = after(back, x_rest, adjoint_other)
+    small = nd * nb * n_img <= 2048
+    if small:
+        x_all = joined(x_own + x_rest)
+        x_other = swap(after(x_all, back))
     ge = embed_grad(own, u, inv_norm, back)
     grad_features = dot(ge, weight, LAST)
 
     near = [along_z(ge, k) for k in range(1, half)]
     own_first = step_d(ge, 0)
     far = [along_z(ge, k) for k in range(half, nz)]
-
     g_own = over_d(ge, own_first)
-    near = after(jnp.concatenate(near), g_own[0])
+    near = after(jnp.concatenate(near), g_own[0], g_own[0])
     near_first = step_d(near, 0)
     g_near = over_d(near, near_first)
-    far = after(jnp.concatenate(far), near)
+    far = after(jnp.concatenate(far), near_first, g_own[1])
     far_first = step_d(far, 0)
-    dlogit = after(dlogit, far_first)
-    adjoint, adjoint_other = caption_sums(both, dlogit, unit)
-    adjoint = adjoint + swap(adjoint_other)
-    if nd * nb * n_img <= 2048:
-        x_all = [joined(x_own + x_near), joined(x_far)]
-        x_all += [swap(after(v, near)) for v in x_all]
-        n = n_img * nd
-        plan = [[], []]
-        for core in (0, 2):
-            plan[0] += [(core, 0, n), (core, n, n), (core + 1, 0, n)]
-            plan[1] += [(core + 1, n, n)]
-        x_early, x_late = turned(x_all, plan)
-        g_own = jnp.concatenate(g_own)
+    sizes = [n_img, n_img * (half - 1), n_img * half]
+    n_rest = sizes[1] + sizes[2]
+    per = nd // 2
+    if small:
+        plan = [[], [], []]
+        for core in range(2):
+            rest = [n_img * nd + i * n_rest for i in range(nd)]
+            far_runs = [(core, at + sizes[1], sizes[2]) for at in rest]
+            plan[0] += [[(core, 0, n_img * nd)]]
+            plan[1] += [[(core, at, sizes[1]) for at in rest], far_runs[:per]]
+            plan[2] += [far_runs[per:]]
+        x_first, x_mid, x_late = turned([x_all, x_other], plan)
+        g_own, g_near = jnp.concatenate(g_own), jnp.concatenate(g_near)
         own_swapped = swap(g_own)
-        g_far = over_d(far, far_first, own_swapped)
-        early = [g_own, jnp.concatenate(g_near), g_far[0]]
-        others = [own_swapped, swap(early[1]), swap(after(early[2], g_near[1]))]
-        acc = weight_sum(None, x_early, early + others, 1.0)
-        late = after(g_far[1], acc)
+        acc = weight_sum(None, x_first, [g_own, own_swapped])
+        near_swapped = swap(g_near)
+        g_far = over_d(far, far_first, )
+        mid = [g_near, g_far[0], near_swapped, swap(g_far[0])]
+        before_late = (acc, grad_features)
+        acc = weight_sum(acc, x_mid, mid)
+        late = after(g_far[1], before_late, adjoint)
         grad_weight = weight_sum(acc, x_late, [late, swap(late)], 1.0 / nd)
     else:
         g_far = over_d(far, far_first)
         grad_weight = 0.0
-        for v, g in zip(x_own + x_near + x_far, g_own + g_near + g_far):
+        for v, g in zip(x_own, g_own):
             grad_weight = grad_weight + dot(v, g, FIRST)
+        for v, g, h in zip(x_rest, g_near, g_far):
+            for i in range(per):
+                g_part = [
+                    g[i * sizes[1] : (i + 1) * sizes[1]],
+                    h[i * sizes[2] : (i + 1) * sizes[2]],
+                ]
+                grad_weight = grad_weight + dot(
+                    v[i * n_rest : (i + 1) * n_rest], jnp.concatenate(g_part), FIRST
+                )
         grad_weight = (grad_weight + swap(grad_weight)) / nd
     return (grad_features[None], adjoint[None], grad_weight)
 

time: 87.4 us -> 100 us (1.14)
  local copies, waits for them, and re-layouts: 0.1 us -> 9.56 us
  Pallas kernels: 11.6 us -> 15.8 us
  starting transfers between devices: 33.1 us -> 29.2 us
  waiting for transfers between devices: 33 us -> 36.9 us
    unnamed x8 -> x52, local copies, waits for them, and re-layouts: 0.03 us -> 9.49 us
    ppermute x12 -> x10, waiting for transfers between devices: 8.21 us -> 14.4 us  [step_d(): return lax.ppermute(v, ('dp', 'blk'), perm)]
    ppermute x9 -> x6, waiting for transfers between devices: 23.9 us -> 17.8 us  [along_z(): return lax.ppermute(v, 'blk', [(i, i ^ 2 * k) for i in range(nb)])]
    all_to_all x0 -> x1, starting transfers between devices: none -> 5.76 us  [on_device(): lax.all_to_all(sent, 'blk', 0, 0, axis_index_groups=chips, tiled=True)]
    all_to_all x0 -> x1, waiting for transfers between devices: none -> 4.79 us  [on_device(): lax.all_to_all(sent, 'blk', 0, 0, axis_index_groups=chips, tiled=True)]
    ppermute x12 -> x10, starting transfers between devices: 17.8 us -> 13.2 us  [step_d(): return lax.ppermute(v, ('dp', 'blk'), perm)]
    ppermute x9 -> x6, starting transfers between devices: 13.4 us -> 9.17 us  [along_z(): return lax.ppermute(v, 'blk', [(i, i ^ 2 * k) for i in range(nb)])]
    add x0 -> x1, other arithmetic: none -> 2.6 us  [on_device(): adjoint = adjoint + adjoint_other]
  transfers between devices with their start and end apart: 30 -> 25, of which waited for: 9 -> 10; matrix products, arithmetic and copies ran while one was open for 8% -> 6% of each run, Pallas kernels for 10% -> 13%
where the time goes in v7:
time: 100 us; the launch traced here: 99.6 us
  waiting for transfers between devices  36.9 us (37%)
  starting transfers between devices  29.2 us (29%)
  Pallas kernels  15.8 us (16%)
  local copies, waits for them, and re-layouts  9.56 us (10%)
  other arithmetic  2.94 us (3%)
  matrix products  2.65 us (3%)
  between operations  2.44 us (2%)
    ppermute x6, waiting for transfers between devices, along_z(): return lax.ppermute(v, 'blk', [(i, i ^ 2 * k) for i in range(nb)])  17.8 us
    ppermute x10, waiting for transfers between devices, step_d(): return lax.ppermute(v, ('dp', 'blk'), perm)  14.4 us
    ppermute x10, starting transfers between devices, step_d(): return lax.ppermute(v, ('dp', 'blk'), perm)  13.2 us
    unnamed x52, local copies, waits for them, and re-layouts  9.49 us
    ppermute x6, starting transfers between devices, along_z(): return lax.ppermute(v, 'blk', [(i, i ^ 2 * k) for i in range(nb)])  9.17 us
    pallas_call x3, Pallas kernels, weight_sum(): pl.pallas_call(kernel, out_shape=jax.ShapeDtypeStruct((depth, depth), F32...  8.02 us
    all_to_all x1, starting transfers between devices, on_device(): lax.all_to_all(sent, 'blk', 0, 0, axis_index_groups=chips, tiled=True)  5.76 us
    all_to_all x1, waiting for transfers between devices, on_device(): lax.all_to_all(sent, 'blk', 0, 0, axis_index_groups=chips, tiled=True)  4.79 us
  transfers between devices with their start and end apart: 25, of which 10 were waited for; matrix products, arithmetic and copies ran while one was open for 6% of the time, Pallas kernels for 13%

profile of v7, /device:TPU:0, one launch (start us, length us, event | category | flops | bytes accessed | tf_op | source)
XLA Modules:
  0.0 99.6 jit_solution(12632287925017254281)
XLA Ops:
  0.6 0.0 copy-start
  0.6 3.1 %collective-permute-start = (bf16[64,1152]{1,0:T(8,128)(2,1)}, bf16[64,1152]{1,0:T(8,128)(2,1)S(1)}, u32[]{:S(2)}, u32[]{:S(2)}) collective-permute-start(bf16[64,1152]{1,0:T(8,128)(2,1)} %bitcast.10), channel_id=1, source_target_pairs={{0,2},{1,3},{2,0},{3,1},{4,6},{5,7},{6,4},{7,5},{8,10},{9,11},{10,... | collective-permute-start | bytes 442376 | tf_op jit(solution)/shard_map/ppermute | solution.py:266
  3.7 2.6 %collective-permute-start.1 = (bf16[64,1152]{1,0:T(8,128)(2,1)}, bf16[64,1152]{1,0:T(8,128)(2,1)S(1)}, u32[]{:S(2)}, u32[]{:S(2)}) collective-permute-start(bf16[64,1152]{1,0:T(8,128)(2,1)} %bitcast.11), channel_id=1, source_target_pairs={{0,4},{1,5},{2,6},{3,7},{4,0},{5,1},{6,2},{7,3},{8,12},{9,13},{10,... | collective-permute-start | bytes 442376 | tf_op jit(solution)/shard_map/ppermute | solution.py:266
  6.3 0.5 collective-permute-start.4
  8.1 1.7 %collective-permute-done.refs_1_ = bf16[64,1152]{1,0:T(8,128)(2,1)S(1)} collective-permute-done((bf16[64,1152]{1,0:T(8,128)(2,1)}, bf16[64,1152]{1,0:T(8,128)(2,1)S(1)}, u32[]{:S(2)}, u32[]{:S(2)}) %collective-permute-start) | collective-permute-done | bytes 147488 | tf_op jit(solution)/shard_map/ppermute | solution.py:266
  9.8 1.7 %collective-permute-start.5 = (bf16[64,1152]{1,0:T(8,128)(2,1)}, bf16[64,1152]{1,0:T(8,128)(2,1)S(1)}, u32[]{:S(2)}, u32[]{:S(2)}) collective-permute-start(bf16[64,1152]{1,0:T(8,128)(2,1)} %bitcast.13), channel_id=1, source_target_pairs={{0,8},{1,17},{2,10},{3,19},{4,12},{5,21},{6,14},{7,23},{8,0},{9,25... | collective-permute-start | bytes 442376 | tf_op jit(solution)/shard_map/ppermute | solution.py:277
  11.5 6.4 %collective-permute-done.1.refs_2_ = bf16[64,1152]{1,0:T(8,128)(2,1)S(1)} collective-permute-done((bf16[64,1152]{1,0:T(8,128)(2,1)}, bf16[64,1152]{1,0:T(8,128)(2,1)S(1)}, u32[]{:S(2)}, u32[]{:S(2)}) %collective-permute-start.1) | collective-permute-done | bytes 147488 | tf_op jit(solution)/shard_map/ppermute | solution.py:266
  18.0 1.6 %collective-permute-start.7 = (bf16[192,1152]{1,0:T(8,128)(2,1)S(1)}, bf16[192,1152]{1,0:T(8,128)(2,1)S(1)}, u32[]{:S(2)}, u32[]{:S(2)}) collective-permute-start(bf16[192,1152]{1,0:T(8,128)(2,1)S(1)} %pad_maximum_fusion.4), channel_id=1, source_target_pairs={{0,8},{1,17},{2,10},{3,19},{4,12},{5,21},{6,14},{7,23},{8,0},{9,25... | collective-permute-start | bytes 1327112 | tf_op jit(solution)/shard_map/ppermute | solution.py:277
  19.5 0.9 copy-done.13
  20.5 0.0 copy-start.14
  20.5 0.0 copy-start.16
  20.5 0.0 copy-start.25
  20.5 1.0 %fusion.embed = f32[256,1152]{1,0:T(8,128)S(1)} fusion(bf16[256,1152]{1,0:T(8,128)(2,1)S(1)} %shard_map.85, bf16[1152,1152]{1,0:T(8,128)(2,1)S(1)} %copy-done), kind=kOutput, calls=%fused_computation.10 | convolution fusion | flops 679477248 | bytes 4423680 | tf_op jit(solution)/shard_map/dot_general | solution.py:17
  21.6 0.0 collective-permute-done.5
  21.6 0.0 copy-start.9
  21.7 1.6 %collective-permute-start.6 = (bf16[128,1152]{1,0:T(8,128)(2,1)S(1)}, bf16[128,1152]{1,0:T(8,128)(2,1)S(1)}, u32[]{:S(2)}, u32[]{:S(2)}) collective-permute-start(bf16[128,1152]{1,0:T(8,128)(2,1)S(1)} %pad_maximum_fusion.5.refs_0_), channel_id=1, source_target_pairs={{0,16},{1,9},{2,18},{3,11},{4,20},{5,13},{6,22},{7,15},{8,24},{9,1... | collective-permute-start | bytes 884744 | tf_op jit(solution)/shard_map/ppermute | solution.py:277
  23.3 0.1 iota.7.both
  23.3 2.3 %shard_map.86 = (f32[64,1152]{1,0:T(8,128)S(1)}, f32[64,1152]{1,0:T(8,128)S(1)}, f32[64,128]{1,0:T(8,128)S(1)}, bf16[256,1152]{1,0:T(8,128)(2,1)S(1)}, bf16[256,...) custom-call(f32[16,128]{1,0:T(8,128)S(1)} %iota.7.both, f32[256,1152]{1,0:T(8,128)S(1)} %fusion.embed, ...), custom_call_target="tpu_custom_call" | custom-call | flops 603979776 | bytes 4718592 | tf_op jit(solution)/shard_map/pallas_call | solution.py:77
  25.7 0.7 copy-done.21
  26.4 1.6 %shard_map.87 = (f32[256,1152]{1,0:T(8,128)S(1)}, f32[256,1152]{1,0:T(8,128)}) custom-call(f32[16,128]{1,0:T(8,128)S(1)} %iota.7.both, bf16[256,512]{1,0:T(8,128)(2,1)S(1)} %get-tuple-element.31.dlogit, bf16[256,1152]{1,0:T(8,128)(2,1)S(1)} %get-tuple-element.32.unit), custom_call_target="tpu_custom_call" | custom-call | flops 301989888 | bytes 3211264 | tf_op jit(solution)/shard_map/pallas_call | solution.py:129
  27.9 1.1 %copy-done.11 = f32[256,1152]{1,0:T(8,128)} copy-done((f32[256,1152]{1,0:T(8,128)}, f32[256,1152]{1,0:T(8,128)S(1)}, u32[]{:S(2)}) %copy-start.11) | copy-done | bytes 1179672
  29.0 0.3 collective-permute-done.7
  29.4 0.1 pad_maximum_fusion.refs_2_
  29.4 0.6 collective-permute-start.8
  30.0 0.7 copy-done.17
  30.8 5.8 %all-to-all-start = ((bf16[4,64,1152]{2,1,0:T(8,128)(2,1)}), bf16[4,64,1152]{2,1,0:T(8,128)(2,1)}, u32[]{:S(2)}, u32[]{:S(2)}) async-start(bf16[4,64,1152]{2,1,0:T(8,128)(2,1)} %bitcast.16), calls=%async_computation | async-start | bytes 1179648 | tf_op jit(solution)/shard_map/all_to_all | solution.py:307
  36.5 6.1 %collective-permute-done.8.refs_3_ = bf16[384,1152]{1,0:T(8,128)(2,1)} collective-permute-done((bf16[384,1152]{1,0:T(8,128)(2,1)S(1)}, bf16[384,1152]{1,0:T(8,128)(2,1)}, u32[]{:S(2)}, u32[]{:S(2)}) %collective-permute-start.8) | collective-permute-done | bytes 884768 | tf_op jit(solution)/shard_map/ppermute | solution.py:277
  42.7 1.0 copy-done.10
  43.6 1.0 copy-done.18
  44.6 1.3 %shard_map.89.refs_0_ = bf16[1024,1152]{1,0:T(8,128)(2,1)S(1)} custom-call(bf16[128,1152]{1,0:T(8,128)(2,1)S(1)} %copy-done.10, bf16[128,1152]{1,0:T(8,128)(2,1)S(1)} %copy-done.18, bf16[384,1152]{1,0:T(8,128)(2,1)S(1)} %pad_maximum_fusion.refs_2_, bf16[384,1152]{1,0:T(8,128)(2,1)} %collective-permute-done.8.refs_3_), custom_call_target="tpu_custom_call" | custom-call | bytes 4718592 | tf_op jit(solution)/shard_map/pallas_call | solution.py:106
  45.9 0.0 copy-start.1
  45.9 1.4 %copy-done.1 = bf16[1024,1152]{1,0:T(8,128)(2,1)} copy-done((bf16[1024,1152]{1,0:T(8,128)(2,1)}, bf16[1024,1152]{1,0:T(8,128)(2,1)S(1)}, u32[]{:S(2)}) %copy-start.1) | copy-done | bytes 2359320
  47.3 4.8 %all-to-all-done = bf16[4,64,1152]{2,1,0:T(8,128)(2,1)} async-done(((bf16[4,64,1152]{2,1,0:T(8,128)(2,1)}), bf16[4,64,1152]{2,1,0:T(8,128)(2,1)}, u32[]{:S(2)}, u32[]{:S(2)}) %all-to-all-start) | async-done | bytes 589856 | tf_op jit(solution)/shard_map/all_to_all | solution.py:307
  52.1 0.0 collective-permute-done.9
  52.1 0.0 collective-permute-start.10
  52.1 1.0 copy-done.20
  53.1 1.0 copy-done.22
  54.1 0.8 copy-done.24
  54.8 1.2 %shard_map.88 = bf16[64,1152]{1,0:T(8,128)(2,1)S(1)} custom-call(f32[64,1152]{1,0:T(8,128)S(1)} %copy-done.20, f32[64,1152]{1,0:T(8,128)S(1)} %copy-done.22, f32[64,128]{1,0:T(8,128)S(1)} %copy-done.24, bf16[256,1152]{1,0:T(8,128)(2,1)} %bitcast.3.back), custom_call_target="tpu_custom_call" | custom-call | flops 589824 | bytes 884736 | tf_op jit(solution)/shard_map/pallas_call | solution.py:160
  56.0 1.6 %collective-permute-start.11 = (bf16[64,1152]{1,0:T(8,128)(2,1)S(1)}, bf16[64,1152]{1,0:T(8,128)(2,1)S(1)}, u32[]{:S(2)}, u32[]{:S(2)}) collective-permute-start(bf16[64,1152]{1,0:T(8,128)(2,1)S(1)} %shard_map.88), channel_id=1, source_target_pairs={{0,8},{1,17},{2,10},{3,19},{4,12},{5,21},{6,14},{7,23},{8,0},{9,25... | collective-permute-start | bytes 442376 | tf_op jit(solution)/shard_map/ppermute | solution.py:277
  57.6 0.0 collective-permute-start.14
  57.6 1.4 %collective-permute-start.18 = (bf16[64,1152]{1,0:T(8,128)(2,1)S(1)}, bf16[64,1152]{1,0:T(8,128)(2,1)S(1)}, u32[]{:S(2)}, u32[]{:S(2)}) collective-permute-start(bf16[64,1152]{1,0:T(8,128)(2,1)S(1)} %shard_map.88), channel_id=1, source_target_pairs={{0,6},{1,7},{2,4},{3,5},{4,2},{5,3},{6,0},{7,1},{8,14},{9,15},{10,... | collective-permute-start | bytes 442376 | tf_op jit(solution)/shard_map/ppermute | solution.py:266
  59.0 2.1 %collective-permute-start.17 = (bf16[64,1152]{1,0:T(8,128)(2,1)S(1)}, bf16[64,1152]{1,0:T(8,128)(2,1)S(1)}, u32[]{:S(2)}, u32[]{:S(2)}) collective-permute-start(bf16[64,1152]{1,0:T(8,128)(2,1)S(1)} %shard_map.88), channel_id=1, source_target_pairs={{0,4},{1,5},{2,6},{3,7},{4,0},{5,1},{6,2},{7,3},{8,12},{9,13},{10,... | collective-permute-start | bytes 442376 | tf_op jit(solution)/shard_map/ppermute | solution.py:266
  61.1 0.2 collective-permute-done.11
  61.3 0.6 collective-permute-start.12
  61.9 3.5 %collective-permute-done.14 = bf16[64,1152]{1,0:T(8,128)(2,1)S(1)} collective-permute-done((bf16[64,1152]{1,0:T(8,128)(2,1)S(1)}, bf16[64,1152]{1,0:T(8,128)(2,1)S(1)}, u32[]{:S(2)}, u32[]{:S(2)}) %collective-permute-start.14) | collective-permute-done | bytes 147488 | tf_op jit(solution)/shard_map/ppermute | solution.py:266
  65.4 1.7 %collective-permute-start.15 = (bf16[64,1152]{1,0:T(8,128)(2,1)S(1)}, bf16[64,1152]{1,0:T(8,128)(2,1)S(1)}, u32[]{:S(2)}, u32[]{:S(2)}) collective-permute-start(bf16[64,1152]{1,0:T(8,128)(2,1)S(1)} %collective-permute-done.14), channel_id=1, source_target_pairs={{0,8},{1,17},{2,10},{3,19},{4,12},{5,21},{6,14},{7,23},{8,0},{9,25... | collective-permute-start | bytes 442376 | tf_op jit(solution)/shard_map/ppermute | solution.py:277
  67.1 0.0 collective-permute-done.18
  67.1 6.1 %collective-permute-done.17 = bf16[64,1152]{1,0:T(8,128)(2,1)S(1)} collective-permute-done((bf16[64,1152]{1,0:T(8,128)(2,1)S(1)}, bf16[64,1152]{1,0:T(8,128)(2,1)S(1)}, u32[]{:S(2)}, u32[]{:S(2)}) %collective-permute-start.17) | collective-permute-done | bytes 147488 | tf_op jit(solution)/shard_map/ppermute | solution.py:266
  73.3 1.6 %collective-permute-start.19 = (bf16[128,1152]{1,0:T(8,128)(2,1)S(1)}, bf16[128,1152]{1,0:T(8,128)(2,1)S(1)}, u32[]{:S(2)}, u32[]{:S(2)}) collective-permute-start(bf16[128,1152]{1,0:T(8,128)(2,1)S(1)} %pad_maximum_fusion.8), channel_id=1, source_target_pairs={{0,8},{1,17},{2,10},{3,19},{4,12},{5,21},{6,14},{7,23},{8,0},{9,25... | collective-permute-start | bytes 884744 | tf_op jit(solution)/shard_map/ppermute | solution.py:277
  74.9 1.6 %collective-permute-start.16 = (bf16[128,1152]{1,0:T(8,128)(2,1)S(1)}, bf16[128,1152]{1,0:T(8,128)(2,1)S(1)}, u32[]{:S(2)}, u32[]{:S(2)}) collective-permute-start(bf16[128,1152]{1,0:T(8,128)(2,1)S(1)} %pad_maximum_fusion.7), channel_id=1, source_target_pairs={{0,16},{1,9},{2,18},{3,11},{4,20},{5,13},{6,22},{7,15},{8,24},{9,1... | collective-permute-start | bytes 884744 | tf_op jit(solution)/shard_map/ppermute | solution.py:277
  76.5 0.1 collective-permute-start.13
  76.6 6.5 %collective-permute-done.19 = bf16[128,1152]{1,0:T(8,128)(2,1)S(1)} collective-permute-done((bf16[128,1152]{1,0:T(8,128)(2,1)S(1)}, bf16[128,1152]{1,0:T(8,128)(2,1)S(1)}, u32[]{:S(2)}, u32[]{:S(2)}) %collective-permute-start.19) | collective-permute-done | bytes 294944 | tf_op jit(solution)/shard_map/ppermute | solution.py:277
  83.1 0.7 collective-permute-start.22
  83.9 0.0 collective-permute-done.16
  83.9 0.1 collective-permute-start.20
  84.0 0.5 collective-permute-start.21
  84.5 1.7 %fusion.1 = f32[64,1152]{1,0:T(8,128)} fusion(bf16[64,1152]{1,0:T(8,128)(2,1)S(1)} %shard_map.88, bf16[1152,1152]{1,0:T(8,128)(2,1)S(1)} %copy-done), kind=kOutput, calls=%fused_computation.11 | convolution fusion | flops 169869312 | bytes 3096576 | tf_op jit(solution)/shard_map/dot_general | solution.py:17
  86.2 2.6 %add.3 = f32[256,1152]{1,0:T(8,128)} add(f32[256,1152]{1,0:T(8,128)S(1)} %copy-done.12, f32[256,1152]{1,0:T(8,128)} %collective-permute-done.9) | non-fusion elementwise | flops 294912 | bytes 3538944 | tf_op jit(solution)/shard_map/add | solution.py:304
  88.8 1.3 %shard_map.90 = (bf16[1152,512]{1,0:T(8,128)(2,1)S(1)}, bf16[1152,1024]{1,0:T(8,128)(2,1)S(1)}, bf16[1152,512]{1,0:T(8,128)(2,1)S(1)}) custom-call(bf16[1024,1152]{1,0:T(8,128)(2,1)S(1)} %copy-done.2, bf16[1024,1152]{1,0:T(8,128)(2,1)S(1)} %collective-permute-done.10.refs_1_), custom_call_target="tpu_custom_call" | custom-call | bytes 9437184 | tf_op jit(solution)/shard_map/pallas_call | solution.py:186
  90.1 1.7 %shard_map.91.refs_0_ = f32[1152,1152]{1,0:T(8,128)S(1)} custom-call(bf16[1152,512]{1,0:T(8,128)(2,1)S(1)} %get-tuple-element.39.x_t, bf16[256,1152]{1,0:T(8,128)(2,1)S(1)} %pad_maximum_fusion.1.refs_0_, bf16[256,1152]{1,0:T(8,128)(2,1)S(1)} %collective-permute-done.13.refs_1_), custom_call_target="tpu_custom_call" | custom-call | flops 1358954496 | bytes 7667712 | tf_op jit(solution)/shard_map/pallas_call | solution.py:242
  91.8 1.3 %collective-permute-done.22.refs_0_ = bf16[256,1152]{1,0:T(8,128)(2,1)S(1)} collective-permute-done((bf16[256,1152]{1,0:T(8,128)(2,1)S(1)}, bf16[256,1152]{1,0:T(8,128)(2,1)S(1)}, u32[]{:S(2)}, u32[]{:S(2)}) %collective-permute-start.22) | collective-permute-done | bytes 589856 | tf_op jit(solution)/shard_map/ppermute | solution.py:277
  93.1 3.2 %shard_map.92.acc = f32[1152,1152]{1,0:T(8,128)S(1)} custom-call(bf16[1152,1024]{1,0:T(8,128)(2,1)S(1)} %get-tuple-element.38.x_t, f32[1152,1152]{1,0:T(8,128)S(1)} %shard_map.91.refs_0_, bf16[256,1152]{1,0:T(8,128)(2,1)S(1)} %pad_maximum_fusion.2.refs_1_, bf16[256,1152]{1,0:T(8,128)(2,1)S(1)} %pad_maximum_fusion.3.refs_2_, ...), custom_call_target="tpu_custom_call" | custom-call | flops 2717908992 | bytes 15335424 | tf_op jit(solution)/shard_map/pallas_call | solution.py:242
  96.3 3.1 %shard_map.93 = f32[1152,1152]{1,0:T(8,128)} custom-call(bf16[1152,512]{1,0:T(8,128)(2,1)S(1)} %get-tuple-element.37.x_t, f32[1152,1152]{1,0:T(8,128)S(1)} %shard_map.92.acc, bf16[256,1152]{1,0:T(8,128)(2,1)S(1)} %collective-permute-done.22.refs_0_, bf16[256,1152]{1,0:T(8,128)(2,1)S(1)} %collective-permute-done.23.refs_1_), custom_call_target="tpu_custom_call" | custom-call | flops 1358954496 | bytes 12976128 | tf_op jit(solution)/shard_map/pallas_call | solution.py:242
  (61 shorter events, 0.4 us)
Async XLA Ops:
  0.6 19.9 %copy-start = (bf16[1152,1152]{1,0:T(8,128)(2,1)S(1)}, bf16[1152,1152]{1,0:T(8,128)(2,1)}, u32[]{:S(2)}) copy-start(bf16[1152,1152]{1,0:T(8,128)(2,1)} %param.9) | copy-start | bytes 7962628
  0.6 9.2 %collective-permute-start = (bf16[64,1152]{1,0:T(8,128)(2,1)}, bf16[64,1152]{1,0:T(8,128)(2,1)S(1)}, u32[]{:S(2)}, u32[]{:S(2)}) collective-permute-start(bf16[64,1152]{1,0:T(8,128)(2,1)} %bitcast.10), channel_id=1, source_target_pairs={{0,2},{1,3},{2,0},{3,1},{4,6},{5,7},{6,4},{7,5},{8,10},{9,11},{10,... | collective-permute-start | bytes 442376 | tf_op jit(solution)/shard_map/ppermute | solution.py:266
  3.7 14.2 %collective-permute-start.1 = (bf16[64,1152]{1,0:T(8,128)(2,1)}, bf16[64,1152]{1,0:T(8,128)(2,1)S(1)}, u32[]{:S(2)}, u32[]{:S(2)}) collective-permute-start(bf16[64,1152]{1,0:T(8,128)(2,1)} %bitcast.11), channel_id=1, source_target_pairs={{0,4},{1,5},{2,6},{3,7},{4,0},{5,1},{6,2},{7,3},{8,12},{9,13},{10,... | collective-permute-start | bytes 442376 | tf_op jit(solution)/shard_map/ppermute | solution.py:266
  6.3 11.6 %collective-permute-start.2 = (bf16[64,1152]{1,0:T(8,128)(2,1)}, bf16[64,1152]{1,0:T(8,128)(2,1)S(1)}, u32[]{:S(2)}, u32[]{:S(2)}) collective-permute-start(bf16[64,1152]{1,0:T(8,128)(2,1)} %bitcast.12), channel_id=1, source_target_pairs={{0,6},{1,7},{2,4},{3,5},{4,2},{5,3},{6,0},{7,1},{8,14},{9,15},{10,... | collective-permute-start | bytes 442376 | tf_op jit(solution)/shard_map/ppermute | solution.py:266
  6.3 16.9 %collective-permute-start.3 = (s32[1,256]{1,0:T(1,128)}, s32[1,256]{1,0:T(1,128)S(1)}, u32[]{:S(2)}, u32[]{:S(2)}) collective-permute-start(s32[1,256]{1,0:T(1,128)} %refs_0_.1), channel_id=1, source_target_pairs={{0,1},{1,0},{2,3},{3,2},{4,5},{5,4},{6,7},{7,6},{8,9},{9,8},{10,11... | collective-permute-start | bytes 3080 | tf_op jit(solution)/shard_map/ppermute | solution.py:269
  6.3 16.9 %collective-permute-start.4 = (bf16[256,1152]{1,0:T(8,128)(2,1)}, bf16[256,1152]{1,0:T(8,128)(2,1)}, u32[]{:S(2)}, u32[]{:S(2)}) collective-permute-start(bf16[256,1152]{1,0:T(8,128)(2,1)} %bitcast.17), channel_id=1, source_target_pairs={{0,1},{1,0},{2,3},{3,2},{4,5},{5,4},{6,7},{7,6},{8,9},{9,8},{10,11... | collective-permute-start | bytes 1769480 | tf_op jit(solution)/shard_map/ppermute | solution.py:269
  9.8 11.7 %copy-start.3 = (bf16[64,1152]{1,0:T(8,128)(2,1)}, bf16[64,1152]{1,0:T(8,128)(2,1)S(1)}, u32[]{:S(2)}) copy-start(bf16[64,1152]{1,0:T(8,128)(2,1)S(1)} %collective-permute-done.refs_1_) | copy-start | bytes 442372
  9.8 11.8 %collective-permute-start.5 = (bf16[64,1152]{1,0:T(8,128)(2,1)}, bf16[64,1152]{1,0:T(8,128)(2,1)S(1)}, u32[]{:S(2)}, u32[]{:S(2)}) collective-permute-start(bf16[64,1152]{1,0:T(8,128)(2,1)} %bitcast.13), channel_id=1, source_target_pairs={{0,8},{1,17},{2,10},{3,19},{4,12},{5,21},{6,14},{7,23},{8,0},{9,25... | collective-permute-start | bytes 442376 | tf_op jit(solution)/shard_map/ppermute | solution.py:277
  17.9 3.6 %copy-start.5 = (bf16[64,1152]{1,0:T(8,128)(2,1)}, bf16[64,1152]{1,0:T(8,128)(2,1)S(1)}, u32[]{:S(2)}) copy-start(bf16[64,1152]{1,0:T(8,128)(2,1)S(1)} %collective-permute-done.1.refs_2_) | copy-start | bytes 442372
  17.9 3.6 %copy-start.7 = (bf16[64,1152]{1,0:T(8,128)(2,1)}, bf16[64,1152]{1,0:T(8,128)(2,1)S(1)}, u32[]{:S(2)}) copy-start(bf16[64,1152]{1,0:T(8,128)(2,1)S(1)} %collective-permute-done.2.refs_3_) | copy-start | bytes 442372
  18.0 11.4 %collective-permute-start.7 = (bf16[192,1152]{1,0:T(8,128)(2,1)S(1)}, bf16[192,1152]{1,0:T(8,128)(2,1)S(1)}, u32[]{:S(2)}, u32[]{:S(2)}) collective-permute-start(bf16[192,1152]{1,0:T(8,128)(2,1)S(1)} %pad_maximum_fusion.4), channel_id=1, source_target_pairs={{0,8},{1,17},{2,10},{3,19},{4,12},{5,21},{6,14},{7,23},{8,0},{9,25... | collective-permute-start | bytes 1327112 | tf_op jit(solution)/shard_map/ppermute | solution.py:277
  19.5 0.9 copy-start.13
  20.5 1.1 %copy-start.14 = (bf16[1,64,1152]{2,1,0:T(8,128)(2,1)S(1)}, bf16[1,64,1152]{2,1,0:T(8,128)(2,1)}, u32[]{:S(2)}) copy-start(bf16[1,64,1152]{2,1,0:T(8,128)(2,1)} %param.6) | copy-start | bytes 442372
  20.5 2.8 %copy-start.16 = (bf16[1,256,1152]{2,1,0:T(8,128)(2,1)S(1)}, bf16[1,256,1152]{2,1,0:T(8,128)(2,1)}, u32[]{:S(2)}) copy-start(bf16[1,256,1152]{2,1,0:T(8,128)(2,1)} %param.7) | copy-start | bytes 1769476
  20.5 2.8 %copy-start.25 = (s32[1,256]{1,0:T(1,128)S(1)}, s32[1,256]{1,0:T(1,128)}, u32[]{:S(2)}) copy-start(s32[1,256]{1,0:T(1,128)} %refs_0_.1) | copy-start | bytes 3076
  21.6 7.8 %copy-start.9 = (bf16[128,1152]{1,0:T(8,128)(2,1)}, bf16[128,1152]{1,0:T(8,128)(2,1)S(1)}, u32[]{:S(2)}) copy-start(bf16[128,1152]{1,0:T(8,128)(2,1)S(1)} %pad_maximum_fusion.5.refs_0_) | copy-start | bytes 884740
  21.6 7.7 %copy-start.4 = (bf16[64,1152]{1,0:T(8,128)(2,1)S(1)}, bf16[64,1152]{1,0:T(8,128)(2,1)}, u32[]{:S(2)}) copy-start(bf16[64,1152]{1,0:T(8,128)(2,1)} %copy-done.3) | copy-start | bytes 442372
  21.7 7.7 %copy-start.6 = (bf16[64,1152]{1,0:T(8,128)(2,1)S(1)}, bf16[64,1152]{1,0:T(8,128)(2,1)}, u32[]{:S(2)}) copy-start(bf16[64,1152]{1,0:T(8,128)(2,1)} %copy-done.5) | copy-start | bytes 442372
  21.7 7.7 %copy-start.8 = (bf16[64,1152]{1,0:T(8,128)(2,1)S(1)}, bf16[64,1152]{1,0:T(8,128)(2,1)}, u32[]{:S(2)}) copy-start(bf16[64,1152]{1,0:T(8,128)(2,1)} %copy-done.7) | copy-start | bytes 442372
  21.7 8.3 %collective-permute-start.6 = (bf16[128,1152]{1,0:T(8,128)(2,1)S(1)}, bf16[128,1152]{1,0:T(8,128)(2,1)S(1)}, u32[]{:S(2)}, u32[]{:S(2)}) collective-permute-start(bf16[128,1152]{1,0:T(8,128)(2,1)S(1)} %pad_maximum_fusion.5.refs_0_), channel_id=1, source_target_pairs={{0,16},{1,9},{2,18},{3,11},{4,20},{5,13},{6,22},{7,15},{8,24},{9,1... | collective-permute-start | bytes 884744 | tf_op jit(solution)/shard_map/ppermute | solution.py:277
  25.7 0.7 copy-start.21
  26.4 3.6 %copy-start.15 = (bf16[256,1152]{1,0:T(8,128)(2,1)}, bf16[256,1152]{1,0:T(8,128)(2,1)S(1)}, u32[]{:S(2)}) copy-start(bf16[256,1152]{1,0:T(8,128)(2,1)S(1)} %get-tuple-element.29) | copy-start | bytes 1769476
  26.4 3.6 %copy-start.19 = (f32[64,1152]{1,0:T(8,128)}, f32[64,1152]{1,0:T(8,128)S(1)}, u32[]{:S(2)}) copy-start(f32[64,1152]{1,0:T(8,128)S(1)} %get-tuple-element.23.own) | copy-start | bytes 884740
  26.4 3.6 %copy-start.23 = (f32[64,128]{1,0:T(8,128)}, f32[64,128]{1,0:T(8,128)S(1)}, u32[]{:S(2)}) copy-start(f32[64,128]{1,0:T(8,128)S(1)} %get-tuple-element.25.inv_norm) | copy-start | bytes 98308
  27.9 1.1 %copy-start.11 = (f32[256,1152]{1,0:T(8,128)}, f32[256,1152]{1,0:T(8,128)S(1)}, u32[]{:S(2)}) copy-start(f32[256,1152]{1,0:T(8,128)S(1)} %get-tuple-element.35) | copy-start | bytes 3538948
  29.0 23.1 %collective-permute-start.9 = (f32[256,1152]{1,0:T(8,128)}, f32[256,1152]{1,0:T(8,128)}, u32[]{:S(2)}, u32[]{:S(2)}) collective-permute-start(f32[256,1152]{1,0:T(8,128)} %get-tuple-element.33), channel_id=1, source_target_pairs={{0,1},{1,0},{2,3},{3,2},{4,5},{5,4},{6,7},{7,6},{8,9},{9,8},{10,11... | collective-permute-start | bytes 3538952 | tf_op jit(solution)/shard_map/ppermute | solution.py:269
  29.4 13.2 %collective-permute-start.8 = (bf16[384,1152]{1,0:T(8,128)(2,1)S(1)}, bf16[384,1152]{1,0:T(8,128)(2,1)}, u32[]{:S(2)}, u32[]{:S(2)}) collective-permute-start(bf16[384,1152]{1,0:T(8,128)(2,1)S(1)} %pad_maximum_fusion.refs_2_), channel_id=1, source_target_pairs={{0,16},{1,9},{2,18},{3,11},{4,20},{5,13},{6,22},{7,15},{8,24},{9,1... | collective-permute-start | bytes 2654216 | tf_op jit(solution)/shard_map/ppermute | solution.py:277
  30.0 0.7 copy-start.17
  30.8 21.4 %all-to-all-start = ((bf16[4,64,1152]{2,1,0:T(8,128)(2,1)}), bf16[4,64,1152]{2,1,0:T(8,128)(2,1)}, u32[]{:S(2)}, u32[]{:S(2)}) async-start(bf16[4,64,1152]{2,1,0:T(8,128)(2,1)} %bitcast.16), calls=%async_computation | async-start | bytes 1179648 | tf_op jit(solution)/shard_map/all_to_all | solution.py:307
  42.7 1.0 copy-start.10
  43.6 1.0 copy-start.18
  45.9 1.4 %copy-start.1 = (bf16[1024,1152]{1,0:T(8,128)(2,1)}, bf16[1024,1152]{1,0:T(8,128)(2,1)S(1)}, u32[]{:S(2)}) copy-start(bf16[1024,1152]{1,0:T(8,128)(2,1)S(1)} %shard_map.89.refs_0_) | copy-start | bytes 7077892
  52.1 36.6 %collective-permute-start.10 = (bf16[1024,1152]{1,0:T(8,128)(2,1)}, bf16[1024,1152]{1,0:T(8,128)(2,1)S(1)}, u32[]{:S(2)}, u32[]{:S(2)}) collective-permute-start(bf16[1024,1152]{1,0:T(8,128)(2,1)} %copy-done.1), channel_id=1, source_target_pairs={{0,1},{1,0},{2,3},{3,2},{4,5},{5,4},{6,7},{7,6},{8,9},{9,8},{10,11... | collective-permute-start | bytes 7077896 | tf_op jit(solution)/shard_map/ppermute | solution.py:269
  52.1 1.0 copy-start.20
  53.1 1.0 copy-start.22
  54.1 0.8 copy-start.24
  56.0 5.2 %collective-permute-start.11 = (bf16[64,1152]{1,0:T(8,128)(2,1)S(1)}, bf16[64,1152]{1,0:T(8,128)(2,1)S(1)}, u32[]{:S(2)}, u32[]{:S(2)}) collective-permute-start(bf16[64,1152]{1,0:T(8,128)(2,1)S(1)} %shard_map.88), channel_id=1, source_target_pairs={{0,8},{1,17},{2,10},{3,19},{4,12},{5,21},{6,14},{7,23},{8,0},{9,25... | collective-permute-start | bytes 442376 | tf_op jit(solution)/shard_map/ppermute | solution.py:277
  57.6 7.8 %collective-permute-start.14 = (bf16[64,1152]{1,0:T(8,128)(2,1)S(1)}, bf16[64,1152]{1,0:T(8,128)(2,1)S(1)}, u32[]{:S(2)}, u32[]{:S(2)}) collective-permute-start(bf16[64,1152]{1,0:T(8,128)(2,1)S(1)} %shard_map.88), channel_id=1, source_target_pairs={{0,2},{1,3},{2,0},{3,1},{4,6},{5,7},{6,4},{7,5},{8,10},{9,11},{10,... | collective-permute-start | bytes 442376 | tf_op jit(solution)/shard_map/ppermute | solution.py:266
  57.6 9.5 %collective-permute-start.18 = (bf16[64,1152]{1,0:T(8,128)(2,1)S(1)}, bf16[64,1152]{1,0:T(8,128)(2,1)S(1)}, u32[]{:S(2)}, u32[]{:S(2)}) collective-permute-start(bf16[64,1152]{1,0:T(8,128)(2,1)S(1)} %shard_map.88), channel_id=1, source_target_pairs={{0,6},{1,7},{2,4},{3,5},{4,2},{5,3},{6,0},{7,1},{8,14},{9,15},{10,... | collective-permute-start | bytes 442376 | tf_op jit(solution)/shard_map/ppermute | solution.py:266
  59.0 14.3 %collective-permute-start.17 = (bf16[64,1152]{1,0:T(8,128)(2,1)S(1)}, bf16[64,1152]{1,0:T(8,128)(2,1)S(1)}, u32[]{:S(2)}, u32[]{:S(2)}) collective-permute-start(bf16[64,1152]{1,0:T(8,128)(2,1)S(1)} %shard_map.88), channel_id=1, source_target_pairs={{0,4},{1,5},{2,6},{3,7},{4,0},{5,1},{6,2},{7,3},{8,12},{9,13},{10,... | collective-permute-start | bytes 442376 | tf_op jit(solution)/shard_map/ppermute | solution.py:266
  61.3 12.0 %collective-permute-start.12 = (bf16[128,1152]{1,0:T(8,128)(2,1)S(1)}, bf16[128,1152]{1,0:T(8,128)(2,1)S(1)}, u32[]{:S(2)}, u32[]{:S(2)}) collective-permute-start(bf16[128,1152]{1,0:T(8,128)(2,1)S(1)} %pad_maximum_fusion.6), channel_id=1, source_target_pairs={{0,16},{1,9},{2,18},{3,11},{4,20},{5,13},{6,22},{7,15},{8,24},{9,1... | collective-permute-start | bytes 884744 | tf_op jit(solution)/shard_map/ppermute | solution.py:277
  65.4 7.9 %collective-permute-start.15 = (bf16[64,1152]{1,0:T(8,128)(2,1)S(1)}, bf16[64,1152]{1,0:T(8,128)(2,1)S(1)}, u32[]{:S(2)}, u32[]{:S(2)}) collective-permute-start(bf16[64,1152]{1,0:T(8,128)(2,1)S(1)} %collective-permute-done.14), channel_id=1, source_target_pairs={{0,8},{1,17},{2,10},{3,19},{4,12},{5,21},{6,14},{7,23},{8,0},{9,25... | collective-permute-start | bytes 442376 | tf_op jit(solution)/shard_map/ppermute | solution.py:277
  73.3 9.8 %collective-permute-start.19 = (bf16[128,1152]{1,0:T(8,128)(2,1)S(1)}, bf16[128,1152]{1,0:T(8,128)(2,1)S(1)}, u32[]{:S(2)}, u32[]{:S(2)}) collective-permute-start(bf16[128,1152]{1,0:T(8,128)(2,1)S(1)} %pad_maximum_fusion.8), channel_id=1, source_target_pairs={{0,8},{1,17},{2,10},{3,19},{4,12},{5,21},{6,14},{7,23},{8,0},{9,25... | collective-permute-start | bytes 884744 | tf_op jit(solution)/shard_map/ppermute | solution.py:277
  74.9 9.0 %collective-permute-start.16 = (bf16[128,1152]{1,0:T(8,128)(2,1)S(1)}, bf16[128,1152]{1,0:T(8,128)(2,1)S(1)}, u32[]{:S(2)}, u32[]{:S(2)}) collective-permute-start(bf16[128,1152]{1,0:T(8,128)(2,1)S(1)} %pad_maximum_fusion.7), channel_id=1, source_target_pairs={{0,16},{1,9},{2,18},{3,11},{4,20},{5,13},{6,22},{7,15},{8,24},{9,1... | collective-permute-start | bytes 884744 | tf_op jit(solution)/shard_map/ppermute | solution.py:277
  76.5 13.6 %collective-permute-start.13 = (bf16[256,1152]{1,0:T(8,128)(2,1)S(1)}, bf16[256,1152]{1,0:T(8,128)(2,1)S(1)}, u32[]{:S(2)}, u32[]{:S(2)}) collective-permute-start(bf16[256,1152]{1,0:T(8,128)(2,1)S(1)} %pad_maximum_fusion.1.refs_0_), channel_id=1, source_target_pairs={{0,1},{1,0},{2,3},{3,2},{4,5},{5,4},{6,7},{7,6},{8,9},{9,8},{10,11... | collective-permute-start | bytes 1769480 | tf_op jit(solution)/shard_map/ppermute | solution.py:269
  83.1 9.9 %collective-permute-start.22 = (bf16[256,1152]{1,0:T(8,128)(2,1)S(1)}, bf16[256,1152]{1,0:T(8,128)(2,1)S(1)}, u32[]{:S(2)}, u32[]{:S(2)}) collective-permute-start(bf16[256,1152]{1,0:T(8,128)(2,1)S(1)} %pad_maximum_fusion.3.refs_2_), channel_id=1, source_target_pairs={{0,16},{1,9},{2,18},{3,11},{4,20},{5,13},{6,22},{7,15},{8,24},{9,1... | collective-permute-start | bytes 1769480 | tf_op jit(solution)/shard_map/ppermute | solution.py:277
  83.9 2.2 %copy-start.12 = (f32[256,1152]{1,0:T(8,128)S(1)}, f32[256,1152]{1,0:T(8,128)}, u32[]{:S(2)}) copy-start(f32[256,1152]{1,0:T(8,128)} %copy-done.11) | copy-start | bytes 3538948
  83.9 9.2 %collective-permute-start.20 = (bf16[256,1152]{1,0:T(8,128)(2,1)S(1)}, bf16[256,1152]{1,0:T(8,128)(2,1)S(1)}, u32[]{:S(2)}, u32[]{:S(2)}) collective-permute-start(bf16[256,1152]{1,0:T(8,128)(2,1)S(1)} %pad_maximum_fusion.2.refs_1_), channel_id=1, source_target_pairs={{0,1},{1,0},{2,3},{3,2},{4,5},{5,4},{6,7},{7,6},{8,9},{9,8},{10,11... | collective-permute-start | bytes 1769480 | tf_op jit(solution)/shard_map/ppermute | solution.py:269
  84.0 9.1 %collective-permute-start.21 = (bf16[256,1152]{1,0:T(8,128)(2,1)S(1)}, bf16[256,1152]{1,0:T(8,128)(2,1)S(1)}, u32[]{:S(2)}, u32[]{:S(2)}) collective-permute-start(bf16[256,1152]{1,0:T(8,128)(2,1)S(1)} %pad_maximum_fusion.3.refs_2_), channel_id=1, source_target_pairs={{0,1},{1,0},{2,3},{3,2},{4,5},{5,4},{6,7},{7,6},{8,9},{9,8},{10,11... | collective-permute-start | bytes 1769480 | tf_op jit(solution)/shard_map/ppermute | solution.py:269
  86.2 2.6 %copy-start.2 = (bf16[1024,1152]{1,0:T(8,128)(2,1)S(1)}, bf16[1024,1152]{1,0:T(8,128)(2,1)}, u32[]{:S(2)}) copy-start(bf16[1024,1152]{1,0:T(8,128)(2,1)} %copy-done.1) | copy-start | bytes 7077892
  93.1 3.3 %collective-permute-start.23 = (bf16[256,1152]{1,0:T(8,128)(2,1)S(1)}, bf16[256,1152]{1,0:T(8,128)(2,1)S(1)}, u32[]{:S(2)}, u32[]{:S(2)}) collective-permute-start(bf16[256,1152]{1,0:T(8,128)(2,1)S(1)} %collective-permute-done.22.refs_0_), channel_id=1, source_target_pairs={{0,1},{1,0},{2,3},{3,2},{4,5},{5,4},{6,7},{7,6},{8,9},{9,8},{10,11... | collective-permute-start | bytes 1769480 | tf_op jit(solution)/shard_map/ppermute | solution.py:269

commit v8 on v7

--- a/solution.py
+++ b/solution.py
@@ -25,7 +25,7 @@
     scale, offset = both[0:1, 0:1], both[8:9, 0:1]
     labels, captions, refs = refs[:2], refs[2:4], refs[4:]
     own, unit_own, inv_own, unit, dlogit = refs[:5]
-    sent, caps, sems = refs[5:]
+    sent, (caps, sems) = refs[5:-2], refs[-2:]
     n_img, n_cap = embed.shape[0] // nz, captions[0].shape[0]
     copies = []
     for i in range(2):
@@ -54,10 +54,8 @@
     dlogit[...] = d
     part = scale * dot(d, caps[...])
     own[...] = part[:n_img]
-    for k in range(nz):
-        row = pl.multiple_of(((index // 2) ^ k) * n_img, n_img)
-        block = part[k * n_img : (k + 1) * n_img]
-        sent[pl.ds(row, n_img), :] = block.astype(BF16)
+    for k in range(1, nz):
+        sent[k - 1][...] = part[k * n_img : (k + 1) * n_img].astype(BF16)
 
 
 def scores(nz, both, embed, labels, captions):
@@ -72,8 +70,7 @@
         jax.ShapeDtypeStruct((n_img, 128), F32),
         jax.ShapeDtypeStruct((images, depth), BF16),
         jax.ShapeDtypeStruct((images, caps), BF16),
-        jax.ShapeDtypeStruct((images, depth), BF16),
-    ]
+    ] + [jax.ShapeDtypeStruct((n_img, depth), BF16)] * (nz - 1)
     return pl.pallas_call(
         functools.partial(score_kernel, nz),
         out_shape=outs,
@@ -142,14 +139,11 @@
     )(both, dlogit, unit)
 
 
-def embed_grad_kernel(own, unit, inv_norm, back, out):
-    n_img = own.shape[0]
-    nz = back.shape[0] // n_img
-    z = lax.axis_index("blk") // 2
+def embed_grad_kernel(own, unit, inv_norm, *refs):
+    back, out = refs[:-1], refs[-1]
     total = own[...]
-    for k in range(1, nz):
-        row = pl.multiple_of((z ^ k) * n_img, n_img)
-        total = total + back[pl.ds(row, n_img), :].astype(F32)
+    for v in back:
+        total = total + v[...].astype(F32)
     u = unit[...]
     radial = jnp.sum(u * total, axis=1, keepdims=True)
     out[...] = ((total - u * radial) * inv_norm[:, :1]).astype(BF16)
@@ -160,13 +154,13 @@
     return pl.pallas_call(
         embed_grad_kernel,
         out_shape=jax.ShapeDtypeStruct(own.shape, BF16),
-        in_specs=[vmem] * 4,
+        in_specs=[vmem] * (3 + len(back)),
         out_specs=vmem,
-        compiler_params=pltpu.CompilerParams(vmem_limit_bytes=12 * 2**20),
+        compiler_params=pltpu.CompilerParams(vmem_limit_bytes=8 * 2**20),
         cost_estimate=pl.CostEstimate(
             flops=8 * own.size, bytes_accessed=12 * own.size, transcendentals=0
         ),
-    )(own, unit, inv_norm, back)
+    )(own, unit, inv_norm, *back)
 
 
 def turn_kernel(plan, *refs):
@@ -276,6 +270,17 @@
                 perm.append((j * nb + m, to * nb + m))
         return lax.ppermute(v, ("dp", "blk"), perm)
 
+    def direct_d(v, chunk):
+        perm = []
+        for j in range(nd):
+            for m in range(nb):
+                to = j
+                for i in range(bits):
+                    if chunk >> i & 1:
+                        to ^= 1 << ((i + m % 2) % bits)
+                perm.append((j * nb + m, to * nb + m))
+        return lax.ppermute(v, ("dp", "blk"), perm)
+
     def over_d(v, first, *before):
         v = [v, first]
         for i in range(1, bits):
@@ -287,65 +292,63 @@
     xs = [x] + [along_z(x, k) for k in range(1, nz)]
     x_own = over_d(x, step_d(after(x, xs[1]), 0))
     x_rest = jnp.concatenate(xs[1:])
-    x_rest_first = step_d(x_rest, 0)
-    embed = dot(joined(xs), weight)
+    embed = dot(joined(after(xs, x)), weight)
     row = lax.broadcasted_iota(jnp.int32, (16, 128), 0)
     both = jnp.where(row < 8, scale, offset)
-    own, u, inv_norm, unit, dlogit, sent = scores(
+    own, u, inv_norm, unit, dlogit, *sent = scores(
         nz,
         both,
         embed,
         [labels, swap(labels)],
         [captions, swap(captions)],
     )
-    x_rest = over_d(x_rest, after(x_rest_first, sent))
+    sent = after(sent, x_own)
+    back = [along_z(v, k + 1) for k, v in enumerate(sent)]
+    x_rest = after(x_rest, x)
+    x_rest = over_d(x_rest, after(step_d(x_rest, 0), sent))
     adjoint, adjoint_other = caption_sums(both, after(dlogit, sent), unit)
     adjoint_other = swap(adjoint_other)
     adjoint = adjoint + adjoint_other
-    chips = [list(range(c, nb, 2)) for c in range(2)]
-    sent = after(sent, x_own, x_rest[0])
-    back = lax.all_to_all(sent, "blk", 0, 0, axis_index_groups=chips, tiled=True)
     back = after(back, x_rest, adjoint_other)
+    ge = embed_grad(own, u, inv_norm, back)
+    grad_features = dot(ge, weight, LAST)
+
     small = nd * nb * n_img <= 2048
+    x_other = []
     if small:
         x_all = joined(x_own + x_rest)
-        x_other = swap(after(x_all, back))
-    ge = embed_grad(own, u, inv_norm, back)
-    grad_features = dot(ge, weight, LAST)
+        x_other = swap(after(x_all, ge))
 
     near = [along_z(ge, k) for k in range(1, half)]
     own_first = step_d(ge, 0)
     far = [along_z(ge, k) for k in range(half, nz)]
     g_own = over_d(ge, own_first)
-    near = after(jnp.concatenate(near), g_own[0], g_own[0])
+    near = after(jnp.concatenate(near), g_own[0], ge)
     near_first = step_d(near, 0)
     g_near = over_d(near, near_first)
-    far = after(jnp.concatenate(far), near_first, g_own[1])
-    far_first = step_d(far, 0)
+    far = after(jnp.concatenate(far), g_own[1], near_first, grad_features, adjoint, x_other)
+    g_far = [far] + [direct_d(far, i) for i in range(1, nd)]
     sizes = [n_img, n_img * (half - 1), n_img * half]
     n_rest = sizes[1] + sizes[2]
     per = nd // 2
     if small:
-        plan = [[], [], []]
+        plan = [[], []]
         for core in range(2):
             rest = [n_img * nd + i * n_rest for i in range(nd)]
             far_runs = [(core, at + sizes[1], sizes[2]) for at in rest]
-            plan[0] += [[(core, 0, n_img * nd)]]
-            plan[1] += [[(core, at, sizes[1]) for at in rest], far_runs[:per]]
-            plan[2] += [far_runs[per:]]
-        x_first, x_mid, x_late = turned([x_all, x_other], plan)
-        g_own, g_near = jnp.concatenate(g_own), jnp.concatenate(g_near)
-        own_swapped = swap(g_own)
-        acc = weight_sum(None, x_first, [g_own, own_swapped])
-        near_swapped = swap(g_near)
-        g_far = over_d(far, far_first, )
-        mid = [g_near, g_far[0], near_swapped, swap(g_far[0])]
-        before_late = (acc, grad_features)
-        acc = weight_sum(acc, x_mid, mid)
-        late = after(g_far[1], before_late, adjoint)
-        grad_weight = weight_sum(acc, x_late, [late, swap(late)], 1.0 / nd)
+            plan[0] += [[(core, 0, n_img * nd)], far_runs[:1]]
+            plan[1] += [[(core, at, sizes[1]) for at in rest], far_runs[1:]]
+        x_early, x_late = turned([x_all, x_other], plan)
+        early = jnp.concatenate(g_own + g_far[:1])
+        early_swapped = swap(early)
+        acc = weight_sum(None, x_early, [early, early_swapped])
+        before_late = (x_early, grad_features, adjoint)
+        late = [after(v, acc) for v in g_far[1:]]
+        g_near = jnp.concatenate(g_near)
+        late = [g_near] + late + [swap(g_near)] + [swap(v) for v in late]
+        grad_weight = weight_sum(acc, x_late, late, 1.0 / nd)
     else:
-        g_far = over_d(far, far_first)
+        g_far = [jnp.concatenate(g_far[:per]), jnp.concatenate(g_far[per:])]
         grad_weight = 0.0
         for v, g in zip(x_own, g_own):
             grad_weight = grad_weight + dot(v, g, FIRST)

time: 100 us -> 93 us (0.930)
  local copies, waits for them, and re-layouts: 9.56 us -> 1.01 us
  waiting for transfers between devices: 36.9 us -> 42.7 us
  Pallas kernels: 15.8 us -> 12.2 us
  other arithmetic: 2.94 us -> 1.51 us
  starting transfers between devices: 29.2 us -> 30.6 us
    unnamed x52 -> x10, local copies, waits for them, and re-layouts: 9.49 us -> 0.94 us
    ppermute x10 -> x8, waiting for transfers between devices: 14.4 us -> 20.6 us  [step_d(): return lax.ppermute(v, ('dp', 'blk'), perm)]
    all_to_all x1 -> x0, starting transfers between devices: 5.76 us -> none  [on_device(): lax.all_to_all(sent, 'blk', 0, 0, axis_index_groups=chips, tiled=True)]
    ppermute x6 -> x9, starting transfers between devices: 9.17 us -> 14.6 us  [along_z(): return lax.ppermute(v, 'blk', [(i, i ^ 2 * k) for i in range(nb)])]
    all_to_all x1 -> x0, waiting for transfers between devices: 4.79 us -> none  [on_device(): lax.all_to_all(sent, 'blk', 0, 0, axis_index_groups=chips, tiled=True)]
    ppermute x0 -> x3, starting transfers between devices: none -> 3.49 us  [direct_d(): return lax.ppermute(v, ('dp', 'blk'), perm)]
    ppermute x10 -> x8, starting transfers between devices: 13.2 us -> 10.4 us  [step_d(): return lax.ppermute(v, ('dp', 'blk'), perm)]
    ppermute x8 -> x9, waiting for transfers between devices: 0.02 us -> 1.92 us  [swap(): return lax.ppermute(v, 'blk', [(i, i ^ 1) for i in range(nb)])]
  transfers between devices with their start and end apart: 25 -> 29, of which waited for: 10 -> 13; matrix products, arithmetic and copies ran while one was open for 6% -> 4% of each run, Pallas kernels for 13% -> 7%
where the time goes in v8:
time: 93 us; the launch traced here: 92.8 us
  waiting for transfers between devices  42.7 us (46%)
  starting transfers between devices  30.6 us (33%)
  Pallas kernels  12.2 us (13%)
  matrix products  2.65 us (3%)
  between operations  2.19 us (2%)
  other arithmetic  1.51 us (2%)
  local copies, waits for them, and re-layouts  1.01 us (1%)
    ppermute x8, waiting for transfers between devices, step_d(): return lax.ppermute(v, ('dp', 'blk'), perm)  20.6 us
    ppermute x9, waiting for transfers between devices, along_z(): return lax.ppermute(v, 'blk', [(i, i ^ 2 * k) for i in range(nb)])  19.3 us
    ppermute x9, starting transfers between devices, along_z(): return lax.ppermute(v, 'blk', [(i, i ^ 2 * k) for i in range(nb)])  14.6 us
    ppermute x8, starting transfers between devices, step_d(): return lax.ppermute(v, ('dp', 'blk'), perm)  10.4 us
    pallas_call x2, Pallas kernels, weight_sum(): pl.pallas_call(kernel, out_shape=jax.ShapeDtypeStruct((depth, depth), F32...  7.7 us
    ppermute x3, starting transfers between devices, direct_d(): return lax.ppermute(v, ('dp', 'blk'), perm)  3.49 us
    dot_general x2, matrix products, dot(): return lax.dot_general(a, b, dims, preferred_element_type=F32)  2.65 us
    pallas_call x1, Pallas kernels, scores(): pl.pallas_call(functools.partial(score_kernel, nz), out_shape=outs, in_sp...  2.3 us
  transfers between devices with their start and end apart: 29, of which 13 were waited for; matrix products, arithmetic and copies ran while one was open for 4% of the time, Pallas kernels for 7%

profile of v8, /device:TPU:0, one launch (start us, length us, event | category | flops | bytes accessed | tf_op | source)
XLA Modules:
  0.0 92.8 jit_solution(6815184502004675734)
XLA Ops:
  0.6 0.0 copy-start
  0.6 0.0 copy-start.2
  0.7 3.1 %collective-permute-start = (bf16[64,1152]{1,0:T(8,128)(2,1)}, bf16[64,1152]{1,0:T(8,128)(2,1)S(1)}, u32[]{:S(2)}, u32[]{:S(2)}) collective-permute-start(bf16[64,1152]{1,0:T(8,128)(2,1)} %bitcast.8), channel_id=1, source_target_pairs={{0,2},{1,3},{2,0},{3,1},{4,6},{5,7},{6,4},{7,5},{8,10},{9,11},{10,... | collective-permute-start | bytes 442376 | tf_op jit(solution)/shard_map/ppermute | solution.py:260
  3.7 2.5 %collective-permute-start.2 = (bf16[64,1152]{1,0:T(8,128)(2,1)}, bf16[64,1152]{1,0:T(8,128)(2,1)S(1)}, u32[]{:S(2)}, u32[]{:S(2)}) collective-permute-start(bf16[64,1152]{1,0:T(8,128)(2,1)} %bitcast.9), channel_id=1, source_target_pairs={{0,6},{1,7},{2,4},{3,5},{4,2},{5,3},{6,0},{7,1},{8,14},{9,15},{10,... | collective-permute-start | bytes 442376 | tf_op jit(solution)/shard_map/ppermute | solution.py:260
  6.2 0.1 collective-permute-start.1
  6.3 0.5 collective-permute-start.4
  8.2 1.6 %collective-permute-start.5 = (bf16[64,1152]{1,0:T(8,128)(2,1)}, bf16[64,1152]{1,0:T(8,128)(2,1)S(1)}, u32[]{:S(2)}, u32[]{:S(2)}) collective-permute-start(bf16[64,1152]{1,0:T(8,128)(2,1)} %bitcast.11), channel_id=1, source_target_pairs={{0,8},{1,17},{2,10},{3,19},{4,12},{5,21},{6,14},{7,23},{8,0},{9,25... | collective-permute-start | bytes 442376 | tf_op jit(solution)/shard_map/ppermute | solution.py:271
  9.7 4.7 %collective-permute-done.2.refs_3_ = bf16[64,1152]{1,0:T(8,128)(2,1)S(1)} collective-permute-done((bf16[64,1152]{1,0:T(8,128)(2,1)}, bf16[64,1152]{1,0:T(8,128)(2,1)S(1)}, u32[]{:S(2)}, u32[]{:S(2)}) %collective-permute-start.2) | collective-permute-done | bytes 147488 | tf_op jit(solution)/shard_map/ppermute | solution.py:260
  14.4 5.2 %collective-permute-done.1.refs_2_ = bf16[64,1152]{1,0:T(8,128)(2,1)S(1)} collective-permute-done((bf16[64,1152]{1,0:T(8,128)(2,1)}, bf16[64,1152]{1,0:T(8,128)(2,1)S(1)}, u32[]{:S(2)}, u32[]{:S(2)}) %collective-permute-start.1) | collective-permute-done | bytes 147488 | tf_op jit(solution)/shard_map/ppermute | solution.py:260
  19.7 1.6 %collective-permute-start.10 = (bf16[192,1152]{1,0:T(8,128)(2,1)S(1)}, bf16[192,1152]{1,0:T(8,128)(2,1)S(1)}, u32[]{:S(2)}, u32[]{:S(2)}) collective-permute-start(bf16[192,1152]{1,0:T(8,128)(2,1)S(1)} %pad_maximum_fusion.3), channel_id=1, source_target_pairs={{0,8},{1,17},{2,10},{3,19},{4,12},{5,21},{6,14},{7,23},{8,0},{9,25... | collective-permute-start | bytes 1327112 | tf_op jit(solution)/shard_map/ppermute | solution.py:271
  21.2 0.9 copy-done.1
  22.2 0.0 copy-start.3
  22.2 0.0 copy-start.4
  22.3 1.6 %collective-permute-start.6 = (bf16[128,1152]{1,0:T(8,128)(2,1)S(1)}, bf16[128,1152]{1,0:T(8,128)(2,1)S(1)}, u32[]{:S(2)}, u32[]{:S(2)}) collective-permute-start(bf16[128,1152]{1,0:T(8,128)(2,1)S(1)} %pad_maximum_fusion.4.refs_0_), channel_id=1, source_target_pairs={{0,16},{1,9},{2,18},{3,11},{4,20},{5,13},{6,22},{7,15},{8,24},{9,1... | collective-permute-start | bytes 884744 | tf_op jit(solution)/shard_map/ppermute | solution.py:271
  23.8 1.0 %fusion.embed = f32[256,1152]{1,0:T(8,128)S(1)} fusion(bf16[256,1152]{1,0:T(8,128)(2,1)S(1)} %shard_map.85, bf16[1152,1152]{1,0:T(8,128)(2,1)S(1)} %copy-done), kind=kOutput, calls=%fused_computation.9 | convolution fusion | flops 679477248 | bytes 4423680 | tf_op jit(solution)/shard_map/dot_general | solution.py:17
  24.9 0.0 collective-permute-done.4.refs_3_
  24.9 0.1 iota.7.both
  24.9 2.3 %shard_map.86 = (f32[64,1152]{1,0:T(8,128)S(1)}, f32[64,1152]{1,0:T(8,128)S(1)}, f32[64,128]{1,0:T(8,128)S(1)}, bf16[256,1152]{1,0:T(8,128)(2,1)S(1)}, bf16[256,...) custom-call(f32[16,128]{1,0:T(8,128)S(1)} %iota.7.both, ...), custom_call_target="tpu_custom_call" | custom-call | flops 603979776 | bytes 4718592 | tf_op jit(solution)/shard_map/pallas_call | solution.py:74
  27.3 2.0 %collective-permute-done.6.refs_1_ = bf16[128,1152]{1,0:T(8,128)(2,1)S(1)} collective-permute-done((bf16[128,1152]{1,0:T(8,128)(2,1)S(1)}, bf16[128,1152]{1,0:T(8,128)(2,1)S(1)}, u32[]{:S(2)}, u32[]{:S(2)}) %collective-permute-start.6) | collective-permute-done | bytes 294944 | tf_op jit(solution)/shard_map/ppermute | solution.py:271
  29.2 0.5 shard_map.87
  29.8 0.8 collective-permute-start.12
  30.6 0.6 collective-permute-done.10
  31.2 0.1 pad_maximum_fusion.refs_2_
  31.3 0.9 %collective-permute-start.11 = (bf16[384,1152]{1,0:T(8,128)(2,1)S(1)}, bf16[384,1152]{1,0:T(8,128)(2,1)S(1)}, u32[]{:S(2)}, u32[]{:S(2)}) collective-permute-start(bf16[384,1152]{1,0:T(8,128)(2,1)S(1)} %pad_maximum_fusion.refs_2_), channel_id=1, source_target_pairs={{0,16},{1,9},{2,18},{3,11},{4,20},{5,13},{6,22},{7,15},{8,24},{9,1... | collective-permute-start | bytes 2654216 | tf_op jit(solution)/shard_map/ppermute | solution.py:271
  32.2 0.0 collective-permute-start.7
  32.2 3.1 %collective-permute-start.8 = (bf16[64,1152]{1,0:T(8,128)(2,1)S(1)}, bf16[64,1152]{1,0:T(8,128)(2,1)S(1)}, u32[]{:S(2)}, u32[]{:S(2)}) collective-permute-start(bf16[64,1152]{1,0:T(8,128)(2,1)S(1)} %get-tuple-element.47), channel_id=1, source_target_pairs={{0,4},{1,5},{2,6},{3,7},{4,0},{5,1},{6,2},{7,3},{8,12},{9,13},{10,... | collective-permute-start | bytes 442376 | tf_op jit(solution)/shard_map/ppermute | solution.py:260
  35.3 1.3 %collective-permute-start.9 = (bf16[64,1152]{1,0:T(8,128)(2,1)S(1)}, bf16[64,1152]{1,0:T(8,128)(2,1)S(1)}, u32[]{:S(2)}, u32[]{:S(2)}) collective-permute-start(bf16[64,1152]{1,0:T(8,128)(2,1)S(1)} %get-tuple-element.48), channel_id=1, source_target_pairs={{0,6},{1,7},{2,4},{3,5},{4,2},{5,3},{6,0},{7,1},{8,14},{9,15},{10,... | collective-permute-start | bytes 442376 | tf_op jit(solution)/shard_map/ppermute | solution.py:260
  36.6 7.8 %collective-permute-done.11.refs_3_ = bf16[384,1152]{1,0:T(8,128)(2,1)S(1)} collective-permute-done((bf16[384,1152]{1,0:T(8,128)(2,1)S(1)}, bf16[384,1152]{1,0:T(8,128)(2,1)S(1)}, u32[]{:S(2)}, u32[]{:S(2)}) %collective-permute-start.11) | collective-permute-done | bytes 884768 | tf_op jit(solution)/shard_map/ppermute | solution.py:271
  44.4 0.2 shard_map.89.refs_0_
  44.5 0.0 collective-permute-done.7.refs_0_
  44.6 1.8 %collective-permute-done.8.refs_1_ = bf16[64,1152]{1,0:T(8,128)(2,1)S(1)} collective-permute-done((bf16[64,1152]{1,0:T(8,128)(2,1)S(1)}, bf16[64,1152]{1,0:T(8,128)(2,1)S(1)}, u32[]{:S(2)}, u32[]{:S(2)}) %collective-permute-start.8) | collective-permute-done | bytes 147488 | tf_op jit(solution)/shard_map/ppermute | solution.py:260
  46.4 0.0 collective-permute-done.9.refs_2_
  46.4 0.0 collective-permute-done.12
  46.4 0.2 shard_map.88
  46.6 0.1 collective-permute-start.13
  46.6 1.1 %collective-permute-start.14 = (bf16[64,1152]{1,0:T(8,128)(2,1)S(1)}, bf16[64,1152]{1,0:T(8,128)(2,1)S(1)}, u32[]{:S(2)}, u32[]{:S(2)}) collective-permute-start(bf16[64,1152]{1,0:T(8,128)(2,1)S(1)} %shard_map.88), channel_id=1, source_target_pairs={{0,8},{1,17},{2,10},{3,19},{4,12},{5,21},{6,14},{7,23},{8,0},{9,25... | collective-permute-start | bytes 442376 | tf_op jit(solution)/shard_map/ppermute | solution.py:271
  47.8 2.2 %collective-permute-start.18 = (bf16[64,1152]{1,0:T(8,128)(2,1)S(1)}, bf16[64,1152]{1,0:T(8,128)(2,1)S(1)}, u32[]{:S(2)}, u32[]{:S(2)}) collective-permute-start(bf16[64,1152]{1,0:T(8,128)(2,1)S(1)} %shard_map.88), channel_id=1, source_target_pairs={{0,2},{1,3},{2,0},{3,1},{4,6},{5,7},{6,4},{7,5},{8,10},{9,11},{10,... | collective-permute-start | bytes 442376 | tf_op jit(solution)/shard_map/ppermute | solution.py:260
  49.9 2.4 %collective-permute-start.17 = (bf16[64,1152]{1,0:T(8,128)(2,1)S(1)}, bf16[64,1152]{1,0:T(8,128)(2,1)S(1)}, u32[]{:S(2)}, u32[]{:S(2)}) collective-permute-start(bf16[64,1152]{1,0:T(8,128)(2,1)S(1)} %shard_map.88), channel_id=1, source_target_pairs={{0,6},{1,7},{2,4},{3,5},{4,2},{5,3},{6,0},{7,1},{8,14},{9,15},{10,... | collective-permute-start | bytes 442376 | tf_op jit(solution)/shard_map/ppermute | solution.py:260
  52.3 0.0 collective-permute-start.16
  52.3 0.0 collective-permute-done.14
  52.3 1.2 %collective-permute-start.15 = (bf16[128,1152]{1,0:T(8,128)(2,1)S(1)}, bf16[128,1152]{1,0:T(8,128)(2,1)S(1)}, u32[]{:S(2)}, u32[]{:S(2)}) collective-permute-start(bf16[128,1152]{1,0:T(8,128)(2,1)S(1)} %pad_maximum_fusion.5), channel_id=1, source_target_pairs={{0,16},{1,9},{2,18},{3,11},{4,20},{5,13},{6,22},{7,15},{8,24},{9,1... | collective-permute-start | bytes 884744 | tf_op jit(solution)/shard_map/ppermute | solution.py:271
  53.5 1.6 %fusion.1 = f32[64,1152]{1,0:T(8,128)} fusion(bf16[64,1152]{1,0:T(8,128)(2,1)S(1)} %shard_map.88, bf16[1152,1152]{1,0:T(8,128)(2,1)S(1)} %copy-done), kind=kOutput, calls=%fused_computation.10 | convolution fusion | flops 169869312 | bytes 3096576 | tf_op jit(solution)/shard_map/dot_general | solution.py:17
  55.2 1.2 %add.3 = f32[256,1152]{1,0:T(8,128)} add(f32[256,1152]{1,0:T(8,128)S(1)} %get-tuple-element.58, f32[256,1152]{1,0:T(8,128)S(1)} %collective-permute-done.12) | non-fusion elementwise | flops 294912 | bytes 3538944 | tf_op jit(solution)/shard_map/add | solution.py:311
  56.3 0.0 collective-permute-done.18
  56.3 1.5 %collective-permute-start.19 = (bf16[64,1152]{1,0:T(8,128)(2,1)S(1)}, bf16[64,1152]{1,0:T(8,128)(2,1)S(1)}, u32[]{:S(2)}, u32[]{:S(2)}) collective-permute-start(bf16[64,1152]{1,0:T(8,128)(2,1)S(1)} %collective-permute-done.18), channel_id=1, source_target_pairs={{0,8},{1,17},{2,10},{3,19},{4,12},{5,21},{6,14},{7,23},{8,0},{9,25... | collective-permute-start | bytes 442376 | tf_op jit(solution)/shard_map/ppermute | solution.py:271
  57.8 2.4 %collective-permute-done.17 = bf16[64,1152]{1,0:T(8,128)(2,1)S(1)} collective-permute-done((bf16[64,1152]{1,0:T(8,128)(2,1)S(1)}, bf16[64,1152]{1,0:T(8,128)(2,1)S(1)}, u32[]{:S(2)}, u32[]{:S(2)}) %collective-permute-start.17) | collective-permute-done | bytes 147488 | tf_op jit(solution)/shard_map/ppermute | solution.py:260
  60.2 5.2 %collective-permute-done.16 = bf16[64,1152]{1,0:T(8,128)(2,1)S(1)} collective-permute-done((bf16[64,1152]{1,0:T(8,128)(2,1)S(1)}, bf16[64,1152]{1,0:T(8,128)(2,1)S(1)}, u32[]{:S(2)}, u32[]{:S(2)}) %collective-permute-start.16) | collective-permute-done | bytes 147488 | tf_op jit(solution)/shard_map/ppermute | solution.py:260
  65.5 0.1 pad_maximum_fusion.1.refs_0_
  65.6 0.1 collective-permute-start.20
  65.7 1.0 %collective-permute-start.21 = (bf16[128,1152]{1,0:T(8,128)(2,1)S(1)}, bf16[128,1152]{1,0:T(8,128)(2,1)S(1)}, u32[]{:S(2)}, u32[]{:S(2)}) collective-permute-start(bf16[128,1152]{1,0:T(8,128)(2,1)S(1)} %pad_maximum_fusion.7), channel_id=1, source_target_pairs={{0,16},{1,9},{2,18},{3,11},{4,20},{5,13},{6,22},{7,15},{8,24},{9,1... | collective-permute-start | bytes 884744 | tf_op jit(solution)/shard_map/ppermute | solution.py:271
  66.6 1.0 %collective-permute-start.24 = (bf16[128,1152]{1,0:T(8,128)(2,1)S(1)}, bf16[128,1152]{1,0:T(8,128)(2,1)S(1)}, u32[]{:S(2)}, u32[]{:S(2)}) collective-permute-start(bf16[128,1152]{1,0:T(8,128)(2,1)S(1)} %pad_maximum_fusion.6), channel_id=1, source_target_pairs={{0,24},{1,25},{2,26},{3,27},{4,28},{5,29},{6,30},{7,31},{8,16},{9,... | collective-permute-start | bytes 884744 | tf_op jit(solution)/shard_map/ppermute | solution.py:282
  67.7 0.9 collective-permute-start.23
  68.5 1.6 %collective-permute-start.22 = (bf16[128,1152]{1,0:T(8,128)(2,1)S(1)}, bf16[128,1152]{1,0:T(8,128)(2,1)S(1)}, u32[]{:S(2)}, u32[]{:S(2)}) collective-permute-start(bf16[128,1152]{1,0:T(8,128)(2,1)S(1)} %pad_maximum_fusion.6), channel_id=1, source_target_pairs={{0,8},{1,17},{2,10},{3,19},{4,12},{5,21},{6,14},{7,23},{8,0},{9,25... | collective-permute-start | bytes 884744 | tf_op jit(solution)/shard_map/ppermute | solution.py:282
  70.1 10.3 %collective-permute-done.21 = bf16[128,1152]{1,0:T(8,128)(2,1)S(1)} collective-permute-done((bf16[128,1152]{1,0:T(8,128)(2,1)S(1)}, bf16[128,1152]{1,0:T(8,128)(2,1)S(1)}, u32[]{:S(2)}, u32[]{:S(2)}) %collective-permute-start.21) | collective-permute-done | bytes 294944 | tf_op jit(solution)/shard_map/ppermute | solution.py:271
  80.5 0.1 collective-permute-start.25
  80.6 1.3 %shard_map.90 = (bf16[1152,768]{1,0:T(8,128)(2,1)S(1)}, bf16[1152,1280]{1,0:T(8,128)(2,1)S(1)}) custom-call(bf16[1024,1152]{1,0:T(8,128)(2,1)S(1)} %shard_map.89.refs_0_, bf16[1024,1152]{1,0:T(8,128)(2,1)S(1)} %collective-permute-done.13.refs_1_), custom_call_target="tpu_custom_call" | custom-call | bytes 9437184 | tf_op jit(solution)/shard_map/pallas_call | solution.py:180
  81.8 2.5 %shard_map.91.acc = f32[1152,1152]{1,0:T(8,128)S(1)} custom-call(bf16[1152,768]{1,0:T(8,128)(2,1)S(1)} %get-tuple-element.61.x_t, bf16[384,1152]{1,0:T(8,128)(2,1)S(1)} %pad_maximum_fusion.1.refs_0_, bf16[384,1152]{1,0:T(8,128)(2,1)S(1)} %collective-permute-done.20.refs_1_), custom_call_target="tpu_custom_call" | custom-call | flops 2038431744 | bytes 8847360 | tf_op jit(solution)/shard_map/pallas_call | solution.py:236
  84.3 0.8 collective-permute-done.23.refs_2_
  85.1 0.5 collective-permute-start.27
  85.6 0.0 collective-permute-start.28
  85.6 1.1 %collective-permute-done.26.refs_5_ = bf16[128,1152]{1,0:T(8,128)(2,1)S(1)} collective-permute-done((bf16[128,1152]{1,0:T(8,128)(2,1)S(1)}, bf16[128,1152]{1,0:T(8,128)(2,1)S(1)}, u32[]{:S(2)}, u32[]{:S(2)}) %collective-permute-start.26) | collective-permute-done | bytes 294944 | tf_op jit(solution)/shard_map/ppermute | solution.py:263
  86.7 0.4 collective-permute-done.27.refs_6_
  87.1 0.4 collective-permute-done.28.refs_7_
  87.6 5.2 %shard_map.92 = f32[1152,1152]{1,0:T(8,128)} custom-call(bf16[1152,1280]{1,0:T(8,128)(2,1)S(1)} %get-tuple-element.60.x_t, f32[1152,1152]{1,0:T(8,128)S(1)} %shard_map.91.acc, bf16[256,1152]{1,0:T(8,128)(2,1)S(1)} %pad_maximum_fusion.2.refs_0_, bf16[128,1152]{1,0:T(8,128)(2,1)S(1)} %collective-permute-done.22.refs_1_, ...), custom_call_target="tpu_custom_call" | custom-call | flops 3397386240 | bytes 16515072 | tf_op jit(solution)/shard_map/pallas_call | solution.py:236
  (25 shorter events, 0.3 us)
Async XLA Ops:
  0.6 23.2 %copy-start = (bf16[1152,1152]{1,0:T(8,128)(2,1)S(1)}, bf16[1152,1152]{1,0:T(8,128)(2,1)}, u32[]{:S(2)}) copy-start(bf16[1152,1152]{1,0:T(8,128)(2,1)} %param.9) | copy-start | bytes 7962628
  0.6 21.5 %copy-start.2 = (bf16[1,64,1152]{2,1,0:T(8,128)(2,1)S(1)}, bf16[1,64,1152]{2,1,0:T(8,128)(2,1)}, u32[]{:S(2)}) copy-start(bf16[1,64,1152]{2,1,0:T(8,128)(2,1)} %param.6) | copy-start | bytes 442372
  0.7 7.5 %collective-permute-start = (bf16[64,1152]{1,0:T(8,128)(2,1)}, bf16[64,1152]{1,0:T(8,128)(2,1)S(1)}, u32[]{:S(2)}, u32[]{:S(2)}) collective-permute-start(bf16[64,1152]{1,0:T(8,128)(2,1)} %bitcast.8), channel_id=1, source_target_pairs={{0,2},{1,3},{2,0},{3,1},{4,6},{5,7},{6,4},{7,5},{8,10},{9,11},{10,... | collective-permute-start | bytes 442376 | tf_op jit(solution)/shard_map/ppermute | solution.py:260
  3.7 10.7 %collective-permute-start.2 = (bf16[64,1152]{1,0:T(8,128)(2,1)}, bf16[64,1152]{1,0:T(8,128)(2,1)S(1)}, u32[]{:S(2)}, u32[]{:S(2)}) collective-permute-start(bf16[64,1152]{1,0:T(8,128)(2,1)} %bitcast.9), channel_id=1, source_target_pairs={{0,6},{1,7},{2,4},{3,5},{4,2},{5,3},{6,0},{7,1},{8,14},{9,15},{10,... | collective-permute-start | bytes 442376 | tf_op jit(solution)/shard_map/ppermute | solution.py:260
  6.2 13.4 %collective-permute-start.1 = (bf16[64,1152]{1,0:T(8,128)(2,1)}, bf16[64,1152]{1,0:T(8,128)(2,1)S(1)}, u32[]{:S(2)}, u32[]{:S(2)}) collective-permute-start(bf16[64,1152]{1,0:T(8,128)(2,1)} %bitcast.10), channel_id=1, source_target_pairs={{0,4},{1,5},{2,6},{3,7},{4,0},{5,1},{6,2},{7,3},{8,12},{9,13},{10,... | collective-permute-start | bytes 442376 | tf_op jit(solution)/shard_map/ppermute | solution.py:260
  6.3 18.5 %collective-permute-start.3 = (s32[1,256]{1,0:T(1,128)}, s32[1,256]{1,0:T(1,128)S(1)}, u32[]{:S(2)}, u32[]{:S(2)}) collective-permute-start(s32[1,256]{1,0:T(1,128)} %refs_0_.1), channel_id=1, source_target_pairs={{0,1},{1,0},{2,3},{3,2},{4,5},{5,4},{6,7},{7,6},{8,9},{9,8},{10,11... | collective-permute-start | bytes 3080 | tf_op jit(solution)/shard_map/ppermute | solution.py:263
  6.3 18.5 %collective-permute-start.4 = (bf16[256,1152]{1,0:T(8,128)(2,1)}, bf16[256,1152]{1,0:T(8,128)(2,1)}, u32[]{:S(2)}, u32[]{:S(2)}) collective-permute-start(bf16[256,1152]{1,0:T(8,128)(2,1)} %bitcast.14), channel_id=1, source_target_pairs={{0,1},{1,0},{2,3},{3,2},{4,5},{5,4},{6,7},{7,6},{8,9},{9,8},{10,11... | collective-permute-start | bytes 1769480 | tf_op jit(solution)/shard_map/ppermute | solution.py:263
  8.2 14.0 %collective-permute-start.5 = (bf16[64,1152]{1,0:T(8,128)(2,1)}, bf16[64,1152]{1,0:T(8,128)(2,1)S(1)}, u32[]{:S(2)}, u32[]{:S(2)}) collective-permute-start(bf16[64,1152]{1,0:T(8,128)(2,1)} %bitcast.11), channel_id=1, source_target_pairs={{0,8},{1,17},{2,10},{3,19},{4,12},{5,21},{6,14},{7,23},{8,0},{9,25... | collective-permute-start | bytes 442376 | tf_op jit(solution)/shard_map/ppermute | solution.py:271
  19.7 11.5 %collective-permute-start.10 = (bf16[192,1152]{1,0:T(8,128)(2,1)S(1)}, bf16[192,1152]{1,0:T(8,128)(2,1)S(1)}, u32[]{:S(2)}, u32[]{:S(2)}) collective-permute-start(bf16[192,1152]{1,0:T(8,128)(2,1)S(1)} %pad_maximum_fusion.3), channel_id=1, source_target_pairs={{0,8},{1,17},{2,10},{3,19},{4,12},{5,21},{6,14},{7,23},{8,0},{9,25... | collective-permute-start | bytes 1327112 | tf_op jit(solution)/shard_map/ppermute | solution.py:271
  21.2 0.9 copy-start.1
  22.2 2.7 %copy-start.3 = (bf16[1,256,1152]{2,1,0:T(8,128)(2,1)S(1)}, bf16[1,256,1152]{2,1,0:T(8,128)(2,1)}, u32[]{:S(2)}) copy-start(bf16[1,256,1152]{2,1,0:T(8,128)(2,1)} %param.7) | copy-start | bytes 1769476
  22.2 2.7 %copy-start.4 = (s32[1,256]{1,0:T(1,128)S(1)}, s32[1,256]{1,0:T(1,128)}, u32[]{:S(2)}) copy-start(s32[1,256]{1,0:T(1,128)} %refs_0_.1) | copy-start | bytes 3076
  22.3 7.0 %collective-permute-start.6 = (bf16[128,1152]{1,0:T(8,128)(2,1)S(1)}, bf16[128,1152]{1,0:T(8,128)(2,1)S(1)}, u32[]{:S(2)}, u32[]{:S(2)}) collective-permute-start(bf16[128,1152]{1,0:T(8,128)(2,1)S(1)} %pad_maximum_fusion.4.refs_0_), channel_id=1, source_target_pairs={{0,16},{1,9},{2,18},{3,11},{4,20},{5,13},{6,22},{7,15},{8,24},{9,1... | collective-permute-start | bytes 884744 | tf_op jit(solution)/shard_map/ppermute | solution.py:271
  29.8 16.6 %collective-permute-start.12 = (f32[256,1152]{1,0:T(8,128)S(1)}, f32[256,1152]{1,0:T(8,128)S(1)}, u32[]{:S(2)}, u32[]{:S(2)}) collective-permute-start(f32[256,1152]{1,0:T(8,128)S(1)} %get-tuple-element.54), channel_id=1, source_target_pairs={{0,1},{1,0},{2,3},{3,2},{4,5},{5,4},{6,7},{7,6},{8,9},{9,8},{10,11... | collective-permute-start | bytes 3538952 | tf_op jit(solution)/shard_map/ppermute | solution.py:263
  31.3 13.1 %collective-permute-start.11 = (bf16[384,1152]{1,0:T(8,128)(2,1)S(1)}, bf16[384,1152]{1,0:T(8,128)(2,1)S(1)}, u32[]{:S(2)}, u32[]{:S(2)}) collective-permute-start(bf16[384,1152]{1,0:T(8,128)(2,1)S(1)} %pad_maximum_fusion.refs_2_), channel_id=1, source_target_pairs={{0,16},{1,9},{2,18},{3,11},{4,20},{5,13},{6,22},{7,15},{8,24},{9,1... | collective-permute-start | bytes 2654216 | tf_op jit(solution)/shard_map/ppermute | solution.py:271
  32.2 12.3 %collective-permute-start.7 = (bf16[64,1152]{1,0:T(8,128)(2,1)S(1)}, bf16[64,1152]{1,0:T(8,128)(2,1)S(1)}, u32[]{:S(2)}, u32[]{:S(2)}) collective-permute-start(bf16[64,1152]{1,0:T(8,128)(2,1)S(1)} %get-tuple-element.46), channel_id=1, source_target_pairs={{0,2},{1,3},{2,0},{3,1},{4,6},{5,7},{6,4},{7,5},{8,10},{9,11},{10,... | collective-permute-start | bytes 442376 | tf_op jit(solution)/shard_map/ppermute | solution.py:260
  32.2 14.2 %collective-permute-start.8 = (bf16[64,1152]{1,0:T(8,128)(2,1)S(1)}, bf16[64,1152]{1,0:T(8,128)(2,1)S(1)}, u32[]{:S(2)}, u32[]{:S(2)}) collective-permute-start(bf16[64,1152]{1,0:T(8,128)(2,1)S(1)} %get-tuple-element.47), channel_id=1, source_target_pairs={{0,4},{1,5},{2,6},{3,7},{4,0},{5,1},{6,2},{7,3},{8,12},{9,13},{10,... | collective-permute-start | bytes 442376 | tf_op jit(solution)/shard_map/ppermute | solution.py:260
  35.3 11.0 %collective-permute-start.9 = (bf16[64,1152]{1,0:T(8,128)(2,1)S(1)}, bf16[64,1152]{1,0:T(8,128)(2,1)S(1)}, u32[]{:S(2)}, u32[]{:S(2)}) collective-permute-start(bf16[64,1152]{1,0:T(8,128)(2,1)S(1)} %get-tuple-element.48), channel_id=1, source_target_pairs={{0,6},{1,7},{2,4},{3,5},{4,2},{5,3},{6,0},{7,1},{8,14},{9,15},{10,... | collective-permute-start | bytes 442376 | tf_op jit(solution)/shard_map/ppermute | solution.py:260
  46.6 18.9 %collective-permute-start.13 = (bf16[1024,1152]{1,0:T(8,128)(2,1)S(1)}, bf16[1024,1152]{1,0:T(8,128)(2,1)S(1)}, u32[]{:S(2)}, u32[]{:S(2)}) collective-permute-start(bf16[1024,1152]{1,0:T(8,128)(2,1)S(1)} %shard_map.89.refs_0_), channel_id=1, source_target_pairs={{0,1},{1,0},{2,3},{3,2},{4,5},{5,4},{6,7},{7,6},{8,9},{9,8},{10,11... | collective-permute-start | bytes 7077896 | tf_op jit(solution)/shard_map/ppermute | solution.py:263
  46.6 5.6 %collective-permute-start.14 = (bf16[64,1152]{1,0:T(8,128)(2,1)S(1)}, bf16[64,1152]{1,0:T(8,128)(2,1)S(1)}, u32[]{:S(2)}, u32[]{:S(2)}) collective-permute-start(bf16[64,1152]{1,0:T(8,128)(2,1)S(1)} %shard_map.88), channel_id=1, source_target_pairs={{0,8},{1,17},{2,10},{3,19},{4,12},{5,21},{6,14},{7,23},{8,0},{9,25... | collective-permute-start | bytes 442376 | tf_op jit(solution)/shard_map/ppermute | solution.py:271
  47.8 8.6 %collective-permute-start.18 = (bf16[64,1152]{1,0:T(8,128)(2,1)S(1)}, bf16[64,1152]{1,0:T(8,128)(2,1)S(1)}, u32[]{:S(2)}, u32[]{:S(2)}) collective-permute-start(bf16[64,1152]{1,0:T(8,128)(2,1)S(1)} %shard_map.88), channel_id=1, source_target_pairs={{0,2},{1,3},{2,0},{3,1},{4,6},{5,7},{6,4},{7,5},{8,10},{9,11},{10,... | collective-permute-start | bytes 442376 | tf_op jit(solution)/shard_map/ppermute | solution.py:260
  49.9 10.3 %collective-permute-start.17 = (bf16[64,1152]{1,0:T(8,128)(2,1)S(1)}, bf16[64,1152]{1,0:T(8,128)(2,1)S(1)}, u32[]{:S(2)}, u32[]{:S(2)}) collective-permute-start(bf16[64,1152]{1,0:T(8,128)(2,1)S(1)} %shard_map.88), channel_id=1, source_target_pairs={{0,6},{1,7},{2,4},{3,5},{4,2},{5,3},{6,0},{7,1},{8,14},{9,15},{10,... | collective-permute-start | bytes 442376 | tf_op jit(solution)/shard_map/ppermute | solution.py:260
  52.3 13.2 %collective-permute-start.16 = (bf16[64,1152]{1,0:T(8,128)(2,1)S(1)}, bf16[64,1152]{1,0:T(8,128)(2,1)S(1)}, u32[]{:S(2)}, u32[]{:S(2)}) collective-permute-start(bf16[64,1152]{1,0:T(8,128)(2,1)S(1)} %shard_map.88), channel_id=1, source_target_pairs={{0,4},{1,5},{2,6},{3,7},{4,0},{5,1},{6,2},{7,3},{8,12},{9,13},{10,... | collective-permute-start | bytes 442376 | tf_op jit(solution)/shard_map/ppermute | solution.py:260
  52.3 13.2 %collective-permute-start.15 = (bf16[128,1152]{1,0:T(8,128)(2,1)S(1)}, bf16[128,1152]{1,0:T(8,128)(2,1)S(1)}, u32[]{:S(2)}, u32[]{:S(2)}) collective-permute-start(bf16[128,1152]{1,0:T(8,128)(2,1)S(1)} %pad_maximum_fusion.5), channel_id=1, source_target_pairs={{0,16},{1,9},{2,18},{3,11},{4,20},{5,13},{6,22},{7,15},{8,24},{9,1... | collective-permute-start | bytes 884744 | tf_op jit(solution)/shard_map/ppermute | solution.py:271
  56.3 9.1 %collective-permute-start.19 = (bf16[64,1152]{1,0:T(8,128)(2,1)S(1)}, bf16[64,1152]{1,0:T(8,128)(2,1)S(1)}, u32[]{:S(2)}, u32[]{:S(2)}) collective-permute-start(bf16[64,1152]{1,0:T(8,128)(2,1)S(1)} %collective-permute-done.18), channel_id=1, source_target_pairs={{0,8},{1,17},{2,10},{3,19},{4,12},{5,21},{6,14},{7,23},{8,0},{9,25... | collective-permute-start | bytes 442376 | tf_op jit(solution)/shard_map/ppermute | solution.py:271
  65.6 16.3 %collective-permute-start.20 = (bf16[384,1152]{1,0:T(8,128)(2,1)S(1)}, bf16[384,1152]{1,0:T(8,128)(2,1)S(1)}, u32[]{:S(2)}, u32[]{:S(2)}) collective-permute-start(bf16[384,1152]{1,0:T(8,128)(2,1)S(1)} %pad_maximum_fusion.1.refs_0_), channel_id=1, source_target_pairs={{0,1},{1,0},{2,3},{3,2},{4,5},{5,4},{6,7},{7,6},{8,9},{9,8},{10,11... | collective-permute-start | bytes 2654216 | tf_op jit(solution)/shard_map/ppermute | solution.py:263
  65.7 14.7 %collective-permute-start.21 = (bf16[128,1152]{1,0:T(8,128)(2,1)S(1)}, bf16[128,1152]{1,0:T(8,128)(2,1)S(1)}, u32[]{:S(2)}, u32[]{:S(2)}) collective-permute-start(bf16[128,1152]{1,0:T(8,128)(2,1)S(1)} %pad_maximum_fusion.7), channel_id=1, source_target_pairs={{0,16},{1,9},{2,18},{3,11},{4,20},{5,13},{6,22},{7,15},{8,24},{9,1... | collective-permute-start | bytes 884744 | tf_op jit(solution)/shard_map/ppermute | solution.py:271
  66.6 17.7 %collective-permute-start.24 = (bf16[128,1152]{1,0:T(8,128)(2,1)S(1)}, bf16[128,1152]{1,0:T(8,128)(2,1)S(1)}, u32[]{:S(2)}, u32[]{:S(2)}) collective-permute-start(bf16[128,1152]{1,0:T(8,128)(2,1)S(1)} %pad_maximum_fusion.6), channel_id=1, source_target_pairs={{0,24},{1,25},{2,26},{3,27},{4,28},{5,29},{6,30},{7,31},{8,16},{9,... | collective-permute-start | bytes 884744 | tf_op jit(solution)/shard_map/ppermute | solution.py:282
  67.7 17.5 %collective-permute-start.23 = (bf16[128,1152]{1,0:T(8,128)(2,1)S(1)}, bf16[128,1152]{1,0:T(8,128)(2,1)S(1)}, u32[]{:S(2)}, u32[]{:S(2)}) collective-permute-start(bf16[128,1152]{1,0:T(8,128)(2,1)S(1)} %pad_maximum_fusion.6), channel_id=1, source_target_pairs={{0,16},{1,9},{2,18},{3,11},{4,20},{5,13},{6,22},{7,15},{8,24},{9,1... | collective-permute-start | bytes 884744 | tf_op jit(solution)/shard_map/ppermute | solution.py:282
  68.5 16.6 %collective-permute-start.22 = (bf16[128,1152]{1,0:T(8,128)(2,1)S(1)}, bf16[128,1152]{1,0:T(8,128)(2,1)S(1)}, u32[]{:S(2)}, u32[]{:S(2)}) collective-permute-start(bf16[128,1152]{1,0:T(8,128)(2,1)S(1)} %pad_maximum_fusion.6), channel_id=1, source_target_pairs={{0,8},{1,17},{2,10},{3,19},{4,12},{5,21},{6,14},{7,23},{8,0},{9,25... | collective-permute-start | bytes 884744 | tf_op jit(solution)/shard_map/ppermute | solution.py:282
  80.5 5.2 %collective-permute-start.25 = (bf16[256,1152]{1,0:T(8,128)(2,1)S(1)}, bf16[256,1152]{1,0:T(8,128)(2,1)S(1)}, u32[]{:S(2)}, u32[]{:S(2)}) collective-permute-start(bf16[256,1152]{1,0:T(8,128)(2,1)S(1)} %pad_maximum_fusion.2.refs_0_), channel_id=1, source_target_pairs={{0,1},{1,0},{2,3},{3,2},{4,5},{5,4},{6,7},{7,6},{8,9},{9,8},{10,11... | collective-permute-start | bytes 1769480 | tf_op jit(solution)/shard_map/ppermute | solution.py:263
  85.1 1.6 %collective-permute-start.26 = (bf16[128,1152]{1,0:T(8,128)(2,1)S(1)}, bf16[128,1152]{1,0:T(8,128)(2,1)S(1)}, u32[]{:S(2)}, u32[]{:S(2)}) collective-permute-start(bf16[128,1152]{1,0:T(8,128)(2,1)S(1)} %collective-permute-done.22.refs_1_), channel_id=1, source_target_pairs={{0,1},{1,0},{2,3},{3,2},{4,5},{5,4},{6,7},{7,6},{8,9},{9,8},{10,11... | collective-permute-start | bytes 884744 | tf_op jit(solution)/shard_map/ppermute | solution.py:263
  85.1 2.0 %collective-permute-start.27 = (bf16[128,1152]{1,0:T(8,128)(2,1)S(1)}, bf16[128,1152]{1,0:T(8,128)(2,1)S(1)}, u32[]{:S(2)}, u32[]{:S(2)}) collective-permute-start(bf16[128,1152]{1,0:T(8,128)(2,1)S(1)} %collective-permute-done.23.refs_2_), channel_id=1, source_target_pairs={{0,1},{1,0},{2,3},{3,2},{4,5},{5,4},{6,7},{7,6},{8,9},{9,8},{10,11... | collective-permute-start | bytes 884744 | tf_op jit(solution)/shard_map/ppermute | solution.py:263
  85.6 1.9 %collective-permute-start.28 = (bf16[128,1152]{1,0:T(8,128)(2,1)S(1)}, bf16[128,1152]{1,0:T(8,128)(2,1)S(1)}, u32[]{:S(2)}, u32[]{:S(2)}) collective-permute-start(bf16[128,1152]{1,0:T(8,128)(2,1)S(1)} %collective-permute-done.24.refs_3_), channel_id=1, source_target_pairs={{0,1},{1,0},{2,3},{3,2},{4,5},{5,4},{6,7},{7,6},{8,9},{9,8},{10,11... | collective-permute-start | bytes 884744 | tf_op jit(solution)/shard_map/ppermute | solution.py:263

commit v9 on v8

--- a/solution.py
+++ b/solution.py
@@ -270,17 +270,6 @@
                 perm.append((j * nb + m, to * nb + m))
         return lax.ppermute(v, ("dp", "blk"), perm)
 
-    def direct_d(v, chunk):
-        perm = []
-        for j in range(nd):
-            for m in range(nb):
-                to = j
-                for i in range(bits):
-                    if chunk >> i & 1:
-                        to ^= 1 << ((i + m % 2) % bits)
-                perm.append((j * nb + m, to * nb + m))
-        return lax.ppermute(v, ("dp", "blk"), perm)
-
     def over_d(v, first, *before):
         v = [v, first]
         for i in range(1, bits):
@@ -290,9 +279,9 @@
 
     half = nz // 2
     xs = [x] + [along_z(x, k) for k in range(1, nz)]
-    x_own = over_d(x, step_d(after(x, xs[1]), 0))
-    x_rest = jnp.concatenate(xs[1:])
-    embed = dot(joined(after(xs, x)), weight)
+    x_own = joined(xs)
+    x_first = step_d(x_own, 0)
+    embed = dot(x_own, weight)
     row = lax.broadcasted_iota(jnp.int32, (16, 128), 0)
     both = jnp.where(row < 8, scale, offset)
     own, u, inv_norm, unit, dlogit, *sent = scores(
@@ -302,23 +291,17 @@
         [labels, swap(labels)],
         [captions, swap(captions)],
     )
-    sent = after(sent, x_own)
+    x_own = [x_own, after(x_first, sent)]
+    for i in range(1, bits):
+        x_own = joined(x_own)
+        x_own = [x_own, step_d(x_own, i)]
+    sent = after(sent, x_own[0])
     back = [along_z(v, k + 1) for k, v in enumerate(sent)]
-    x_rest = after(x_rest, x)
-    x_rest = over_d(x_rest, after(step_d(x_rest, 0), sent))
-    adjoint, adjoint_other = caption_sums(both, after(dlogit, sent), unit)
-    adjoint_other = swap(adjoint_other)
-    adjoint = adjoint + adjoint_other
-    back = after(back, x_rest, adjoint_other)
+    back = after(back, x_own[0])
     ge = embed_grad(own, u, inv_norm, back)
     grad_features = dot(ge, weight, LAST)
 
     small = nd * nb * n_img <= 2048
-    x_other = []
-    if small:
-        x_all = joined(x_own + x_rest)
-        x_other = swap(after(x_all, ge))
-
     near = [along_z(ge, k) for k in range(1, half)]
     own_first = step_d(ge, 0)
     far = [along_z(ge, k) for k in range(half, nz)]
@@ -326,40 +309,48 @@
     near = after(jnp.concatenate(near), g_own[0], ge)
     near_first = step_d(near, 0)
     g_near = over_d(near, near_first)
-    far = after(jnp.concatenate(far), g_own[1], near_first, grad_features, adjoint, x_other)
-    g_far = [far] + [direct_d(far, i) for i in range(1, nd)]
+    far = after(jnp.concatenate(far), g_own[1], near_first, grad_features)
+    far_first = step_d(far, 0)
+    adjoint, adjoint_other = caption_sums(both, after(dlogit, far_first), unit)
+    adjoint = adjoint + swap(adjoint_other)
     sizes = [n_img, n_img * (half - 1), n_img * half]
-    n_rest = sizes[1] + sizes[2]
+    n_own = nz * n_img
     per = nd // 2
     if small:
+        x_all = joined(x_own)
+        x_other = swap(after(x_all, far))
         plan = [[], []]
         for core in range(2):
-            rest = [n_img * nd + i * n_rest for i in range(nd)]
-            far_runs = [(core, at + sizes[1], sizes[2]) for at in rest]
-            plan[0] += [[(core, 0, n_img * nd)], far_runs[:1]]
-            plan[1] += [[(core, at, sizes[1]) for at in rest], far_runs[1:]]
+            at = 0
+            for g, size in enumerate(sizes):
+                runs = [(core, i * n_own + at, size) for i in range(nd)]
+                if g < 2:
+                    plan[0].append(runs)
+                else:
+                    plan[0].append(runs[:per])
+                    plan[1].append(runs[per:])
+                at += size
         x_early, x_late = turned([x_all, x_other], plan)
-        early = jnp.concatenate(g_own + g_far[:1])
-        early_swapped = swap(early)
-        acc = weight_sum(None, x_early, [early, early_swapped])
-        before_late = (x_early, grad_features, adjoint)
-        late = [after(v, acc) for v in g_far[1:]]
-        g_near = jnp.concatenate(g_near)
-        late = [g_near] + late + [swap(g_near)] + [swap(v) for v in late]
-        grad_weight = weight_sum(acc, x_late, late, 1.0 / nd)
+        g_two = [jnp.concatenate(g_own + g_near)]
+        g_two.append(swap(g_two[0]))
+        g_far = over_d(far, far_first, far_first)
+        early = [g_two[0], g_far[0], g_two[1], swap(g_far[0])]
+        acc = weight_sum(None, x_early, early)
+        late = after(g_far[1], acc, adjoint)
+        grad_weight = weight_sum(acc, x_late, [late, swap(late)], 1.0 / nd)
     else:
-        g_far = [jnp.concatenate(g_far[:per]), jnp.concatenate(g_far[per:])]
+        g_far = over_d(far, far_first)
         grad_weight = 0.0
-        for v, g in zip(x_own, g_own):
-            grad_weight = grad_weight + dot(v, g, FIRST)
-        for v, g, h in zip(x_rest, g_near, g_far):
-            for i in range(per):
+        for i, x_part in enumerate(x_own):
+            for at in range(per):
                 g_part = [
-                    g[i * sizes[1] : (i + 1) * sizes[1]],
-                    h[i * sizes[2] : (i + 1) * sizes[2]],
+                    g[i][at * m : (at + 1) * m]
+                    for m, g in zip(sizes, (g_own, g_near, g_far))
                 ]
                 grad_weight = grad_weight + dot(
-                    v[i * n_rest : (i + 1) * n_rest], jnp.concatenate(g_part), FIRST
+                    x_part[at * n_own : (at + 1) * n_own],
+                    jnp.concatenate(g_part),
+                    FIRST,
                 )
         grad_weight = (grad_weight + swap(grad_weight)) / nd
     return (grad_features[None], adjoint[None], grad_weight)

time: 93 us -> 90.4 us (0.972)
  starting transfers between devices: 30.6 us -> 25.5 us
  Pallas kernels: 12.2 us -> 13.5 us
  waiting for transfers between devices: 42.7 us -> 43.9 us
    ppermute x9, waiting for transfers between devices: 19.3 us -> 28.3 us  [along_z(): return lax.ppermute(v, 'blk', [(i, i ^ 2 * k) for i in range(nb)])]
    ppermute x8, waiting for transfers between devices: 20.6 us -> 12.1 us  [step_d(): return lax.ppermute(v, ('dp', 'blk'), perm)]
    ppermute x3 -> x0, starting transfers between devices: 3.49 us -> none  [direct_d(): return lax.ppermute(v, ('dp', 'blk'), perm)]
    ppermute x9 -> x7, waiting for transfers between devices: 1.92 us -> 3.48 us  [swap(): return lax.ppermute(v, 'blk', [(i, i ^ 1) for i in range(nb)])]
    ppermute x9 -> x7, starting transfers between devices: 2.07 us -> 0.79 us  [swap(): return lax.ppermute(v, 'blk', [(i, i ^ 1) for i in range(nb)])]
    pallas_call x2 -> x3, Pallas kernels: 0.21 us -> 1.36 us  [joined(): pl.pallas_call(join_kernel, out_shape=jax.ShapeDtypeStruct((rows, depth),...]
  transfers between devices with their start and end apart: 29 -> 24, of which waited for: 13 -> 12; matrix products, arithmetic and copies ran while one was open for 4% -> 5% of each run, Pallas kernels for 7% -> 10%
where the time goes in v9:
time: 90.4 us; the launch traced here: 90.1 us
  waiting for transfers between devices  43.9 us (49%)
  starting transfers between devices  25.5 us (28%)
  Pallas kernels  13.5 us (15%)
  matrix products  2.65 us (3%)
  between operations  2.14 us (2%)
  other arithmetic  1.38 us (2%)
  local copies, waits for them, and re-layouts  1 us (1%)
    ppermute x9, waiting for transfers between devices, along_z(): return lax.ppermute(v, 'blk', [(i, i ^ 2 * k) for i in range(nb)])  28.3 us
    ppermute x9, starting transfers between devices, along_z(): return lax.ppermute(v, 'blk', [(i, i ^ 2 * k) for i in range(nb)])  15.3 us
    ppermute x8, waiting for transfers between devices, step_d(): return lax.ppermute(v, ('dp', 'blk'), perm)  12.1 us
    ppermute x8, starting transfers between devices, step_d(): return lax.ppermute(v, ('dp', 'blk'), perm)  9.48 us
    pallas_call x2, Pallas kernels, weight_sum(): pl.pallas_call(kernel, out_shape=jax.ShapeDtypeStruct((depth, depth), F32...  7.85 us
    ppermute x7, waiting for transfers between devices, swap(): return lax.ppermute(v, 'blk', [(i, i ^ 1) for i in range(nb)])  3.48 us
    dot_general x2, matrix products, dot(): return lax.dot_general(a, b, dims, preferred_element_type=F32)  2.65 us
    pallas_call x1, Pallas kernels, scores(): pl.pallas_call(functools.partial(score_kernel, nz), out_shape=outs, in_sp...  2.3 us
  transfers between devices with their start and end apart: 24, of which 12 were waited for; matrix products, arithmetic and copies ran while one was open for 5% of the time, Pallas kernels for 10%

profile of v9, /device:TPU:0, one launch (start us, length us, event | category | flops | bytes accessed | tf_op | source)
XLA Modules:
  0.0 90.1 jit_solution(9116013224331240818)
XLA Ops:
  0.6 0.0 copy-start
  0.6 3.1 %collective-permute-start = (bf16[64,1152]{1,0:T(8,128)(2,1)}, bf16[64,1152]{1,0:T(8,128)(2,1)S(1)}, u32[]{:S(2)}, u32[]{:S(2)}) collective-permute-start(bf16[64,1152]{1,0:T(8,128)(2,1)} %bitcast.10), channel_id=1, source_target_pairs={{0,2},{1,3},{2,0},{3,1},{4,6},{5,7},{6,4},{7,5},{8,10},{9,11},{10,... | collective-permute-start | bytes 442376 | tf_op jit(solution)/shard_map/ppermute | solution.py:260
  3.7 2.6 %collective-permute-start.1 = (bf16[64,1152]{1,0:T(8,128)(2,1)}, bf16[64,1152]{1,0:T(8,128)(2,1)S(1)}, u32[]{:S(2)}, u32[]{:S(2)}) collective-permute-start(bf16[64,1152]{1,0:T(8,128)(2,1)} %bitcast.11), channel_id=1, source_target_pairs={{0,4},{1,5},{2,6},{3,7},{4,0},{5,1},{6,2},{7,3},{8,12},{9,13},{10,... | collective-permute-start | bytes 442376 | tf_op jit(solution)/shard_map/ppermute | solution.py:260
  6.3 0.0 collective-permute-start.2
  6.3 0.0 collective-permute-start.4
  6.3 3.5 %collective-permute-done.refs_1_ = bf16[64,1152]{1,0:T(8,128)(2,1)S(1)} collective-permute-done((bf16[64,1152]{1,0:T(8,128)(2,1)}, bf16[64,1152]{1,0:T(8,128)(2,1)S(1)}, u32[]{:S(2)}, u32[]{:S(2)}) %collective-permute-start) | collective-permute-done | bytes 147488 | tf_op jit(solution)/shard_map/ppermute | solution.py:260
  9.8 8.1 %collective-permute-done.1.refs_2_ = bf16[64,1152]{1,0:T(8,128)(2,1)S(1)} collective-permute-done((bf16[64,1152]{1,0:T(8,128)(2,1)}, bf16[64,1152]{1,0:T(8,128)(2,1)S(1)}, u32[]{:S(2)}, u32[]{:S(2)}) %collective-permute-start.1) | collective-permute-done | bytes 147488 | tf_op jit(solution)/shard_map/ppermute | solution.py:260
  17.9 0.0 collective-permute-done.2.refs_3_
  17.9 0.9 %copy-done.2 = bf16[1,64,1152]{2,1,0:T(8,128)(2,1)S(1)} copy-done((bf16[1,64,1152]{2,1,0:T(8,128)(2,1)S(1)}, bf16[1,64,1152]{2,1,0:T(8,128)(2,1)}, u32[]{:S(2)}) %copy-start.2) | copy-done | bytes 147480
  18.9 0.0 copy-start.3
  18.9 1.6 %collective-permute-start.5 = (bf16[256,1152]{1,0:T(8,128)(2,1)S(1)}, bf16[256,1152]{1,0:T(8,128)(2,1)}, u32[]{:S(2)}, u32[]{:S(2)}) collective-permute-start(bf16[256,1152]{1,0:T(8,128)(2,1)S(1)} %shard_map.85.refs_0_), channel_id=1, source_target_pairs={{0,8},{1,17},{2,10},{3,19},{4,12},{5,21},{6,14},{7,23},{8,0},{9,25... | collective-permute-start | bytes 1769480 | tf_op jit(solution)/shard_map/ppermute | solution.py:271
  20.5 0.0 collective-permute-start.3
  21.8 0.0 copy-start.1
  21.8 1.0 %fusion.embed = f32[256,1152]{1,0:T(8,128)S(1)} fusion(bf16[256,1152]{1,0:T(8,128)(2,1)S(1)} %shard_map.85.refs_0_, bf16[1152,1152]{1,0:T(8,128)(2,1)S(1)} %copy-done), kind=kOutput, calls=%fused_computation.6 | convolution fusion | flops 679477248 | bytes 4423680 | tf_op jit(solution)/shard_map/dot_general | solution.py:17
  22.8 0.0 collective-permute-done.3.refs_1_
  22.8 0.0 collective-permute-done.4.refs_3_
  22.8 0.1 iota.7.both
  22.9 2.3 %shard_map.86 = (f32[64,1152]{1,0:T(8,128)S(1)}, f32[64,1152]{1,0:T(8,128)S(1)}, f32[64,128]{1,0:T(8,128)S(1)}, bf16[256,1152]{1,0:T(8,128)(2,1)S(1)}, bf16[256,...) custom-call(f32[16,128]{1,0:T(8,128)S(1)} %iota.7.both, ...), custom_call_target="tpu_custom_call" | custom-call | flops 603979776 | bytes 4718592 | tf_op jit(solution)/shard_map/pallas_call | solution.py:74
  25.2 3.8 %collective-permute-done.5.refs_1_ = bf16[256,1152]{1,0:T(8,128)(2,1)} collective-permute-done((bf16[256,1152]{1,0:T(8,128)(2,1)S(1)}, bf16[256,1152]{1,0:T(8,128)(2,1)}, u32[]{:S(2)}, u32[]{:S(2)}) %collective-permute-start.5) | collective-permute-done | bytes 589856 | tf_op jit(solution)/shard_map/ppermute | solution.py:271
  29.0 1.1 %shard_map.87.refs_0_ = bf16[512,1152]{1,0:T(8,128)(2,1)S(1)} custom-call(bf16[256,1152]{1,0:T(8,128)(2,1)S(1)} %shard_map.85.refs_0_, bf16[256,1152]{1,0:T(8,128)(2,1)} %collective-permute-done.5.refs_1_), custom_call_target="tpu_custom_call" | custom-call | bytes 2359296 | tf_op jit(solution)/shard_map/pallas_call | solution.py:103
  30.1 1.6 %collective-permute-start.17 = (bf16[512,1152]{1,0:T(8,128)(2,1)S(1)}, bf16[512,1152]{1,0:T(8,128)(2,1)S(1)}, u32[]{:S(2)}, u32[]{:S(2)}) collective-permute-start(bf16[512,1152]{1,0:T(8,128)(2,1)S(1)} %shard_map.87.refs_0_), channel_id=1, source_target_pairs={{0,16},{1,9},{2,18},{3,11},{4,20},{5,13},{6,22},{7,15},{8,24},{9,1... | collective-permute-start | bytes 3538952 | tf_op jit(solution)/shard_map/ppermute | solution.py:271
  31.7 2.3 %collective-permute-start.6 = (bf16[64,1152]{1,0:T(8,128)(2,1)S(1)}, bf16[64,1152]{1,0:T(8,128)(2,1)S(1)}, u32[]{:S(2)}, u32[]{:S(2)}) collective-permute-start(bf16[64,1152]{1,0:T(8,128)(2,1)S(1)} %get-tuple-element.35), channel_id=1, source_target_pairs={{0,2},{1,3},{2,0},{3,1},{4,6},{5,7},{6,4},{7,5},{8,10},{9,11},{10,... | collective-permute-start | bytes 442376 | tf_op jit(solution)/shard_map/ppermute | solution.py:260
  34.0 1.0 %collective-permute-start.7 = (bf16[64,1152]{1,0:T(8,128)(2,1)S(1)}, bf16[64,1152]{1,0:T(8,128)(2,1)S(1)}, u32[]{:S(2)}, u32[]{:S(2)}) collective-permute-start(bf16[64,1152]{1,0:T(8,128)(2,1)S(1)} %get-tuple-element.36), channel_id=1, source_target_pairs={{0,4},{1,5},{2,6},{3,7},{4,0},{5,1},{6,2},{7,3},{8,12},{9,13},{10,... | collective-permute-start | bytes 442376 | tf_op jit(solution)/shard_map/ppermute | solution.py:260
  35.0 1.5 %collective-permute-start.8 = (bf16[64,1152]{1,0:T(8,128)(2,1)S(1)}, bf16[64,1152]{1,0:T(8,128)(2,1)S(1)}, u32[]{:S(2)}, u32[]{:S(2)}) collective-permute-start(bf16[64,1152]{1,0:T(8,128)(2,1)S(1)} %get-tuple-element.37), channel_id=1, source_target_pairs={{0,6},{1,7},{2,4},{3,5},{4,2},{5,3},{6,0},{7,1},{8,14},{9,15},{10,... | collective-permute-start | bytes 442376 | tf_op jit(solution)/shard_map/ppermute | solution.py:260
  36.5 1.6 %collective-permute-done.6.refs_0_ = bf16[64,1152]{1,0:T(8,128)(2,1)S(1)} collective-permute-done((bf16[64,1152]{1,0:T(8,128)(2,1)S(1)}, bf16[64,1152]{1,0:T(8,128)(2,1)S(1)}, u32[]{:S(2)}, u32[]{:S(2)}) %collective-permute-start.6) | collective-permute-done | bytes 147488 | tf_op jit(solution)/shard_map/ppermute | solution.py:260
  38.0 7.8 %collective-permute-done.7.refs_1_ = bf16[64,1152]{1,0:T(8,128)(2,1)S(1)} collective-permute-done((bf16[64,1152]{1,0:T(8,128)(2,1)S(1)}, bf16[64,1152]{1,0:T(8,128)(2,1)S(1)}, u32[]{:S(2)}, u32[]{:S(2)}) %collective-permute-start.7) | collective-permute-done | bytes 147488 | tf_op jit(solution)/shard_map/ppermute | solution.py:260
  45.8 0.0 collective-permute-done.8.refs_2_
  45.8 0.2 shard_map.88
  46.0 0.6 collective-permute-start.11
  46.6 2.1 %collective-permute-start.13 = (bf16[64,1152]{1,0:T(8,128)(2,1)S(1)}, bf16[64,1152]{1,0:T(8,128)(2,1)S(1)}, u32[]{:S(2)}, u32[]{:S(2)}) collective-permute-start(bf16[64,1152]{1,0:T(8,128)(2,1)S(1)} %shard_map.88), channel_id=1, source_target_pairs={{0,2},{1,3},{2,0},{3,1},{4,6},{5,7},{6,4},{7,5},{8,10},{9,11},{10,... | collective-permute-start | bytes 442376 | tf_op jit(solution)/shard_map/ppermute | solution.py:260
  48.8 2.7 %collective-permute-start.10 = (bf16[64,1152]{1,0:T(8,128)(2,1)S(1)}, bf16[64,1152]{1,0:T(8,128)(2,1)S(1)}, u32[]{:S(2)}, u32[]{:S(2)}) collective-permute-start(bf16[64,1152]{1,0:T(8,128)(2,1)S(1)} %shard_map.88), channel_id=1, source_target_pairs={{0,6},{1,7},{2,4},{3,5},{4,2},{5,3},{6,0},{7,1},{8,14},{9,15},{10,... | collective-permute-start | bytes 442376 | tf_op jit(solution)/shard_map/ppermute | solution.py:260
  51.5 0.0 collective-permute-start.9
  51.5 0.0 collective-permute-done.11
  51.5 1.6 %collective-permute-start.12 = (bf16[128,1152]{1,0:T(8,128)(2,1)S(1)}, bf16[128,1152]{1,0:T(8,128)(2,1)S(1)}, u32[]{:S(2)}, u32[]{:S(2)}) collective-permute-start(bf16[128,1152]{1,0:T(8,128)(2,1)S(1)} %pad_maximum_fusion.3), channel_id=1, source_target_pairs={{0,16},{1,9},{2,18},{3,11},{4,20},{5,13},{6,22},{7,15},{8,24},{9,1... | collective-permute-start | bytes 884744 | tf_op jit(solution)/shard_map/ppermute | solution.py:271
  53.1 1.7 %fusion.1 = f32[64,1152]{1,0:T(8,128)} fusion(bf16[64,1152]{1,0:T(8,128)(2,1)S(1)} %shard_map.88, bf16[1152,1152]{1,0:T(8,128)(2,1)S(1)} %copy-done), kind=kOutput, calls=%fused_computation.7 | convolution fusion | flops 169869312 | bytes 3096576 | tf_op jit(solution)/shard_map/dot_general | solution.py:17
  54.7 0.0 collective-permute-done.13
  54.7 1.4 %collective-permute-start.14 = (bf16[64,1152]{1,0:T(8,128)(2,1)S(1)}, bf16[64,1152]{1,0:T(8,128)(2,1)S(1)}, u32[]{:S(2)}, u32[]{:S(2)}) collective-permute-start(bf16[64,1152]{1,0:T(8,128)(2,1)S(1)} %collective-permute-done.13), channel_id=1, source_target_pairs={{0,8},{1,17},{2,10},{3,19},{4,12},{5,21},{6,14},{7,23},{8,0},{9,25... | collective-permute-start | bytes 442376 | tf_op jit(solution)/shard_map/ppermute | solution.py:271
  56.2 3.2 %collective-permute-done.10 = bf16[64,1152]{1,0:T(8,128)(2,1)S(1)} collective-permute-done((bf16[64,1152]{1,0:T(8,128)(2,1)S(1)}, bf16[64,1152]{1,0:T(8,128)(2,1)S(1)}, u32[]{:S(2)}, u32[]{:S(2)}) %collective-permute-start.10) | collective-permute-done | bytes 147488 | tf_op jit(solution)/shard_map/ppermute | solution.py:260
  59.4 4.1 %collective-permute-done.9 = bf16[64,1152]{1,0:T(8,128)(2,1)S(1)} collective-permute-done((bf16[64,1152]{1,0:T(8,128)(2,1)S(1)}, bf16[64,1152]{1,0:T(8,128)(2,1)S(1)}, u32[]{:S(2)}, u32[]{:S(2)}) %collective-permute-start.9) | collective-permute-done | bytes 147488 | tf_op jit(solution)/shard_map/ppermute | solution.py:260
  63.5 0.0 collective-permute-done.14
  63.6 0.0 collective-permute-done.12
  63.6 0.0 collective-permute-done.17.refs_1_
  63.6 0.2 shard_map.90.refs_0_
  63.8 0.1 collective-permute-start.18
  63.8 0.9 collective-permute-start.15
  64.7 1.2 %collective-permute-start.19 = (bf16[128,1152]{1,0:T(8,128)(2,1)S(1)}, bf16[128,1152]{1,0:T(8,128)(2,1)S(1)}, u32[]{:S(2)}, u32[]{:S(2)}) collective-permute-start(bf16[128,1152]{1,0:T(8,128)(2,1)S(1)} %pad_maximum_fusion.4), channel_id=1, source_target_pairs={{0,16},{1,9},{2,18},{3,11},{4,20},{5,13},{6,22},{7,15},{8,24},{9,1... | collective-permute-start | bytes 884744 | tf_op jit(solution)/shard_map/ppermute | solution.py:271
  65.9 7.7 %collective-permute-done.15 = bf16[128,1152]{1,0:T(8,128)(2,1)S(1)} collective-permute-done((bf16[128,1152]{1,0:T(8,128)(2,1)S(1)}, bf16[128,1152]{1,0:T(8,128)(2,1)S(1)}, u32[]{:S(2)}, u32[]{:S(2)}) %collective-permute-start.15) | collective-permute-done | bytes 294944 | tf_op jit(solution)/shard_map/ppermute | solution.py:271
  73.7 0.5 shard_map.89
  74.2 0.1 collective-permute-start.16
  74.3 0.0 collective-permute-done.19
  74.3 0.1 pad_maximum_fusion.refs_0_
  74.4 0.5 collective-permute-start.20
  75.0 0.1 collective-permute-start.21
  75.1 0.6 collective-permute-start.22
  75.7 1.4 %collective-permute-done.16 = f32[256,1152]{1,0:T(8,128)S(1)} collective-permute-done((f32[256,1152]{1,0:T(8,128)S(1)}, f32[256,1152]{1,0:T(8,128)S(1)}, u32[]{:S(2)}, u32[]{:S(2)}) %collective-permute-start.16) | collective-permute-done | bytes 1179680 | tf_op jit(solution)/shard_map/ppermute | solution.py:263
  77.1 1.2 %add.3 = f32[256,1152]{1,0:T(8,128)} add(f32[256,1152]{1,0:T(8,128)S(1)} %get-tuple-element.46, f32[256,1152]{1,0:T(8,128)S(1)} %collective-permute-done.16) | non-fusion elementwise | flops 294912 | bytes 3538944 | tf_op jit(solution)/shard_map/add | solution.py:315
  78.3 0.0 collective-permute-done.18.refs_1_
  78.3 1.3 %shard_map.91 = (bf16[1152,1536]{1,0:T(8,128)(2,1)S(1)}, bf16[1152,512]{1,0:T(8,128)(2,1)S(1)}) custom-call(bf16[1024,1152]{1,0:T(8,128)(2,1)S(1)} %shard_map.90.refs_0_, bf16[1024,1152]{1,0:T(8,128)(2,1)S(1)} %collective-permute-done.18.refs_1_), custom_call_target="tpu_custom_call" | custom-call | bytes 9437184 | tf_op jit(solution)/shard_map/pallas_call | solution.py:180
  79.6 0.1 collective-permute-done.21.refs_3_
  79.7 4.8 %shard_map.92.acc = f32[1152,1152]{1,0:T(8,128)S(1)} custom-call(bf16[1152,1536]{1,0:T(8,128)(2,1)S(1)} %get-tuple-element.50.x_t, bf16[512,1152]{1,0:T(8,128)(2,1)S(1)} %pad_maximum_fusion.refs_0_, bf16[256,1152]{1,0:T(8,128)(2,1)S(1)} %pad_maximum_fusion.1.refs_1_, bf16[512,1152]{1,0:T(8,128)(2,1)S(1)} %collective-permute-done.20.refs_2_, ...), custom_call_target="tpu_custom_call" | custom-call | flops 4076863488 | bytes 12386304 | tf_op jit(solution)/shard_map/pallas_call | solution.py:236
  84.4 0.6 collective-permute-done.22.refs_0_
  85.0 0.0 collective-permute-start.23
  85.0 2.0 %collective-permute-done.23.refs_1_ = bf16[256,1152]{1,0:T(8,128)(2,1)S(1)} collective-permute-done((bf16[256,1152]{1,0:T(8,128)(2,1)S(1)}, bf16[256,1152]{1,0:T(8,128)(2,1)S(1)}, u32[]{:S(2)}, u32[]{:S(2)}) %collective-permute-start.23) | collective-permute-done | bytes 589856 | tf_op jit(solution)/shard_map/ppermute | solution.py:263
  87.0 3.1 %shard_map.93 = f32[1152,1152]{1,0:T(8,128)} custom-call(bf16[1152,512]{1,0:T(8,128)(2,1)S(1)} %get-tuple-element.49.x_t, f32[1152,1152]{1,0:T(8,128)S(1)} %shard_map.92.acc, bf16[256,1152]{1,0:T(8,128)(2,1)S(1)} %collective-permute-done.22.refs_0_, bf16[256,1152]{1,0:T(8,128)(2,1)S(1)} %collective-permute-done.23.refs_1_), custom_call_target="tpu_custom_call" | custom-call | flops 1358954496 | bytes 12976128 | tf_op jit(solution)/shard_map/pallas_call | solution.py:236
  (11 shorter events, 0.2 us)
Async XLA Ops:
  0.6 21.2 %copy-start = (bf16[1152,1152]{1,0:T(8,128)(2,1)S(1)}, bf16[1152,1152]{1,0:T(8,128)(2,1)}, u32[]{:S(2)}) copy-start(bf16[1152,1152]{1,0:T(8,128)(2,1)} %param.9) | copy-start | bytes 7962628
  0.6 9.2 %collective-permute-start = (bf16[64,1152]{1,0:T(8,128)(2,1)}, bf16[64,1152]{1,0:T(8,128)(2,1)S(1)}, u32[]{:S(2)}, u32[]{:S(2)}) collective-permute-start(bf16[64,1152]{1,0:T(8,128)(2,1)} %bitcast.10), channel_id=1, source_target_pairs={{0,2},{1,3},{2,0},{3,1},{4,6},{5,7},{6,4},{7,5},{8,10},{9,11},{10,... | collective-permute-start | bytes 442376 | tf_op jit(solution)/shard_map/ppermute | solution.py:260
  3.7 14.2 %collective-permute-start.1 = (bf16[64,1152]{1,0:T(8,128)(2,1)}, bf16[64,1152]{1,0:T(8,128)(2,1)S(1)}, u32[]{:S(2)}, u32[]{:S(2)}) collective-permute-start(bf16[64,1152]{1,0:T(8,128)(2,1)} %bitcast.11), channel_id=1, source_target_pairs={{0,4},{1,5},{2,6},{3,7},{4,0},{5,1},{6,2},{7,3},{8,12},{9,13},{10,... | collective-permute-start | bytes 442376 | tf_op jit(solution)/shard_map/ppermute | solution.py:260
  6.3 11.6 %collective-permute-start.2 = (bf16[64,1152]{1,0:T(8,128)(2,1)}, bf16[64,1152]{1,0:T(8,128)(2,1)S(1)}, u32[]{:S(2)}, u32[]{:S(2)}) collective-permute-start(bf16[64,1152]{1,0:T(8,128)(2,1)} %bitcast.12), channel_id=1, source_target_pairs={{0,6},{1,7},{2,4},{3,5},{4,2},{5,3},{6,0},{7,1},{8,14},{9,15},{10,... | collective-permute-start | bytes 442376 | tf_op jit(solution)/shard_map/ppermute | solution.py:260
  6.3 16.5 %collective-permute-start.4 = (bf16[256,1152]{1,0:T(8,128)(2,1)}, bf16[256,1152]{1,0:T(8,128)(2,1)}, u32[]{:S(2)}, u32[]{:S(2)}) collective-permute-start(bf16[256,1152]{1,0:T(8,128)(2,1)} %bitcast.8), channel_id=1, source_target_pairs={{0,1},{1,0},{2,3},{3,2},{4,5},{5,4},{6,7},{7,6},{8,9},{9,8},{10,11... | collective-permute-start | bytes 1769480 | tf_op jit(solution)/shard_map/ppermute | solution.py:263
  17.9 0.9 %copy-start.2 = (bf16[1,64,1152]{2,1,0:T(8,128)(2,1)S(1)}, bf16[1,64,1152]{2,1,0:T(8,128)(2,1)}, u32[]{:S(2)}) copy-start(bf16[1,64,1152]{2,1,0:T(8,128)(2,1)} %param.6) | copy-start | bytes 442372
  18.9 4.0 %copy-start.3 = (s32[1,256]{1,0:T(1,128)S(1)}, s32[1,256]{1,0:T(1,128)}, u32[]{:S(2)}) copy-start(s32[1,256]{1,0:T(1,128)} %refs_0_.1) | copy-start | bytes 3076
  18.9 10.1 %collective-permute-start.5 = (bf16[256,1152]{1,0:T(8,128)(2,1)S(1)}, bf16[256,1152]{1,0:T(8,128)(2,1)}, u32[]{:S(2)}, u32[]{:S(2)}) collective-permute-start(bf16[256,1152]{1,0:T(8,128)(2,1)S(1)} %shard_map.85.refs_0_), channel_id=1, source_target_pairs={{0,8},{1,17},{2,10},{3,19},{4,12},{5,21},{6,14},{7,23},{8,0},{9,25... | collective-permute-start | bytes 1769480 | tf_op jit(solution)/shard_map/ppermute | solution.py:271
  20.5 2.3 %collective-permute-start.3 = (s32[1,256]{1,0:T(1,128)}, s32[1,256]{1,0:T(1,128)S(1)}, u32[]{:S(2)}, u32[]{:S(2)}) collective-permute-start(s32[1,256]{1,0:T(1,128)} %refs_0_.1), channel_id=1, source_target_pairs={{0,1},{1,0},{2,3},{3,2},{4,5},{5,4},{6,7},{7,6},{8,9},{9,8},{10,11... | collective-permute-start | bytes 3080 | tf_op jit(solution)/shard_map/ppermute | solution.py:263
  21.8 1.1 %copy-start.1 = (bf16[1,256,1152]{2,1,0:T(8,128)(2,1)S(1)}, bf16[1,256,1152]{2,1,0:T(8,128)(2,1)}, u32[]{:S(2)}) copy-start(bf16[1,256,1152]{2,1,0:T(8,128)(2,1)} %param.7) | copy-start | bytes 1769476
  30.1 33.5 %collective-permute-start.17 = (bf16[512,1152]{1,0:T(8,128)(2,1)S(1)}, bf16[512,1152]{1,0:T(8,128)(2,1)S(1)}, u32[]{:S(2)}, u32[]{:S(2)}) collective-permute-start(bf16[512,1152]{1,0:T(8,128)(2,1)S(1)} %shard_map.87.refs_0_), channel_id=1, source_target_pairs={{0,16},{1,9},{2,18},{3,11},{4,20},{5,13},{6,22},{7,15},{8,24},{9,1... | collective-permute-start | bytes 3538952 | tf_op jit(solution)/shard_map/ppermute | solution.py:271
  31.7 6.3 %collective-permute-start.6 = (bf16[64,1152]{1,0:T(8,128)(2,1)S(1)}, bf16[64,1152]{1,0:T(8,128)(2,1)S(1)}, u32[]{:S(2)}, u32[]{:S(2)}) collective-permute-start(bf16[64,1152]{1,0:T(8,128)(2,1)S(1)} %get-tuple-element.35), channel_id=1, source_target_pairs={{0,2},{1,3},{2,0},{3,1},{4,6},{5,7},{6,4},{7,5},{8,10},{9,11},{10,... | collective-permute-start | bytes 442376 | tf_op jit(solution)/shard_map/ppermute | solution.py:260
  34.0 11.8 %collective-permute-start.7 = (bf16[64,1152]{1,0:T(8,128)(2,1)S(1)}, bf16[64,1152]{1,0:T(8,128)(2,1)S(1)}, u32[]{:S(2)}, u32[]{:S(2)}) collective-permute-start(bf16[64,1152]{1,0:T(8,128)(2,1)S(1)} %get-tuple-element.36), channel_id=1, source_target_pairs={{0,4},{1,5},{2,6},{3,7},{4,0},{5,1},{6,2},{7,3},{8,12},{9,13},{10,... | collective-permute-start | bytes 442376 | tf_op jit(solution)/shard_map/ppermute | solution.py:260
  35.0 10.8 %collective-permute-start.8 = (bf16[64,1152]{1,0:T(8,128)(2,1)S(1)}, bf16[64,1152]{1,0:T(8,128)(2,1)S(1)}, u32[]{:S(2)}, u32[]{:S(2)}) collective-permute-start(bf16[64,1152]{1,0:T(8,128)(2,1)S(1)} %get-tuple-element.37), channel_id=1, source_target_pairs={{0,6},{1,7},{2,4},{3,5},{4,2},{5,3},{6,0},{7,1},{8,14},{9,15},{10,... | collective-permute-start | bytes 442376 | tf_op jit(solution)/shard_map/ppermute | solution.py:260
  46.0 5.4 %collective-permute-start.11 = (bf16[64,1152]{1,0:T(8,128)(2,1)S(1)}, bf16[64,1152]{1,0:T(8,128)(2,1)S(1)}, u32[]{:S(2)}, u32[]{:S(2)}) collective-permute-start(bf16[64,1152]{1,0:T(8,128)(2,1)S(1)} %shard_map.88), channel_id=1, source_target_pairs={{0,8},{1,17},{2,10},{3,19},{4,12},{5,21},{6,14},{7,23},{8,0},{9,25... | collective-permute-start | bytes 442376 | tf_op jit(solution)/shard_map/ppermute | solution.py:271
  46.6 8.1 %collective-permute-start.13 = (bf16[64,1152]{1,0:T(8,128)(2,1)S(1)}, bf16[64,1152]{1,0:T(8,128)(2,1)S(1)}, u32[]{:S(2)}, u32[]{:S(2)}) collective-permute-start(bf16[64,1152]{1,0:T(8,128)(2,1)S(1)} %shard_map.88), channel_id=1, source_target_pairs={{0,2},{1,3},{2,0},{3,1},{4,6},{5,7},{6,4},{7,5},{8,10},{9,11},{10,... | collective-permute-start | bytes 442376 | tf_op jit(solution)/shard_map/ppermute | solution.py:260
  48.8 10.6 %collective-permute-start.10 = (bf16[64,1152]{1,0:T(8,128)(2,1)S(1)}, bf16[64,1152]{1,0:T(8,128)(2,1)S(1)}, u32[]{:S(2)}, u32[]{:S(2)}) collective-permute-start(bf16[64,1152]{1,0:T(8,128)(2,1)S(1)} %shard_map.88), channel_id=1, source_target_pairs={{0,6},{1,7},{2,4},{3,5},{4,2},{5,3},{6,0},{7,1},{8,14},{9,15},{10,... | collective-permute-start | bytes 442376 | tf_op jit(solution)/shard_map/ppermute | solution.py:260
  51.5 12.1 %collective-permute-start.9 = (bf16[64,1152]{1,0:T(8,128)(2,1)S(1)}, bf16[64,1152]{1,0:T(8,128)(2,1)S(1)}, u32[]{:S(2)}, u32[]{:S(2)}) collective-permute-start(bf16[64,1152]{1,0:T(8,128)(2,1)S(1)} %shard_map.88), channel_id=1, source_target_pairs={{0,4},{1,5},{2,6},{3,7},{4,0},{5,1},{6,2},{7,3},{8,12},{9,13},{10,... | collective-permute-start | bytes 442376 | tf_op jit(solution)/shard_map/ppermute | solution.py:260
  51.5 12.1 %collective-permute-start.12 = (bf16[128,1152]{1,0:T(8,128)(2,1)S(1)}, bf16[128,1152]{1,0:T(8,128)(2,1)S(1)}, u32[]{:S(2)}, u32[]{:S(2)}) collective-permute-start(bf16[128,1152]{1,0:T(8,128)(2,1)S(1)} %pad_maximum_fusion.3), channel_id=1, source_target_pairs={{0,16},{1,9},{2,18},{3,11},{4,20},{5,13},{6,22},{7,15},{8,24},{9,1... | collective-permute-start | bytes 884744 | tf_op jit(solution)/shard_map/ppermute | solution.py:271
  54.7 8.8 %collective-permute-start.14 = (bf16[64,1152]{1,0:T(8,128)(2,1)S(1)}, bf16[64,1152]{1,0:T(8,128)(2,1)S(1)}, u32[]{:S(2)}, u32[]{:S(2)}) collective-permute-start(bf16[64,1152]{1,0:T(8,128)(2,1)S(1)} %collective-permute-done.13), channel_id=1, source_target_pairs={{0,8},{1,17},{2,10},{3,19},{4,12},{5,21},{6,14},{7,23},{8,0},{9,25... | collective-permute-start | bytes 442376 | tf_op jit(solution)/shard_map/ppermute | solution.py:271
  63.8 14.5 %collective-permute-start.18 = (bf16[1024,1152]{1,0:T(8,128)(2,1)S(1)}, bf16[1024,1152]{1,0:T(8,128)(2,1)S(1)}, u32[]{:S(2)}, u32[]{:S(2)}) collective-permute-start(bf16[1024,1152]{1,0:T(8,128)(2,1)S(1)} %shard_map.90.refs_0_), channel_id=1, source_target_pairs={{0,1},{1,0},{2,3},{3,2},{4,5},{5,4},{6,7},{7,6},{8,9},{9,8},{10,11... | collective-permute-start | bytes 7077896 | tf_op jit(solution)/shard_map/ppermute | solution.py:263
  63.8 9.8 %collective-permute-start.15 = (bf16[128,1152]{1,0:T(8,128)(2,1)S(1)}, bf16[128,1152]{1,0:T(8,128)(2,1)S(1)}, u32[]{:S(2)}, u32[]{:S(2)}) collective-permute-start(bf16[128,1152]{1,0:T(8,128)(2,1)S(1)} %pad_maximum_fusion.2), channel_id=1, source_target_pairs={{0,8},{1,17},{2,10},{3,19},{4,12},{5,21},{6,14},{7,23},{8,0},{9,25... | collective-permute-start | bytes 884744 | tf_op jit(solution)/shard_map/ppermute | solution.py:271
  64.7 9.5 %collective-permute-start.19 = (bf16[128,1152]{1,0:T(8,128)(2,1)S(1)}, bf16[128,1152]{1,0:T(8,128)(2,1)S(1)}, u32[]{:S(2)}, u32[]{:S(2)}) collective-permute-start(bf16[128,1152]{1,0:T(8,128)(2,1)S(1)} %pad_maximum_fusion.4), channel_id=1, source_target_pairs={{0,16},{1,9},{2,18},{3,11},{4,20},{5,13},{6,22},{7,15},{8,24},{9,1... | collective-permute-start | bytes 884744 | tf_op jit(solution)/shard_map/ppermute | solution.py:271
  74.2 2.9 %collective-permute-start.16 = (f32[256,1152]{1,0:T(8,128)S(1)}, f32[256,1152]{1,0:T(8,128)S(1)}, u32[]{:S(2)}, u32[]{:S(2)}) collective-permute-start(f32[256,1152]{1,0:T(8,128)S(1)} %get-tuple-element.47), channel_id=1, source_target_pairs={{0,1},{1,0},{2,3},{3,2},{4,5},{5,4},{6,7},{7,6},{8,9},{9,8},{10,11... | collective-permute-start | bytes 3538952 | tf_op jit(solution)/shard_map/ppermute | solution.py:263
  74.4 5.3 %collective-permute-start.20 = (bf16[512,1152]{1,0:T(8,128)(2,1)S(1)}, bf16[512,1152]{1,0:T(8,128)(2,1)S(1)}, u32[]{:S(2)}, u32[]{:S(2)}) collective-permute-start(bf16[512,1152]{1,0:T(8,128)(2,1)S(1)} %pad_maximum_fusion.refs_0_), channel_id=1, source_target_pairs={{0,1},{1,0},{2,3},{3,2},{4,5},{5,4},{6,7},{7,6},{8,9},{9,8},{10,11... | collective-permute-start | bytes 3538952 | tf_op jit(solution)/shard_map/ppermute | solution.py:263
  75.0 4.7 %collective-permute-start.21 = (bf16[256,1152]{1,0:T(8,128)(2,1)S(1)}, bf16[256,1152]{1,0:T(8,128)(2,1)S(1)}, u32[]{:S(2)}, u32[]{:S(2)}) collective-permute-start(bf16[256,1152]{1,0:T(8,128)(2,1)S(1)} %pad_maximum_fusion.1.refs_1_), channel_id=1, source_target_pairs={{0,1},{1,0},{2,3},{3,2},{4,5},{5,4},{6,7},{7,6},{8,9},{9,8},{10,11... | collective-permute-start | bytes 1769480 | tf_op jit(solution)/shard_map/ppermute | solution.py:263
  75.1 9.9 %collective-permute-start.22 = (bf16[256,1152]{1,0:T(8,128)(2,1)S(1)}, bf16[256,1152]{1,0:T(8,128)(2,1)S(1)}, u32[]{:S(2)}, u32[]{:S(2)}) collective-permute-start(bf16[256,1152]{1,0:T(8,128)(2,1)S(1)} %pad_maximum_fusion.1.refs_1_), channel_id=1, source_target_pairs={{0,16},{1,9},{2,18},{3,11},{4,20},{5,13},{6,22},{7,15},{8,24},{9,1... | collective-permute-start | bytes 1769480 | tf_op jit(solution)/shard_map/ppermute | solution.py:271
  85.0 2.0 %collective-permute-start.23 = (bf16[256,1152]{1,0:T(8,128)(2,1)S(1)}, bf16[256,1152]{1,0:T(8,128)(2,1)S(1)}, u32[]{:S(2)}, u32[]{:S(2)}) collective-permute-start(bf16[256,1152]{1,0:T(8,128)(2,1)S(1)} %collective-permute-done.22.refs_0_), channel_id=1, source_target_pairs={{0,1},{1,0},{2,3},{3,2},{4,5},{5,4},{6,7},{7,6},{8,9},{9,8},{10,11... | collective-permute-start | bytes 1769480 | tf_op jit(solution)/shard_map/ppermute | solution.py:263

commit v10 on v9

--- a/solution.py
+++ b/solution.py
@@ -280,7 +280,6 @@
     half = nz // 2
     xs = [x] + [along_z(x, k) for k in range(1, nz)]
     x_own = joined(xs)
-    x_first = step_d(x_own, 0)
     embed = dot(x_own, weight)
     row = lax.broadcasted_iota(jnp.int32, (16, 128), 0)
     both = jnp.where(row < 8, scale, offset)
@@ -291,13 +290,14 @@
         [labels, swap(labels)],
         [captions, swap(captions)],
     )
-    x_own = [x_own, after(x_first, sent)]
+    sent = sent
+    back = [along_z(v, k + 1) for k, v in enumerate(sent)]
+    x_first = step_d(after(x_own, sent), 0)
+    x_own = [x_own, after(x_first, back)]
     for i in range(1, bits):
         x_own = joined(x_own)
         x_own = [x_own, step_d(x_own, i)]
-    sent = after(sent, x_own[0])
-    back = [along_z(v, k + 1) for k, v in enumerate(sent)]
-    back = after(back, x_own[0])
+    back = back
     ge = embed_grad(own, u, inv_norm, back)
     grad_features = dot(ge, weight, LAST)
 
@@ -309,7 +309,7 @@
     near = after(jnp.concatenate(near), g_own[0], ge)
     near_first = step_d(near, 0)
     g_near = over_d(near, near_first)
-    far = after(jnp.concatenate(far), g_own[1], near_first, grad_features)
+    far = after(jnp.concatenate(far), near_first, g_own[1], grad_features)
     far_first = step_d(far, 0)
     adjoint, adjoint_other = caption_sums(both, after(dlogit, far_first), unit)
     adjoint = adjoint + swap(adjoint_other)
@@ -318,7 +318,7 @@
     per = nd // 2
     if small:
         x_all = joined(x_own)
-        x_other = swap(after(x_all, far))
+        x_other = swap(after(x_all, far_first))
         plan = [[], []]
         for core in range(2):
             at = 0

time: 90.4 us -> 93.1 us (1.030)
  waiting for transfers between devices: 43.9 us -> 49.3 us
  starting transfers between devices: 25.5 us -> 23.8 us
    ppermute x8, waiting for transfers between devices: 12.1 us -> 19.6 us  [step_d(): return lax.ppermute(v, ('dp', 'blk'), perm)]
    ppermute x8, starting transfers between devices: 9.48 us -> 7.08 us  [step_d(): return lax.ppermute(v, ('dp', 'blk'), perm)]
    ppermute x7, waiting for transfers between devices: 3.48 us -> 2.25 us  [swap(): return lax.ppermute(v, 'blk', [(i, i ^ 1) for i in range(nb)])]
  transfers between devices with their start and end apart: 24 -> 24, of which waited for: 12 -> 12; matrix products, arithmetic and copies ran while one was open for 5% -> 4% of each run, Pallas kernels for 10% -> 9%
where the time goes in v10:
time: 93.1 us; the launch traced here: 92.9 us
  waiting for transfers between devices  49.3 us (53%)
  starting transfers between devices  23.8 us (26%)
  Pallas kernels  12.6 us (14%)
  matrix products  2.65 us (3%)
  between operations  2.1 us (2%)
  other arithmetic  1.35 us (1%)
  local copies, waits for them, and re-layouts  1 us (1%)
    ppermute x9, waiting for transfers between devices, along_z(): return lax.ppermute(v, 'blk', [(i, i ^ 2 * k) for i in range(nb)])  27.5 us
    ppermute x8, waiting for transfers between devices, step_d(): return lax.ppermute(v, ('dp', 'blk'), perm)  19.6 us
    ppermute x9, starting transfers between devices, along_z(): return lax.ppermute(v, 'blk', [(i, i ^ 2 * k) for i in range(nb)])  15.3 us
    pallas_call x2, Pallas kernels, weight_sum(): pl.pallas_call(kernel, out_shape=jax.ShapeDtypeStruct((depth, depth), F32...  7.85 us
    ppermute x8, starting transfers between devices, step_d(): return lax.ppermute(v, ('dp', 'blk'), perm)  7.08 us
    dot_general x2, matrix products, dot(): return lax.dot_general(a, b, dims, preferred_element_type=F32)  2.65 us
    ppermute x7, waiting for transfers between devices, swap(): return lax.ppermute(v, 'blk', [(i, i ^ 1) for i in range(nb)])  2.25 us
  transfers between devices with their start and end apart: 24, of which 12 were waited for; matrix products, arithmetic and copies ran while one was open for 4% of the time, Pallas kernels for 9%

profile of v10, /device:TPU:0, one launch (start us, length us, event | category | flops | bytes accessed | tf_op | source)
XLA Modules:
  0.0 92.9 jit_solution(1414997658367823532)
XLA Ops:
  0.6 0.0 copy-start
  0.6 0.5 collective-permute-start.4
  1.2 2.7 %collective-permute-start = (bf16[64,1152]{1,0:T(8,128)(2,1)}, bf16[64,1152]{1,0:T(8,128)(2,1)S(1)}, u32[]{:S(2)}, u32[]{:S(2)}) collective-permute-start(bf16[64,1152]{1,0:T(8,128)(2,1)} %bitcast.10), channel_id=1, source_target_pairs={{0,2},{1,3},{2,0},{3,1},{4,6},{5,7},{6,4},{7,5},{8,10},{9,11},{10,... | collective-permute-start | bytes 442376 | tf_op jit(solution)/shard_map/ppermute | solution.py:260
  3.8 2.6 %collective-permute-start.1 = (bf16[64,1152]{1,0:T(8,128)(2,1)}, bf16[64,1152]{1,0:T(8,128)(2,1)S(1)}, u32[]{:S(2)}, u32[]{:S(2)}) collective-permute-start(bf16[64,1152]{1,0:T(8,128)(2,1)} %bitcast.11), channel_id=1, source_target_pairs={{0,4},{1,5},{2,6},{3,7},{4,0},{5,1},{6,2},{7,3},{8,12},{9,13},{10,... | collective-permute-start | bytes 442376 | tf_op jit(solution)/shard_map/ppermute | solution.py:260
  6.4 0.0 collective-permute-start.2
  6.4 0.0 collective-permute-start.3
  7.7 3.4 %collective-permute-done.refs_1_ = bf16[64,1152]{1,0:T(8,128)(2,1)S(1)} collective-permute-done((bf16[64,1152]{1,0:T(8,128)(2,1)}, bf16[64,1152]{1,0:T(8,128)(2,1)S(1)}, u32[]{:S(2)}, u32[]{:S(2)}) %collective-permute-start) | collective-permute-done | bytes 147488 | tf_op jit(solution)/shard_map/ppermute | solution.py:260
  11.1 6.8 %collective-permute-done.1.refs_2_ = bf16[64,1152]{1,0:T(8,128)(2,1)S(1)} collective-permute-done((bf16[64,1152]{1,0:T(8,128)(2,1)}, bf16[64,1152]{1,0:T(8,128)(2,1)S(1)}, u32[]{:S(2)}, u32[]{:S(2)}) %collective-permute-start.1) | collective-permute-done | bytes 147488 | tf_op jit(solution)/shard_map/ppermute | solution.py:260
  18.0 0.0 collective-permute-done.2.refs_3_
  18.0 0.9 copy-done.2
  18.9 1.0 %shard_map.85.refs_0_ = bf16[256,1152]{1,0:T(8,128)(2,1)S(1)} custom-call(bf16[64,1152]{1,0:T(8,128)(2,1)S(1)} %bitcast.13, bf16[64,1152]{1,0:T(8,128)(2,1)S(1)} %collective-permute-done.refs_1_, bf16[64,1152]{1,0:T(8,128)(2,1)S(1)} %collective-permute-done.1.refs_2_, bf16[64,1152]{1,0:T(8,128)(2,1)} %collective-permute-done.2.refs_3_), custom_call_target="tpu_custom_call" | custom-call | bytes 1179648 | tf_op jit(solution)/shard_map/pallas_call | solution.py:103
  19.9 0.0 copy-start.1
  19.9 0.0 copy-start.3
  19.9 1.0 %fusion.embed = f32[256,1152]{1,0:T(8,128)S(1)} fusion(bf16[256,1152]{1,0:T(8,128)(2,1)S(1)} %shard_map.85.refs_0_, bf16[1152,1152]{1,0:T(8,128)(2,1)S(1)} %copy-done), kind=kOutput, calls=%fused_computation.6 | convolution fusion | flops 679477248 | bytes 4423680 | tf_op jit(solution)/shard_map/dot_general | solution.py:17
  20.9 0.0 collective-permute-done.4.refs_3_
  20.9 0.1 iota.7.both
  21.0 1.6 %shard_map.86 = (f32[64,1152]{1,0:T(8,128)S(1)}, f32[64,1152]{1,0:T(8,128)S(1)}, f32[64,128]{1,0:T(8,128)S(1)}, bf16[256,1152]{1,0:T(8,128)(2,1)S(1)}, bf16[256,...) custom-call(f32[16,128]{1,0:T(8,128)S(1)} %iota.7.both, ...), custom_call_target="tpu_custom_call" | custom-call | flops 603979776 | bytes 4718592 | tf_op jit(solution)/shard_map/pallas_call | solution.py:74
  22.6 1.6 %collective-permute-start.16 = (bf16[256,1152]{1,0:T(8,128)(2,1)S(1)}, bf16[256,1152]{1,0:T(8,128)(2,1)S(1)}, u32[]{:S(2)}, u32[]{:S(2)}) collective-permute-start(bf16[256,1152]{1,0:T(8,128)(2,1)S(1)} %shard_map.85.refs_0_), channel_id=1, source_target_pairs={{0,8},{1,17},{2,10},{3,19},{4,12},{5,21},{6,14},{7,23},{8,0},{9,25... | collective-permute-start | bytes 1769480 | tf_op jit(solution)/shard_map/ppermute | solution.py:271
  24.1 3.1 %collective-permute-start.5 = (bf16[64,1152]{1,0:T(8,128)(2,1)S(1)}, bf16[64,1152]{1,0:T(8,128)(2,1)S(1)}, u32[]{:S(2)}, u32[]{:S(2)}) collective-permute-start(bf16[64,1152]{1,0:T(8,128)(2,1)S(1)} %get-tuple-element.26), channel_id=1, source_target_pairs={{0,2},{1,3},{2,0},{3,1},{4,6},{5,7},{6,4},{7,5},{8,10},{9,11},{10,... | collective-permute-start | bytes 442376 | tf_op jit(solution)/shard_map/ppermute | solution.py:260
  27.2 1.0 %collective-permute-start.6 = (bf16[64,1152]{1,0:T(8,128)(2,1)S(1)}, bf16[64,1152]{1,0:T(8,128)(2,1)S(1)}, u32[]{:S(2)}, u32[]{:S(2)}) collective-permute-start(bf16[64,1152]{1,0:T(8,128)(2,1)S(1)} %get-tuple-element.27), channel_id=1, source_target_pairs={{0,4},{1,5},{2,6},{3,7},{4,0},{5,1},{6,2},{7,3},{8,12},{9,13},{10,... | collective-permute-start | bytes 442376 | tf_op jit(solution)/shard_map/ppermute | solution.py:260
  28.2 1.5 %collective-permute-start.7 = (bf16[64,1152]{1,0:T(8,128)(2,1)S(1)}, bf16[64,1152]{1,0:T(8,128)(2,1)S(1)}, u32[]{:S(2)}, u32[]{:S(2)}) collective-permute-start(bf16[64,1152]{1,0:T(8,128)(2,1)S(1)} %get-tuple-element.28), channel_id=1, source_target_pairs={{0,6},{1,7},{2,4},{3,5},{4,2},{5,3},{6,0},{7,1},{8,14},{9,15},{10,... | collective-permute-start | bytes 442376 | tf_op jit(solution)/shard_map/ppermute | solution.py:260
  29.7 2.3 %collective-permute-done.5.refs_0_ = bf16[64,1152]{1,0:T(8,128)(2,1)S(1)} collective-permute-done((bf16[64,1152]{1,0:T(8,128)(2,1)S(1)}, bf16[64,1152]{1,0:T(8,128)(2,1)S(1)}, u32[]{:S(2)}, u32[]{:S(2)}) %collective-permute-start.5) | collective-permute-done | bytes 147488 | tf_op jit(solution)/shard_map/ppermute | solution.py:260
  31.9 8.7 %collective-permute-done.6.refs_1_ = bf16[64,1152]{1,0:T(8,128)(2,1)S(1)} collective-permute-done((bf16[64,1152]{1,0:T(8,128)(2,1)S(1)}, bf16[64,1152]{1,0:T(8,128)(2,1)S(1)}, u32[]{:S(2)}, u32[]{:S(2)}) %collective-permute-start.6) | collective-permute-done | bytes 147488 | tf_op jit(solution)/shard_map/ppermute | solution.py:260
  40.6 0.0 collective-permute-done.7.refs_2_
  40.6 0.2 shard_map.87
  40.8 1.1 %collective-permute-start.11 = (bf16[64,1152]{1,0:T(8,128)(2,1)S(1)}, bf16[64,1152]{1,0:T(8,128)(2,1)S(1)}, u32[]{:S(2)}, u32[]{:S(2)}) collective-permute-start(bf16[64,1152]{1,0:T(8,128)(2,1)S(1)} %shard_map.87), channel_id=1, source_target_pairs={{0,8},{1,17},{2,10},{3,19},{4,12},{5,21},{6,14},{7,23},{8,0},{9,25... | collective-permute-start | bytes 442376 | tf_op jit(solution)/shard_map/ppermute | solution.py:271
  42.0 0.0 collective-permute-done.16.refs_1_
  42.0 0.1 shard_map.89.refs_0_
  42.1 1.0 %collective-permute-start.17 = (bf16[512,1152]{1,0:T(8,128)(2,1)S(1)}, bf16[512,1152]{1,0:T(8,128)(2,1)S(1)}, u32[]{:S(2)}, u32[]{:S(2)}) collective-permute-start(bf16[512,1152]{1,0:T(8,128)(2,1)S(1)} %shard_map.89.refs_0_), channel_id=1, source_target_pairs={{0,16},{1,9},{2,18},{3,11},{4,20},{5,13},{6,22},{7,15},{8,24},{9,1... | collective-permute-start | bytes 3538952 | tf_op jit(solution)/shard_map/ppermute | solution.py:271
  43.0 2.1 %collective-permute-start.10 = (bf16[64,1152]{1,0:T(8,128)(2,1)S(1)}, bf16[64,1152]{1,0:T(8,128)(2,1)S(1)}, u32[]{:S(2)}, u32[]{:S(2)}) collective-permute-start(bf16[64,1152]{1,0:T(8,128)(2,1)S(1)} %shard_map.87), channel_id=1, source_target_pairs={{0,2},{1,3},{2,0},{3,1},{4,6},{5,7},{6,4},{7,5},{8,10},{9,11},{10,... | collective-permute-start | bytes 442376 | tf_op jit(solution)/shard_map/ppermute | solution.py:260
  45.2 0.9 %collective-permute-start.8 = (bf16[64,1152]{1,0:T(8,128)(2,1)S(1)}, bf16[64,1152]{1,0:T(8,128)(2,1)S(1)}, u32[]{:S(2)}, u32[]{:S(2)}) collective-permute-start(bf16[64,1152]{1,0:T(8,128)(2,1)S(1)} %shard_map.87), channel_id=1, source_target_pairs={{0,4},{1,5},{2,6},{3,7},{4,0},{5,1},{6,2},{7,3},{8,12},{9,13},{10,... | collective-permute-start | bytes 442376 | tf_op jit(solution)/shard_map/ppermute | solution.py:260
  46.1 1.5 %collective-permute-start.9 = (bf16[64,1152]{1,0:T(8,128)(2,1)S(1)}, bf16[64,1152]{1,0:T(8,128)(2,1)S(1)}, u32[]{:S(2)}, u32[]{:S(2)}) collective-permute-start(bf16[64,1152]{1,0:T(8,128)(2,1)S(1)} %shard_map.87), channel_id=1, source_target_pairs={{0,6},{1,7},{2,4},{3,5},{4,2},{5,3},{6,0},{7,1},{8,14},{9,15},{10,... | collective-permute-start | bytes 442376 | tf_op jit(solution)/shard_map/ppermute | solution.py:260
  47.6 0.1 collective-permute-done.11
  47.7 1.5 %collective-permute-start.13 = (bf16[128,1152]{1,0:T(8,128)(2,1)S(1)}, bf16[128,1152]{1,0:T(8,128)(2,1)S(1)}, u32[]{:S(2)}, u32[]{:S(2)}) collective-permute-start(bf16[128,1152]{1,0:T(8,128)(2,1)S(1)} %pad_maximum_fusion.3), channel_id=1, source_target_pairs={{0,16},{1,9},{2,18},{3,11},{4,20},{5,13},{6,22},{7,15},{8,24},{9,1... | collective-permute-start | bytes 884744 | tf_op jit(solution)/shard_map/ppermute | solution.py:271
  49.2 1.7 %fusion.1 = f32[64,1152]{1,0:T(8,128)} fusion(bf16[64,1152]{1,0:T(8,128)(2,1)S(1)} %shard_map.87, bf16[1152,1152]{1,0:T(8,128)(2,1)S(1)} %copy-done), kind=kOutput, calls=%fused_computation.7 | convolution fusion | flops 169869312 | bytes 3096576 | tf_op jit(solution)/shard_map/dot_general | solution.py:17
  50.9 0.0 collective-permute-done.10
  50.9 0.5 collective-permute-start.12
  51.4 6.2 %collective-permute-done.8 = bf16[64,1152]{1,0:T(8,128)(2,1)S(1)} collective-permute-done((bf16[64,1152]{1,0:T(8,128)(2,1)S(1)}, bf16[64,1152]{1,0:T(8,128)(2,1)S(1)}, u32[]{:S(2)}, u32[]{:S(2)}) %collective-permute-start.8) | collective-permute-done | bytes 147488 | tf_op jit(solution)/shard_map/ppermute | solution.py:260
  57.7 0.0 collective-permute-done.12
  57.7 5.9 %collective-permute-done.13 = bf16[128,1152]{1,0:T(8,128)(2,1)S(1)} collective-permute-done((bf16[128,1152]{1,0:T(8,128)(2,1)S(1)}, bf16[128,1152]{1,0:T(8,128)(2,1)S(1)}, u32[]{:S(2)}, u32[]{:S(2)}) %collective-permute-start.13) | collective-permute-done | bytes 294944 | tf_op jit(solution)/shard_map/ppermute | solution.py:271
  63.6 0.4 collective-permute-start.14
  64.0 0.0 collective-permute-done.17.refs_1_
  64.0 0.2 shard_map.90.refs_0_
  64.2 6.1 %collective-permute-done.14 = bf16[128,1152]{1,0:T(8,128)(2,1)S(1)} collective-permute-done((bf16[128,1152]{1,0:T(8,128)(2,1)S(1)}, bf16[128,1152]{1,0:T(8,128)(2,1)S(1)}, u32[]{:S(2)}, u32[]{:S(2)}) %collective-permute-start.14) | collective-permute-done | bytes 294944 | tf_op jit(solution)/shard_map/ppermute | solution.py:271
  70.3 0.0 collective-permute-start.18
  70.3 0.5 collective-permute-start.19
  70.8 0.5 shard_map.88
  71.4 0.3 collective-permute-start.15
  71.7 5.4 %collective-permute-done.19 = bf16[128,1152]{1,0:T(8,128)(2,1)S(1)} collective-permute-done((bf16[128,1152]{1,0:T(8,128)(2,1)S(1)}, bf16[128,1152]{1,0:T(8,128)(2,1)S(1)}, u32[]{:S(2)}, u32[]{:S(2)}) %collective-permute-start.19) | collective-permute-done | bytes 294944 | tf_op jit(solution)/shard_map/ppermute | solution.py:271
  77.1 0.1 pad_maximum_fusion.refs_0_
  77.2 0.1 collective-permute-start.20
  77.3 0.6 collective-permute-start.21
  77.9 0.4 collective-permute-start.22
  78.3 0.0 collective-permute-done.15
  78.3 1.1 %add.3 = f32[256,1152]{1,0:T(8,128)} add(f32[256,1152]{1,0:T(8,128)S(1)} %get-tuple-element.34, f32[256,1152]{1,0:T(8,128)S(1)} %collective-permute-done.15) | non-fusion elementwise | flops 294912 | bytes 3538944 | tf_op jit(solution)/shard_map/add | solution.py:315
  79.5 0.0 collective-permute-done.18.refs_1_
  79.5 1.3 %shard_map.91 = (bf16[1152,1536]{1,0:T(8,128)(2,1)S(1)}, bf16[1152,512]{1,0:T(8,128)(2,1)S(1)}) custom-call(bf16[1024,1152]{1,0:T(8,128)(2,1)S(1)} %shard_map.90.refs_0_, bf16[1024,1152]{1,0:T(8,128)(2,1)S(1)} %collective-permute-done.18.refs_1_), custom_call_target="tpu_custom_call" | custom-call | bytes 9437184 | tf_op jit(solution)/shard_map/pallas_call | solution.py:180
  80.7 0.2 collective-permute-done.21.refs_3_
  81.0 0.0 collective-permute-done.20.refs_2_
  81.0 4.8 %shard_map.92.acc = f32[1152,1152]{1,0:T(8,128)S(1)} custom-call(bf16[1152,1536]{1,0:T(8,128)(2,1)S(1)} %get-tuple-element.40.x_t, bf16[512,1152]{1,0:T(8,128)(2,1)S(1)} %pad_maximum_fusion.refs_0_, bf16[256,1152]{1,0:T(8,128)(2,1)S(1)} %pad_maximum_fusion.1.refs_1_, bf16[512,1152]{1,0:T(8,128)(2,1)S(1)} %collective-permute-done.20.refs_2_, ...), custom_call_target="tpu_custom_call" | custom-call | flops 4076863488 | bytes 12386304 | tf_op jit(solution)/shard_map/pallas_call | solution.py:236
  85.7 2.0 %collective-permute-done.22.refs_0_ = bf16[256,1152]{1,0:T(8,128)(2,1)S(1)} collective-permute-done((bf16[256,1152]{1,0:T(8,128)(2,1)S(1)}, bf16[256,1152]{1,0:T(8,128)(2,1)S(1)}, u32[]{:S(2)}, u32[]{:S(2)}) %collective-permute-start.22) | collective-permute-done | bytes 589856 | tf_op jit(solution)/shard_map/ppermute | solution.py:271
  87.8 0.0 collective-permute-start.23
  87.8 2.0 %collective-permute-done.23.refs_1_ = bf16[256,1152]{1,0:T(8,128)(2,1)S(1)} collective-permute-done((bf16[256,1152]{1,0:T(8,128)(2,1)S(1)}, bf16[256,1152]{1,0:T(8,128)(2,1)S(1)}, u32[]{:S(2)}, u32[]{:S(2)}) %collective-permute-start.23) | collective-permute-done | bytes 589856 | tf_op jit(solution)/shard_map/ppermute | solution.py:263
  89.8 3.1 %shard_map.93 = f32[1152,1152]{1,0:T(8,128)} custom-call(bf16[1152,512]{1,0:T(8,128)(2,1)S(1)} %get-tuple-element.39.x_t, f32[1152,1152]{1,0:T(8,128)S(1)} %shard_map.92.acc, bf16[256,1152]{1,0:T(8,128)(2,1)S(1)} %collective-permute-done.22.refs_0_, bf16[256,1152]{1,0:T(8,128)(2,1)S(1)} %collective-permute-done.23.refs_1_), custom_call_target="tpu_custom_call" | custom-call | flops 1358954496 | bytes 12976128 | tf_op jit(solution)/shard_map/pallas_call | solution.py:236
  (11 shorter events, 0.1 us)
Async XLA Ops:
  0.6 19.2 %copy-start = (bf16[1152,1152]{1,0:T(8,128)(2,1)S(1)}, bf16[1152,1152]{1,0:T(8,128)(2,1)}, u32[]{:S(2)}) copy-start(bf16[1152,1152]{1,0:T(8,128)(2,1)} %param.9) | copy-start | bytes 7962628
  0.6 20.3 %collective-permute-start.4 = (bf16[256,1152]{1,0:T(8,128)(2,1)}, bf16[256,1152]{1,0:T(8,128)(2,1)S(1)}, u32[]{:S(2)}, u32[]{:S(2)}) collective-permute-start(bf16[256,1152]{1,0:T(8,128)(2,1)} %bitcast.8), channel_id=1, source_target_pairs={{0,1},{1,0},{2,3},{3,2},{4,5},{5,4},{6,7},{7,6},{8,9},{9,8},{10,11... | collective-permute-start | bytes 1769480 | tf_op jit(solution)/shard_map/ppermute | solution.py:263
  1.2 10.0 %collective-permute-start = (bf16[64,1152]{1,0:T(8,128)(2,1)}, bf16[64,1152]{1,0:T(8,128)(2,1)S(1)}, u32[]{:S(2)}, u32[]{:S(2)}) collective-permute-start(bf16[64,1152]{1,0:T(8,128)(2,1)} %bitcast.10), channel_id=1, source_target_pairs={{0,2},{1,3},{2,0},{3,1},{4,6},{5,7},{6,4},{7,5},{8,10},{9,11},{10,... | collective-permute-start | bytes 442376 | tf_op jit(solution)/shard_map/ppermute | solution.py:260
  3.8 14.2 %collective-permute-start.1 = (bf16[64,1152]{1,0:T(8,128)(2,1)}, bf16[64,1152]{1,0:T(8,128)(2,1)S(1)}, u32[]{:S(2)}, u32[]{:S(2)}) collective-permute-start(bf16[64,1152]{1,0:T(8,128)(2,1)} %bitcast.11), channel_id=1, source_target_pairs={{0,4},{1,5},{2,6},{3,7},{4,0},{5,1},{6,2},{7,3},{8,12},{9,13},{10,... | collective-permute-start | bytes 442376 | tf_op jit(solution)/shard_map/ppermute | solution.py:260
  6.4 11.6 %collective-permute-start.2 = (bf16[64,1152]{1,0:T(8,128)(2,1)}, bf16[64,1152]{1,0:T(8,128)(2,1)}, u32[]{:S(2)}, u32[]{:S(2)}) collective-permute-start(bf16[64,1152]{1,0:T(8,128)(2,1)} %bitcast.12), channel_id=1, source_target_pairs={{0,6},{1,7},{2,4},{3,5},{4,2},{5,3},{6,0},{7,1},{8,14},{9,15},{10,... | collective-permute-start | bytes 442376 | tf_op jit(solution)/shard_map/ppermute | solution.py:260
  6.4 14.5 %collective-permute-start.3 = (s32[1,256]{1,0:T(1,128)}, s32[1,256]{1,0:T(1,128)S(1)}, u32[]{:S(2)}, u32[]{:S(2)}) collective-permute-start(s32[1,256]{1,0:T(1,128)} %refs_0_.1), channel_id=1, source_target_pairs={{0,1},{1,0},{2,3},{3,2},{4,5},{5,4},{6,7},{7,6},{8,9},{9,8},{10,11... | collective-permute-start | bytes 3080 | tf_op jit(solution)/shard_map/ppermute | solution.py:263
  18.0 0.9 copy-start.2
  19.9 1.1 %copy-start.1 = (bf16[1,256,1152]{2,1,0:T(8,128)(2,1)S(1)}, bf16[1,256,1152]{2,1,0:T(8,128)(2,1)}, u32[]{:S(2)}) copy-start(bf16[1,256,1152]{2,1,0:T(8,128)(2,1)} %param.7) | copy-start | bytes 1769476
  19.9 1.1 %copy-start.3 = (s32[1,256]{1,0:T(1,128)S(1)}, s32[1,256]{1,0:T(1,128)}, u32[]{:S(2)}) copy-start(s32[1,256]{1,0:T(1,128)} %refs_0_.1) | copy-start | bytes 3076
  22.6 19.4 %collective-permute-start.16 = (bf16[256,1152]{1,0:T(8,128)(2,1)S(1)}, bf16[256,1152]{1,0:T(8,128)(2,1)S(1)}, u32[]{:S(2)}, u32[]{:S(2)}) collective-permute-start(bf16[256,1152]{1,0:T(8,128)(2,1)S(1)} %shard_map.85.refs_0_), channel_id=1, source_target_pairs={{0,8},{1,17},{2,10},{3,19},{4,12},{5,21},{6,14},{7,23},{8,0},{9,25... | collective-permute-start | bytes 1769480 | tf_op jit(solution)/shard_map/ppermute | solution.py:271
  24.1 7.8 %collective-permute-start.5 = (bf16[64,1152]{1,0:T(8,128)(2,1)S(1)}, bf16[64,1152]{1,0:T(8,128)(2,1)S(1)}, u32[]{:S(2)}, u32[]{:S(2)}) collective-permute-start(bf16[64,1152]{1,0:T(8,128)(2,1)S(1)} %get-tuple-element.26), channel_id=1, source_target_pairs={{0,2},{1,3},{2,0},{3,1},{4,6},{5,7},{6,4},{7,5},{8,10},{9,11},{10,... | collective-permute-start | bytes 442376 | tf_op jit(solution)/shard_map/ppermute | solution.py:260
  27.2 13.4 %collective-permute-start.6 = (bf16[64,1152]{1,0:T(8,128)(2,1)S(1)}, bf16[64,1152]{1,0:T(8,128)(2,1)S(1)}, u32[]{:S(2)}, u32[]{:S(2)}) collective-permute-start(bf16[64,1152]{1,0:T(8,128)(2,1)S(1)} %get-tuple-element.27), channel_id=1, source_target_pairs={{0,4},{1,5},{2,6},{3,7},{4,0},{5,1},{6,2},{7,3},{8,12},{9,13},{10,... | collective-permute-start | bytes 442376 | tf_op jit(solution)/shard_map/ppermute | solution.py:260
  28.2 12.4 %collective-permute-start.7 = (bf16[64,1152]{1,0:T(8,128)(2,1)S(1)}, bf16[64,1152]{1,0:T(8,128)(2,1)S(1)}, u32[]{:S(2)}, u32[]{:S(2)}) collective-permute-start(bf16[64,1152]{1,0:T(8,128)(2,1)S(1)} %get-tuple-element.28), channel_id=1, source_target_pairs={{0,6},{1,7},{2,4},{3,5},{4,2},{5,3},{6,0},{7,1},{8,14},{9,15},{10,... | collective-permute-start | bytes 442376 | tf_op jit(solution)/shard_map/ppermute | solution.py:260
  40.8 6.9 %collective-permute-start.11 = (bf16[64,1152]{1,0:T(8,128)(2,1)S(1)}, bf16[64,1152]{1,0:T(8,128)(2,1)S(1)}, u32[]{:S(2)}, u32[]{:S(2)}) collective-permute-start(bf16[64,1152]{1,0:T(8,128)(2,1)S(1)} %shard_map.87), channel_id=1, source_target_pairs={{0,8},{1,17},{2,10},{3,19},{4,12},{5,21},{6,14},{7,23},{8,0},{9,25... | collective-permute-start | bytes 442376 | tf_op jit(solution)/shard_map/ppermute | solution.py:271
  42.1 22.0 %collective-permute-start.17 = (bf16[512,1152]{1,0:T(8,128)(2,1)S(1)}, bf16[512,1152]{1,0:T(8,128)(2,1)S(1)}, u32[]{:S(2)}, u32[]{:S(2)}) collective-permute-start(bf16[512,1152]{1,0:T(8,128)(2,1)S(1)} %shard_map.89.refs_0_), channel_id=1, source_target_pairs={{0,16},{1,9},{2,18},{3,11},{4,20},{5,13},{6,22},{7,15},{8,24},{9,1... | collective-permute-start | bytes 3538952 | tf_op jit(solution)/shard_map/ppermute | solution.py:271
  43.0 7.8 %collective-permute-start.10 = (bf16[64,1152]{1,0:T(8,128)(2,1)S(1)}, bf16[64,1152]{1,0:T(8,128)(2,1)S(1)}, u32[]{:S(2)}, u32[]{:S(2)}) collective-permute-start(bf16[64,1152]{1,0:T(8,128)(2,1)S(1)} %shard_map.87), channel_id=1, source_target_pairs={{0,2},{1,3},{2,0},{3,1},{4,6},{5,7},{6,4},{7,5},{8,10},{9,11},{10,... | collective-permute-start | bytes 442376 | tf_op jit(solution)/shard_map/ppermute | solution.py:260
  45.2 12.5 %collective-permute-start.8 = (bf16[64,1152]{1,0:T(8,128)(2,1)S(1)}, bf16[64,1152]{1,0:T(8,128)(2,1)S(1)}, u32[]{:S(2)}, u32[]{:S(2)}) collective-permute-start(bf16[64,1152]{1,0:T(8,128)(2,1)S(1)} %shard_map.87), channel_id=1, source_target_pairs={{0,4},{1,5},{2,6},{3,7},{4,0},{5,1},{6,2},{7,3},{8,12},{9,13},{10,... | collective-permute-start | bytes 442376 | tf_op jit(solution)/shard_map/ppermute | solution.py:260
  46.1 11.5 %collective-permute-start.9 = (bf16[64,1152]{1,0:T(8,128)(2,1)S(1)}, bf16[64,1152]{1,0:T(8,128)(2,1)S(1)}, u32[]{:S(2)}, u32[]{:S(2)}) collective-permute-start(bf16[64,1152]{1,0:T(8,128)(2,1)S(1)} %shard_map.87), channel_id=1, source_target_pairs={{0,6},{1,7},{2,4},{3,5},{4,2},{5,3},{6,0},{7,1},{8,14},{9,15},{10,... | collective-permute-start | bytes 442376 | tf_op jit(solution)/shard_map/ppermute | solution.py:260
  47.7 15.9 %collective-permute-start.13 = (bf16[128,1152]{1,0:T(8,128)(2,1)S(1)}, bf16[128,1152]{1,0:T(8,128)(2,1)S(1)}, u32[]{:S(2)}, u32[]{:S(2)}) collective-permute-start(bf16[128,1152]{1,0:T(8,128)(2,1)S(1)} %pad_maximum_fusion.3), channel_id=1, source_target_pairs={{0,16},{1,9},{2,18},{3,11},{4,20},{5,13},{6,22},{7,15},{8,24},{9,1... | collective-permute-start | bytes 884744 | tf_op jit(solution)/shard_map/ppermute | solution.py:271
  50.9 6.8 %collective-permute-start.12 = (bf16[64,1152]{1,0:T(8,128)(2,1)S(1)}, bf16[64,1152]{1,0:T(8,128)(2,1)S(1)}, u32[]{:S(2)}, u32[]{:S(2)}) collective-permute-start(bf16[64,1152]{1,0:T(8,128)(2,1)S(1)} %collective-permute-done.10), channel_id=1, source_target_pairs={{0,8},{1,17},{2,10},{3,19},{4,12},{5,21},{6,14},{7,23},{8,0},{9,25... | collective-permute-start | bytes 442376 | tf_op jit(solution)/shard_map/ppermute | solution.py:271
  63.6 6.7 %collective-permute-start.14 = (bf16[128,1152]{1,0:T(8,128)(2,1)S(1)}, bf16[128,1152]{1,0:T(8,128)(2,1)S(1)}, u32[]{:S(2)}, u32[]{:S(2)}) collective-permute-start(bf16[128,1152]{1,0:T(8,128)(2,1)S(1)} %pad_maximum_fusion.2), channel_id=1, source_target_pairs={{0,8},{1,17},{2,10},{3,19},{4,12},{5,21},{6,14},{7,23},{8,0},{9,25... | collective-permute-start | bytes 884744 | tf_op jit(solution)/shard_map/ppermute | solution.py:271
  70.3 9.2 %collective-permute-start.18 = (bf16[1024,1152]{1,0:T(8,128)(2,1)S(1)}, bf16[1024,1152]{1,0:T(8,128)(2,1)S(1)}, u32[]{:S(2)}, u32[]{:S(2)}) collective-permute-start(bf16[1024,1152]{1,0:T(8,128)(2,1)S(1)} %shard_map.90.refs_0_), channel_id=1, source_target_pairs={{0,1},{1,0},{2,3},{3,2},{4,5},{5,4},{6,7},{7,6},{8,9},{9,8},{10,11... | collective-permute-start | bytes 7077896 | tf_op jit(solution)/shard_map/ppermute | solution.py:263
  70.3 6.8 %collective-permute-start.19 = (bf16[128,1152]{1,0:T(8,128)(2,1)S(1)}, bf16[128,1152]{1,0:T(8,128)(2,1)S(1)}, u32[]{:S(2)}, u32[]{:S(2)}) collective-permute-start(bf16[128,1152]{1,0:T(8,128)(2,1)S(1)} %pad_maximum_fusion.4), channel_id=1, source_target_pairs={{0,16},{1,9},{2,18},{3,11},{4,20},{5,13},{6,22},{7,15},{8,24},{9,1... | collective-permute-start | bytes 884744 | tf_op jit(solution)/shard_map/ppermute | solution.py:271
  71.4 7.0 %collective-permute-start.15 = (f32[256,1152]{1,0:T(8,128)S(1)}, f32[256,1152]{1,0:T(8,128)S(1)}, u32[]{:S(2)}, u32[]{:S(2)}) collective-permute-start(f32[256,1152]{1,0:T(8,128)S(1)} %get-tuple-element.35), channel_id=1, source_target_pairs={{0,1},{1,0},{2,3},{3,2},{4,5},{5,4},{6,7},{7,6},{8,9},{9,8},{10,11... | collective-permute-start | bytes 3538952 | tf_op jit(solution)/shard_map/ppermute | solution.py:263
  77.2 3.8 %collective-permute-start.20 = (bf16[512,1152]{1,0:T(8,128)(2,1)S(1)}, bf16[512,1152]{1,0:T(8,128)(2,1)S(1)}, u32[]{:S(2)}, u32[]{:S(2)}) collective-permute-start(bf16[512,1152]{1,0:T(8,128)(2,1)S(1)} %pad_maximum_fusion.refs_0_), channel_id=1, source_target_pairs={{0,1},{1,0},{2,3},{3,2},{4,5},{5,4},{6,7},{7,6},{8,9},{9,8},{10,11... | collective-permute-start | bytes 3538952 | tf_op jit(solution)/shard_map/ppermute | solution.py:263
  77.3 3.6 %collective-permute-start.21 = (bf16[256,1152]{1,0:T(8,128)(2,1)S(1)}, bf16[256,1152]{1,0:T(8,128)(2,1)S(1)}, u32[]{:S(2)}, u32[]{:S(2)}) collective-permute-start(bf16[256,1152]{1,0:T(8,128)(2,1)S(1)} %pad_maximum_fusion.1.refs_1_), channel_id=1, source_target_pairs={{0,1},{1,0},{2,3},{3,2},{4,5},{5,4},{6,7},{7,6},{8,9},{9,8},{10,11... | collective-permute-start | bytes 1769480 | tf_op jit(solution)/shard_map/ppermute | solution.py:263
  77.9 9.9 %collective-permute-start.22 = (bf16[256,1152]{1,0:T(8,128)(2,1)S(1)}, bf16[256,1152]{1,0:T(8,128)(2,1)S(1)}, u32[]{:S(2)}, u32[]{:S(2)}) collective-permute-start(bf16[256,1152]{1,0:T(8,128)(2,1)S(1)} %pad_maximum_fusion.1.refs_1_), channel_id=1, source_target_pairs={{0,16},{1,9},{2,18},{3,11},{4,20},{5,13},{6,22},{7,15},{8,24},{9,1... | collective-permute-start | bytes 1769480 | tf_op jit(solution)/shard_map/ppermute | solution.py:271
  87.8 2.0 %collective-permute-start.23 = (bf16[256,1152]{1,0:T(8,128)(2,1)S(1)}, bf16[256,1152]{1,0:T(8,128)(2,1)S(1)}, u32[]{:S(2)}, u32[]{:S(2)}) collective-permute-start(bf16[256,1152]{1,0:T(8,128)(2,1)S(1)} %collective-permute-done.22.refs_0_), channel_id=1, source_target_pairs={{0,1},{1,0},{2,3},{3,2},{4,5},{5,4},{6,7},{7,6},{8,9},{9,8},{10,11... | collective-permute-start | bytes 1769480 | tf_op jit(solution)/shard_map/ppermute | solution.py:263

commit v11 on v6

--- a/solution.py
+++ b/solution.py
@@ -165,16 +165,18 @@
 
 def turn_kernel(plan, *refs):
     ins, outs = refs[: -len(plan)], refs[-len(plan) :]
-    for out, runs in zip(outs, plan):
+    for out, pieces in zip(outs, plan):
         col = 0
-        for i, at, size in runs:
-            out[:, col : col + size] = ins[i][at : at + size, :].T
-            col += size
+        for runs in pieces:
+            rows = [ins[i][at : at + size, :] for i, at, size in runs]
+            rows = jnp.concatenate(rows)
+            out[:, col : col + rows.shape[0]] = rows.T
+            col += rows.shape[0]
 
 
 def turned(xs, plan):
     depth = xs[0].shape[1]
-    images = [sum(size for _, _, size in runs) for runs in plan]
+    images = [sum(size for runs in pieces for _, _, size in runs) for pieces in plan]
     return pl.pallas_call(
         functools.partial(turn_kernel, plan),
         out_shape=[jax.ShapeDtypeStruct((depth, n), BF16) for n in images],
@@ -275,12 +277,18 @@
         return v
 
     half = nz // 2
-    xs = [x] + [along_z(x, k) for k in range(1, nz)]
-    x_near, x_far = jnp.concatenate(xs[1:half]), jnp.concatenate(xs[half:])
-    x_own = over_d(x, step_d(x, 0))
+
+    def over_z(vs):
+        out = list(vs)
+        for k in [*range(half, nz), *range(1, half)]:
+            out[k] = along_z(vs[k], k)
+        return out
+
+    xs = over_z([x] * nz)
+    x_near, x_far = jnp.concatenate(xs[:half]), jnp.concatenate(xs[half:])
     x_near_first = step_d(x_near, 0)
     x_far_first = step_d(x_far, 0)
-    embed = dot(jnp.concatenate(xs), weight)
+    embed = dot(joined(xs), weight)
     row = lax.broadcasted_iota(jnp.int32, (16, 128), 0)
     both = jnp.where(row < 8, scale, offset)
     own, u, inv_norm, unit, dlogit, *sent = scores(
@@ -290,8 +298,8 @@
         [labels, swap(labels)],
         [captions, swap(captions)],
     )
-    sent = after(sent, x_own)
-    back = [along_z(v, k + 1) for k, v in enumerate(sent)]
+    sent = sent
+    back = over_z([own] + sent)[1:]
 
     x_near = over_d(x_near, after(x_near_first, sent))
     x_far = over_d(x_far, after(x_far_first, sent))
@@ -299,11 +307,9 @@
     ge = embed_grad(own, u, inv_norm, back)
     grad_features = dot(ge, weight, LAST)
 
-    near = [along_z(ge, k) for k in range(1, half)]
-    own_first = step_d(ge, 0)
-    far = [along_z(ge, k) for k in range(half, nz)]
-
-    g_own = over_d(ge, own_first)
+    ges = over_z([ge] * nz)
+    near, far = ges[1:half], ges[half:]
+    g_own = over_d(ge, step_d(ge, 0))
     near = after(jnp.concatenate(near), g_own[0])
     near_first = step_d(near, 0)
     g_near = over_d(near, near_first)
@@ -312,14 +318,21 @@
     dlogit = after(dlogit, far_first)
     adjoint, adjoint_other = caption_sums(both, dlogit, unit)
     adjoint = adjoint + swap(adjoint_other)
+    per = nd // 2
     if nd * nb * n_img <= 2048:
-        x_all = [joined(x_own + x_near), joined(x_far)]
+        x_all = [joined(x_near), joined(x_far)]
         x_all += [swap(after(v, near)) for v in x_all]
-        n = n_img * nd
         plan = [[], []]
-        for core in (0, 2):
-            plan[0] += [(core, 0, n), (core, n, n), (core + 1, 0, n)]
-            plan[1] += [(core + 1, n, n)]
+        n = half * n_img
+        for core in range(2):
+            near_at = [(2 * core, i * n) for i in range(nd)]
+            far_runs = [(2 * core + 1, i * n, n) for i in range(nd)]
+            plan[0] += [
+                [(i, at, n_img) for i, at in near_at],
+                [(i, at + n_img, n - n_img) for i, at in near_at],
+                far_runs[:per],
+            ]
+            plan[1] += [far_runs[per:]]
         x_early, x_late = turned(x_all, plan)
         g_own = jnp.concatenate(g_own)
         own_swapped = swap(g_own)
@@ -332,8 +345,19 @@
     else:
         g_far = over_d(far, far_first)
         grad_weight = 0.0
-        for v, g in zip(x_own + x_near + x_far, g_own + g_near + g_far):
-            grad_weight = grad_weight + dot(v, g, FIRST)
+        n = half * n_img
+        for i in range(2):
+            for at in range(per):
+                m = n - n_img
+                g_part = [
+                    g_own[i][at * n_img : (at + 1) * n_img],
+                    g_near[i][at * m : (at + 1) * m],
+                    g_far[i][at * n : (at + 1) * n],
+                ]
+                x_part = [v[i][at * n : (at + 1) * n] for v in (x_near, x_far)]
+                grad_weight = grad_weight + dot(
+                    jnp.concatenate(x_part), jnp.concatenate(g_part), FIRST
+                )
         grad_weight = (grad_weight + swap(grad_weight)) / nd
     return (grad_features[None], adjoint[None], grad_weight)
 

time: 87.4 us -> 86.5 us (0.990)
  waiting for transfers between devices: 33 us -> 37.9 us
  starting transfers between devices: 33.1 us -> 28.7 us
  other arithmetic: 3.37 us -> 2.4 us
  matrix products: 3.59 us -> 2.66 us
    ppermute x12 -> x10, starting transfers between devices: 17.8 us -> 12.2 us  [step_d(): return lax.ppermute(v, ('dp', 'blk'), perm)]
    ppermute x12 -> x10, waiting for transfers between devices: 8.21 us -> 12.2 us  [step_d(): return lax.ppermute(v, ('dp', 'blk'), perm)]
    concatenate x6 -> x5, other arithmetic: 2.09 us -> 0.19 us  [over_d(): v = after(jnp.concatenate(v), before)]
    ppermute x9, starting transfers between devices: 13.4 us -> 14.7 us  [along_z(): return lax.ppermute(v, 'blk', [(i, i ^ 2 * k) for i in range(nb)])]
    concatenate x1 -> x2, other arithmetic: 0.02 us -> 0.96 us  [on_device(): x_near, x_far = (jnp.concatenate(xs[:half]), jnp.concatenate(xs[half:]))]
    ppermute x9, waiting for transfers between devices: 23.9 us -> 24.8 us  [along_z(): return lax.ppermute(v, 'blk', [(i, i ^ 2 * k) for i in range(nb)])]
    dot_general x2, matrix products: 3.59 us -> 2.66 us  [dot(): return lax.dot_general(a, b, dims, preferred_element_type=F32)]
  transfers between devices with their start and end apart: 30 -> 28, of which waited for: 9 -> 10; matrix products, arithmetic and copies ran while one was open for 8% -> 6% of each run, Pallas kernels for 10% -> 11%
where the time goes in v11:
time: 86.5 us; the launch traced here: 86.3 us
  waiting for transfers between devices  37.9 us (44%)
  starting transfers between devices  28.7 us (33%)
  Pallas kernels  12.4 us (14%)
  matrix products  2.66 us (3%)
  other arithmetic  2.4 us (3%)
  between operations  2.17 us (3%)
    ppermute x9, waiting for transfers between devices, along_z(): return lax.ppermute(v, 'blk', [(i, i ^ 2 * k) for i in range(nb)])  24.8 us
    ppermute x9, starting transfers between devices, along_z(): return lax.ppermute(v, 'blk', [(i, i ^ 2 * k) for i in range(nb)])  14.7 us
    ppermute x10, waiting for transfers between devices, step_d(): return lax.ppermute(v, ('dp', 'blk'), perm)  12.2 us
    ppermute x10, starting transfers between devices, step_d(): return lax.ppermute(v, ('dp', 'blk'), perm)  12.2 us
    pallas_call x2, Pallas kernels, weight_sum(): pl.pallas_call(kernel, out_shape=jax.ShapeDtypeStruct((depth, depth), F32...  7.85 us
    dot_general x2, matrix products, dot(): return lax.dot_general(a, b, dims, preferred_element_type=F32)  2.66 us
    pallas_call x1, Pallas kernels, scores(): pl.pallas_call(functools.partial(score_kernel, nz), out_shape=outs, in_sp...  2.3 us
    ppermute x9, starting transfers between devices, swap(): return lax.ppermute(v, 'blk', [(i, i ^ 1) for i in range(nb)])  1.81 us
  transfers between devices with their start and end apart: 28, of which 10 were waited for; matrix products, arithmetic and copies ran while one was open for 6% of the time, Pallas kernels for 11%

profile of v11, /device:TPU:0, one launch (start us, length us, event | category | flops | bytes accessed | tf_op | source)
XLA Modules:
  0.0 86.3 jit_solution(7058099407576294011)
XLA Ops:
  0.6 0.0 copy-start
  0.6 0.0 copy-start.1
  0.7 4.1 %collective-permute-start.1 = (bf16[64,1152]{1,0:T(8,128)(2,1)}, bf16[64,1152]{1,0:T(8,128)(2,1)S(1)}, u32[]{:S(2)}, u32[]{:S(2)}) collective-permute-start(bf16[64,1152]{1,0:T(8,128)(2,1)} %bitcast.10), channel_id=1, source_target_pairs={{0,4},{1,5},{2,6},{3,7},{4,0},{5,1},{6,2},{7,3},{8,12},{9,13},{10,... | collective-permute-start | bytes 442376 | tf_op jit(solution)/shard_map/ppermute | solution.py:259
  4.8 1.3 %collective-permute-start.2 = (bf16[64,1152]{1,0:T(8,128)(2,1)}, bf16[64,1152]{1,0:T(8,128)(2,1)S(1)}, u32[]{:S(2)}, u32[]{:S(2)}) collective-permute-start(bf16[64,1152]{1,0:T(8,128)(2,1)} %bitcast.11), channel_id=1, source_target_pairs={{0,6},{1,7},{2,4},{3,5},{4,2},{5,3},{6,0},{7,1},{8,14},{9,15},{10,... | collective-permute-start | bytes 442376 | tf_op jit(solution)/shard_map/ppermute | solution.py:259
  6.1 0.2 collective-permute-start
  6.3 0.0 collective-permute-start.4
  6.3 0.5 collective-permute-start.3
  8.2 7.9 %collective-permute-done.1.refs_2_ = bf16[64,1152]{1,0:T(8,128)(2,1)S(1)} collective-permute-done((bf16[64,1152]{1,0:T(8,128)(2,1)}, bf16[64,1152]{1,0:T(8,128)(2,1)S(1)}, u32[]{:S(2)}, u32[]{:S(2)}) %collective-permute-start.1) | collective-permute-done | bytes 147488 | tf_op jit(solution)/shard_map/ppermute | solution.py:259
  16.0 0.0 collective-permute-done.2.refs_3_
  16.0 1.9 %collective-permute-start.8 = (bf16[128,1152]{1,0:T(8,128)(2,1)S(1)}, bf16[128,1152]{1,0:T(8,128)(2,1)S(1)}, u32[]{:S(2)}, u32[]{:S(2)}) collective-permute-start(bf16[128,1152]{1,0:T(8,128)(2,1)S(1)} %pad_maximum_fusion.5), channel_id=1, source_target_pairs={{0,8},{1,17},{2,10},{3,19},{4,12},{5,21},{6,14},{7,23},{8,0},{9,25... | collective-permute-start | bytes 884744 | tf_op jit(solution)/shard_map/ppermute | solution.py:270
  18.0 0.9 %pad_maximum_fusion.6 = bf16[128,1152]{1,0:T(8,128)(2,1)S(1)} fusion(bf16[64,1152]{1,0:T(8,128)(2,1)S(1)} %collective-permute-done.refs_1_, bf16[64,1152]{1,0:T(8,128)(2,1)} %bitcast.13), kind=kLoop, calls=%fused_computation.8 | loop fusion | flops 589824 | bytes 589824 | tf_op jit(solution)/shard_map/concatenate | solution.py:288
  18.9 0.3 collective-permute-start.10
  19.2 0.0 copy-start.2
  19.2 0.0 copy-start.3
  19.2 1.0 %fusion.embed = f32[256,1152]{1,0:T(8,128)S(1)} fusion(bf16[256,1152]{1,0:T(8,128)(2,1)S(1)} %shard_map.85, bf16[1152,1152]{1,0:T(8,128)(2,1)S(1)} %copy-done), kind=kOutput, calls=%fused_computation.13 | convolution fusion | flops 679477248 | bytes 4423680 | tf_op jit(solution)/shard_map/dot_general | solution.py:17
  20.2 0.0 collective-permute-done.3.refs_1_
  20.2 0.0 collective-permute-done.4.refs_3_
  20.3 0.1 iota.7.both
  20.3 2.3 %shard_map.86 = (f32[64,1152]{1,0:T(8,128)S(1)}, f32[64,1152]{1,0:T(8,128)S(1)}, f32[64,128]{1,0:T(8,128)S(1)}, bf16[256,1152]{1,0:T(8,128)(2,1)S(1)}, bf16[256,...) custom-call(f32[16,128]{1,0:T(8,128)S(1)} %iota.7.both, ...), custom_call_target="tpu_custom_call" | custom-call | flops 603979776 | bytes 4718592 | tf_op jit(solution)/shard_map/pallas_call | solution.py:74
  22.6 0.2 collective-permute-done.8
  22.9 2.0 %collective-permute-start.9 = (bf16[256,1152]{1,0:T(8,128)(2,1)S(1)}, bf16[256,1152]{1,0:T(8,128)(2,1)S(1)}, u32[]{:S(2)}, u32[]{:S(2)}) collective-permute-start(bf16[256,1152]{1,0:T(8,128)(2,1)S(1)} %pad_maximum_fusion.refs_0_), channel_id=1, source_target_pairs={{0,16},{1,9},{2,18},{3,11},{4,20},{5,13},{6,22},{7,15},{8,24},{9,1... | collective-permute-start | bytes 1769480 | tf_op jit(solution)/shard_map/ppermute | solution.py:270
  24.9 3.8 %collective-permute-done.10 = bf16[128,1152]{1,0:T(8,128)(2,1)S(1)} collective-permute-done((bf16[128,1152]{1,0:T(8,128)(2,1)S(1)}, bf16[128,1152]{1,0:T(8,128)(2,1)S(1)}, u32[]{:S(2)}, u32[]{:S(2)}) %collective-permute-start.10) | collective-permute-done | bytes 294944 | tf_op jit(solution)/shard_map/ppermute | solution.py:270
  28.7 2.5 %collective-permute-start.11 = (bf16[256,1152]{1,0:T(8,128)(2,1)S(1)}, bf16[256,1152]{1,0:T(8,128)(2,1)S(1)}, u32[]{:S(2)}, u32[]{:S(2)}) collective-permute-start(bf16[256,1152]{1,0:T(8,128)(2,1)S(1)} %pad_maximum_fusion.1.refs_0_), channel_id=1, source_target_pairs={{0,16},{1,9},{2,18},{3,11},{4,20},{5,13},{6,22},{7,15},{8,24},{9,1... | collective-permute-start | bytes 1769480 | tf_op jit(solution)/shard_map/ppermute | solution.py:270
  31.2 0.7 collective-permute-start.5
  31.9 1.8 %collective-permute-start.6 = (bf16[64,1152]{1,0:T(8,128)(2,1)S(1)}, bf16[64,1152]{1,0:T(8,128)(2,1)S(1)}, u32[]{:S(2)}, u32[]{:S(2)}) collective-permute-start(bf16[64,1152]{1,0:T(8,128)(2,1)S(1)} %get-tuple-element.32), channel_id=1, source_target_pairs={{0,4},{1,5},{2,6},{3,7},{4,0},{5,1},{6,2},{7,3},{8,12},{9,13},{10,... | collective-permute-start | bytes 442376 | tf_op jit(solution)/shard_map/ppermute | solution.py:259
  33.7 1.9 %collective-permute-start.7 = (bf16[64,1152]{1,0:T(8,128)(2,1)S(1)}, bf16[64,1152]{1,0:T(8,128)(2,1)S(1)}, u32[]{:S(2)}, u32[]{:S(2)}) collective-permute-start(bf16[64,1152]{1,0:T(8,128)(2,1)S(1)} %get-tuple-element.33), channel_id=1, source_target_pairs={{0,6},{1,7},{2,4},{3,5},{4,2},{5,3},{6,0},{7,1},{8,14},{9,15},{10,... | collective-permute-start | bytes 442376 | tf_op jit(solution)/shard_map/ppermute | solution.py:259
  35.6 0.8 collective-permute-done.5.refs_0_
  36.4 8.0 %collective-permute-done.6.refs_1_ = bf16[64,1152]{1,0:T(8,128)(2,1)S(1)} collective-permute-done((bf16[64,1152]{1,0:T(8,128)(2,1)S(1)}, bf16[64,1152]{1,0:T(8,128)(2,1)S(1)}, u32[]{:S(2)}, u32[]{:S(2)}) %collective-permute-start.6) | collective-permute-done | bytes 147488 | tf_op jit(solution)/shard_map/ppermute | solution.py:259
  44.4 0.0 collective-permute-done.7.refs_2_
  44.4 0.0 collective-permute-done.9.refs_1_
  44.4 0.0 collective-permute-done.11.refs_1_
  44.4 0.2 shard_map.87
  44.6 0.6 collective-permute-start.15
  45.3 2.1 %collective-permute-start.14 = (bf16[64,1152]{1,0:T(8,128)(2,1)S(1)}, bf16[64,1152]{1,0:T(8,128)(2,1)S(1)}, u32[]{:S(2)}, u32[]{:S(2)}) collective-permute-start(bf16[64,1152]{1,0:T(8,128)(2,1)S(1)} %shard_map.87), channel_id=1, source_target_pairs={{0,2},{1,3},{2,0},{3,1},{4,6},{5,7},{6,4},{7,5},{8,10},{9,11},{10,... | collective-permute-start | bytes 442376 | tf_op jit(solution)/shard_map/ppermute | solution.py:259
  47.4 1.0 %collective-permute-start.12 = (bf16[64,1152]{1,0:T(8,128)(2,1)S(1)}, bf16[64,1152]{1,0:T(8,128)(2,1)S(1)}, u32[]{:S(2)}, u32[]{:S(2)}) collective-permute-start(bf16[64,1152]{1,0:T(8,128)(2,1)S(1)} %shard_map.87), channel_id=1, source_target_pairs={{0,4},{1,5},{2,6},{3,7},{4,0},{5,1},{6,2},{7,3},{8,12},{9,13},{10,... | collective-permute-start | bytes 442376 | tf_op jit(solution)/shard_map/ppermute | solution.py:259
  48.4 1.5 %collective-permute-start.13 = (bf16[64,1152]{1,0:T(8,128)(2,1)S(1)}, bf16[64,1152]{1,0:T(8,128)(2,1)S(1)}, u32[]{:S(2)}, u32[]{:S(2)}) collective-permute-start(bf16[64,1152]{1,0:T(8,128)(2,1)S(1)} %shard_map.87), channel_id=1, source_target_pairs={{0,6},{1,7},{2,4},{3,5},{4,2},{5,3},{6,0},{7,1},{8,14},{9,15},{10,... | collective-permute-start | bytes 442376 | tf_op jit(solution)/shard_map/ppermute | solution.py:259
  49.9 1.6 %collective-permute-start.20 = (bf16[128,1152]{1,0:T(8,128)(2,1)S(1)}, bf16[128,1152]{1,0:T(8,128)(2,1)S(1)}, u32[]{:S(2)}, u32[]{:S(2)}) collective-permute-start(bf16[128,1152]{1,0:T(8,128)(2,1)S(1)} %pad_maximum_fusion.8), channel_id=1, source_target_pairs={{0,16},{1,9},{2,18},{3,11},{4,20},{5,13},{6,22},{7,15},{8,24},{9,1... | collective-permute-start | bytes 884744 | tf_op jit(solution)/shard_map/ppermute | solution.py:270
  51.5 0.1 shard_map.90.refs_1_
  51.6 0.1 shard_map.89.refs_0_
  51.7 0.5 collective-permute-done.14
  52.2 1.0 %collective-permute-start.21 = (bf16[64,1152]{1,0:T(8,128)(2,1)S(1)}, bf16[64,1152]{1,0:T(8,128)(2,1)S(1)}, u32[]{:S(2)}, u32[]{:S(2)}) collective-permute-start(bf16[64,1152]{1,0:T(8,128)(2,1)S(1)} %collective-permute-done.14), channel_id=1, source_target_pairs={{0,8},{1,17},{2,10},{3,19},{4,12},{5,21},{6,14},{7,23},{8,0},{9,25... | collective-permute-start | bytes 442376 | tf_op jit(solution)/shard_map/ppermute | solution.py:270
  53.2 7.7 %collective-permute-done.12 = bf16[64,1152]{1,0:T(8,128)(2,1)S(1)} collective-permute-done((bf16[64,1152]{1,0:T(8,128)(2,1)S(1)}, bf16[64,1152]{1,0:T(8,128)(2,1)S(1)}, u32[]{:S(2)}, u32[]{:S(2)}) %collective-permute-start.12) | collective-permute-done | bytes 147488 | tf_op jit(solution)/shard_map/ppermute | solution.py:259
  60.9 0.0 collective-permute-done.13
  60.9 0.8 collective-permute-start.16
  61.7 0.0 collective-permute-start.19
  61.7 0.5 collective-permute-start.18
  62.2 0.1 collective-permute-start.23
  62.3 0.0 collective-permute-done.21
  62.4 0.4 collective-permute-start.22
  62.8 7.1 %collective-permute-done.16 = bf16[128,1152]{1,0:T(8,128)(2,1)S(1)} collective-permute-done((bf16[128,1152]{1,0:T(8,128)(2,1)S(1)}, bf16[128,1152]{1,0:T(8,128)(2,1)S(1)}, u32[]{:S(2)}, u32[]{:S(2)}) %collective-permute-start.16) | collective-permute-done | bytes 294944 | tf_op jit(solution)/shard_map/ppermute | solution.py:270
  69.9 0.5 shard_map.88
  70.4 0.1 collective-permute-start.17
  70.6 0.0 collective-permute-done.22
  70.6 0.6 collective-permute-start.24
  71.2 0.1 collective-permute-start.25
  71.3 1.0 %collective-permute-start.26 = (bf16[256,1152]{1,0:T(8,128)(2,1)S(1)}, bf16[256,1152]{1,0:T(8,128)(2,1)S(1)}, u32[]{:S(2)}, u32[]{:S(2)}) collective-permute-start(bf16[256,1152]{1,0:T(8,128)(2,1)S(1)} %pad_maximum_fusion.4.refs_2_), channel_id=1, source_target_pairs={{0,16},{1,9},{2,18},{3,11},{4,20},{5,13},{6,22},{7,15},{8,24},{9,1... | collective-permute-start | bytes 1769480 | tf_op jit(solution)/shard_map/ppermute | solution.py:270
  72.3 1.7 %convolution_bitcast_fusion = f32[1,64,1152]{2,1,0:T(8,128)} fusion(bf16[64,1152]{1,0:T(8,128)(2,1)S(1)} %shard_map.87, bf16[1152,1152]{1,0:T(8,128)(2,1)S(1)} %copy-done), kind=kOutput, calls=%fused_computation | convolution fusion | flops 169869312 | bytes 3096576 | tf_op jit(solution)/shard_map/dot_general | solution.py:17
  74.0 1.3 %shard_map.91 = (bf16[1152,1536]{1,0:T(8,128)(2,1)S(1)}, bf16[1152,512]{1,0:T(8,128)(2,1)S(1)}) custom-call(bf16[512,1152]{1,0:T(8,128)(2,1)S(1)} %shard_map.89.refs_0_, bf16[512,1152]{1,0:T(8,128)(2,1)S(1)} %shard_map.90.refs_1_, bf16[512,1152]{1,0:T(8,128)(2,1)S(1)} %collective-permute-done.18.refs_2_, bf16[512,1152]{1,0:T(8,128)(2,1)S(1)} %collective-permute-done.19.refs_3_), custom_call_target="tpu_custom_call" | custom-call | bytes 9437184 | tf_op jit(solution)/shard_map/pallas_call | solution.py:180
  75.2 0.0 collective-permute-done.24.refs_4_
  75.3 4.8 %shard_map.92.acc = f32[1152,1152]{1,0:T(8,128)S(1)} custom-call(bf16[1152,1536]{1,0:T(8,128)(2,1)S(1)} %get-tuple-element.49.x_t, bf16[256,1152]{1,0:T(8,128)(2,1)S(1)} %pad_maximum_fusion.2.refs_0_, bf16[256,1152]{1,0:T(8,128)(2,1)S(1)} %pad_maximum_fusion.3.refs_1_, bf16[256,1152]{1,0:T(8,128)(2,1)S(1)} %pad_maximum_fusion.4.refs_2_, ...), custom_call_target="tpu_custom_call" | custom-call | flops 4076863488 | bytes 12386304 | tf_op jit(solution)/shard_map/pallas_call | solution.py:235
  80.0 1.1 %collective-permute-done.26.refs_0_ = bf16[256,1152]{1,0:T(8,128)(2,1)S(1)} collective-permute-done((bf16[256,1152]{1,0:T(8,128)(2,1)S(1)}, bf16[256,1152]{1,0:T(8,128)(2,1)S(1)}, u32[]{:S(2)}, u32[]{:S(2)}) %collective-permute-start.26) | collective-permute-done | bytes 589856 | tf_op jit(solution)/shard_map/ppermute | solution.py:270
  81.2 1.1 %add_bitcast_fusion = f32[1,256,1152]{2,1,0:T(8,128)} fusion(f32[256,1152]{1,0:T(8,128)S(1)} %get-tuple-element.44, f32[256,1152]{1,0:T(8,128)S(1)} %collective-permute-done.17), kind=kLoop, calls=%fused_computation.1 | loop fusion | flops 294912 | bytes 3538944 | tf_op jit(solution)/shard_map/broadcast_in_dim | solution.py:362
  82.3 0.9 %collective-permute-done.27.refs_1_ = bf16[256,1152]{1,0:T(8,128)(2,1)S(1)} collective-permute-done((bf16[256,1152]{1,0:T(8,128)(2,1)S(1)}, bf16[256,1152]{1,0:T(8,128)(2,1)S(1)}, u32[]{:S(2)}, u32[]{:S(2)}) %collective-permute-start.27) | collective-permute-done | bytes 589856 | tf_op jit(solution)/shard_map/ppermute | solution.py:262
  83.2 3.1 %shard_map.93 = f32[1152,1152]{1,0:T(8,128)} custom-call(bf16[1152,512]{1,0:T(8,128)(2,1)S(1)} %get-tuple-element.48.x_t, f32[1152,1152]{1,0:T(8,128)S(1)} %shard_map.92.acc, bf16[256,1152]{1,0:T(8,128)(2,1)S(1)} %collective-permute-done.26.refs_0_, bf16[256,1152]{1,0:T(8,128)(2,1)S(1)} %collective-permute-done.27.refs_1_), custom_call_target="tpu_custom_call" | custom-call | flops 1358954496 | bytes 12976128 | tf_op jit(solution)/shard_map/pallas_call | solution.py:235
  (24 shorter events, 0.4 us)
Async XLA Ops:
  0.6 18.6 %copy-start = (bf16[1152,1152]{1,0:T(8,128)(2,1)S(1)}, bf16[1152,1152]{1,0:T(8,128)(2,1)}, u32[]{:S(2)}) copy-start(bf16[1152,1152]{1,0:T(8,128)(2,1)} %param.9) | copy-start | bytes 7962628
  0.6 18.5 %copy-start.1 = (bf16[1,64,1152]{2,1,0:T(8,128)(2,1)S(1)}, bf16[1,64,1152]{2,1,0:T(8,128)(2,1)}, u32[]{:S(2)}) copy-start(bf16[1,64,1152]{2,1,0:T(8,128)(2,1)} %param.6) | copy-start | bytes 442372
  0.7 15.4 %collective-permute-start.1 = (bf16[64,1152]{1,0:T(8,128)(2,1)}, bf16[64,1152]{1,0:T(8,128)(2,1)S(1)}, u32[]{:S(2)}, u32[]{:S(2)}) collective-permute-start(bf16[64,1152]{1,0:T(8,128)(2,1)} %bitcast.10), channel_id=1, source_target_pairs={{0,4},{1,5},{2,6},{3,7},{4,0},{5,1},{6,2},{7,3},{8,12},{9,13},{10,... | collective-permute-start | bytes 442376 | tf_op jit(solution)/shard_map/ppermute | solution.py:259
  4.8 11.3 %collective-permute-start.2 = (bf16[64,1152]{1,0:T(8,128)(2,1)}, bf16[64,1152]{1,0:T(8,128)(2,1)S(1)}, u32[]{:S(2)}, u32[]{:S(2)}) collective-permute-start(bf16[64,1152]{1,0:T(8,128)(2,1)} %bitcast.11), channel_id=1, source_target_pairs={{0,6},{1,7},{2,4},{3,5},{4,2},{5,3},{6,0},{7,1},{8,14},{9,15},{10,... | collective-permute-start | bytes 442376 | tf_op jit(solution)/shard_map/ppermute | solution.py:259
  6.1 11.8 %collective-permute-start = (bf16[64,1152]{1,0:T(8,128)(2,1)}, bf16[64,1152]{1,0:T(8,128)(2,1)S(1)}, u32[]{:S(2)}, u32[]{:S(2)}) collective-permute-start(bf16[64,1152]{1,0:T(8,128)(2,1)} %bitcast.12), channel_id=1, source_target_pairs={{0,2},{1,3},{2,0},{3,1},{4,6},{5,7},{6,4},{7,5},{8,10},{9,11},{10,... | collective-permute-start | bytes 442376 | tf_op jit(solution)/shard_map/ppermute | solution.py:259
  6.3 13.9 %collective-permute-start.4 = (bf16[256,1152]{1,0:T(8,128)(2,1)}, bf16[256,1152]{1,0:T(8,128)(2,1)}, u32[]{:S(2)}, u32[]{:S(2)}) collective-permute-start(bf16[256,1152]{1,0:T(8,128)(2,1)} %bitcast.16), channel_id=1, source_target_pairs={{0,1},{1,0},{2,3},{3,2},{4,5},{5,4},{6,7},{7,6},{8,9},{9,8},{10,11... | collective-permute-start | bytes 1769480 | tf_op jit(solution)/shard_map/ppermute | solution.py:262
  6.3 13.9 %collective-permute-start.3 = (s32[1,256]{1,0:T(1,128)}, s32[1,256]{1,0:T(1,128)S(1)}, u32[]{:S(2)}, u32[]{:S(2)}) collective-permute-start(s32[1,256]{1,0:T(1,128)} %refs_0_.1), channel_id=1, source_target_pairs={{0,1},{1,0},{2,3},{3,2},{4,5},{5,4},{6,7},{7,6},{8,9},{9,8},{10,11... | collective-permute-start | bytes 3080 | tf_op jit(solution)/shard_map/ppermute | solution.py:262
  16.0 6.8 %collective-permute-start.8 = (bf16[128,1152]{1,0:T(8,128)(2,1)S(1)}, bf16[128,1152]{1,0:T(8,128)(2,1)S(1)}, u32[]{:S(2)}, u32[]{:S(2)}) collective-permute-start(bf16[128,1152]{1,0:T(8,128)(2,1)S(1)} %pad_maximum_fusion.5), channel_id=1, source_target_pairs={{0,8},{1,17},{2,10},{3,19},{4,12},{5,21},{6,14},{7,23},{8,0},{9,25... | collective-permute-start | bytes 884744 | tf_op jit(solution)/shard_map/ppermute | solution.py:270
  18.9 9.8 %collective-permute-start.10 = (bf16[128,1152]{1,0:T(8,128)(2,1)S(1)}, bf16[128,1152]{1,0:T(8,128)(2,1)S(1)}, u32[]{:S(2)}, u32[]{:S(2)}) collective-permute-start(bf16[128,1152]{1,0:T(8,128)(2,1)S(1)} %pad_maximum_fusion.6), channel_id=1, source_target_pairs={{0,8},{1,17},{2,10},{3,19},{4,12},{5,21},{6,14},{7,23},{8,0},{9,25... | collective-permute-start | bytes 884744 | tf_op jit(solution)/shard_map/ppermute | solution.py:270
  19.2 1.1 %copy-start.2 = (bf16[1,256,1152]{2,1,0:T(8,128)(2,1)S(1)}, bf16[1,256,1152]{2,1,0:T(8,128)(2,1)}, u32[]{:S(2)}) copy-start(bf16[1,256,1152]{2,1,0:T(8,128)(2,1)} %param.7) | copy-start | bytes 1769476
  19.2 1.1 %copy-start.3 = (s32[1,256]{1,0:T(1,128)S(1)}, s32[1,256]{1,0:T(1,128)}, u32[]{:S(2)}) copy-start(s32[1,256]{1,0:T(1,128)} %refs_0_.1) | copy-start | bytes 3076
  22.9 21.5 %collective-permute-start.9 = (bf16[256,1152]{1,0:T(8,128)(2,1)S(1)}, bf16[256,1152]{1,0:T(8,128)(2,1)S(1)}, u32[]{:S(2)}, u32[]{:S(2)}) collective-permute-start(bf16[256,1152]{1,0:T(8,128)(2,1)S(1)} %pad_maximum_fusion.refs_0_), channel_id=1, source_target_pairs={{0,16},{1,9},{2,18},{3,11},{4,20},{5,13},{6,22},{7,15},{8,24},{9,1... | collective-permute-start | bytes 1769480 | tf_op jit(solution)/shard_map/ppermute | solution.py:270
  28.7 15.7 %collective-permute-start.11 = (bf16[256,1152]{1,0:T(8,128)(2,1)S(1)}, bf16[256,1152]{1,0:T(8,128)(2,1)S(1)}, u32[]{:S(2)}, u32[]{:S(2)}) collective-permute-start(bf16[256,1152]{1,0:T(8,128)(2,1)S(1)} %pad_maximum_fusion.1.refs_0_), channel_id=1, source_target_pairs={{0,16},{1,9},{2,18},{3,11},{4,20},{5,13},{6,22},{7,15},{8,24},{9,1... | collective-permute-start | bytes 1769480 | tf_op jit(solution)/shard_map/ppermute | solution.py:270
  31.2 5.1 %collective-permute-start.5 = (bf16[64,1152]{1,0:T(8,128)(2,1)S(1)}, bf16[64,1152]{1,0:T(8,128)(2,1)S(1)}, u32[]{:S(2)}, u32[]{:S(2)}) collective-permute-start(bf16[64,1152]{1,0:T(8,128)(2,1)S(1)} %get-tuple-element.31), channel_id=1, source_target_pairs={{0,2},{1,3},{2,0},{3,1},{4,6},{5,7},{6,4},{7,5},{8,10},{9,11},{10,... | collective-permute-start | bytes 442376 | tf_op jit(solution)/shard_map/ppermute | solution.py:259
  31.9 12.5 %collective-permute-start.6 = (bf16[64,1152]{1,0:T(8,128)(2,1)S(1)}, bf16[64,1152]{1,0:T(8,128)(2,1)S(1)}, u32[]{:S(2)}, u32[]{:S(2)}) collective-permute-start(bf16[64,1152]{1,0:T(8,128)(2,1)S(1)} %get-tuple-element.32), channel_id=1, source_target_pairs={{0,4},{1,5},{2,6},{3,7},{4,0},{5,1},{6,2},{7,3},{8,12},{9,13},{10,... | collective-permute-start | bytes 442376 | tf_op jit(solution)/shard_map/ppermute | solution.py:259
  33.7 10.7 %collective-permute-start.7 = (bf16[64,1152]{1,0:T(8,128)(2,1)S(1)}, bf16[64,1152]{1,0:T(8,128)(2,1)S(1)}, u32[]{:S(2)}, u32[]{:S(2)}) collective-permute-start(bf16[64,1152]{1,0:T(8,128)(2,1)S(1)} %get-tuple-element.33), channel_id=1, source_target_pairs={{0,6},{1,7},{2,4},{3,5},{4,2},{5,3},{6,0},{7,1},{8,14},{9,15},{10,... | collective-permute-start | bytes 442376 | tf_op jit(solution)/shard_map/ppermute | solution.py:259
  44.6 5.3 %collective-permute-start.15 = (bf16[64,1152]{1,0:T(8,128)(2,1)S(1)}, bf16[64,1152]{1,0:T(8,128)(2,1)S(1)}, u32[]{:S(2)}, u32[]{:S(2)}) collective-permute-start(bf16[64,1152]{1,0:T(8,128)(2,1)S(1)} %shard_map.87), channel_id=1, source_target_pairs={{0,8},{1,17},{2,10},{3,19},{4,12},{5,21},{6,14},{7,23},{8,0},{9,25... | collective-permute-start | bytes 442376 | tf_op jit(solution)/shard_map/ppermute | solution.py:270
  45.3 6.9 %collective-permute-start.14 = (bf16[64,1152]{1,0:T(8,128)(2,1)S(1)}, bf16[64,1152]{1,0:T(8,128)(2,1)S(1)}, u32[]{:S(2)}, u32[]{:S(2)}) collective-permute-start(bf16[64,1152]{1,0:T(8,128)(2,1)S(1)} %shard_map.87), channel_id=1, source_target_pairs={{0,2},{1,3},{2,0},{3,1},{4,6},{5,7},{6,4},{7,5},{8,10},{9,11},{10,... | collective-permute-start | bytes 442376 | tf_op jit(solution)/shard_map/ppermute | solution.py:259
  47.4 13.5 %collective-permute-start.12 = (bf16[64,1152]{1,0:T(8,128)(2,1)S(1)}, bf16[64,1152]{1,0:T(8,128)(2,1)S(1)}, u32[]{:S(2)}, u32[]{:S(2)}) collective-permute-start(bf16[64,1152]{1,0:T(8,128)(2,1)S(1)} %shard_map.87), channel_id=1, source_target_pairs={{0,4},{1,5},{2,6},{3,7},{4,0},{5,1},{6,2},{7,3},{8,12},{9,13},{10,... | collective-permute-start | bytes 442376 | tf_op jit(solution)/shard_map/ppermute | solution.py:259
  48.4 12.5 %collective-permute-start.13 = (bf16[64,1152]{1,0:T(8,128)(2,1)S(1)}, bf16[64,1152]{1,0:T(8,128)(2,1)S(1)}, u32[]{:S(2)}, u32[]{:S(2)}) collective-permute-start(bf16[64,1152]{1,0:T(8,128)(2,1)S(1)} %shard_map.87), channel_id=1, source_target_pairs={{0,6},{1,7},{2,4},{3,5},{4,2},{5,3},{6,0},{7,1},{8,14},{9,15},{10,... | collective-permute-start | bytes 442376 | tf_op jit(solution)/shard_map/ppermute | solution.py:259
  49.9 12.3 %collective-permute-start.20 = (bf16[128,1152]{1,0:T(8,128)(2,1)S(1)}, bf16[128,1152]{1,0:T(8,128)(2,1)S(1)}, u32[]{:S(2)}, u32[]{:S(2)}) collective-permute-start(bf16[128,1152]{1,0:T(8,128)(2,1)S(1)} %pad_maximum_fusion.8), channel_id=1, source_target_pairs={{0,16},{1,9},{2,18},{3,11},{4,20},{5,13},{6,22},{7,15},{8,24},{9,1... | collective-permute-start | bytes 884744 | tf_op jit(solution)/shard_map/ppermute | solution.py:270
  52.2 10.1 %collective-permute-start.21 = (bf16[64,1152]{1,0:T(8,128)(2,1)S(1)}, bf16[64,1152]{1,0:T(8,128)(2,1)S(1)}, u32[]{:S(2)}, u32[]{:S(2)}) collective-permute-start(bf16[64,1152]{1,0:T(8,128)(2,1)S(1)} %collective-permute-done.14), channel_id=1, source_target_pairs={{0,8},{1,17},{2,10},{3,19},{4,12},{5,21},{6,14},{7,23},{8,0},{9,25... | collective-permute-start | bytes 442376 | tf_op jit(solution)/shard_map/ppermute | solution.py:270
  60.9 9.0 %collective-permute-start.16 = (bf16[128,1152]{1,0:T(8,128)(2,1)S(1)}, bf16[128,1152]{1,0:T(8,128)(2,1)S(1)}, u32[]{:S(2)}, u32[]{:S(2)}) collective-permute-start(bf16[128,1152]{1,0:T(8,128)(2,1)S(1)} %pad_maximum_fusion.7), channel_id=1, source_target_pairs={{0,8},{1,17},{2,10},{3,19},{4,12},{5,21},{6,14},{7,23},{8,0},{9,25... | collective-permute-start | bytes 884744 | tf_op jit(solution)/shard_map/ppermute | solution.py:270
  61.7 9.6 %collective-permute-start.19 = (bf16[512,1152]{1,0:T(8,128)(2,1)S(1)}, bf16[512,1152]{1,0:T(8,128)(2,1)S(1)}, u32[]{:S(2)}, u32[]{:S(2)}) collective-permute-start(bf16[512,1152]{1,0:T(8,128)(2,1)S(1)} %shard_map.90.refs_1_), channel_id=1, source_target_pairs={{0,1},{1,0},{2,3},{3,2},{4,5},{5,4},{6,7},{7,6},{8,9},{9,8},{10,11... | collective-permute-start | bytes 3538952 | tf_op jit(solution)/shard_map/ppermute | solution.py:262
  61.7 12.3 %collective-permute-start.18 = (bf16[512,1152]{1,0:T(8,128)(2,1)S(1)}, bf16[512,1152]{1,0:T(8,128)(2,1)S(1)}, u32[]{:S(2)}, u32[]{:S(2)}) collective-permute-start(bf16[512,1152]{1,0:T(8,128)(2,1)S(1)} %shard_map.89.refs_0_), channel_id=1, source_target_pairs={{0,1},{1,0},{2,3},{3,2},{4,5},{5,4},{6,7},{7,6},{8,9},{9,8},{10,11... | collective-permute-start | bytes 3538952 | tf_op jit(solution)/shard_map/ppermute | solution.py:262
  62.2 9.0 %collective-permute-start.23 = (bf16[256,1152]{1,0:T(8,128)(2,1)S(1)}, bf16[256,1152]{1,0:T(8,128)(2,1)S(1)}, u32[]{:S(2)}, u32[]{:S(2)}) collective-permute-start(bf16[256,1152]{1,0:T(8,128)(2,1)S(1)} %pad_maximum_fusion.2.refs_0_), channel_id=1, source_target_pairs={{0,1},{1,0},{2,3},{3,2},{4,5},{5,4},{6,7},{7,6},{8,9},{9,8},{10,11... | collective-permute-start | bytes 1769480 | tf_op jit(solution)/shard_map/ppermute | solution.py:262
  62.4 8.2 %collective-permute-start.22 = (bf16[128,1152]{1,0:T(8,128)(2,1)S(1)}, bf16[128,1152]{1,0:T(8,128)(2,1)S(1)}, u32[]{:S(2)}, u32[]{:S(2)}) collective-permute-start(bf16[128,1152]{1,0:T(8,128)(2,1)S(1)} %pad_maximum_fusion.9), channel_id=1, source_target_pairs={{0,16},{1,9},{2,18},{3,11},{4,20},{5,13},{6,22},{7,15},{8,24},{9,1... | collective-permute-start | bytes 884744 | tf_op jit(solution)/shard_map/ppermute | solution.py:270
  70.4 10.7 %collective-permute-start.17 = (f32[256,1152]{1,0:T(8,128)S(1)}, f32[256,1152]{1,0:T(8,128)S(1)}, u32[]{:S(2)}, u32[]{:S(2)}) collective-permute-start(f32[256,1152]{1,0:T(8,128)S(1)} %get-tuple-element.45), channel_id=1, source_target_pairs={{0,1},{1,0},{2,3},{3,2},{4,5},{5,4},{6,7},{7,6},{8,9},{9,8},{10,11... | collective-permute-start | bytes 3538952 | tf_op jit(solution)/shard_map/ppermute | solution.py:262
  70.6 4.6 %collective-permute-start.24 = (bf16[256,1152]{1,0:T(8,128)(2,1)S(1)}, bf16[256,1152]{1,0:T(8,128)(2,1)S(1)}, u32[]{:S(2)}, u32[]{:S(2)}) collective-permute-start(bf16[256,1152]{1,0:T(8,128)(2,1)S(1)} %pad_maximum_fusion.3.refs_1_), channel_id=1, source_target_pairs={{0,1},{1,0},{2,3},{3,2},{4,5},{5,4},{6,7},{7,6},{8,9},{9,8},{10,11... | collective-permute-start | bytes 1769480 | tf_op jit(solution)/shard_map/ppermute | solution.py:262
  71.2 4.0 %collective-permute-start.25 = (bf16[256,1152]{1,0:T(8,128)(2,1)S(1)}, bf16[256,1152]{1,0:T(8,128)(2,1)S(1)}, u32[]{:S(2)}, u32[]{:S(2)}) collective-permute-start(bf16[256,1152]{1,0:T(8,128)(2,1)S(1)} %pad_maximum_fusion.4.refs_2_), channel_id=1, source_target_pairs={{0,1},{1,0},{2,3},{3,2},{4,5},{5,4},{6,7},{7,6},{8,9},{9,8},{10,11... | collective-permute-start | bytes 1769480 | tf_op jit(solution)/shard_map/ppermute | solution.py:262
  71.3 9.9 %collective-permute-start.26 = (bf16[256,1152]{1,0:T(8,128)(2,1)S(1)}, bf16[256,1152]{1,0:T(8,128)(2,1)S(1)}, u32[]{:S(2)}, u32[]{:S(2)}) collective-permute-start(bf16[256,1152]{1,0:T(8,128)(2,1)S(1)} %pad_maximum_fusion.4.refs_2_), channel_id=1, source_target_pairs={{0,16},{1,9},{2,18},{3,11},{4,20},{5,13},{6,22},{7,15},{8,24},{9,1... | collective-permute-start | bytes 1769480 | tf_op jit(solution)/shard_map/ppermute | solution.py:270
  81.2 2.0 %collective-permute-start.27 = (bf16[256,1152]{1,0:T(8,128)(2,1)S(1)}, bf16[256,1152]{1,0:T(8,128)(2,1)S(1)}, u32[]{:S(2)}, u32[]{:S(2)}) collective-permute-start(bf16[256,1152]{1,0:T(8,128)(2,1)S(1)} %collective-permute-done.26.refs_0_), channel_id=1, source_target_pairs={{0,1},{1,0},{2,3},{3,2},{4,5},{5,4},{6,7},{7,6},{8,9},{9,8},{10,11... | collective-permute-start | bytes 1769480 | tf_op jit(solution)/shard_map/ppermute | solution.py:262

commit v12 on v11

--- a/solution.py
+++ b/solution.py
@@ -301,9 +301,9 @@
     sent = sent
     back = over_z([own] + sent)[1:]
 
-    x_near = over_d(x_near, after(x_near_first, sent))
+    x_near = over_d(x_near, after(x_near_first, back))
     x_far = over_d(x_far, after(x_far_first, sent))
-    back = after(back, x_far, x_near)
+    back = after(back, x_far)
     ge = embed_grad(own, u, inv_norm, back)
     grad_features = dot(ge, weight, LAST)
 

time: 86.5 us -> 84 us (0.971)
  waiting for transfers between devices: 37.9 us -> 33 us
  starting transfers between devices: 28.7 us -> 31.1 us
  local copies, waits for them, and re-layouts: 0.1 us -> 1.01 us
  other arithmetic: 2.4 us -> 1.5 us
    ppermute x10, waiting for transfers between devices: 12.2 us -> 7.07 us  [step_d(): return lax.ppermute(v, ('dp', 'blk'), perm)]
    ppermute x9, starting transfers between devices: 14.7 us -> 16.2 us  [along_z(): return lax.ppermute(v, 'blk', [(i, i ^ 2 * k) for i in range(nb)])]
    unnamed x8 -> x10, local copies, waits for them, and re-layouts: 0.03 us -> 0.94 us
    concatenate x2, other arithmetic: 0.96 us -> 0.05 us  [on_device(): x_near, x_far = (jnp.concatenate(xs[:half]), jnp.concatenate(xs[half:]))]
  transfers between devices with their start and end apart: 28 -> 28, of which waited for: 10 -> 11; matrix products, arithmetic and copies ran while one was open for 6% -> 5% of each run, Pallas kernels for 11% -> 11%
where the time goes in v12:
time: 84 us; the launch traced here: 83.8 us
  waiting for transfers between devices  33 us (39%)
  starting transfers between devices  31.1 us (37%)
  Pallas kernels  12.4 us (15%)
  matrix products  2.65 us (3%)
  between operations  2.15 us (3%)
  other arithmetic  1.5 us (2%)
  local copies, waits for them, and re-layouts  1.01 us (1%)
    ppermute x9, waiting for transfers between devices, along_z(): return lax.ppermute(v, 'blk', [(i, i ^ 2 * k) for i in range(nb)])  25.1 us
    ppermute x9, starting transfers between devices, along_z(): return lax.ppermute(v, 'blk', [(i, i ^ 2 * k) for i in range(nb)])  16.2 us
    ppermute x10, starting transfers between devices, step_d(): return lax.ppermute(v, ('dp', 'blk'), perm)  12.8 us
    pallas_call x2, Pallas kernels, weight_sum(): pl.pallas_call(kernel, out_shape=jax.ShapeDtypeStruct((depth, depth), F32...  7.85 us
    ppermute x10, waiting for transfers between devices, step_d(): return lax.ppermute(v, ('dp', 'blk'), perm)  7.07 us
    dot_general x2, matrix products, dot(): return lax.dot_general(a, b, dims, preferred_element_type=F32)  2.65 us
    pallas_call x1, Pallas kernels, scores(): pl.pallas_call(functools.partial(score_kernel, nz), out_shape=outs, in_sp...  2.3 us
    ppermute x9, starting transfers between devices, swap(): return lax.ppermute(v, 'blk', [(i, i ^ 1) for i in range(nb)])  2.12 us
  transfers between devices with their start and end apart: 28, of which 11 were waited for; matrix products, arithmetic and copies ran while one was open for 5% of the time, Pallas kernels for 11%

profile of v12, /device:TPU:0, one launch (start us, length us, event | category | flops | bytes accessed | tf_op | source)
XLA Modules:
  0.0 83.8 jit_solution(9656040333223937745)
XLA Ops:
  0.6 0.0 copy-start
  0.6 4.1 %collective-permute-start.1 = (bf16[64,1152]{1,0:T(8,128)(2,1)}, bf16[64,1152]{1,0:T(8,128)(2,1)S(1)}, u32[]{:S(2)}, u32[]{:S(2)}) collective-permute-start(bf16[64,1152]{1,0:T(8,128)(2,1)} %bitcast.10), channel_id=1, source_target_pairs={{0,4},{1,5},{2,6},{3,7},{4,0},{5,1},{6,2},{7,3},{8,12},{9,13},{10,... | collective-permute-start | bytes 442376 | tf_op jit(solution)/shard_map/ppermute | solution.py:259
  4.7 1.3 %collective-permute-start.2 = (bf16[64,1152]{1,0:T(8,128)(2,1)}, bf16[64,1152]{1,0:T(8,128)(2,1)S(1)}, u32[]{:S(2)}, u32[]{:S(2)}) collective-permute-start(bf16[64,1152]{1,0:T(8,128)(2,1)} %bitcast.11), channel_id=1, source_target_pairs={{0,6},{1,7},{2,4},{3,5},{4,2},{5,3},{6,0},{7,1},{8,14},{9,15},{10,... | collective-permute-start | bytes 442376 | tf_op jit(solution)/shard_map/ppermute | solution.py:259
  6.1 0.2 collective-permute-start
  6.3 0.0 collective-permute-start.4
  6.3 0.5 collective-permute-start.3
  8.1 7.9 %collective-permute-done.1.refs_2_ = bf16[64,1152]{1,0:T(8,128)(2,1)S(1)} collective-permute-done((bf16[64,1152]{1,0:T(8,128)(2,1)}, bf16[64,1152]{1,0:T(8,128)(2,1)S(1)}, u32[]{:S(2)}, u32[]{:S(2)}) %collective-permute-start.1) | collective-permute-done | bytes 147488 | tf_op jit(solution)/shard_map/ppermute | solution.py:259
  16.0 0.0 collective-permute-done.2.refs_3_
  16.0 1.9 %collective-permute-start.8 = (bf16[128,1152]{1,0:T(8,128)(2,1)S(1)}, bf16[128,1152]{1,0:T(8,128)(2,1)S(1)}, u32[]{:S(2)}, u32[]{:S(2)}) collective-permute-start(bf16[128,1152]{1,0:T(8,128)(2,1)S(1)} %pad_maximum_fusion.5), channel_id=1, source_target_pairs={{0,8},{1,17},{2,10},{3,19},{4,12},{5,21},{6,14},{7,23},{8,0},{9,25... | collective-permute-start | bytes 884744 | tf_op jit(solution)/shard_map/ppermute | solution.py:270
  17.9 0.0 collective-permute-done.refs_1_
  17.9 0.9 %copy-done.1 = bf16[1,64,1152]{2,1,0:T(8,128)(2,1)S(1)} copy-done((bf16[1,64,1152]{2,1,0:T(8,128)(2,1)S(1)}, bf16[1,64,1152]{2,1,0:T(8,128)(2,1)}, u32[]{:S(2)}) %copy-start.1) | copy-done | bytes 147480
  18.9 0.0 copy-start.3
  18.9 0.0 copy-start.4
  18.9 1.0 %fusion.embed = f32[256,1152]{1,0:T(8,128)S(1)} fusion(bf16[256,1152]{1,0:T(8,128)(2,1)S(1)} %shard_map.85, bf16[1152,1152]{1,0:T(8,128)(2,1)S(1)} %copy-done), kind=kOutput, calls=%fused_computation.13 | convolution fusion | flops 679477248 | bytes 4423680 | tf_op jit(solution)/shard_map/dot_general | solution.py:17
  19.9 0.0 collective-permute-done.3.refs_1_
  20.0 0.1 iota.7.both
  20.0 2.3 %shard_map.86 = (f32[64,1152]{1,0:T(8,128)S(1)}, f32[64,1152]{1,0:T(8,128)S(1)}, f32[64,128]{1,0:T(8,128)S(1)}, bf16[256,1152]{1,0:T(8,128)(2,1)S(1)}, bf16[256,...) custom-call(f32[16,128]{1,0:T(8,128)S(1)} %iota.7.both, ...), custom_call_target="tpu_custom_call" | custom-call | flops 603979776 | bytes 4718592 | tf_op jit(solution)/shard_map/pallas_call | solution.py:74
  22.3 0.0 copy-start.2
  22.4 0.5 collective-permute-done.8
  22.9 2.1 %collective-permute-start.9 = (bf16[256,1152]{1,0:T(8,128)(2,1)S(1)}, bf16[256,1152]{1,0:T(8,128)(2,1)S(1)}, u32[]{:S(2)}, u32[]{:S(2)}) collective-permute-start(bf16[256,1152]{1,0:T(8,128)(2,1)S(1)} %pad_maximum_fusion.refs_0_), channel_id=1, source_target_pairs={{0,16},{1,9},{2,18},{3,11},{4,20},{5,13},{6,22},{7,15},{8,24},{9,1... | collective-permute-start | bytes 1769480 | tf_op jit(solution)/shard_map/ppermute | solution.py:270
  25.1 1.6 %collective-permute-start.16 = (bf16[128,1152]{1,0:T(8,128)(2,1)S(1)}, bf16[128,1152]{1,0:T(8,128)(2,1)S(1)}, u32[]{:S(2)}, u32[]{:S(2)}) collective-permute-start(bf16[128,1152]{1,0:T(8,128)(2,1)S(1)} %pad_maximum_fusion.8), channel_id=1, source_target_pairs={{0,8},{1,17},{2,10},{3,19},{4,12},{5,21},{6,14},{7,23},{8,0},{9,25... | collective-permute-start | bytes 884744 | tf_op jit(solution)/shard_map/ppermute | solution.py:270
  26.6 2.6 %collective-permute-start.5 = (bf16[64,1152]{1,0:T(8,128)(2,1)S(1)}, bf16[64,1152]{1,0:T(8,128)(2,1)S(1)}, u32[]{:S(2)}, u32[]{:S(2)}) collective-permute-start(bf16[64,1152]{1,0:T(8,128)(2,1)S(1)} %get-tuple-element.31), channel_id=1, source_target_pairs={{0,2},{1,3},{2,0},{3,1},{4,6},{5,7},{6,4},{7,5},{8,10},{9,11},{10,... | collective-permute-start | bytes 442376 | tf_op jit(solution)/shard_map/ppermute | solution.py:259
  29.2 1.8 %collective-permute-start.6 = (bf16[64,1152]{1,0:T(8,128)(2,1)S(1)}, bf16[64,1152]{1,0:T(8,128)(2,1)S(1)}, u32[]{:S(2)}, u32[]{:S(2)}) collective-permute-start(bf16[64,1152]{1,0:T(8,128)(2,1)S(1)} %get-tuple-element.32), channel_id=1, source_target_pairs={{0,4},{1,5},{2,6},{3,7},{4,0},{5,1},{6,2},{7,3},{8,12},{9,13},{10,... | collective-permute-start | bytes 442376 | tf_op jit(solution)/shard_map/ppermute | solution.py:259
  31.0 1.5 %collective-permute-start.7 = (bf16[64,1152]{1,0:T(8,128)(2,1)S(1)}, bf16[64,1152]{1,0:T(8,128)(2,1)S(1)}, u32[]{:S(2)}, u32[]{:S(2)}) collective-permute-start(bf16[64,1152]{1,0:T(8,128)(2,1)S(1)} %get-tuple-element.33), channel_id=1, source_target_pairs={{0,6},{1,7},{2,4},{3,5},{4,2},{5,3},{6,0},{7,1},{8,14},{9,15},{10,... | collective-permute-start | bytes 442376 | tf_op jit(solution)/shard_map/ppermute | solution.py:259
  32.5 0.1 collective-permute-done.16
  32.6 1.3 %collective-permute-done.5.refs_0_ = bf16[64,1152]{1,0:T(8,128)(2,1)S(1)} collective-permute-done((bf16[64,1152]{1,0:T(8,128)(2,1)S(1)}, bf16[64,1152]{1,0:T(8,128)(2,1)S(1)}, u32[]{:S(2)}, u32[]{:S(2)}) %collective-permute-start.5) | collective-permute-done | bytes 147488 | tf_op jit(solution)/shard_map/ppermute | solution.py:259
  33.9 8.7 %collective-permute-done.6.refs_1_ = bf16[64,1152]{1,0:T(8,128)(2,1)S(1)} collective-permute-done((bf16[64,1152]{1,0:T(8,128)(2,1)S(1)}, bf16[64,1152]{1,0:T(8,128)(2,1)S(1)}, u32[]{:S(2)}, u32[]{:S(2)}) %collective-permute-start.6) | collective-permute-done | bytes 147488 | tf_op jit(solution)/shard_map/ppermute | solution.py:259
  42.6 0.2 shard_map.87
  42.8 0.6 collective-permute-start.13
  43.4 0.9 %collective-permute-start.17 = (bf16[256,1152]{1,0:T(8,128)(2,1)S(1)}, bf16[256,1152]{1,0:T(8,128)(2,1)S(1)}, u32[]{:S(2)}, u32[]{:S(2)}) collective-permute-start(bf16[256,1152]{1,0:T(8,128)(2,1)S(1)} %pad_maximum_fusion.1.refs_0_), channel_id=1, source_target_pairs={{0,16},{1,9},{2,18},{3,11},{4,20},{5,13},{6,22},{7,15},{8,24},{9,1... | collective-permute-start | bytes 1769480 | tf_op jit(solution)/shard_map/ppermute | solution.py:270
  44.3 2.1 %collective-permute-start.12 = (bf16[64,1152]{1,0:T(8,128)(2,1)S(1)}, bf16[64,1152]{1,0:T(8,128)(2,1)S(1)}, u32[]{:S(2)}, u32[]{:S(2)}) collective-permute-start(bf16[64,1152]{1,0:T(8,128)(2,1)S(1)} %shard_map.87), channel_id=1, source_target_pairs={{0,2},{1,3},{2,0},{3,1},{4,6},{5,7},{6,4},{7,5},{8,10},{9,11},{10,... | collective-permute-start | bytes 442376 | tf_op jit(solution)/shard_map/ppermute | solution.py:259
  46.5 1.0 %collective-permute-start.10 = (bf16[64,1152]{1,0:T(8,128)(2,1)S(1)}, bf16[64,1152]{1,0:T(8,128)(2,1)S(1)}, u32[]{:S(2)}, u32[]{:S(2)}) collective-permute-start(bf16[64,1152]{1,0:T(8,128)(2,1)S(1)} %shard_map.87), channel_id=1, source_target_pairs={{0,4},{1,5},{2,6},{3,7},{4,0},{5,1},{6,2},{7,3},{8,12},{9,13},{10,... | collective-permute-start | bytes 442376 | tf_op jit(solution)/shard_map/ppermute | solution.py:259
  47.5 1.5 %collective-permute-start.11 = (bf16[64,1152]{1,0:T(8,128)(2,1)S(1)}, bf16[64,1152]{1,0:T(8,128)(2,1)S(1)}, u32[]{:S(2)}, u32[]{:S(2)}) collective-permute-start(bf16[64,1152]{1,0:T(8,128)(2,1)S(1)} %shard_map.87), channel_id=1, source_target_pairs={{0,6},{1,7},{2,4},{3,5},{4,2},{5,3},{6,0},{7,1},{8,14},{9,15},{10,... | collective-permute-start | bytes 442376 | tf_op jit(solution)/shard_map/ppermute | solution.py:259
  49.0 0.7 collective-permute-done.13
  49.7 0.6 collective-permute-start.20
  50.2 0.1 shard_map.90.refs_1_
  50.3 0.3 collective-permute-done.12
  50.7 1.2 %collective-permute-start.21 = (bf16[64,1152]{1,0:T(8,128)(2,1)S(1)}, bf16[64,1152]{1,0:T(8,128)(2,1)S(1)}, u32[]{:S(2)}, u32[]{:S(2)}) collective-permute-start(bf16[64,1152]{1,0:T(8,128)(2,1)S(1)} %collective-permute-done.12), channel_id=1, source_target_pairs={{0,8},{1,17},{2,10},{3,19},{4,12},{5,21},{6,14},{7,23},{8,0},{9,25... | collective-permute-start | bytes 442376 | tf_op jit(solution)/shard_map/ppermute | solution.py:270
  51.9 6.9 %collective-permute-done.10 = bf16[64,1152]{1,0:T(8,128)(2,1)S(1)} collective-permute-done((bf16[64,1152]{1,0:T(8,128)(2,1)S(1)}, bf16[64,1152]{1,0:T(8,128)(2,1)S(1)}, u32[]{:S(2)}, u32[]{:S(2)}) %collective-permute-start.10) | collective-permute-done | bytes 147488 | tf_op jit(solution)/shard_map/ppermute | solution.py:259
  58.8 0.0 collective-permute-done.11
  58.8 1.2 %collective-permute-start.14 = (bf16[128,1152]{1,0:T(8,128)(2,1)S(1)}, bf16[128,1152]{1,0:T(8,128)(2,1)S(1)}, u32[]{:S(2)}, u32[]{:S(2)}) collective-permute-start(bf16[128,1152]{1,0:T(8,128)(2,1)S(1)} %pad_maximum_fusion.6), channel_id=1, source_target_pairs={{0,8},{1,17},{2,10},{3,19},{4,12},{5,21},{6,14},{7,23},{8,0},{9,25... | collective-permute-start | bytes 884744 | tf_op jit(solution)/shard_map/ppermute | solution.py:270
  60.0 0.0 collective-permute-start.19
  60.0 0.0 collective-permute-done.17.refs_1_
  60.0 0.1 shard_map.89.refs_0_
  60.1 0.6 collective-permute-start.18
  60.7 0.1 collective-permute-start.23
  60.8 0.0 collective-permute-done.21
  60.8 1.6 %collective-permute-start.22 = (bf16[128,1152]{1,0:T(8,128)(2,1)S(1)}, bf16[128,1152]{1,0:T(8,128)(2,1)S(1)}, u32[]{:S(2)}, u32[]{:S(2)}) collective-permute-start(bf16[128,1152]{1,0:T(8,128)(2,1)S(1)} %pad_maximum_fusion.9), channel_id=1, source_target_pairs={{0,16},{1,9},{2,18},{3,11},{4,20},{5,13},{6,22},{7,15},{8,24},{9,1... | collective-permute-start | bytes 884744 | tf_op jit(solution)/shard_map/ppermute | solution.py:270
  62.4 4.8 %collective-permute-done.14 = bf16[128,1152]{1,0:T(8,128)(2,1)S(1)} collective-permute-done((bf16[128,1152]{1,0:T(8,128)(2,1)S(1)}, bf16[128,1152]{1,0:T(8,128)(2,1)S(1)}, u32[]{:S(2)}, u32[]{:S(2)}) %collective-permute-start.14) | collective-permute-done | bytes 294944 | tf_op jit(solution)/shard_map/ppermute | solution.py:270
  67.2 0.5 shard_map.88
  67.7 0.1 collective-permute-start.15
  67.9 0.0 collective-permute-done.22
  67.9 0.8 collective-permute-start.24
  68.7 0.0 collective-permute-done.23.refs_3_
  68.7 0.1 collective-permute-start.25
  68.8 1.1 %collective-permute-start.26 = (bf16[256,1152]{1,0:T(8,128)(2,1)S(1)}, bf16[256,1152]{1,0:T(8,128)(2,1)S(1)}, u32[]{:S(2)}, u32[]{:S(2)}) collective-permute-start(bf16[256,1152]{1,0:T(8,128)(2,1)S(1)} %pad_maximum_fusion.4.refs_2_), channel_id=1, source_target_pairs={{0,16},{1,9},{2,18},{3,11},{4,20},{5,13},{6,22},{7,15},{8,24},{9,1... | collective-permute-start | bytes 1769480 | tf_op jit(solution)/shard_map/ppermute | solution.py:270
  69.9 1.7 %convolution_bitcast_fusion = f32[1,64,1152]{2,1,0:T(8,128)} fusion(bf16[64,1152]{1,0:T(8,128)(2,1)S(1)} %shard_map.87, bf16[1152,1152]{1,0:T(8,128)(2,1)S(1)} %copy-done), kind=kOutput, calls=%fused_computation | convolution fusion | flops 169869312 | bytes 3096576 | tf_op jit(solution)/shard_map/dot_general | solution.py:17
  71.6 1.3 %shard_map.91 = (bf16[1152,1536]{1,0:T(8,128)(2,1)S(1)}, bf16[1152,512]{1,0:T(8,128)(2,1)S(1)}) custom-call(bf16[512,1152]{1,0:T(8,128)(2,1)S(1)} %shard_map.89.refs_0_, bf16[512,1152]{1,0:T(8,128)(2,1)S(1)} %shard_map.90.refs_1_, bf16[512,1152]{1,0:T(8,128)(2,1)S(1)} %collective-permute-done.18.refs_2_, bf16[512,1152]{1,0:T(8,128)(2,1)S(1)} %collective-permute-done.19.refs_3_), custom_call_target="tpu_custom_call" | custom-call | bytes 9437184 | tf_op jit(solution)/shard_map/pallas_call | solution.py:180
  72.9 0.0 collective-permute-done.25.refs_5_
  72.9 4.8 %shard_map.92.acc = f32[1152,1152]{1,0:T(8,128)S(1)} custom-call(bf16[1152,1536]{1,0:T(8,128)(2,1)S(1)} %get-tuple-element.49.x_t, bf16[256,1152]{1,0:T(8,128)(2,1)S(1)} %pad_maximum_fusion.2.refs_0_, bf16[256,1152]{1,0:T(8,128)(2,1)S(1)} %pad_maximum_fusion.3.refs_1_, bf16[256,1152]{1,0:T(8,128)(2,1)S(1)} %pad_maximum_fusion.4.refs_2_, ...), custom_call_target="tpu_custom_call" | custom-call | flops 4076863488 | bytes 12386304 | tf_op jit(solution)/shard_map/pallas_call | solution.py:235
  77.7 1.0 %collective-permute-done.26.refs_0_ = bf16[256,1152]{1,0:T(8,128)(2,1)S(1)} collective-permute-done((bf16[256,1152]{1,0:T(8,128)(2,1)S(1)}, bf16[256,1152]{1,0:T(8,128)(2,1)S(1)}, u32[]{:S(2)}, u32[]{:S(2)}) %collective-permute-start.26) | collective-permute-done | bytes 589856 | tf_op jit(solution)/shard_map/ppermute | solution.py:270
  78.7 1.1 %add_bitcast_fusion = f32[1,256,1152]{2,1,0:T(8,128)} fusion(f32[256,1152]{1,0:T(8,128)S(1)} %get-tuple-element.43, f32[256,1152]{1,0:T(8,128)S(1)} %collective-permute-done.15), kind=kLoop, calls=%fused_computation.1 | loop fusion | flops 294912 | bytes 3538944 | tf_op jit(solution)/shard_map/broadcast_in_dim | solution.py:362
  79.8 0.9 %collective-permute-done.27.refs_1_ = bf16[256,1152]{1,0:T(8,128)(2,1)S(1)} collective-permute-done((bf16[256,1152]{1,0:T(8,128)(2,1)S(1)}, bf16[256,1152]{1,0:T(8,128)(2,1)S(1)}, u32[]{:S(2)}, u32[]{:S(2)}) %collective-permute-start.27) | collective-permute-done | bytes 589856 | tf_op jit(solution)/shard_map/ppermute | solution.py:262
  80.7 3.1 %shard_map.93 = f32[1152,1152]{1,0:T(8,128)} custom-call(bf16[1152,512]{1,0:T(8,128)(2,1)S(1)} %get-tuple-element.48.x_t, f32[1152,1152]{1,0:T(8,128)S(1)} %shard_map.92.acc, bf16[256,1152]{1,0:T(8,128)(2,1)S(1)} %collective-permute-done.26.refs_0_, bf16[256,1152]{1,0:T(8,128)(2,1)S(1)} %collective-permute-done.27.refs_1_), custom_call_target="tpu_custom_call" | custom-call | flops 1358954496 | bytes 12976128 | tf_op jit(solution)/shard_map/pallas_call | solution.py:235
  (26 shorter events, 0.4 us)
Async XLA Ops:
  0.6 18.3 %copy-start = (bf16[1152,1152]{1,0:T(8,128)(2,1)S(1)}, bf16[1152,1152]{1,0:T(8,128)(2,1)}, u32[]{:S(2)}) copy-start(bf16[1152,1152]{1,0:T(8,128)(2,1)} %param.9) | copy-start | bytes 7962628
  0.6 15.4 %collective-permute-start.1 = (bf16[64,1152]{1,0:T(8,128)(2,1)}, bf16[64,1152]{1,0:T(8,128)(2,1)S(1)}, u32[]{:S(2)}, u32[]{:S(2)}) collective-permute-start(bf16[64,1152]{1,0:T(8,128)(2,1)} %bitcast.10), channel_id=1, source_target_pairs={{0,4},{1,5},{2,6},{3,7},{4,0},{5,1},{6,2},{7,3},{8,12},{9,13},{10,... | collective-permute-start | bytes 442376 | tf_op jit(solution)/shard_map/ppermute | solution.py:259
  4.7 11.3 %collective-permute-start.2 = (bf16[64,1152]{1,0:T(8,128)(2,1)}, bf16[64,1152]{1,0:T(8,128)(2,1)S(1)}, u32[]{:S(2)}, u32[]{:S(2)}) collective-permute-start(bf16[64,1152]{1,0:T(8,128)(2,1)} %bitcast.11), channel_id=1, source_target_pairs={{0,6},{1,7},{2,4},{3,5},{4,2},{5,3},{6,0},{7,1},{8,14},{9,15},{10,... | collective-permute-start | bytes 442376 | tf_op jit(solution)/shard_map/ppermute | solution.py:259
  6.1 11.8 %collective-permute-start = (bf16[64,1152]{1,0:T(8,128)(2,1)}, bf16[64,1152]{1,0:T(8,128)(2,1)S(1)}, u32[]{:S(2)}, u32[]{:S(2)}) collective-permute-start(bf16[64,1152]{1,0:T(8,128)(2,1)} %bitcast.12), channel_id=1, source_target_pairs={{0,2},{1,3},{2,0},{3,1},{4,6},{5,7},{6,4},{7,5},{8,10},{9,11},{10,... | collective-permute-start | bytes 442376 | tf_op jit(solution)/shard_map/ppermute | solution.py:259
  6.3 13.6 %collective-permute-start.4 = (bf16[256,1152]{1,0:T(8,128)(2,1)}, bf16[256,1152]{1,0:T(8,128)(2,1)}, u32[]{:S(2)}, u32[]{:S(2)}) collective-permute-start(bf16[256,1152]{1,0:T(8,128)(2,1)} %bitcast.16), channel_id=1, source_target_pairs={{0,1},{1,0},{2,3},{3,2},{4,5},{5,4},{6,7},{7,6},{8,9},{9,8},{10,11... | collective-permute-start | bytes 1769480 | tf_op jit(solution)/shard_map/ppermute | solution.py:262
  6.3 13.6 %collective-permute-start.3 = (s32[1,256]{1,0:T(1,128)}, s32[1,256]{1,0:T(1,128)S(1)}, u32[]{:S(2)}, u32[]{:S(2)}) collective-permute-start(s32[1,256]{1,0:T(1,128)} %refs_0_.1), channel_id=1, source_target_pairs={{0,1},{1,0},{2,3},{3,2},{4,5},{5,4},{6,7},{7,6},{8,9},{9,8},{10,11... | collective-permute-start | bytes 3080 | tf_op jit(solution)/shard_map/ppermute | solution.py:262
  16.0 6.8 %collective-permute-start.8 = (bf16[128,1152]{1,0:T(8,128)(2,1)S(1)}, bf16[128,1152]{1,0:T(8,128)(2,1)S(1)}, u32[]{:S(2)}, u32[]{:S(2)}) collective-permute-start(bf16[128,1152]{1,0:T(8,128)(2,1)S(1)} %pad_maximum_fusion.5), channel_id=1, source_target_pairs={{0,8},{1,17},{2,10},{3,19},{4,12},{5,21},{6,14},{7,23},{8,0},{9,25... | collective-permute-start | bytes 884744 | tf_op jit(solution)/shard_map/ppermute | solution.py:270
  17.9 0.9 %copy-start.1 = (bf16[1,64,1152]{2,1,0:T(8,128)(2,1)S(1)}, bf16[1,64,1152]{2,1,0:T(8,128)(2,1)}, u32[]{:S(2)}) copy-start(bf16[1,64,1152]{2,1,0:T(8,128)(2,1)} %param.6) | copy-start | bytes 442372
  18.9 1.1 %copy-start.3 = (bf16[1,256,1152]{2,1,0:T(8,128)(2,1)S(1)}, bf16[1,256,1152]{2,1,0:T(8,128)(2,1)}, u32[]{:S(2)}) copy-start(bf16[1,256,1152]{2,1,0:T(8,128)(2,1)} %param.7) | copy-start | bytes 1769476
  18.9 1.1 %copy-start.4 = (s32[1,256]{1,0:T(1,128)S(1)}, s32[1,256]{1,0:T(1,128)}, u32[]{:S(2)}) copy-start(s32[1,256]{1,0:T(1,128)} %refs_0_.1) | copy-start | bytes 3076
  22.3 2.7 %copy-start.2 = (bf16[1,64,1152]{2,1,0:T(8,128)(2,1)S(1)}, bf16[1,64,1152]{2,1,0:T(8,128)(2,1)}, u32[]{:S(2)}) copy-start(bf16[1,64,1152]{2,1,0:T(8,128)(2,1)} %param.6) | copy-start | bytes 442372
  22.9 19.7 %collective-permute-start.9 = (bf16[256,1152]{1,0:T(8,128)(2,1)S(1)}, bf16[256,1152]{1,0:T(8,128)(2,1)S(1)}, u32[]{:S(2)}, u32[]{:S(2)}) collective-permute-start(bf16[256,1152]{1,0:T(8,128)(2,1)S(1)} %pad_maximum_fusion.refs_0_), channel_id=1, source_target_pairs={{0,16},{1,9},{2,18},{3,11},{4,20},{5,13},{6,22},{7,15},{8,24},{9,1... | collective-permute-start | bytes 1769480 | tf_op jit(solution)/shard_map/ppermute | solution.py:270
  25.1 7.6 %collective-permute-start.16 = (bf16[128,1152]{1,0:T(8,128)(2,1)S(1)}, bf16[128,1152]{1,0:T(8,128)(2,1)S(1)}, u32[]{:S(2)}, u32[]{:S(2)}) collective-permute-start(bf16[128,1152]{1,0:T(8,128)(2,1)S(1)} %pad_maximum_fusion.8), channel_id=1, source_target_pairs={{0,8},{1,17},{2,10},{3,19},{4,12},{5,21},{6,14},{7,23},{8,0},{9,25... | collective-permute-start | bytes 884744 | tf_op jit(solution)/shard_map/ppermute | solution.py:270
  26.6 7.3 %collective-permute-start.5 = (bf16[64,1152]{1,0:T(8,128)(2,1)S(1)}, bf16[64,1152]{1,0:T(8,128)(2,1)S(1)}, u32[]{:S(2)}, u32[]{:S(2)}) collective-permute-start(bf16[64,1152]{1,0:T(8,128)(2,1)S(1)} %get-tuple-element.31), channel_id=1, source_target_pairs={{0,2},{1,3},{2,0},{3,1},{4,6},{5,7},{6,4},{7,5},{8,10},{9,11},{10,... | collective-permute-start | bytes 442376 | tf_op jit(solution)/shard_map/ppermute | solution.py:259
  29.2 13.4 %collective-permute-start.6 = (bf16[64,1152]{1,0:T(8,128)(2,1)S(1)}, bf16[64,1152]{1,0:T(8,128)(2,1)S(1)}, u32[]{:S(2)}, u32[]{:S(2)}) collective-permute-start(bf16[64,1152]{1,0:T(8,128)(2,1)S(1)} %get-tuple-element.32), channel_id=1, source_target_pairs={{0,4},{1,5},{2,6},{3,7},{4,0},{5,1},{6,2},{7,3},{8,12},{9,13},{10,... | collective-permute-start | bytes 442376 | tf_op jit(solution)/shard_map/ppermute | solution.py:259
  31.0 11.6 %collective-permute-start.7 = (bf16[64,1152]{1,0:T(8,128)(2,1)S(1)}, bf16[64,1152]{1,0:T(8,128)(2,1)S(1)}, u32[]{:S(2)}, u32[]{:S(2)}) collective-permute-start(bf16[64,1152]{1,0:T(8,128)(2,1)S(1)} %get-tuple-element.33), channel_id=1, source_target_pairs={{0,6},{1,7},{2,4},{3,5},{4,2},{5,3},{6,0},{7,1},{8,14},{9,15},{10,... | collective-permute-start | bytes 442376 | tf_op jit(solution)/shard_map/ppermute | solution.py:259
  42.8 6.9 %collective-permute-start.13 = (bf16[64,1152]{1,0:T(8,128)(2,1)S(1)}, bf16[64,1152]{1,0:T(8,128)(2,1)S(1)}, u32[]{:S(2)}, u32[]{:S(2)}) collective-permute-start(bf16[64,1152]{1,0:T(8,128)(2,1)S(1)} %shard_map.87), channel_id=1, source_target_pairs={{0,8},{1,17},{2,10},{3,19},{4,12},{5,21},{6,14},{7,23},{8,0},{9,25... | collective-permute-start | bytes 442376 | tf_op jit(solution)/shard_map/ppermute | solution.py:270
  43.4 16.6 %collective-permute-start.17 = (bf16[256,1152]{1,0:T(8,128)(2,1)S(1)}, bf16[256,1152]{1,0:T(8,128)(2,1)S(1)}, u32[]{:S(2)}, u32[]{:S(2)}) collective-permute-start(bf16[256,1152]{1,0:T(8,128)(2,1)S(1)} %pad_maximum_fusion.1.refs_0_), channel_id=1, source_target_pairs={{0,16},{1,9},{2,18},{3,11},{4,20},{5,13},{6,22},{7,15},{8,24},{9,1... | collective-permute-start | bytes 1769480 | tf_op jit(solution)/shard_map/ppermute | solution.py:270
  44.3 6.4 %collective-permute-start.12 = (bf16[64,1152]{1,0:T(8,128)(2,1)S(1)}, bf16[64,1152]{1,0:T(8,128)(2,1)S(1)}, u32[]{:S(2)}, u32[]{:S(2)}) collective-permute-start(bf16[64,1152]{1,0:T(8,128)(2,1)S(1)} %shard_map.87), channel_id=1, source_target_pairs={{0,2},{1,3},{2,0},{3,1},{4,6},{5,7},{6,4},{7,5},{8,10},{9,11},{10,... | collective-permute-start | bytes 442376 | tf_op jit(solution)/shard_map/ppermute | solution.py:259
  46.5 12.3 %collective-permute-start.10 = (bf16[64,1152]{1,0:T(8,128)(2,1)S(1)}, bf16[64,1152]{1,0:T(8,128)(2,1)S(1)}, u32[]{:S(2)}, u32[]{:S(2)}) collective-permute-start(bf16[64,1152]{1,0:T(8,128)(2,1)S(1)} %shard_map.87), channel_id=1, source_target_pairs={{0,4},{1,5},{2,6},{3,7},{4,0},{5,1},{6,2},{7,3},{8,12},{9,13},{10,... | collective-permute-start | bytes 442376 | tf_op jit(solution)/shard_map/ppermute | solution.py:259
  47.5 11.3 %collective-permute-start.11 = (bf16[64,1152]{1,0:T(8,128)(2,1)S(1)}, bf16[64,1152]{1,0:T(8,128)(2,1)S(1)}, u32[]{:S(2)}, u32[]{:S(2)}) collective-permute-start(bf16[64,1152]{1,0:T(8,128)(2,1)S(1)} %shard_map.87), channel_id=1, source_target_pairs={{0,6},{1,7},{2,4},{3,5},{4,2},{5,3},{6,0},{7,1},{8,14},{9,15},{10,... | collective-permute-start | bytes 442376 | tf_op jit(solution)/shard_map/ppermute | solution.py:259
  49.7 11.0 %collective-permute-start.20 = (bf16[128,1152]{1,0:T(8,128)(2,1)S(1)}, bf16[128,1152]{1,0:T(8,128)(2,1)S(1)}, u32[]{:S(2)}, u32[]{:S(2)}) collective-permute-start(bf16[128,1152]{1,0:T(8,128)(2,1)S(1)} %pad_maximum_fusion.7), channel_id=1, source_target_pairs={{0,16},{1,9},{2,18},{3,11},{4,20},{5,13},{6,22},{7,15},{8,24},{9,1... | collective-permute-start | bytes 884744 | tf_op jit(solution)/shard_map/ppermute | solution.py:270
  50.7 10.1 %collective-permute-start.21 = (bf16[64,1152]{1,0:T(8,128)(2,1)S(1)}, bf16[64,1152]{1,0:T(8,128)(2,1)S(1)}, u32[]{:S(2)}, u32[]{:S(2)}) collective-permute-start(bf16[64,1152]{1,0:T(8,128)(2,1)S(1)} %collective-permute-done.12), channel_id=1, source_target_pairs={{0,8},{1,17},{2,10},{3,19},{4,12},{5,21},{6,14},{7,23},{8,0},{9,25... | collective-permute-start | bytes 442376 | tf_op jit(solution)/shard_map/ppermute | solution.py:270
  58.8 8.4 %collective-permute-start.14 = (bf16[128,1152]{1,0:T(8,128)(2,1)S(1)}, bf16[128,1152]{1,0:T(8,128)(2,1)S(1)}, u32[]{:S(2)}, u32[]{:S(2)}) collective-permute-start(bf16[128,1152]{1,0:T(8,128)(2,1)S(1)} %pad_maximum_fusion.6), channel_id=1, source_target_pairs={{0,8},{1,17},{2,10},{3,19},{4,12},{5,21},{6,14},{7,23},{8,0},{9,25... | collective-permute-start | bytes 884744 | tf_op jit(solution)/shard_map/ppermute | solution.py:270
  60.0 8.8 %collective-permute-start.19 = (bf16[512,1152]{1,0:T(8,128)(2,1)S(1)}, bf16[512,1152]{1,0:T(8,128)(2,1)S(1)}, u32[]{:S(2)}, u32[]{:S(2)}) collective-permute-start(bf16[512,1152]{1,0:T(8,128)(2,1)S(1)} %shard_map.90.refs_1_), channel_id=1, source_target_pairs={{0,1},{1,0},{2,3},{3,2},{4,5},{5,4},{6,7},{7,6},{8,9},{9,8},{10,11... | collective-permute-start | bytes 3538952 | tf_op jit(solution)/shard_map/ppermute | solution.py:262
  60.1 11.5 %collective-permute-start.18 = (bf16[512,1152]{1,0:T(8,128)(2,1)S(1)}, bf16[512,1152]{1,0:T(8,128)(2,1)S(1)}, u32[]{:S(2)}, u32[]{:S(2)}) collective-permute-start(bf16[512,1152]{1,0:T(8,128)(2,1)S(1)} %shard_map.89.refs_0_), channel_id=1, source_target_pairs={{0,1},{1,0},{2,3},{3,2},{4,5},{5,4},{6,7},{7,6},{8,9},{9,8},{10,11... | collective-permute-start | bytes 3538952 | tf_op jit(solution)/shard_map/ppermute | solution.py:262
  60.7 8.0 %collective-permute-start.23 = (bf16[256,1152]{1,0:T(8,128)(2,1)S(1)}, bf16[256,1152]{1,0:T(8,128)(2,1)S(1)}, u32[]{:S(2)}, u32[]{:S(2)}) collective-permute-start(bf16[256,1152]{1,0:T(8,128)(2,1)S(1)} %pad_maximum_fusion.2.refs_0_), channel_id=1, source_target_pairs={{0,1},{1,0},{2,3},{3,2},{4,5},{5,4},{6,7},{7,6},{8,9},{9,8},{10,11... | collective-permute-start | bytes 1769480 | tf_op jit(solution)/shard_map/ppermute | solution.py:262
  60.8 7.0 %collective-permute-start.22 = (bf16[128,1152]{1,0:T(8,128)(2,1)S(1)}, bf16[128,1152]{1,0:T(8,128)(2,1)S(1)}, u32[]{:S(2)}, u32[]{:S(2)}) collective-permute-start(bf16[128,1152]{1,0:T(8,128)(2,1)S(1)} %pad_maximum_fusion.9), channel_id=1, source_target_pairs={{0,16},{1,9},{2,18},{3,11},{4,20},{5,13},{6,22},{7,15},{8,24},{9,1... | collective-permute-start | bytes 884744 | tf_op jit(solution)/shard_map/ppermute | solution.py:270
  67.7 11.0 %collective-permute-start.15 = (f32[256,1152]{1,0:T(8,128)S(1)}, f32[256,1152]{1,0:T(8,128)S(1)}, u32[]{:S(2)}, u32[]{:S(2)}) collective-permute-start(f32[256,1152]{1,0:T(8,128)S(1)} %get-tuple-element.44), channel_id=1, source_target_pairs={{0,1},{1,0},{2,3},{3,2},{4,5},{5,4},{6,7},{7,6},{8,9},{9,8},{10,11... | collective-permute-start | bytes 3538952 | tf_op jit(solution)/shard_map/ppermute | solution.py:262
  67.9 4.9 %collective-permute-start.24 = (bf16[256,1152]{1,0:T(8,128)(2,1)S(1)}, bf16[256,1152]{1,0:T(8,128)(2,1)S(1)}, u32[]{:S(2)}, u32[]{:S(2)}) collective-permute-start(bf16[256,1152]{1,0:T(8,128)(2,1)S(1)} %pad_maximum_fusion.3.refs_1_), channel_id=1, source_target_pairs={{0,1},{1,0},{2,3},{3,2},{4,5},{5,4},{6,7},{7,6},{8,9},{9,8},{10,11... | collective-permute-start | bytes 1769480 | tf_op jit(solution)/shard_map/ppermute | solution.py:262
  68.7 4.2 %collective-permute-start.25 = (bf16[256,1152]{1,0:T(8,128)(2,1)S(1)}, bf16[256,1152]{1,0:T(8,128)(2,1)S(1)}, u32[]{:S(2)}, u32[]{:S(2)}) collective-permute-start(bf16[256,1152]{1,0:T(8,128)(2,1)S(1)} %pad_maximum_fusion.4.refs_2_), channel_id=1, source_target_pairs={{0,1},{1,0},{2,3},{3,2},{4,5},{5,4},{6,7},{7,6},{8,9},{9,8},{10,11... | collective-permute-start | bytes 1769480 | tf_op jit(solution)/shard_map/ppermute | solution.py:262
  68.8 9.9 %collective-permute-start.26 = (bf16[256,1152]{1,0:T(8,128)(2,1)S(1)}, bf16[256,1152]{1,0:T(8,128)(2,1)S(1)}, u32[]{:S(2)}, u32[]{:S(2)}) collective-permute-start(bf16[256,1152]{1,0:T(8,128)(2,1)S(1)} %pad_maximum_fusion.4.refs_2_), channel_id=1, source_target_pairs={{0,16},{1,9},{2,18},{3,11},{4,20},{5,13},{6,22},{7,15},{8,24},{9,1... | collective-permute-start | bytes 1769480 | tf_op jit(solution)/shard_map/ppermute | solution.py:270
  78.7 2.0 %collective-permute-start.27 = (bf16[256,1152]{1,0:T(8,128)(2,1)S(1)}, bf16[256,1152]{1,0:T(8,128)(2,1)S(1)}, u32[]{:S(2)}, u32[]{:S(2)}) collective-permute-start(bf16[256,1152]{1,0:T(8,128)(2,1)S(1)} %collective-permute-done.26.refs_0_), channel_id=1, source_target_pairs={{0,1},{1,0},{2,3},{3,2},{4,5},{5,4},{6,7},{7,6},{8,9},{9,8},{10,11... | collective-permute-start | bytes 1769480 | tf_op jit(solution)/shard_map/ppermute | solution.py:262

commit v13 on v12

--- a/solution.py
+++ b/solution.py
@@ -303,7 +303,7 @@
 
     x_near = over_d(x_near, after(x_near_first, back))
     x_far = over_d(x_far, after(x_far_first, sent))
-    back = after(back, x_far)
+    back = after(back[::-1], x_far)
     ge = embed_grad(own, u, inv_norm, back)
     grad_features = dot(ge, weight, LAST)
 

time: 84 us -> 82.3 us (0.980)
  starting transfers between devices: 31.1 us -> 29.7 us
    ppermute x9, waiting for transfers between devices: 25.1 us -> 23.6 us  [along_z(): return lax.ppermute(v, 'blk', [(i, i ^ 2 * k) for i in range(nb)])]
    ppermute x10, waiting for transfers between devices: 7.07 us -> 8.27 us  [step_d(): return lax.ppermute(v, ('dp', 'blk'), perm)]
    ppermute x9, starting transfers between devices: 16.2 us -> 15 us  [along_z(): return lax.ppermute(v, 'blk', [(i, i ^ 2 * k) for i in range(nb)])]
where the time goes in v13:
time: 82.3 us; the launch traced here: 82.1 us
  waiting for transfers between devices  32.7 us (40%)
  starting transfers between devices  29.7 us (36%)
  Pallas kernels  12.3 us (15%)
  matrix products  2.65 us (3%)
  between operations  2.15 us (3%)
  other arithmetic  1.5 us (2%)
  local copies, waits for them, and re-layouts  1.01 us (1%)
    ppermute x9, waiting for transfers between devices, along_z(): return lax.ppermute(v, 'blk', [(i, i ^ 2 * k) for i in range(nb)])  23.6 us
    ppermute x9, starting transfers between devices, along_z(): return lax.ppermute(v, 'blk', [(i, i ^ 2 * k) for i in range(nb)])  15 us
    ppermute x10, starting transfers between devices, step_d(): return lax.ppermute(v, ('dp', 'blk'), perm)  12.6 us
    ppermute x10, waiting for transfers between devices, step_d(): return lax.ppermute(v, ('dp', 'blk'), perm)  8.27 us
    pallas_call x2, Pallas kernels, weight_sum(): pl.pallas_call(kernel, out_shape=jax.ShapeDtypeStruct((depth, depth), F32...  7.85 us
    dot_general x2, matrix products, dot(): return lax.dot_general(a, b, dims, preferred_element_type=F32)  2.65 us
    pallas_call x1, Pallas kernels, scores(): pl.pallas_call(functools.partial(score_kernel, nz), out_shape=outs, in_sp...  2.3 us
    ppermute x9, starting transfers between devices, swap(): return lax.ppermute(v, 'blk', [(i, i ^ 1) for i in range(nb)])  2.11 us
  transfers between devices with their start and end apart: 28, of which 11 were waited for; matrix products, arithmetic and copies ran while one was open for 5% of the time, Pallas kernels for 11%

profile of v13, /device:TPU:0, one launch (start us, length us, event | category | flops | bytes accessed | tf_op | source)
XLA Modules:
  0.0 82.1 jit_solution(10317724371362274563)
XLA Ops:
  0.6 0.0 copy-start
  0.6 4.1 %collective-permute-start.1 = (bf16[64,1152]{1,0:T(8,128)(2,1)}, bf16[64,1152]{1,0:T(8,128)(2,1)S(1)}, u32[]{:S(2)}, u32[]{:S(2)}) collective-permute-start(bf16[64,1152]{1,0:T(8,128)(2,1)} %bitcast.10), channel_id=1, source_target_pairs={{0,4},{1,5},{2,6},{3,7},{4,0},{5,1},{6,2},{7,3},{8,12},{9,13},{10,... | collective-permute-start | bytes 442376 | tf_op jit(solution)/shard_map/ppermute | solution.py:259
  4.7 1.3 %collective-permute-start.2 = (bf16[64,1152]{1,0:T(8,128)(2,1)}, bf16[64,1152]{1,0:T(8,128)(2,1)S(1)}, u32[]{:S(2)}, u32[]{:S(2)}) collective-permute-start(bf16[64,1152]{1,0:T(8,128)(2,1)} %bitcast.11), channel_id=1, source_target_pairs={{0,6},{1,7},{2,4},{3,5},{4,2},{5,3},{6,0},{7,1},{8,14},{9,15},{10,... | collective-permute-start | bytes 442376 | tf_op jit(solution)/shard_map/ppermute | solution.py:259
  6.1 0.2 collective-permute-start
  6.3 0.5 collective-permute-start.3
  8.1 7.9 %collective-permute-done.1.refs_2_ = bf16[64,1152]{1,0:T(8,128)(2,1)S(1)} collective-permute-done((bf16[64,1152]{1,0:T(8,128)(2,1)}, bf16[64,1152]{1,0:T(8,128)(2,1)S(1)}, u32[]{:S(2)}, u32[]{:S(2)}) %collective-permute-start.1) | collective-permute-done | bytes 147488 | tf_op jit(solution)/shard_map/ppermute | solution.py:259
  16.0 0.0 collective-permute-done.2.refs_3_
  16.0 1.9 %collective-permute-start.8 = (bf16[128,1152]{1,0:T(8,128)(2,1)S(1)}, bf16[128,1152]{1,0:T(8,128)(2,1)S(1)}, u32[]{:S(2)}, u32[]{:S(2)}) collective-permute-start(bf16[128,1152]{1,0:T(8,128)(2,1)S(1)} %pad_maximum_fusion.5), channel_id=1, source_target_pairs={{0,8},{1,17},{2,10},{3,19},{4,12},{5,21},{6,14},{7,23},{8,0},{9,25... | collective-permute-start | bytes 884744 | tf_op jit(solution)/shard_map/ppermute | solution.py:270
  17.9 0.0 collective-permute-done.refs_1_
  17.9 0.9 %copy-done.1 = bf16[1,64,1152]{2,1,0:T(8,128)(2,1)S(1)} copy-done((bf16[1,64,1152]{2,1,0:T(8,128)(2,1)S(1)}, bf16[1,64,1152]{2,1,0:T(8,128)(2,1)}, u32[]{:S(2)}) %copy-start.1) | copy-done | bytes 147480
  18.9 0.0 copy-start.3
  18.9 0.0 copy-start.4
  18.9 1.0 %fusion.embed = f32[256,1152]{1,0:T(8,128)S(1)} fusion(bf16[256,1152]{1,0:T(8,128)(2,1)S(1)} %shard_map.85, bf16[1152,1152]{1,0:T(8,128)(2,1)S(1)} %copy-done), kind=kOutput, calls=%fused_computation.13 | convolution fusion | flops 679477248 | bytes 4423680 | tf_op jit(solution)/shard_map/dot_general | solution.py:17
  19.9 0.0 collective-permute-done.3.refs_1_
  19.9 0.0 collective-permute-done.4.refs_3_
  20.0 0.1 iota.7.both
  20.0 2.3 %shard_map.86 = (f32[64,1152]{1,0:T(8,128)S(1)}, f32[64,1152]{1,0:T(8,128)S(1)}, f32[64,128]{1,0:T(8,128)S(1)}, bf16[256,1152]{1,0:T(8,128)(2,1)S(1)}, bf16[256,...) custom-call(f32[16,128]{1,0:T(8,128)S(1)} %iota.7.both, ...), custom_call_target="tpu_custom_call" | custom-call | flops 603979776 | bytes 4718592 | tf_op jit(solution)/shard_map/pallas_call | solution.py:74
  22.3 0.0 copy-start.2
  22.4 0.5 collective-permute-done.8
  22.9 2.1 %collective-permute-start.9 = (bf16[256,1152]{1,0:T(8,128)(2,1)S(1)}, bf16[256,1152]{1,0:T(8,128)(2,1)S(1)}, u32[]{:S(2)}, u32[]{:S(2)}) collective-permute-start(bf16[256,1152]{1,0:T(8,128)(2,1)S(1)} %pad_maximum_fusion.refs_0_), channel_id=1, source_target_pairs={{0,16},{1,9},{2,18},{3,11},{4,20},{5,13},{6,22},{7,15},{8,24},{9,1... | collective-permute-start | bytes 1769480 | tf_op jit(solution)/shard_map/ppermute | solution.py:270
  25.1 1.6 %collective-permute-start.16 = (bf16[128,1152]{1,0:T(8,128)(2,1)S(1)}, bf16[128,1152]{1,0:T(8,128)(2,1)S(1)}, u32[]{:S(2)}, u32[]{:S(2)}) collective-permute-start(bf16[128,1152]{1,0:T(8,128)(2,1)S(1)} %pad_maximum_fusion.8), channel_id=1, source_target_pairs={{0,8},{1,17},{2,10},{3,19},{4,12},{5,21},{6,14},{7,23},{8,0},{9,25... | collective-permute-start | bytes 884744 | tf_op jit(solution)/shard_map/ppermute | solution.py:270
  26.6 2.2 %collective-permute-start.5 = (bf16[64,1152]{1,0:T(8,128)(2,1)S(1)}, bf16[64,1152]{1,0:T(8,128)(2,1)S(1)}, u32[]{:S(2)}, u32[]{:S(2)}) collective-permute-start(bf16[64,1152]{1,0:T(8,128)(2,1)S(1)} %get-tuple-element.31), channel_id=1, source_target_pairs={{0,6},{1,7},{2,4},{3,5},{4,2},{5,3},{6,0},{7,1},{8,14},{9,15},{10,... | collective-permute-start | bytes 442376 | tf_op jit(solution)/shard_map/ppermute | solution.py:259
  28.8 2.2 %collective-permute-start.6 = (bf16[64,1152]{1,0:T(8,128)(2,1)S(1)}, bf16[64,1152]{1,0:T(8,128)(2,1)S(1)}, u32[]{:S(2)}, u32[]{:S(2)}) collective-permute-start(bf16[64,1152]{1,0:T(8,128)(2,1)S(1)} %get-tuple-element.32), channel_id=1, source_target_pairs={{0,4},{1,5},{2,6},{3,7},{4,0},{5,1},{6,2},{7,3},{8,12},{9,13},{10,... | collective-permute-start | bytes 442376 | tf_op jit(solution)/shard_map/ppermute | solution.py:259
  31.0 0.6 collective-permute-start.7
  31.6 1.0 %collective-permute-done.16 = bf16[128,1152]{1,0:T(8,128)(2,1)S(1)} collective-permute-done((bf16[128,1152]{1,0:T(8,128)(2,1)S(1)}, bf16[128,1152]{1,0:T(8,128)(2,1)S(1)}, u32[]{:S(2)}, u32[]{:S(2)}) %collective-permute-start.16) | collective-permute-done | bytes 294944 | tf_op jit(solution)/shard_map/ppermute | solution.py:270
  32.6 1.8 %collective-permute-done.5.refs_0_ = bf16[64,1152]{1,0:T(8,128)(2,1)S(1)} collective-permute-done((bf16[64,1152]{1,0:T(8,128)(2,1)S(1)}, bf16[64,1152]{1,0:T(8,128)(2,1)S(1)}, u32[]{:S(2)}, u32[]{:S(2)}) %collective-permute-start.5) | collective-permute-done | bytes 147488 | tf_op jit(solution)/shard_map/ppermute | solution.py:259
  34.4 7.1 %collective-permute-done.6.refs_1_ = bf16[64,1152]{1,0:T(8,128)(2,1)S(1)} collective-permute-done((bf16[64,1152]{1,0:T(8,128)(2,1)S(1)}, bf16[64,1152]{1,0:T(8,128)(2,1)S(1)}, u32[]{:S(2)}, u32[]{:S(2)}) %collective-permute-start.6) | collective-permute-done | bytes 147488 | tf_op jit(solution)/shard_map/ppermute | solution.py:259
  41.5 0.0 collective-permute-done.9.refs_1_
  41.5 0.2 shard_map.87
  41.7 0.6 collective-permute-start.13
  42.4 0.9 %collective-permute-start.17 = (bf16[256,1152]{1,0:T(8,128)(2,1)S(1)}, bf16[256,1152]{1,0:T(8,128)(2,1)S(1)}, u32[]{:S(2)}, u32[]{:S(2)}) collective-permute-start(bf16[256,1152]{1,0:T(8,128)(2,1)S(1)} %pad_maximum_fusion.1.refs_0_), channel_id=1, source_target_pairs={{0,16},{1,9},{2,18},{3,11},{4,20},{5,13},{6,22},{7,15},{8,24},{9,1... | collective-permute-start | bytes 1769480 | tf_op jit(solution)/shard_map/ppermute | solution.py:270
  43.3 0.0 collective-permute-start.12
  43.3 3.4 %collective-permute-start.10 = (bf16[64,1152]{1,0:T(8,128)(2,1)S(1)}, bf16[64,1152]{1,0:T(8,128)(2,1)S(1)}, u32[]{:S(2)}, u32[]{:S(2)}) collective-permute-start(bf16[64,1152]{1,0:T(8,128)(2,1)S(1)} %shard_map.87), channel_id=1, source_target_pairs={{0,4},{1,5},{2,6},{3,7},{4,0},{5,1},{6,2},{7,3},{8,12},{9,13},{10,... | collective-permute-start | bytes 442376 | tf_op jit(solution)/shard_map/ppermute | solution.py:259
  46.7 1.0 %collective-permute-start.11 = (bf16[64,1152]{1,0:T(8,128)(2,1)S(1)}, bf16[64,1152]{1,0:T(8,128)(2,1)S(1)}, u32[]{:S(2)}, u32[]{:S(2)}) collective-permute-start(bf16[64,1152]{1,0:T(8,128)(2,1)S(1)} %shard_map.87), channel_id=1, source_target_pairs={{0,6},{1,7},{2,4},{3,5},{4,2},{5,3},{6,0},{7,1},{8,14},{9,15},{10,... | collective-permute-start | bytes 442376 | tf_op jit(solution)/shard_map/ppermute | solution.py:259
  47.6 0.9 %collective-permute-done.13 = bf16[64,1152]{1,0:T(8,128)(2,1)S(1)} collective-permute-done((bf16[64,1152]{1,0:T(8,128)(2,1)S(1)}, bf16[64,1152]{1,0:T(8,128)(2,1)S(1)}, u32[]{:S(2)}, u32[]{:S(2)}) %collective-permute-start.13) | collective-permute-done | bytes 147488 | tf_op jit(solution)/shard_map/ppermute | solution.py:270
  48.6 0.6 collective-permute-start.20
  49.2 0.1 shard_map.90.refs_1_
  49.3 0.3 collective-permute-done.12
  49.5 1.1 %collective-permute-start.21 = (bf16[64,1152]{1,0:T(8,128)(2,1)S(1)}, bf16[64,1152]{1,0:T(8,128)(2,1)S(1)}, u32[]{:S(2)}, u32[]{:S(2)}) collective-permute-start(bf16[64,1152]{1,0:T(8,128)(2,1)S(1)} %collective-permute-done.12), channel_id=1, source_target_pairs={{0,8},{1,17},{2,10},{3,19},{4,12},{5,21},{6,14},{7,23},{8,0},{9,25... | collective-permute-start | bytes 442376 | tf_op jit(solution)/shard_map/ppermute | solution.py:270
  50.6 6.5 %collective-permute-done.10 = bf16[64,1152]{1,0:T(8,128)(2,1)S(1)} collective-permute-done((bf16[64,1152]{1,0:T(8,128)(2,1)S(1)}, bf16[64,1152]{1,0:T(8,128)(2,1)S(1)}, u32[]{:S(2)}, u32[]{:S(2)}) %collective-permute-start.10) | collective-permute-done | bytes 147488 | tf_op jit(solution)/shard_map/ppermute | solution.py:259
  57.2 1.2 %collective-permute-start.14 = (bf16[128,1152]{1,0:T(8,128)(2,1)S(1)}, bf16[128,1152]{1,0:T(8,128)(2,1)S(1)}, u32[]{:S(2)}, u32[]{:S(2)}) collective-permute-start(bf16[128,1152]{1,0:T(8,128)(2,1)S(1)} %pad_maximum_fusion.6), channel_id=1, source_target_pairs={{0,8},{1,17},{2,10},{3,19},{4,12},{5,21},{6,14},{7,23},{8,0},{9,25... | collective-permute-start | bytes 884744 | tf_op jit(solution)/shard_map/ppermute | solution.py:270
  58.3 0.0 collective-permute-start.19
  58.3 0.0 collective-permute-done.17.refs_1_
  58.3 0.1 shard_map.89.refs_0_
  58.4 0.6 collective-permute-start.18
  59.0 0.0 collective-permute-done.20
  59.0 0.1 collective-permute-start.23
  59.1 0.0 collective-permute-done.21
  59.1 1.6 %collective-permute-start.22 = (bf16[128,1152]{1,0:T(8,128)(2,1)S(1)}, bf16[128,1152]{1,0:T(8,128)(2,1)S(1)}, u32[]{:S(2)}, u32[]{:S(2)}) collective-permute-start(bf16[128,1152]{1,0:T(8,128)(2,1)S(1)} %pad_maximum_fusion.9), channel_id=1, source_target_pairs={{0,16},{1,9},{2,18},{3,11},{4,20},{5,13},{6,22},{7,15},{8,24},{9,1... | collective-permute-start | bytes 884744 | tf_op jit(solution)/shard_map/ppermute | solution.py:270
  60.7 4.8 %collective-permute-done.14 = bf16[128,1152]{1,0:T(8,128)(2,1)S(1)} collective-permute-done((bf16[128,1152]{1,0:T(8,128)(2,1)S(1)}, bf16[128,1152]{1,0:T(8,128)(2,1)S(1)}, u32[]{:S(2)}, u32[]{:S(2)}) %collective-permute-start.14) | collective-permute-done | bytes 294944 | tf_op jit(solution)/shard_map/ppermute | solution.py:270
  65.5 0.5 shard_map.88
  66.1 0.1 collective-permute-start.15
  66.2 0.0 collective-permute-done.22
  66.3 0.8 collective-permute-start.24
  67.0 0.1 collective-permute-start.25
  67.1 0.0 collective-permute-done.19.refs_3_
  67.1 1.1 %collective-permute-start.26 = (bf16[256,1152]{1,0:T(8,128)(2,1)S(1)}, bf16[256,1152]{1,0:T(8,128)(2,1)S(1)}, u32[]{:S(2)}, u32[]{:S(2)}) collective-permute-start(bf16[256,1152]{1,0:T(8,128)(2,1)S(1)} %pad_maximum_fusion.4.refs_2_), channel_id=1, source_target_pairs={{0,16},{1,9},{2,18},{3,11},{4,20},{5,13},{6,22},{7,15},{8,24},{9,1... | collective-permute-start | bytes 1769480 | tf_op jit(solution)/shard_map/ppermute | solution.py:270
  68.2 1.7 %convolution_bitcast_fusion = f32[1,64,1152]{2,1,0:T(8,128)} fusion(bf16[64,1152]{1,0:T(8,128)(2,1)S(1)} %shard_map.87, bf16[1152,1152]{1,0:T(8,128)(2,1)S(1)} %copy-done), kind=kOutput, calls=%fused_computation | convolution fusion | flops 169869312 | bytes 3096576 | tf_op jit(solution)/shard_map/dot_general | solution.py:17
  69.9 1.3 %shard_map.91 = (bf16[1152,1536]{1,0:T(8,128)(2,1)S(1)}, bf16[1152,512]{1,0:T(8,128)(2,1)S(1)}) custom-call(bf16[512,1152]{1,0:T(8,128)(2,1)S(1)} %shard_map.89.refs_0_, bf16[512,1152]{1,0:T(8,128)(2,1)S(1)} %shard_map.90.refs_1_, bf16[512,1152]{1,0:T(8,128)(2,1)S(1)} %collective-permute-done.18.refs_2_, bf16[512,1152]{1,0:T(8,128)(2,1)S(1)} %collective-permute-done.19.refs_3_), custom_call_target="tpu_custom_call" | custom-call | bytes 9437184 | tf_op jit(solution)/shard_map/pallas_call | solution.py:180
  71.2 4.8 %shard_map.92.acc = f32[1152,1152]{1,0:T(8,128)S(1)} custom-call(bf16[1152,1536]{1,0:T(8,128)(2,1)S(1)} %get-tuple-element.49.x_t, bf16[256,1152]{1,0:T(8,128)(2,1)S(1)} %pad_maximum_fusion.2.refs_0_, bf16[256,1152]{1,0:T(8,128)(2,1)S(1)} %pad_maximum_fusion.3.refs_1_, bf16[256,1152]{1,0:T(8,128)(2,1)S(1)} %pad_maximum_fusion.4.refs_2_, ...), custom_call_target="tpu_custom_call" | custom-call | flops 4076863488 | bytes 12386304 | tf_op jit(solution)/shard_map/pallas_call | solution.py:235
  76.0 1.0 %collective-permute-done.26.refs_0_ = bf16[256,1152]{1,0:T(8,128)(2,1)S(1)} collective-permute-done((bf16[256,1152]{1,0:T(8,128)(2,1)S(1)}, bf16[256,1152]{1,0:T(8,128)(2,1)S(1)}, u32[]{:S(2)}, u32[]{:S(2)}) %collective-permute-start.26) | collective-permute-done | bytes 589856 | tf_op jit(solution)/shard_map/ppermute | solution.py:270
  77.0 1.1 %add_bitcast_fusion = f32[1,256,1152]{2,1,0:T(8,128)} fusion(f32[256,1152]{1,0:T(8,128)S(1)} %get-tuple-element.43, f32[256,1152]{1,0:T(8,128)S(1)} %collective-permute-done.15), kind=kLoop, calls=%fused_computation.1 | loop fusion | flops 294912 | bytes 3538944 | tf_op jit(solution)/shard_map/broadcast_in_dim | solution.py:362
  78.2 0.9 %collective-permute-done.27.refs_1_ = bf16[256,1152]{1,0:T(8,128)(2,1)S(1)} collective-permute-done((bf16[256,1152]{1,0:T(8,128)(2,1)S(1)}, bf16[256,1152]{1,0:T(8,128)(2,1)S(1)}, u32[]{:S(2)}, u32[]{:S(2)}) %collective-permute-start.27) | collective-permute-done | bytes 589856 | tf_op jit(solution)/shard_map/ppermute | solution.py:262
  79.0 3.1 %shard_map.93 = f32[1152,1152]{1,0:T(8,128)} custom-call(bf16[1152,512]{1,0:T(8,128)(2,1)S(1)} %get-tuple-element.48.x_t, f32[1152,1152]{1,0:T(8,128)S(1)} %shard_map.92.acc, bf16[256,1152]{1,0:T(8,128)(2,1)S(1)} %collective-permute-done.26.refs_0_, bf16[256,1152]{1,0:T(8,128)(2,1)S(1)} %collective-permute-done.27.refs_1_), custom_call_target="tpu_custom_call" | custom-call | flops 1358954496 | bytes 12976128 | tf_op jit(solution)/shard_map/pallas_call | solution.py:235
  (26 shorter events, 0.4 us)
Async XLA Ops:
  0.6 18.3 %copy-start = (bf16[1152,1152]{1,0:T(8,128)(2,1)S(1)}, bf16[1152,1152]{1,0:T(8,128)(2,1)}, u32[]{:S(2)}) copy-start(bf16[1152,1152]{1,0:T(8,128)(2,1)} %param.9) | copy-start | bytes 7962628
  0.6 15.4 %collective-permute-start.1 = (bf16[64,1152]{1,0:T(8,128)(2,1)}, bf16[64,1152]{1,0:T(8,128)(2,1)S(1)}, u32[]{:S(2)}, u32[]{:S(2)}) collective-permute-start(bf16[64,1152]{1,0:T(8,128)(2,1)} %bitcast.10), channel_id=1, source_target_pairs={{0,4},{1,5},{2,6},{3,7},{4,0},{5,1},{6,2},{7,3},{8,12},{9,13},{10,... | collective-permute-start | bytes 442376 | tf_op jit(solution)/shard_map/ppermute | solution.py:259
  4.7 11.3 %collective-permute-start.2 = (bf16[64,1152]{1,0:T(8,128)(2,1)}, bf16[64,1152]{1,0:T(8,128)(2,1)S(1)}, u32[]{:S(2)}, u32[]{:S(2)}) collective-permute-start(bf16[64,1152]{1,0:T(8,128)(2,1)} %bitcast.11), channel_id=1, source_target_pairs={{0,6},{1,7},{2,4},{3,5},{4,2},{5,3},{6,0},{7,1},{8,14},{9,15},{10,... | collective-permute-start | bytes 442376 | tf_op jit(solution)/shard_map/ppermute | solution.py:259
  6.1 11.8 %collective-permute-start = (bf16[64,1152]{1,0:T(8,128)(2,1)}, bf16[64,1152]{1,0:T(8,128)(2,1)S(1)}, u32[]{:S(2)}, u32[]{:S(2)}) collective-permute-start(bf16[64,1152]{1,0:T(8,128)(2,1)} %bitcast.12), channel_id=1, source_target_pairs={{0,2},{1,3},{2,0},{3,1},{4,6},{5,7},{6,4},{7,5},{8,10},{9,11},{10,... | collective-permute-start | bytes 442376 | tf_op jit(solution)/shard_map/ppermute | solution.py:259
  6.3 13.6 %collective-permute-start.4 = (bf16[256,1152]{1,0:T(8,128)(2,1)}, bf16[256,1152]{1,0:T(8,128)(2,1)}, u32[]{:S(2)}, u32[]{:S(2)}) collective-permute-start(bf16[256,1152]{1,0:T(8,128)(2,1)} %bitcast.16), channel_id=1, source_target_pairs={{0,1},{1,0},{2,3},{3,2},{4,5},{5,4},{6,7},{7,6},{8,9},{9,8},{10,11... | collective-permute-start | bytes 1769480 | tf_op jit(solution)/shard_map/ppermute | solution.py:262
  6.3 13.6 %collective-permute-start.3 = (s32[1,256]{1,0:T(1,128)}, s32[1,256]{1,0:T(1,128)S(1)}, u32[]{:S(2)}, u32[]{:S(2)}) collective-permute-start(s32[1,256]{1,0:T(1,128)} %refs_0_.1), channel_id=1, source_target_pairs={{0,1},{1,0},{2,3},{3,2},{4,5},{5,4},{6,7},{7,6},{8,9},{9,8},{10,11... | collective-permute-start | bytes 3080 | tf_op jit(solution)/shard_map/ppermute | solution.py:262
  16.0 6.8 %collective-permute-start.8 = (bf16[128,1152]{1,0:T(8,128)(2,1)S(1)}, bf16[128,1152]{1,0:T(8,128)(2,1)S(1)}, u32[]{:S(2)}, u32[]{:S(2)}) collective-permute-start(bf16[128,1152]{1,0:T(8,128)(2,1)S(1)} %pad_maximum_fusion.5), channel_id=1, source_target_pairs={{0,8},{1,17},{2,10},{3,19},{4,12},{5,21},{6,14},{7,23},{8,0},{9,25... | collective-permute-start | bytes 884744 | tf_op jit(solution)/shard_map/ppermute | solution.py:270
  17.9 0.9 %copy-start.1 = (bf16[1,64,1152]{2,1,0:T(8,128)(2,1)S(1)}, bf16[1,64,1152]{2,1,0:T(8,128)(2,1)}, u32[]{:S(2)}) copy-start(bf16[1,64,1152]{2,1,0:T(8,128)(2,1)} %param.6) | copy-start | bytes 442372
  18.9 1.1 %copy-start.3 = (bf16[1,256,1152]{2,1,0:T(8,128)(2,1)S(1)}, bf16[1,256,1152]{2,1,0:T(8,128)(2,1)}, u32[]{:S(2)}) copy-start(bf16[1,256,1152]{2,1,0:T(8,128)(2,1)} %param.7) | copy-start | bytes 1769476
  18.9 1.1 %copy-start.4 = (s32[1,256]{1,0:T(1,128)S(1)}, s32[1,256]{1,0:T(1,128)}, u32[]{:S(2)}) copy-start(s32[1,256]{1,0:T(1,128)} %refs_0_.1) | copy-start | bytes 3076
  22.3 2.7 %copy-start.2 = (bf16[1,64,1152]{2,1,0:T(8,128)(2,1)S(1)}, bf16[1,64,1152]{2,1,0:T(8,128)(2,1)}, u32[]{:S(2)}) copy-start(bf16[1,64,1152]{2,1,0:T(8,128)(2,1)} %param.6) | copy-start | bytes 442372
  22.9 18.7 %collective-permute-start.9 = (bf16[256,1152]{1,0:T(8,128)(2,1)S(1)}, bf16[256,1152]{1,0:T(8,128)(2,1)S(1)}, u32[]{:S(2)}, u32[]{:S(2)}) collective-permute-start(bf16[256,1152]{1,0:T(8,128)(2,1)S(1)} %pad_maximum_fusion.refs_0_), channel_id=1, source_target_pairs={{0,16},{1,9},{2,18},{3,11},{4,20},{5,13},{6,22},{7,15},{8,24},{9,1... | collective-permute-start | bytes 1769480 | tf_op jit(solution)/shard_map/ppermute | solution.py:270
  25.1 7.6 %collective-permute-start.16 = (bf16[128,1152]{1,0:T(8,128)(2,1)S(1)}, bf16[128,1152]{1,0:T(8,128)(2,1)S(1)}, u32[]{:S(2)}, u32[]{:S(2)}) collective-permute-start(bf16[128,1152]{1,0:T(8,128)(2,1)S(1)} %pad_maximum_fusion.8), channel_id=1, source_target_pairs={{0,8},{1,17},{2,10},{3,19},{4,12},{5,21},{6,14},{7,23},{8,0},{9,25... | collective-permute-start | bytes 884744 | tf_op jit(solution)/shard_map/ppermute | solution.py:270
  26.6 7.8 %collective-permute-start.5 = (bf16[64,1152]{1,0:T(8,128)(2,1)S(1)}, bf16[64,1152]{1,0:T(8,128)(2,1)S(1)}, u32[]{:S(2)}, u32[]{:S(2)}) collective-permute-start(bf16[64,1152]{1,0:T(8,128)(2,1)S(1)} %get-tuple-element.31), channel_id=1, source_target_pairs={{0,6},{1,7},{2,4},{3,5},{4,2},{5,3},{6,0},{7,1},{8,14},{9,15},{10,... | collective-permute-start | bytes 442376 | tf_op jit(solution)/shard_map/ppermute | solution.py:259
  28.8 12.7 %collective-permute-start.6 = (bf16[64,1152]{1,0:T(8,128)(2,1)S(1)}, bf16[64,1152]{1,0:T(8,128)(2,1)S(1)}, u32[]{:S(2)}, u32[]{:S(2)}) collective-permute-start(bf16[64,1152]{1,0:T(8,128)(2,1)S(1)} %get-tuple-element.32), channel_id=1, source_target_pairs={{0,4},{1,5},{2,6},{3,7},{4,0},{5,1},{6,2},{7,3},{8,12},{9,13},{10,... | collective-permute-start | bytes 442376 | tf_op jit(solution)/shard_map/ppermute | solution.py:259
  31.0 10.5 %collective-permute-start.7 = (bf16[64,1152]{1,0:T(8,128)(2,1)S(1)}, bf16[64,1152]{1,0:T(8,128)(2,1)S(1)}, u32[]{:S(2)}, u32[]{:S(2)}) collective-permute-start(bf16[64,1152]{1,0:T(8,128)(2,1)S(1)} %get-tuple-element.33), channel_id=1, source_target_pairs={{0,2},{1,3},{2,0},{3,1},{4,6},{5,7},{6,4},{7,5},{8,10},{9,11},{10,... | collective-permute-start | bytes 442376 | tf_op jit(solution)/shard_map/ppermute | solution.py:259
  41.7 6.9 %collective-permute-start.13 = (bf16[64,1152]{1,0:T(8,128)(2,1)S(1)}, bf16[64,1152]{1,0:T(8,128)(2,1)S(1)}, u32[]{:S(2)}, u32[]{:S(2)}) collective-permute-start(bf16[64,1152]{1,0:T(8,128)(2,1)S(1)} %shard_map.87), channel_id=1, source_target_pairs={{0,8},{1,17},{2,10},{3,19},{4,12},{5,21},{6,14},{7,23},{8,0},{9,25... | collective-permute-start | bytes 442376 | tf_op jit(solution)/shard_map/ppermute | solution.py:270
  42.4 15.9 %collective-permute-start.17 = (bf16[256,1152]{1,0:T(8,128)(2,1)S(1)}, bf16[256,1152]{1,0:T(8,128)(2,1)S(1)}, u32[]{:S(2)}, u32[]{:S(2)}) collective-permute-start(bf16[256,1152]{1,0:T(8,128)(2,1)S(1)} %pad_maximum_fusion.1.refs_0_), channel_id=1, source_target_pairs={{0,16},{1,9},{2,18},{3,11},{4,20},{5,13},{6,22},{7,15},{8,24},{9,1... | collective-permute-start | bytes 1769480 | tf_op jit(solution)/shard_map/ppermute | solution.py:270
  43.3 6.3 %collective-permute-start.12 = (bf16[64,1152]{1,0:T(8,128)(2,1)S(1)}, bf16[64,1152]{1,0:T(8,128)(2,1)S(1)}, u32[]{:S(2)}, u32[]{:S(2)}) collective-permute-start(bf16[64,1152]{1,0:T(8,128)(2,1)S(1)} %shard_map.87), channel_id=1, source_target_pairs={{0,2},{1,3},{2,0},{3,1},{4,6},{5,7},{6,4},{7,5},{8,10},{9,11},{10,... | collective-permute-start | bytes 442376 | tf_op jit(solution)/shard_map/ppermute | solution.py:259
  43.3 13.8 %collective-permute-start.10 = (bf16[64,1152]{1,0:T(8,128)(2,1)S(1)}, bf16[64,1152]{1,0:T(8,128)(2,1)S(1)}, u32[]{:S(2)}, u32[]{:S(2)}) collective-permute-start(bf16[64,1152]{1,0:T(8,128)(2,1)S(1)} %shard_map.87), channel_id=1, source_target_pairs={{0,4},{1,5},{2,6},{3,7},{4,0},{5,1},{6,2},{7,3},{8,12},{9,13},{10,... | collective-permute-start | bytes 442376 | tf_op jit(solution)/shard_map/ppermute | solution.py:259
  46.7 10.4 %collective-permute-start.11 = (bf16[64,1152]{1,0:T(8,128)(2,1)S(1)}, bf16[64,1152]{1,0:T(8,128)(2,1)S(1)}, u32[]{:S(2)}, u32[]{:S(2)}) collective-permute-start(bf16[64,1152]{1,0:T(8,128)(2,1)S(1)} %shard_map.87), channel_id=1, source_target_pairs={{0,6},{1,7},{2,4},{3,5},{4,2},{5,3},{6,0},{7,1},{8,14},{9,15},{10,... | collective-permute-start | bytes 442376 | tf_op jit(solution)/shard_map/ppermute | solution.py:259
  48.6 10.4 %collective-permute-start.20 = (bf16[128,1152]{1,0:T(8,128)(2,1)S(1)}, bf16[128,1152]{1,0:T(8,128)(2,1)S(1)}, u32[]{:S(2)}, u32[]{:S(2)}) collective-permute-start(bf16[128,1152]{1,0:T(8,128)(2,1)S(1)} %pad_maximum_fusion.7), channel_id=1, source_target_pairs={{0,16},{1,9},{2,18},{3,11},{4,20},{5,13},{6,22},{7,15},{8,24},{9,1... | collective-permute-start | bytes 884744 | tf_op jit(solution)/shard_map/ppermute | solution.py:270
  49.5 9.6 %collective-permute-start.21 = (bf16[64,1152]{1,0:T(8,128)(2,1)S(1)}, bf16[64,1152]{1,0:T(8,128)(2,1)S(1)}, u32[]{:S(2)}, u32[]{:S(2)}) collective-permute-start(bf16[64,1152]{1,0:T(8,128)(2,1)S(1)} %collective-permute-done.12), channel_id=1, source_target_pairs={{0,8},{1,17},{2,10},{3,19},{4,12},{5,21},{6,14},{7,23},{8,0},{9,25... | collective-permute-start | bytes 442376 | tf_op jit(solution)/shard_map/ppermute | solution.py:270
  57.2 8.4 %collective-permute-start.14 = (bf16[128,1152]{1,0:T(8,128)(2,1)S(1)}, bf16[128,1152]{1,0:T(8,128)(2,1)S(1)}, u32[]{:S(2)}, u32[]{:S(2)}) collective-permute-start(bf16[128,1152]{1,0:T(8,128)(2,1)S(1)} %pad_maximum_fusion.6), channel_id=1, source_target_pairs={{0,8},{1,17},{2,10},{3,19},{4,12},{5,21},{6,14},{7,23},{8,0},{9,25... | collective-permute-start | bytes 884744 | tf_op jit(solution)/shard_map/ppermute | solution.py:270
  58.3 8.8 %collective-permute-start.19 = (bf16[512,1152]{1,0:T(8,128)(2,1)S(1)}, bf16[512,1152]{1,0:T(8,128)(2,1)S(1)}, u32[]{:S(2)}, u32[]{:S(2)}) collective-permute-start(bf16[512,1152]{1,0:T(8,128)(2,1)S(1)} %shard_map.90.refs_1_), channel_id=1, source_target_pairs={{0,1},{1,0},{2,3},{3,2},{4,5},{5,4},{6,7},{7,6},{8,9},{9,8},{10,11... | collective-permute-start | bytes 3538952 | tf_op jit(solution)/shard_map/ppermute | solution.py:262
  58.4 11.5 %collective-permute-start.18 = (bf16[512,1152]{1,0:T(8,128)(2,1)S(1)}, bf16[512,1152]{1,0:T(8,128)(2,1)S(1)}, u32[]{:S(2)}, u32[]{:S(2)}) collective-permute-start(bf16[512,1152]{1,0:T(8,128)(2,1)S(1)} %shard_map.89.refs_0_), channel_id=1, source_target_pairs={{0,1},{1,0},{2,3},{3,2},{4,5},{5,4},{6,7},{7,6},{8,9},{9,8},{10,11... | collective-permute-start | bytes 3538952 | tf_op jit(solution)/shard_map/ppermute | solution.py:262
  59.0 8.0 %collective-permute-start.23 = (bf16[256,1152]{1,0:T(8,128)(2,1)S(1)}, bf16[256,1152]{1,0:T(8,128)(2,1)S(1)}, u32[]{:S(2)}, u32[]{:S(2)}) collective-permute-start(bf16[256,1152]{1,0:T(8,128)(2,1)S(1)} %pad_maximum_fusion.2.refs_0_), channel_id=1, source_target_pairs={{0,1},{1,0},{2,3},{3,2},{4,5},{5,4},{6,7},{7,6},{8,9},{9,8},{10,11... | collective-permute-start | bytes 1769480 | tf_op jit(solution)/shard_map/ppermute | solution.py:262
  59.1 7.0 %collective-permute-start.22 = (bf16[128,1152]{1,0:T(8,128)(2,1)S(1)}, bf16[128,1152]{1,0:T(8,128)(2,1)S(1)}, u32[]{:S(2)}, u32[]{:S(2)}) collective-permute-start(bf16[128,1152]{1,0:T(8,128)(2,1)S(1)} %pad_maximum_fusion.9), channel_id=1, source_target_pairs={{0,16},{1,9},{2,18},{3,11},{4,20},{5,13},{6,22},{7,15},{8,24},{9,1... | collective-permute-start | bytes 884744 | tf_op jit(solution)/shard_map/ppermute | solution.py:270
  66.1 11.0 %collective-permute-start.15 = (f32[256,1152]{1,0:T(8,128)S(1)}, f32[256,1152]{1,0:T(8,128)S(1)}, u32[]{:S(2)}, u32[]{:S(2)}) collective-permute-start(f32[256,1152]{1,0:T(8,128)S(1)} %get-tuple-element.44), channel_id=1, source_target_pairs={{0,1},{1,0},{2,3},{3,2},{4,5},{5,4},{6,7},{7,6},{8,9},{9,8},{10,11... | collective-permute-start | bytes 3538952 | tf_op jit(solution)/shard_map/ppermute | solution.py:262
  66.3 4.9 %collective-permute-start.24 = (bf16[256,1152]{1,0:T(8,128)(2,1)S(1)}, bf16[256,1152]{1,0:T(8,128)(2,1)S(1)}, u32[]{:S(2)}, u32[]{:S(2)}) collective-permute-start(bf16[256,1152]{1,0:T(8,128)(2,1)S(1)} %pad_maximum_fusion.3.refs_1_), channel_id=1, source_target_pairs={{0,1},{1,0},{2,3},{3,2},{4,5},{5,4},{6,7},{7,6},{8,9},{9,8},{10,11... | collective-permute-start | bytes 1769480 | tf_op jit(solution)/shard_map/ppermute | solution.py:262
  67.0 4.1 %collective-permute-start.25 = (bf16[256,1152]{1,0:T(8,128)(2,1)S(1)}, bf16[256,1152]{1,0:T(8,128)(2,1)S(1)}, u32[]{:S(2)}, u32[]{:S(2)}) collective-permute-start(bf16[256,1152]{1,0:T(8,128)(2,1)S(1)} %pad_maximum_fusion.4.refs_2_), channel_id=1, source_target_pairs={{0,1},{1,0},{2,3},{3,2},{4,5},{5,4},{6,7},{7,6},{8,9},{9,8},{10,11... | collective-permute-start | bytes 1769480 | tf_op jit(solution)/shard_map/ppermute | solution.py:262
  67.1 9.9 %collective-permute-start.26 = (bf16[256,1152]{1,0:T(8,128)(2,1)S(1)}, bf16[256,1152]{1,0:T(8,128)(2,1)S(1)}, u32[]{:S(2)}, u32[]{:S(2)}) collective-permute-start(bf16[256,1152]{1,0:T(8,128)(2,1)S(1)} %pad_maximum_fusion.4.refs_2_), channel_id=1, source_target_pairs={{0,16},{1,9},{2,18},{3,11},{4,20},{5,13},{6,22},{7,15},{8,24},{9,1... | collective-permute-start | bytes 1769480 | tf_op jit(solution)/shard_map/ppermute | solution.py:270
  77.0 2.0 %collective-permute-start.27 = (bf16[256,1152]{1,0:T(8,128)(2,1)S(1)}, bf16[256,1152]{1,0:T(8,128)(2,1)S(1)}, u32[]{:S(2)}, u32[]{:S(2)}) collective-permute-start(bf16[256,1152]{1,0:T(8,128)(2,1)S(1)} %collective-permute-done.26.refs_0_), channel_id=1, source_target_pairs={{0,1},{1,0},{2,3},{3,2},{4,5},{5,4},{6,7},{7,6},{8,9},{9,8},{10,11... | collective-permute-start | bytes 1769480 | tf_op jit(solution)/shard_map/ppermute | solution.py:262

commit v14 on v13

--- a/solution.py
+++ b/solution.py
@@ -315,7 +315,7 @@
     g_near = over_d(near, near_first)
     far = after(jnp.concatenate(far), near)
     far_first = step_d(far, 0)
-    dlogit = after(dlogit, far_first)
+    dlogit = after(dlogit, near)
     adjoint, adjoint_other = caption_sums(both, dlogit, unit)
     adjoint = adjoint + swap(adjoint_other)
     per = nd // 2

time: 82.3 us -> 84 us (1.021)
  waiting for transfers between devices: 32.7 us -> 37.9 us
  starting transfers between devices: 29.7 us -> 26.3 us
    ppermute x10, waiting for transfers between devices: 8.27 us -> 13.2 us  [step_d(): return lax.ppermute(v, ('dp', 'blk'), perm)]
    ppermute x10, starting transfers between devices: 12.6 us -> 10.4 us  [step_d(): return lax.ppermute(v, ('dp', 'blk'), perm)]
    ppermute x9, starting transfers between devices: 15 us -> 14.1 us  [along_z(): return lax.ppermute(v, 'blk', [(i, i ^ 2 * k) for i in range(nb)])]
  transfers between devices with their start and end apart: 28 -> 28, of which waited for: 11 -> 12; matrix products, arithmetic and copies ran while one was open for 5% -> 5% of each run, Pallas kernels for 11% -> 11%
where the time goes in v14:
time: 84 us; the launch traced here: 83.8 us
  waiting for transfers between devices  37.9 us (45%)
  starting transfers between devices  26.3 us (31%)
  Pallas kernels  12.4 us (15%)
  matrix products  2.65 us (3%)
  between operations  2.14 us (3%)
  other arithmetic  1.49 us (2%)
  local copies, waits for them, and re-layouts  1.01 us (1%)
    ppermute x9, waiting for transfers between devices, along_z(): return lax.ppermute(v, 'blk', [(i, i ^ 2 * k) for i in range(nb)])  23.8 us
    ppermute x9, starting transfers between devices, along_z(): return lax.ppermute(v, 'blk', [(i, i ^ 2 * k) for i in range(nb)])  14.1 us
    ppermute x10, waiting for transfers between devices, step_d(): return lax.ppermute(v, ('dp', 'blk'), perm)  13.2 us
    ppermute x10, starting transfers between devices, step_d(): return lax.ppermute(v, ('dp', 'blk'), perm)  10.4 us
    pallas_call x2, Pallas kernels, weight_sum(): pl.pallas_call(kernel, out_shape=jax.ShapeDtypeStruct((depth, depth), F32...  7.85 us
    dot_general x2, matrix products, dot(): return lax.dot_general(a, b, dims, preferred_element_type=F32)  2.65 us
    pallas_call x1, Pallas kernels, scores(): pl.pallas_call(functools.partial(score_kernel, nz), out_shape=outs, in_sp...  2.3 us
    ppermute x9, starting transfers between devices, swap(): return lax.ppermute(v, 'blk', [(i, i ^ 1) for i in range(nb)])  1.74 us
  transfers between devices with their start and end apart: 28, of which 12 were waited for; matrix products, arithmetic and copies ran while one was open for 5% of the time, Pallas kernels for 11%

profile of v14, /device:TPU:0, one launch (start us, length us, event | category | flops | bytes accessed | tf_op | source)
XLA Modules:
  0.0 83.8 jit_solution(8149238858922492025)
XLA Ops:
  0.6 0.0 copy-start
  0.6 4.1 %collective-permute-start.1 = (bf16[64,1152]{1,0:T(8,128)(2,1)}, bf16[64,1152]{1,0:T(8,128)(2,1)S(1)}, u32[]{:S(2)}, u32[]{:S(2)}) collective-permute-start(bf16[64,1152]{1,0:T(8,128)(2,1)} %bitcast.10), channel_id=1, source_target_pairs={{0,4},{1,5},{2,6},{3,7},{4,0},{5,1},{6,2},{7,3},{8,12},{9,13},{10,... | collective-permute-start | bytes 442376 | tf_op jit(solution)/shard_map/ppermute | solution.py:259
  4.7 1.3 %collective-permute-start.2 = (bf16[64,1152]{1,0:T(8,128)(2,1)}, bf16[64,1152]{1,0:T(8,128)(2,1)S(1)}, u32[]{:S(2)}, u32[]{:S(2)}) collective-permute-start(bf16[64,1152]{1,0:T(8,128)(2,1)} %bitcast.11), channel_id=1, source_target_pairs={{0,6},{1,7},{2,4},{3,5},{4,2},{5,3},{6,0},{7,1},{8,14},{9,15},{10,... | collective-permute-start | bytes 442376 | tf_op jit(solution)/shard_map/ppermute | solution.py:259
  6.1 0.2 collective-permute-start
  6.3 0.5 collective-permute-start.3
  8.1 7.9 %collective-permute-done.1.refs_2_ = bf16[64,1152]{1,0:T(8,128)(2,1)S(1)} collective-permute-done((bf16[64,1152]{1,0:T(8,128)(2,1)}, bf16[64,1152]{1,0:T(8,128)(2,1)S(1)}, u32[]{:S(2)}, u32[]{:S(2)}) %collective-permute-start.1) | collective-permute-done | bytes 147488 | tf_op jit(solution)/shard_map/ppermute | solution.py:259
  16.0 0.0 collective-permute-done.2.refs_3_
  16.0 1.9 %collective-permute-start.8 = (bf16[128,1152]{1,0:T(8,128)(2,1)S(1)}, bf16[128,1152]{1,0:T(8,128)(2,1)S(1)}, u32[]{:S(2)}, u32[]{:S(2)}) collective-permute-start(bf16[128,1152]{1,0:T(8,128)(2,1)S(1)} %pad_maximum_fusion.5), channel_id=1, source_target_pairs={{0,8},{1,17},{2,10},{3,19},{4,12},{5,21},{6,14},{7,23},{8,0},{9,25... | collective-permute-start | bytes 884744 | tf_op jit(solution)/shard_map/ppermute | solution.py:270
  17.9 0.0 collective-permute-done.refs_1_
  17.9 0.9 %copy-done.1 = bf16[1,64,1152]{2,1,0:T(8,128)(2,1)S(1)} copy-done((bf16[1,64,1152]{2,1,0:T(8,128)(2,1)S(1)}, bf16[1,64,1152]{2,1,0:T(8,128)(2,1)}, u32[]{:S(2)}) %copy-start.1) | copy-done | bytes 147480
  18.9 0.0 copy-start.3
  18.9 0.0 copy-start.4
  18.9 1.0 %fusion.embed = f32[256,1152]{1,0:T(8,128)S(1)} fusion(bf16[256,1152]{1,0:T(8,128)(2,1)S(1)} %shard_map.85, bf16[1152,1152]{1,0:T(8,128)(2,1)S(1)} %copy-done), kind=kOutput, calls=%fused_computation.13 | convolution fusion | flops 679477248 | bytes 4423680 | tf_op jit(solution)/shard_map/dot_general | solution.py:17
  19.9 0.0 collective-permute-done.3.refs_1_
  19.9 0.0 collective-permute-done.4.refs_3_
  20.0 0.1 iota.7.both
  20.0 2.3 %shard_map.86 = (f32[64,1152]{1,0:T(8,128)S(1)}, f32[64,1152]{1,0:T(8,128)S(1)}, f32[64,128]{1,0:T(8,128)S(1)}, bf16[256,1152]{1,0:T(8,128)(2,1)S(1)}, bf16[256,...) custom-call(f32[16,128]{1,0:T(8,128)S(1)} %iota.7.both, ...), custom_call_target="tpu_custom_call" | custom-call | flops 603979776 | bytes 4718592 | tf_op jit(solution)/shard_map/pallas_call | solution.py:74
  22.3 0.0 copy-start.2
  22.4 0.5 collective-permute-done.8
  22.9 2.1 %collective-permute-start.9 = (bf16[256,1152]{1,0:T(8,128)(2,1)S(1)}, bf16[256,1152]{1,0:T(8,128)(2,1)S(1)}, u32[]{:S(2)}, u32[]{:S(2)}) collective-permute-start(bf16[256,1152]{1,0:T(8,128)(2,1)S(1)} %pad_maximum_fusion.refs_0_), channel_id=1, source_target_pairs={{0,16},{1,9},{2,18},{3,11},{4,20},{5,13},{6,22},{7,15},{8,24},{9,1... | collective-permute-start | bytes 1769480 | tf_op jit(solution)/shard_map/ppermute | solution.py:270
  25.1 1.6 %collective-permute-start.13 = (bf16[128,1152]{1,0:T(8,128)(2,1)S(1)}, bf16[128,1152]{1,0:T(8,128)(2,1)S(1)}, u32[]{:S(2)}, u32[]{:S(2)}) collective-permute-start(bf16[128,1152]{1,0:T(8,128)(2,1)S(1)} %pad_maximum_fusion.7), channel_id=1, source_target_pairs={{0,8},{1,17},{2,10},{3,19},{4,12},{5,21},{6,14},{7,23},{8,0},{9,25... | collective-permute-start | bytes 884744 | tf_op jit(solution)/shard_map/ppermute | solution.py:270
  26.6 2.2 %collective-permute-start.5 = (bf16[64,1152]{1,0:T(8,128)(2,1)S(1)}, bf16[64,1152]{1,0:T(8,128)(2,1)S(1)}, u32[]{:S(2)}, u32[]{:S(2)}) collective-permute-start(bf16[64,1152]{1,0:T(8,128)(2,1)S(1)} %get-tuple-element.31), channel_id=1, source_target_pairs={{0,6},{1,7},{2,4},{3,5},{4,2},{5,3},{6,0},{7,1},{8,14},{9,15},{10,... | collective-permute-start | bytes 442376 | tf_op jit(solution)/shard_map/ppermute | solution.py:259
  28.8 2.2 %collective-permute-start.6 = (bf16[64,1152]{1,0:T(8,128)(2,1)S(1)}, bf16[64,1152]{1,0:T(8,128)(2,1)S(1)}, u32[]{:S(2)}, u32[]{:S(2)}) collective-permute-start(bf16[64,1152]{1,0:T(8,128)(2,1)S(1)} %get-tuple-element.32), channel_id=1, source_target_pairs={{0,4},{1,5},{2,6},{3,7},{4,0},{5,1},{6,2},{7,3},{8,12},{9,13},{10,... | collective-permute-start | bytes 442376 | tf_op jit(solution)/shard_map/ppermute | solution.py:259
  31.0 0.6 collective-permute-start.7
  31.6 1.0 %collective-permute-done.13 = bf16[128,1152]{1,0:T(8,128)(2,1)S(1)} collective-permute-done((bf16[128,1152]{1,0:T(8,128)(2,1)S(1)}, bf16[128,1152]{1,0:T(8,128)(2,1)S(1)}, u32[]{:S(2)}, u32[]{:S(2)}) %collective-permute-start.13) | collective-permute-done | bytes 294944 | tf_op jit(solution)/shard_map/ppermute | solution.py:270
  32.6 1.8 %collective-permute-done.5.refs_0_ = bf16[64,1152]{1,0:T(8,128)(2,1)S(1)} collective-permute-done((bf16[64,1152]{1,0:T(8,128)(2,1)S(1)}, bf16[64,1152]{1,0:T(8,128)(2,1)S(1)}, u32[]{:S(2)}, u32[]{:S(2)}) %collective-permute-start.5) | collective-permute-done | bytes 147488 | tf_op jit(solution)/shard_map/ppermute | solution.py:259
  34.4 7.1 %collective-permute-done.6.refs_1_ = bf16[64,1152]{1,0:T(8,128)(2,1)S(1)} collective-permute-done((bf16[64,1152]{1,0:T(8,128)(2,1)S(1)}, bf16[64,1152]{1,0:T(8,128)(2,1)S(1)}, u32[]{:S(2)}, u32[]{:S(2)}) %collective-permute-start.6) | collective-permute-done | bytes 147488 | tf_op jit(solution)/shard_map/ppermute | solution.py:259
  41.5 0.0 collective-permute-done.9.refs_1_
  41.5 0.2 shard_map.87
  41.7 0.6 collective-permute-start.11
  42.4 0.9 %collective-permute-start.14 = (bf16[256,1152]{1,0:T(8,128)(2,1)S(1)}, bf16[256,1152]{1,0:T(8,128)(2,1)S(1)}, u32[]{:S(2)}, u32[]{:S(2)}) collective-permute-start(bf16[256,1152]{1,0:T(8,128)(2,1)S(1)} %pad_maximum_fusion.1.refs_0_), channel_id=1, source_target_pairs={{0,16},{1,9},{2,18},{3,11},{4,20},{5,13},{6,22},{7,15},{8,24},{9,1... | collective-permute-start | bytes 1769480 | tf_op jit(solution)/shard_map/ppermute | solution.py:270
  43.3 2.9 %collective-permute-start.21 = (bf16[64,1152]{1,0:T(8,128)(2,1)S(1)}, bf16[64,1152]{1,0:T(8,128)(2,1)S(1)}, u32[]{:S(2)}, u32[]{:S(2)}) collective-permute-start(bf16[64,1152]{1,0:T(8,128)(2,1)S(1)} %shard_map.87), channel_id=1, source_target_pairs={{0,6},{1,7},{2,4},{3,5},{4,2},{5,3},{6,0},{7,1},{8,14},{9,15},{10,... | collective-permute-start | bytes 442376 | tf_op jit(solution)/shard_map/ppermute | solution.py:259
  46.1 0.6 collective-permute-start.10
  46.8 1.8 %collective-permute-done.11 = bf16[64,1152]{1,0:T(8,128)(2,1)S(1)} collective-permute-done((bf16[64,1152]{1,0:T(8,128)(2,1)S(1)}, bf16[64,1152]{1,0:T(8,128)(2,1)S(1)}, u32[]{:S(2)}, u32[]{:S(2)}) %collective-permute-start.11) | collective-permute-done | bytes 147488 | tf_op jit(solution)/shard_map/ppermute | solution.py:270
  48.6 0.6 collective-permute-start.17
  49.2 0.1 shard_map.90.refs_1_
  49.3 7.0 %collective-permute-done.10 = bf16[64,1152]{1,0:T(8,128)(2,1)S(1)} collective-permute-done((bf16[64,1152]{1,0:T(8,128)(2,1)S(1)}, bf16[64,1152]{1,0:T(8,128)(2,1)S(1)}, u32[]{:S(2)}, u32[]{:S(2)}) %collective-permute-start.10) | collective-permute-done | bytes 147488 | tf_op jit(solution)/shard_map/ppermute | solution.py:259
  56.2 0.4 collective-permute-start.18
  56.6 0.0 collective-permute-done.20
  56.6 1.7 %collective-permute-start.22 = (bf16[128,1152]{1,0:T(8,128)(2,1)S(1)}, bf16[128,1152]{1,0:T(8,128)(2,1)S(1)}, u32[]{:S(2)}, u32[]{:S(2)}) collective-permute-start(bf16[128,1152]{1,0:T(8,128)(2,1)S(1)} %pad_maximum_fusion.9), channel_id=1, source_target_pairs={{0,8},{1,17},{2,10},{3,19},{4,12},{5,21},{6,14},{7,23},{8,0},{9,25... | collective-permute-start | bytes 884744 | tf_op jit(solution)/shard_map/ppermute | solution.py:270
  58.4 0.0 collective-permute-start.16
  58.4 0.0 collective-permute-done.14.refs_1_
  58.4 0.1 shard_map.89.refs_0_
  58.5 0.6 collective-permute-start.15
  59.0 0.0 collective-permute-done.17
  59.1 0.1 collective-permute-start.23
  59.2 2.2 %collective-permute-done.18 = bf16[64,1152]{1,0:T(8,128)(2,1)S(1)} collective-permute-done((bf16[64,1152]{1,0:T(8,128)(2,1)S(1)}, bf16[64,1152]{1,0:T(8,128)(2,1)S(1)}, u32[]{:S(2)}, u32[]{:S(2)}) %collective-permute-start.18) | collective-permute-done | bytes 147488 | tf_op jit(solution)/shard_map/ppermute | solution.py:270
  61.4 0.4 collective-permute-start.19
  61.8 0.5 shard_map.88
  62.3 4.3 %collective-permute-done.22 = bf16[128,1152]{1,0:T(8,128)(2,1)S(1)} collective-permute-done((bf16[128,1152]{1,0:T(8,128)(2,1)S(1)}, bf16[128,1152]{1,0:T(8,128)(2,1)S(1)}, u32[]{:S(2)}, u32[]{:S(2)}) %collective-permute-start.22) | collective-permute-done | bytes 294944 | tf_op jit(solution)/shard_map/ppermute | solution.py:270
  66.7 0.0 collective-permute-start.12
  66.7 1.5 %collective-permute-done.19 = bf16[128,1152]{1,0:T(8,128)(2,1)S(1)} collective-permute-done((bf16[128,1152]{1,0:T(8,128)(2,1)S(1)}, bf16[128,1152]{1,0:T(8,128)(2,1)S(1)}, u32[]{:S(2)}, u32[]{:S(2)}) %collective-permute-start.19) | collective-permute-done | bytes 294944 | tf_op jit(solution)/shard_map/ppermute | solution.py:270
  68.3 0.1 collective-permute-start.24
  68.3 0.0 collective-permute-done.23.refs_3_
  68.3 0.5 collective-permute-start.25
  68.8 0.3 collective-permute-start.26
  69.1 1.7 %convolution_bitcast_fusion = f32[1,64,1152]{2,1,0:T(8,128)} fusion(bf16[64,1152]{1,0:T(8,128)(2,1)S(1)} %shard_map.87, bf16[1152,1152]{1,0:T(8,128)(2,1)S(1)} %copy-done), kind=kOutput, calls=%fused_computation | convolution fusion | flops 169869312 | bytes 3096576 | tf_op jit(solution)/shard_map/dot_general | solution.py:17
  70.8 1.3 %shard_map.91 = (bf16[1152,1536]{1,0:T(8,128)(2,1)S(1)}, bf16[1152,512]{1,0:T(8,128)(2,1)S(1)}) custom-call(bf16[512,1152]{1,0:T(8,128)(2,1)S(1)} %shard_map.89.refs_0_, bf16[512,1152]{1,0:T(8,128)(2,1)S(1)} %shard_map.90.refs_1_, bf16[512,1152]{1,0:T(8,128)(2,1)S(1)} %collective-permute-done.15.refs_2_, bf16[512,1152]{1,0:T(8,128)(2,1)S(1)} %collective-permute-done.16.refs_3_), custom_call_target="tpu_custom_call" | custom-call | bytes 9437184 | tf_op jit(solution)/shard_map/pallas_call | solution.py:180
  72.1 0.0 collective-permute-done.24.refs_4_
  72.1 4.8 %shard_map.92.acc = f32[1152,1152]{1,0:T(8,128)S(1)} custom-call(bf16[1152,1536]{1,0:T(8,128)(2,1)S(1)} %get-tuple-element.48.x_t, bf16[256,1152]{1,0:T(8,128)(2,1)S(1)} %pad_maximum_fusion.2.refs_0_, bf16[256,1152]{1,0:T(8,128)(2,1)S(1)} %pad_maximum_fusion.3.refs_1_, bf16[256,1152]{1,0:T(8,128)(2,1)S(1)} %pad_maximum_fusion.4.refs_2_, ...), custom_call_target="tpu_custom_call" | custom-call | flops 4076863488 | bytes 12386304 | tf_op jit(solution)/shard_map/pallas_call | solution.py:235
  76.9 1.9 %collective-permute-done.26.refs_0_ = bf16[256,1152]{1,0:T(8,128)(2,1)S(1)} collective-permute-done((bf16[256,1152]{1,0:T(8,128)(2,1)S(1)}, bf16[256,1152]{1,0:T(8,128)(2,1)S(1)}, u32[]{:S(2)}, u32[]{:S(2)}) %collective-permute-start.26) | collective-permute-done | bytes 589856 | tf_op jit(solution)/shard_map/ppermute | solution.py:270
  78.7 1.1 %add_bitcast_fusion = f32[1,256,1152]{2,1,0:T(8,128)} fusion(f32[256,1152]{1,0:T(8,128)S(1)} %get-tuple-element.42, f32[256,1152]{1,0:T(8,128)S(1)} %collective-permute-done.12), kind=kLoop, calls=%fused_computation.1 | loop fusion | flops 294912 | bytes 3538944 | tf_op jit(solution)/shard_map/broadcast_in_dim | solution.py:362
  79.9 0.9 %collective-permute-done.27.refs_1_ = bf16[256,1152]{1,0:T(8,128)(2,1)S(1)} collective-permute-done((bf16[256,1152]{1,0:T(8,128)(2,1)S(1)}, bf16[256,1152]{1,0:T(8,128)(2,1)S(1)}, u32[]{:S(2)}, u32[]{:S(2)}) %collective-permute-start.27) | collective-permute-done | bytes 589856 | tf_op jit(solution)/shard_map/ppermute | solution.py:262
  80.7 3.1 %shard_map.93 = f32[1152,1152]{1,0:T(8,128)} custom-call(bf16[1152,512]{1,0:T(8,128)(2,1)S(1)} %get-tuple-element.47.x_t, f32[1152,1152]{1,0:T(8,128)S(1)} %shard_map.92.acc, bf16[256,1152]{1,0:T(8,128)(2,1)S(1)} %collective-permute-done.26.refs_0_, bf16[256,1152]{1,0:T(8,128)(2,1)S(1)} %collective-permute-done.27.refs_1_), custom_call_target="tpu_custom_call" | custom-call | flops 1358954496 | bytes 12976128 | tf_op jit(solution)/shard_map/pallas_call | solution.py:235
  (26 shorter events, 0.4 us)
Async XLA Ops:
  0.6 18.3 %copy-start = (bf16[1152,1152]{1,0:T(8,128)(2,1)S(1)}, bf16[1152,1152]{1,0:T(8,128)(2,1)}, u32[]{:S(2)}) copy-start(bf16[1152,1152]{1,0:T(8,128)(2,1)} %param.9) | copy-start | bytes 7962628
  0.6 15.4 %collective-permute-start.1 = (bf16[64,1152]{1,0:T(8,128)(2,1)}, bf16[64,1152]{1,0:T(8,128)(2,1)S(1)}, u32[]{:S(2)}, u32[]{:S(2)}) collective-permute-start(bf16[64,1152]{1,0:T(8,128)(2,1)} %bitcast.10), channel_id=1, source_target_pairs={{0,4},{1,5},{2,6},{3,7},{4,0},{5,1},{6,2},{7,3},{8,12},{9,13},{10,... | collective-permute-start | bytes 442376 | tf_op jit(solution)/shard_map/ppermute | solution.py:259
  4.7 11.3 %collective-permute-start.2 = (bf16[64,1152]{1,0:T(8,128)(2,1)}, bf16[64,1152]{1,0:T(8,128)(2,1)S(1)}, u32[]{:S(2)}, u32[]{:S(2)}) collective-permute-start(bf16[64,1152]{1,0:T(8,128)(2,1)} %bitcast.11), channel_id=1, source_target_pairs={{0,6},{1,7},{2,4},{3,5},{4,2},{5,3},{6,0},{7,1},{8,14},{9,15},{10,... | collective-permute-start | bytes 442376 | tf_op jit(solution)/shard_map/ppermute | solution.py:259
  6.1 11.8 %collective-permute-start = (bf16[64,1152]{1,0:T(8,128)(2,1)}, bf16[64,1152]{1,0:T(8,128)(2,1)S(1)}, u32[]{:S(2)}, u32[]{:S(2)}) collective-permute-start(bf16[64,1152]{1,0:T(8,128)(2,1)} %bitcast.12), channel_id=1, source_target_pairs={{0,2},{1,3},{2,0},{3,1},{4,6},{5,7},{6,4},{7,5},{8,10},{9,11},{10,... | collective-permute-start | bytes 442376 | tf_op jit(solution)/shard_map/ppermute | solution.py:259
  6.3 13.6 %collective-permute-start.4 = (bf16[256,1152]{1,0:T(8,128)(2,1)}, bf16[256,1152]{1,0:T(8,128)(2,1)}, u32[]{:S(2)}, u32[]{:S(2)}) collective-permute-start(bf16[256,1152]{1,0:T(8,128)(2,1)} %bitcast.16), channel_id=1, source_target_pairs={{0,1},{1,0},{2,3},{3,2},{4,5},{5,4},{6,7},{7,6},{8,9},{9,8},{10,11... | collective-permute-start | bytes 1769480 | tf_op jit(solution)/shard_map/ppermute | solution.py:262
  6.3 13.6 %collective-permute-start.3 = (s32[1,256]{1,0:T(1,128)}, s32[1,256]{1,0:T(1,128)S(1)}, u32[]{:S(2)}, u32[]{:S(2)}) collective-permute-start(s32[1,256]{1,0:T(1,128)} %refs_0_.1), channel_id=1, source_target_pairs={{0,1},{1,0},{2,3},{3,2},{4,5},{5,4},{6,7},{7,6},{8,9},{9,8},{10,11... | collective-permute-start | bytes 3080 | tf_op jit(solution)/shard_map/ppermute | solution.py:262
  16.0 6.8 %collective-permute-start.8 = (bf16[128,1152]{1,0:T(8,128)(2,1)S(1)}, bf16[128,1152]{1,0:T(8,128)(2,1)S(1)}, u32[]{:S(2)}, u32[]{:S(2)}) collective-permute-start(bf16[128,1152]{1,0:T(8,128)(2,1)S(1)} %pad_maximum_fusion.5), channel_id=1, source_target_pairs={{0,8},{1,17},{2,10},{3,19},{4,12},{5,21},{6,14},{7,23},{8,0},{9,25... | collective-permute-start | bytes 884744 | tf_op jit(solution)/shard_map/ppermute | solution.py:270
  17.9 0.9 %copy-start.1 = (bf16[1,64,1152]{2,1,0:T(8,128)(2,1)S(1)}, bf16[1,64,1152]{2,1,0:T(8,128)(2,1)}, u32[]{:S(2)}) copy-start(bf16[1,64,1152]{2,1,0:T(8,128)(2,1)} %param.6) | copy-start | bytes 442372
  18.9 1.1 %copy-start.3 = (bf16[1,256,1152]{2,1,0:T(8,128)(2,1)S(1)}, bf16[1,256,1152]{2,1,0:T(8,128)(2,1)}, u32[]{:S(2)}) copy-start(bf16[1,256,1152]{2,1,0:T(8,128)(2,1)} %param.7) | copy-start | bytes 1769476
  18.9 1.1 %copy-start.4 = (s32[1,256]{1,0:T(1,128)S(1)}, s32[1,256]{1,0:T(1,128)}, u32[]{:S(2)}) copy-start(s32[1,256]{1,0:T(1,128)} %refs_0_.1) | copy-start | bytes 3076
  22.3 2.7 %copy-start.2 = (bf16[1,64,1152]{2,1,0:T(8,128)(2,1)S(1)}, bf16[1,64,1152]{2,1,0:T(8,128)(2,1)}, u32[]{:S(2)}) copy-start(bf16[1,64,1152]{2,1,0:T(8,128)(2,1)} %param.6) | copy-start | bytes 442372
  22.9 18.7 %collective-permute-start.9 = (bf16[256,1152]{1,0:T(8,128)(2,1)S(1)}, bf16[256,1152]{1,0:T(8,128)(2,1)S(1)}, u32[]{:S(2)}, u32[]{:S(2)}) collective-permute-start(bf16[256,1152]{1,0:T(8,128)(2,1)S(1)} %pad_maximum_fusion.refs_0_), channel_id=1, source_target_pairs={{0,16},{1,9},{2,18},{3,11},{4,20},{5,13},{6,22},{7,15},{8,24},{9,1... | collective-permute-start | bytes 1769480 | tf_op jit(solution)/shard_map/ppermute | solution.py:270
  25.1 7.6 %collective-permute-start.13 = (bf16[128,1152]{1,0:T(8,128)(2,1)S(1)}, bf16[128,1152]{1,0:T(8,128)(2,1)S(1)}, u32[]{:S(2)}, u32[]{:S(2)}) collective-permute-start(bf16[128,1152]{1,0:T(8,128)(2,1)S(1)} %pad_maximum_fusion.7), channel_id=1, source_target_pairs={{0,8},{1,17},{2,10},{3,19},{4,12},{5,21},{6,14},{7,23},{8,0},{9,25... | collective-permute-start | bytes 884744 | tf_op jit(solution)/shard_map/ppermute | solution.py:270
  26.6 7.8 %collective-permute-start.5 = (bf16[64,1152]{1,0:T(8,128)(2,1)S(1)}, bf16[64,1152]{1,0:T(8,128)(2,1)S(1)}, u32[]{:S(2)}, u32[]{:S(2)}) collective-permute-start(bf16[64,1152]{1,0:T(8,128)(2,1)S(1)} %get-tuple-element.31), channel_id=1, source_target_pairs={{0,6},{1,7},{2,4},{3,5},{4,2},{5,3},{6,0},{7,1},{8,14},{9,15},{10,... | collective-permute-start | bytes 442376 | tf_op jit(solution)/shard_map/ppermute | solution.py:259
  28.8 12.7 %collective-permute-start.6 = (bf16[64,1152]{1,0:T(8,128)(2,1)S(1)}, bf16[64,1152]{1,0:T(8,128)(2,1)S(1)}, u32[]{:S(2)}, u32[]{:S(2)}) collective-permute-start(bf16[64,1152]{1,0:T(8,128)(2,1)S(1)} %get-tuple-element.32), channel_id=1, source_target_pairs={{0,4},{1,5},{2,6},{3,7},{4,0},{5,1},{6,2},{7,3},{8,12},{9,13},{10,... | collective-permute-start | bytes 442376 | tf_op jit(solution)/shard_map/ppermute | solution.py:259
  31.0 10.5 %collective-permute-start.7 = (bf16[64,1152]{1,0:T(8,128)(2,1)S(1)}, bf16[64,1152]{1,0:T(8,128)(2,1)S(1)}, u32[]{:S(2)}, u32[]{:S(2)}) collective-permute-start(bf16[64,1152]{1,0:T(8,128)(2,1)S(1)} %get-tuple-element.33), channel_id=1, source_target_pairs={{0,2},{1,3},{2,0},{3,1},{4,6},{5,7},{6,4},{7,5},{8,10},{9,11},{10,... | collective-permute-start | bytes 442376 | tf_op jit(solution)/shard_map/ppermute | solution.py:259
  41.7 6.9 %collective-permute-start.11 = (bf16[64,1152]{1,0:T(8,128)(2,1)S(1)}, bf16[64,1152]{1,0:T(8,128)(2,1)S(1)}, u32[]{:S(2)}, u32[]{:S(2)}) collective-permute-start(bf16[64,1152]{1,0:T(8,128)(2,1)S(1)} %shard_map.87), channel_id=1, source_target_pairs={{0,8},{1,17},{2,10},{3,19},{4,12},{5,21},{6,14},{7,23},{8,0},{9,25... | collective-permute-start | bytes 442376 | tf_op jit(solution)/shard_map/ppermute | solution.py:270
  42.4 16.0 %collective-permute-start.14 = (bf16[256,1152]{1,0:T(8,128)(2,1)S(1)}, bf16[256,1152]{1,0:T(8,128)(2,1)S(1)}, u32[]{:S(2)}, u32[]{:S(2)}) collective-permute-start(bf16[256,1152]{1,0:T(8,128)(2,1)S(1)} %pad_maximum_fusion.1.refs_0_), channel_id=1, source_target_pairs={{0,16},{1,9},{2,18},{3,11},{4,20},{5,13},{6,22},{7,15},{8,24},{9,1... | collective-permute-start | bytes 1769480 | tf_op jit(solution)/shard_map/ppermute | solution.py:270
  43.3 13.3 %collective-permute-start.20 = (bf16[64,1152]{1,0:T(8,128)(2,1)S(1)}, bf16[64,1152]{1,0:T(8,128)(2,1)S(1)}, u32[]{:S(2)}, u32[]{:S(2)}) collective-permute-start(bf16[64,1152]{1,0:T(8,128)(2,1)S(1)} %shard_map.87), channel_id=1, source_target_pairs={{0,4},{1,5},{2,6},{3,7},{4,0},{5,1},{6,2},{7,3},{8,12},{9,13},{10,... | collective-permute-start | bytes 442376 | tf_op jit(solution)/shard_map/ppermute | solution.py:259
  43.3 13.3 %collective-permute-start.21 = (bf16[64,1152]{1,0:T(8,128)(2,1)S(1)}, bf16[64,1152]{1,0:T(8,128)(2,1)S(1)}, u32[]{:S(2)}, u32[]{:S(2)}) collective-permute-start(bf16[64,1152]{1,0:T(8,128)(2,1)S(1)} %shard_map.87), channel_id=1, source_target_pairs={{0,6},{1,7},{2,4},{3,5},{4,2},{5,3},{6,0},{7,1},{8,14},{9,15},{10,... | collective-permute-start | bytes 442376 | tf_op jit(solution)/shard_map/ppermute | solution.py:259
  46.1 10.1 %collective-permute-start.10 = (bf16[64,1152]{1,0:T(8,128)(2,1)S(1)}, bf16[64,1152]{1,0:T(8,128)(2,1)S(1)}, u32[]{:S(2)}, u32[]{:S(2)}) collective-permute-start(bf16[64,1152]{1,0:T(8,128)(2,1)S(1)} %shard_map.87), channel_id=1, source_target_pairs={{0,2},{1,3},{2,0},{3,1},{4,6},{5,7},{6,4},{7,5},{8,10},{9,11},{10,... | collective-permute-start | bytes 442376 | tf_op jit(solution)/shard_map/ppermute | solution.py:259
  48.6 10.4 %collective-permute-start.17 = (bf16[128,1152]{1,0:T(8,128)(2,1)S(1)}, bf16[128,1152]{1,0:T(8,128)(2,1)S(1)}, u32[]{:S(2)}, u32[]{:S(2)}) collective-permute-start(bf16[128,1152]{1,0:T(8,128)(2,1)S(1)} %pad_maximum_fusion.6), channel_id=1, source_target_pairs={{0,16},{1,9},{2,18},{3,11},{4,20},{5,13},{6,22},{7,15},{8,24},{9,1... | collective-permute-start | bytes 884744 | tf_op jit(solution)/shard_map/ppermute | solution.py:270
  56.2 5.1 %collective-permute-start.18 = (bf16[64,1152]{1,0:T(8,128)(2,1)S(1)}, bf16[64,1152]{1,0:T(8,128)(2,1)S(1)}, u32[]{:S(2)}, u32[]{:S(2)}) collective-permute-start(bf16[64,1152]{1,0:T(8,128)(2,1)S(1)} %collective-permute-done.10), channel_id=1, source_target_pairs={{0,8},{1,17},{2,10},{3,19},{4,12},{5,21},{6,14},{7,23},{8,0},{9,25... | collective-permute-start | bytes 442376 | tf_op jit(solution)/shard_map/ppermute | solution.py:270
  56.6 10.0 %collective-permute-start.22 = (bf16[128,1152]{1,0:T(8,128)(2,1)S(1)}, bf16[128,1152]{1,0:T(8,128)(2,1)S(1)}, u32[]{:S(2)}, u32[]{:S(2)}) collective-permute-start(bf16[128,1152]{1,0:T(8,128)(2,1)S(1)} %pad_maximum_fusion.9), channel_id=1, source_target_pairs={{0,8},{1,17},{2,10},{3,19},{4,12},{5,21},{6,14},{7,23},{8,0},{9,25... | collective-permute-start | bytes 884744 | tf_op jit(solution)/shard_map/ppermute | solution.py:270
  58.4 10.5 %collective-permute-start.16 = (bf16[512,1152]{1,0:T(8,128)(2,1)S(1)}, bf16[512,1152]{1,0:T(8,128)(2,1)S(1)}, u32[]{:S(2)}, u32[]{:S(2)}) collective-permute-start(bf16[512,1152]{1,0:T(8,128)(2,1)S(1)} %shard_map.90.refs_1_), channel_id=1, source_target_pairs={{0,1},{1,0},{2,3},{3,2},{4,5},{5,4},{6,7},{7,6},{8,9},{9,8},{10,11... | collective-permute-start | bytes 3538952 | tf_op jit(solution)/shard_map/ppermute | solution.py:262
  58.5 12.3 %collective-permute-start.15 = (bf16[512,1152]{1,0:T(8,128)(2,1)S(1)}, bf16[512,1152]{1,0:T(8,128)(2,1)S(1)}, u32[]{:S(2)}, u32[]{:S(2)}) collective-permute-start(bf16[512,1152]{1,0:T(8,128)(2,1)S(1)} %shard_map.89.refs_0_), channel_id=1, source_target_pairs={{0,1},{1,0},{2,3},{3,2},{4,5},{5,4},{6,7},{7,6},{8,9},{9,8},{10,11... | collective-permute-start | bytes 3538952 | tf_op jit(solution)/shard_map/ppermute | solution.py:262
  59.1 9.2 %collective-permute-start.23 = (bf16[256,1152]{1,0:T(8,128)(2,1)S(1)}, bf16[256,1152]{1,0:T(8,128)(2,1)S(1)}, u32[]{:S(2)}, u32[]{:S(2)}) collective-permute-start(bf16[256,1152]{1,0:T(8,128)(2,1)S(1)} %pad_maximum_fusion.2.refs_0_), channel_id=1, source_target_pairs={{0,1},{1,0},{2,3},{3,2},{4,5},{5,4},{6,7},{7,6},{8,9},{9,8},{10,11... | collective-permute-start | bytes 1769480 | tf_op jit(solution)/shard_map/ppermute | solution.py:262
  61.4 6.8 %collective-permute-start.19 = (bf16[128,1152]{1,0:T(8,128)(2,1)S(1)}, bf16[128,1152]{1,0:T(8,128)(2,1)S(1)}, u32[]{:S(2)}, u32[]{:S(2)}) collective-permute-start(bf16[128,1152]{1,0:T(8,128)(2,1)S(1)} %pad_maximum_fusion.8), channel_id=1, source_target_pairs={{0,16},{1,9},{2,18},{3,11},{4,20},{5,13},{6,22},{7,15},{8,24},{9,1... | collective-permute-start | bytes 884744 | tf_op jit(solution)/shard_map/ppermute | solution.py:270
  66.7 12.1 %collective-permute-start.12 = (f32[256,1152]{1,0:T(8,128)S(1)}, f32[256,1152]{1,0:T(8,128)S(1)}, u32[]{:S(2)}, u32[]{:S(2)}) collective-permute-start(f32[256,1152]{1,0:T(8,128)S(1)} %get-tuple-element.43), channel_id=1, source_target_pairs={{0,1},{1,0},{2,3},{3,2},{4,5},{5,4},{6,7},{7,6},{8,9},{9,8},{10,11... | collective-permute-start | bytes 3538952 | tf_op jit(solution)/shard_map/ppermute | solution.py:262
  68.3 3.8 %collective-permute-start.24 = (bf16[256,1152]{1,0:T(8,128)(2,1)S(1)}, bf16[256,1152]{1,0:T(8,128)(2,1)S(1)}, u32[]{:S(2)}, u32[]{:S(2)}) collective-permute-start(bf16[256,1152]{1,0:T(8,128)(2,1)S(1)} %pad_maximum_fusion.3.refs_1_), channel_id=1, source_target_pairs={{0,1},{1,0},{2,3},{3,2},{4,5},{5,4},{6,7},{7,6},{8,9},{9,8},{10,11... | collective-permute-start | bytes 1769480 | tf_op jit(solution)/shard_map/ppermute | solution.py:262
  68.3 3.7 %collective-permute-start.25 = (bf16[256,1152]{1,0:T(8,128)(2,1)S(1)}, bf16[256,1152]{1,0:T(8,128)(2,1)S(1)}, u32[]{:S(2)}, u32[]{:S(2)}) collective-permute-start(bf16[256,1152]{1,0:T(8,128)(2,1)S(1)} %pad_maximum_fusion.4.refs_2_), channel_id=1, source_target_pairs={{0,1},{1,0},{2,3},{3,2},{4,5},{5,4},{6,7},{7,6},{8,9},{9,8},{10,11... | collective-permute-start | bytes 1769480 | tf_op jit(solution)/shard_map/ppermute | solution.py:262
  68.8 9.9 %collective-permute-start.26 = (bf16[256,1152]{1,0:T(8,128)(2,1)S(1)}, bf16[256,1152]{1,0:T(8,128)(2,1)S(1)}, u32[]{:S(2)}, u32[]{:S(2)}) collective-permute-start(bf16[256,1152]{1,0:T(8,128)(2,1)S(1)} %pad_maximum_fusion.4.refs_2_), channel_id=1, source_target_pairs={{0,16},{1,9},{2,18},{3,11},{4,20},{5,13},{6,22},{7,15},{8,24},{9,1... | collective-permute-start | bytes 1769480 | tf_op jit(solution)/shard_map/ppermute | solution.py:270
  78.7 2.0 %collective-permute-start.27 = (bf16[256,1152]{1,0:T(8,128)(2,1)S(1)}, bf16[256,1152]{1,0:T(8,128)(2,1)S(1)}, u32[]{:S(2)}, u32[]{:S(2)}) collective-permute-start(bf16[256,1152]{1,0:T(8,128)(2,1)S(1)} %collective-permute-done.26.refs_0_), channel_id=1, source_target_pairs={{0,1},{1,0},{2,3},{3,2},{4,5},{5,4},{6,7},{7,6},{8,9},{9,8},{10,11... | collective-permute-start | bytes 1769480 | tf_op jit(solution)/shard_map/ppermute | solution.py:262

commit v15 on v14

--- a/solution.py
+++ b/solution.py
@@ -313,9 +313,9 @@
     near = after(jnp.concatenate(near), g_own[0])
     near_first = step_d(near, 0)
     g_near = over_d(near, near_first)
-    far = after(jnp.concatenate(far), near)
+    far = after(jnp.concatenate(far), near, grad_features)
     far_first = step_d(far, 0)
-    dlogit = after(dlogit, near)
+    dlogit = after(dlogit, far)
     adjoint, adjoint_other = caption_sums(both, dlogit, unit)
     adjoint = adjoint + swap(adjoint_other)
     per = nd // 2

time: 84 us -> 82.3 us (0.980)
  waiting for transfers between devices: 37.9 us -> 32.3 us
  starting transfers between devices: 26.3 us -> 30.2 us
    ppermute x10, waiting for transfers between devices: 13.2 us -> 9.22 us  [step_d(): return lax.ppermute(v, ('dp', 'blk'), perm)]
    ppermute x10, starting transfers between devices: 10.4 us -> 12.9 us  [step_d(): return lax.ppermute(v, ('dp', 'blk'), perm)]
    ppermute x9, waiting for transfers between devices: 23.8 us -> 21.6 us  [along_z(): return lax.ppermute(v, 'blk', [(i, i ^ 2 * k) for i in range(nb)])]
    ppermute x9, starting transfers between devices: 14.1 us -> 15 us  [along_z(): return lax.ppermute(v, 'blk', [(i, i ^ 2 * k) for i in range(nb)])]
where the time goes in v15:
time: 82.3 us; the launch traced here: 82.1 us
  waiting for transfers between devices  32.3 us (39%)
  starting transfers between devices  30.2 us (37%)
  Pallas kernels  12.4 us (15%)
  matrix products  2.65 us (3%)
  between operations  2.13 us (3%)
  other arithmetic  1.49 us (2%)
  local copies, waits for them, and re-layouts  1.01 us (1%)
    ppermute x9, waiting for transfers between devices, along_z(): return lax.ppermute(v, 'blk', [(i, i ^ 2 * k) for i in range(nb)])  21.6 us
    ppermute x9, starting transfers between devices, along_z(): return lax.ppermute(v, 'blk', [(i, i ^ 2 * k) for i in range(nb)])  15 us
    ppermute x10, starting transfers between devices, step_d(): return lax.ppermute(v, ('dp', 'blk'), perm)  12.9 us
    ppermute x10, waiting for transfers between devices, step_d(): return lax.ppermute(v, ('dp', 'blk'), perm)  9.22 us
    pallas_call x2, Pallas kernels, weight_sum(): pl.pallas_call(kernel, out_shape=jax.ShapeDtypeStruct((depth, depth), F32...  7.84 us
    dot_general x2, matrix products, dot(): return lax.dot_general(a, b, dims, preferred_element_type=F32)  2.65 us
    ppermute x9, starting transfers between devices, swap(): return lax.ppermute(v, 'blk', [(i, i ^ 1) for i in range(nb)])  2.32 us
    pallas_call x1, Pallas kernels, scores(): pl.pallas_call(functools.partial(score_kernel, nz), out_shape=outs, in_sp...  2.3 us
  transfers between devices with their start and end apart: 28, of which 12 were waited for; matrix products, arithmetic and copies ran while one was open for 5% of the time, Pallas kernels for 11%

profile of v15, /device:TPU:0, one launch (start us, length us, event | category | flops | bytes accessed | tf_op | source)
XLA Modules:
  0.0 82.1 jit_solution(3878545072795216399)
XLA Ops:
  0.6 0.0 copy-start
  0.6 4.1 %collective-permute-start.1 = (bf16[64,1152]{1,0:T(8,128)(2,1)}, bf16[64,1152]{1,0:T(8,128)(2,1)S(1)}, u32[]{:S(2)}, u32[]{:S(2)}) collective-permute-start(bf16[64,1152]{1,0:T(8,128)(2,1)} %bitcast.9), channel_id=1, source_target_pairs={{0,4},{1,5},{2,6},{3,7},{4,0},{5,1},{6,2},{7,3},{8,12},{9,13},{10,... | collective-permute-start | bytes 442376 | tf_op jit(solution)/shard_map/ppermute | solution.py:259
  4.7 1.3 %collective-permute-start.2 = (bf16[64,1152]{1,0:T(8,128)(2,1)}, bf16[64,1152]{1,0:T(8,128)(2,1)S(1)}, u32[]{:S(2)}, u32[]{:S(2)}) collective-permute-start(bf16[64,1152]{1,0:T(8,128)(2,1)} %bitcast.10), channel_id=1, source_target_pairs={{0,6},{1,7},{2,4},{3,5},{4,2},{5,3},{6,0},{7,1},{8,14},{9,15},{10,... | collective-permute-start | bytes 442376 | tf_op jit(solution)/shard_map/ppermute | solution.py:259
  6.1 0.2 collective-permute-start
  6.3 0.5 collective-permute-start.3
  8.1 7.9 %collective-permute-done.1.refs_2_ = bf16[64,1152]{1,0:T(8,128)(2,1)S(1)} collective-permute-done((bf16[64,1152]{1,0:T(8,128)(2,1)}, bf16[64,1152]{1,0:T(8,128)(2,1)S(1)}, u32[]{:S(2)}, u32[]{:S(2)}) %collective-permute-start.1) | collective-permute-done | bytes 147488 | tf_op jit(solution)/shard_map/ppermute | solution.py:259
  16.0 0.0 collective-permute-done.2.refs_3_
  16.0 1.9 %collective-permute-start.8 = (bf16[128,1152]{1,0:T(8,128)(2,1)S(1)}, bf16[128,1152]{1,0:T(8,128)(2,1)S(1)}, u32[]{:S(2)}, u32[]{:S(2)}) collective-permute-start(bf16[128,1152]{1,0:T(8,128)(2,1)S(1)} %pad_maximum_fusion.5), channel_id=1, source_target_pairs={{0,8},{1,17},{2,10},{3,19},{4,12},{5,21},{6,14},{7,23},{8,0},{9,25... | collective-permute-start | bytes 884744 | tf_op jit(solution)/shard_map/ppermute | solution.py:270
  17.9 0.0 collective-permute-done.refs_1_
  17.9 0.9 %copy-done.1 = bf16[1,64,1152]{2,1,0:T(8,128)(2,1)S(1)} copy-done((bf16[1,64,1152]{2,1,0:T(8,128)(2,1)S(1)}, bf16[1,64,1152]{2,1,0:T(8,128)(2,1)}, u32[]{:S(2)}) %copy-start.1) | copy-done | bytes 147480
  18.9 0.0 copy-start.3
  18.9 0.0 copy-start.4
  18.9 1.0 %fusion.embed = f32[256,1152]{1,0:T(8,128)S(1)} fusion(bf16[256,1152]{1,0:T(8,128)(2,1)S(1)} %shard_map.85, bf16[1152,1152]{1,0:T(8,128)(2,1)S(1)} %copy-done), kind=kOutput, calls=%fused_computation.12 | convolution fusion | flops 679477248 | bytes 4423680 | tf_op jit(solution)/shard_map/dot_general | solution.py:17
  19.9 0.0 collective-permute-done.3.refs_1_
  20.0 0.1 iota.7.both
  20.0 2.3 %shard_map.86 = (f32[64,1152]{1,0:T(8,128)S(1)}, f32[64,1152]{1,0:T(8,128)S(1)}, f32[64,128]{1,0:T(8,128)S(1)}, bf16[256,1152]{1,0:T(8,128)(2,1)S(1)}, bf16[256,...) custom-call(f32[16,128]{1,0:T(8,128)S(1)} %iota.7.both, ...), custom_call_target="tpu_custom_call" | custom-call | flops 603979776 | bytes 4718592 | tf_op jit(solution)/shard_map/pallas_call | solution.py:74
  22.3 0.0 copy-start.2
  22.4 0.5 collective-permute-done.8
  22.9 2.1 %collective-permute-start.9 = (bf16[256,1152]{1,0:T(8,128)(2,1)S(1)}, bf16[256,1152]{1,0:T(8,128)(2,1)S(1)}, u32[]{:S(2)}, u32[]{:S(2)}) collective-permute-start(bf16[256,1152]{1,0:T(8,128)(2,1)S(1)} %pad_maximum_fusion.refs_0_), channel_id=1, source_target_pairs={{0,16},{1,9},{2,18},{3,11},{4,20},{5,13},{6,22},{7,15},{8,24},{9,1... | collective-permute-start | bytes 1769480 | tf_op jit(solution)/shard_map/ppermute | solution.py:270
  25.0 1.6 %collective-permute-start.15 = (bf16[128,1152]{1,0:T(8,128)(2,1)S(1)}, bf16[128,1152]{1,0:T(8,128)(2,1)S(1)}, u32[]{:S(2)}, u32[]{:S(2)}) collective-permute-start(bf16[128,1152]{1,0:T(8,128)(2,1)S(1)} %pad_maximum_fusion.8), channel_id=1, source_target_pairs={{0,8},{1,17},{2,10},{3,19},{4,12},{5,21},{6,14},{7,23},{8,0},{9,25... | collective-permute-start | bytes 884744 | tf_op jit(solution)/shard_map/ppermute | solution.py:270
  26.6 2.2 %collective-permute-start.5 = (bf16[64,1152]{1,0:T(8,128)(2,1)S(1)}, bf16[64,1152]{1,0:T(8,128)(2,1)S(1)}, u32[]{:S(2)}, u32[]{:S(2)}) collective-permute-start(bf16[64,1152]{1,0:T(8,128)(2,1)S(1)} %get-tuple-element.31), channel_id=1, source_target_pairs={{0,6},{1,7},{2,4},{3,5},{4,2},{5,3},{6,0},{7,1},{8,14},{9,15},{10,... | collective-permute-start | bytes 442376 | tf_op jit(solution)/shard_map/ppermute | solution.py:259
  28.8 2.2 %collective-permute-start.6 = (bf16[64,1152]{1,0:T(8,128)(2,1)S(1)}, bf16[64,1152]{1,0:T(8,128)(2,1)S(1)}, u32[]{:S(2)}, u32[]{:S(2)}) collective-permute-start(bf16[64,1152]{1,0:T(8,128)(2,1)S(1)} %get-tuple-element.32), channel_id=1, source_target_pairs={{0,4},{1,5},{2,6},{3,7},{4,0},{5,1},{6,2},{7,3},{8,12},{9,13},{10,... | collective-permute-start | bytes 442376 | tf_op jit(solution)/shard_map/ppermute | solution.py:259
  31.0 0.6 collective-permute-start.7
  31.6 1.0 %collective-permute-done.15 = bf16[128,1152]{1,0:T(8,128)(2,1)S(1)} collective-permute-done((bf16[128,1152]{1,0:T(8,128)(2,1)S(1)}, bf16[128,1152]{1,0:T(8,128)(2,1)S(1)}, u32[]{:S(2)}, u32[]{:S(2)}) %collective-permute-start.15) | collective-permute-done | bytes 294944 | tf_op jit(solution)/shard_map/ppermute | solution.py:270
  32.6 1.8 %collective-permute-done.5.refs_0_ = bf16[64,1152]{1,0:T(8,128)(2,1)S(1)} collective-permute-done((bf16[64,1152]{1,0:T(8,128)(2,1)S(1)}, bf16[64,1152]{1,0:T(8,128)(2,1)S(1)}, u32[]{:S(2)}, u32[]{:S(2)}) %collective-permute-start.5) | collective-permute-done | bytes 147488 | tf_op jit(solution)/shard_map/ppermute | solution.py:259
  34.4 7.1 %collective-permute-done.6.refs_1_ = bf16[64,1152]{1,0:T(8,128)(2,1)S(1)} collective-permute-done((bf16[64,1152]{1,0:T(8,128)(2,1)S(1)}, bf16[64,1152]{1,0:T(8,128)(2,1)S(1)}, u32[]{:S(2)}, u32[]{:S(2)}) %collective-permute-start.6) | collective-permute-done | bytes 147488 | tf_op jit(solution)/shard_map/ppermute | solution.py:259
  41.5 0.0 collective-permute-done.7.refs_2_
  41.5 0.0 collective-permute-done.9.refs_1_
  41.5 0.2 shard_map.87
  41.7 0.6 collective-permute-start.13
  42.4 0.9 %collective-permute-start.16 = (bf16[256,1152]{1,0:T(8,128)(2,1)S(1)}, bf16[256,1152]{1,0:T(8,128)(2,1)S(1)}, u32[]{:S(2)}, u32[]{:S(2)}) collective-permute-start(bf16[256,1152]{1,0:T(8,128)(2,1)S(1)} %pad_maximum_fusion.1.refs_0_), channel_id=1, source_target_pairs={{0,16},{1,9},{2,18},{3,11},{4,20},{5,13},{6,22},{7,15},{8,24},{9,1... | collective-permute-start | bytes 1769480 | tf_op jit(solution)/shard_map/ppermute | solution.py:270
  43.3 0.0 collective-permute-start.12
  43.3 3.4 %collective-permute-start.10 = (bf16[64,1152]{1,0:T(8,128)(2,1)S(1)}, bf16[64,1152]{1,0:T(8,128)(2,1)S(1)}, u32[]{:S(2)}, u32[]{:S(2)}) collective-permute-start(bf16[64,1152]{1,0:T(8,128)(2,1)S(1)} %shard_map.87), channel_id=1, source_target_pairs={{0,4},{1,5},{2,6},{3,7},{4,0},{5,1},{6,2},{7,3},{8,12},{9,13},{10,... | collective-permute-start | bytes 442376 | tf_op jit(solution)/shard_map/ppermute | solution.py:259
  46.7 1.0 %collective-permute-start.11 = (bf16[64,1152]{1,0:T(8,128)(2,1)S(1)}, bf16[64,1152]{1,0:T(8,128)(2,1)S(1)}, u32[]{:S(2)}, u32[]{:S(2)}) collective-permute-start(bf16[64,1152]{1,0:T(8,128)(2,1)S(1)} %shard_map.87), channel_id=1, source_target_pairs={{0,6},{1,7},{2,4},{3,5},{4,2},{5,3},{6,0},{7,1},{8,14},{9,15},{10,... | collective-permute-start | bytes 442376 | tf_op jit(solution)/shard_map/ppermute | solution.py:259
  47.6 0.9 %collective-permute-done.13 = bf16[64,1152]{1,0:T(8,128)(2,1)S(1)} collective-permute-done((bf16[64,1152]{1,0:T(8,128)(2,1)S(1)}, bf16[64,1152]{1,0:T(8,128)(2,1)S(1)}, u32[]{:S(2)}, u32[]{:S(2)}) %collective-permute-start.13) | collective-permute-done | bytes 147488 | tf_op jit(solution)/shard_map/ppermute | solution.py:270
  48.6 0.6 collective-permute-start.19
  49.2 1.7 %fusion.1 = f32[64,1152]{1,0:T(8,128)} fusion(bf16[64,1152]{1,0:T(8,128)(2,1)S(1)} %shard_map.87, bf16[1152,1152]{1,0:T(8,128)(2,1)S(1)} %copy-done), kind=kOutput, calls=%fused_computation.13 | convolution fusion | flops 169869312 | bytes 3096576 | tf_op jit(solution)/shard_map/dot_general | solution.py:17
  50.8 0.1 shard_map.90.refs_1_
  50.9 0.0 collective-permute-done.12
  50.9 1.3 %collective-permute-start.20 = (bf16[64,1152]{1,0:T(8,128)(2,1)S(1)}, bf16[64,1152]{1,0:T(8,128)(2,1)S(1)}, u32[]{:S(2)}, u32[]{:S(2)}) collective-permute-start(bf16[64,1152]{1,0:T(8,128)(2,1)S(1)} %collective-permute-done.12), channel_id=1, source_target_pairs={{0,8},{1,17},{2,10},{3,19},{4,12},{5,21},{6,14},{7,23},{8,0},{9,25... | collective-permute-start | bytes 442376 | tf_op jit(solution)/shard_map/ppermute | solution.py:270
  52.3 4.9 %collective-permute-done.10 = bf16[64,1152]{1,0:T(8,128)(2,1)S(1)} collective-permute-done((bf16[64,1152]{1,0:T(8,128)(2,1)S(1)}, bf16[64,1152]{1,0:T(8,128)(2,1)S(1)}, u32[]{:S(2)}, u32[]{:S(2)}) %collective-permute-start.10) | collective-permute-done | bytes 147488 | tf_op jit(solution)/shard_map/ppermute | solution.py:259
  57.1 0.0 collective-permute-done.11
  57.2 1.2 %collective-permute-start.22 = (bf16[128,1152]{1,0:T(8,128)(2,1)S(1)}, bf16[128,1152]{1,0:T(8,128)(2,1)S(1)}, u32[]{:S(2)}, u32[]{:S(2)}) collective-permute-start(bf16[128,1152]{1,0:T(8,128)(2,1)S(1)} %pad_maximum_fusion.6), channel_id=1, source_target_pairs={{0,8},{1,17},{2,10},{3,19},{4,12},{5,21},{6,14},{7,23},{8,0},{9,25... | collective-permute-start | bytes 884744 | tf_op jit(solution)/shard_map/ppermute | solution.py:270
  58.3 0.0 collective-permute-done.16.refs_1_
  58.3 0.1 shard_map.89.refs_0_
  58.4 0.6 collective-permute-start.17
  59.0 0.0 collective-permute-done.19
  59.0 0.1 collective-permute-start.23
  59.1 1.6 %collective-permute-start.21 = (bf16[128,1152]{1,0:T(8,128)(2,1)S(1)}, bf16[128,1152]{1,0:T(8,128)(2,1)S(1)}, u32[]{:S(2)}, u32[]{:S(2)}) collective-permute-start(bf16[128,1152]{1,0:T(8,128)(2,1)S(1)} %pad_maximum_fusion.9), channel_id=1, source_target_pairs={{0,16},{1,9},{2,18},{3,11},{4,20},{5,13},{6,22},{7,15},{8,24},{9,1... | collective-permute-start | bytes 884744 | tf_op jit(solution)/shard_map/ppermute | solution.py:270
  60.7 0.5 shard_map.88
  61.3 4.2 %collective-permute-done.22 = bf16[128,1152]{1,0:T(8,128)(2,1)S(1)} collective-permute-done((bf16[128,1152]{1,0:T(8,128)(2,1)S(1)}, bf16[128,1152]{1,0:T(8,128)(2,1)S(1)}, u32[]{:S(2)}, u32[]{:S(2)}) %collective-permute-start.22) | collective-permute-done | bytes 294944 | tf_op jit(solution)/shard_map/ppermute | solution.py:270
  65.5 0.0 collective-permute-start.14
  65.6 0.4 collective-permute-done.21
  66.0 1.0 %collective-permute-start.24 = (bf16[256,1152]{1,0:T(8,128)(2,1)S(1)}, bf16[256,1152]{1,0:T(8,128)(2,1)S(1)}, u32[]{:S(2)}, u32[]{:S(2)}) collective-permute-start(bf16[256,1152]{1,0:T(8,128)(2,1)S(1)} %pad_maximum_fusion.3.refs_1_), channel_id=1, source_target_pairs={{0,1},{1,0},{2,3},{3,2},{4,5},{5,4},{6,7},{7,6},{8,9},{9,8},{10,11... | collective-permute-start | bytes 1769480 | tf_op jit(solution)/shard_map/ppermute | solution.py:262
  67.0 0.1 collective-permute-start.25
  67.1 0.0 collective-permute-done.18.refs_3_
  67.1 1.1 %collective-permute-start.26 = (bf16[256,1152]{1,0:T(8,128)(2,1)S(1)}, bf16[256,1152]{1,0:T(8,128)(2,1)S(1)}, u32[]{:S(2)}, u32[]{:S(2)}) collective-permute-start(bf16[256,1152]{1,0:T(8,128)(2,1)S(1)} %pad_maximum_fusion.4.refs_2_), channel_id=1, source_target_pairs={{0,16},{1,9},{2,18},{3,11},{4,20},{5,13},{6,22},{7,15},{8,24},{9,1... | collective-permute-start | bytes 1769480 | tf_op jit(solution)/shard_map/ppermute | solution.py:270
  68.2 1.3 %shard_map.91 = (bf16[1152,1536]{1,0:T(8,128)(2,1)S(1)}, bf16[1152,512]{1,0:T(8,128)(2,1)S(1)}) custom-call(bf16[512,1152]{1,0:T(8,128)(2,1)S(1)} %shard_map.89.refs_0_, bf16[512,1152]{1,0:T(8,128)(2,1)S(1)} %shard_map.90.refs_1_, bf16[512,1152]{1,0:T(8,128)(2,1)S(1)} %collective-permute-done.17.refs_2_, bf16[512,1152]{1,0:T(8,128)(2,1)S(1)} %collective-permute-done.18.refs_3_), custom_call_target="tpu_custom_call" | custom-call | bytes 9437184 | tf_op jit(solution)/shard_map/pallas_call | solution.py:180
  69.5 0.5 collective-permute-done.25.refs_5_
  70.1 4.8 %shard_map.92.acc = f32[1152,1152]{1,0:T(8,128)S(1)} custom-call(bf16[1152,1536]{1,0:T(8,128)(2,1)S(1)} %get-tuple-element.49.x_t, bf16[256,1152]{1,0:T(8,128)(2,1)S(1)} %pad_maximum_fusion.2.refs_0_, bf16[256,1152]{1,0:T(8,128)(2,1)S(1)} %pad_maximum_fusion.3.refs_1_, bf16[256,1152]{1,0:T(8,128)(2,1)S(1)} %pad_maximum_fusion.4.refs_2_, ...), custom_call_target="tpu_custom_call" | custom-call | flops 4076863488 | bytes 12386304 | tf_op jit(solution)/shard_map/pallas_call | solution.py:235
  74.8 2.2 %collective-permute-done.26.refs_0_ = bf16[256,1152]{1,0:T(8,128)(2,1)S(1)} collective-permute-done((bf16[256,1152]{1,0:T(8,128)(2,1)S(1)}, bf16[256,1152]{1,0:T(8,128)(2,1)S(1)}, u32[]{:S(2)}, u32[]{:S(2)}) %collective-permute-start.26) | collective-permute-done | bytes 589856 | tf_op jit(solution)/shard_map/ppermute | solution.py:270
  77.0 1.1 %add_bitcast_fusion = f32[1,256,1152]{2,1,0:T(8,128)} fusion(f32[256,1152]{1,0:T(8,128)S(1)} %get-tuple-element.43, f32[256,1152]{1,0:T(8,128)S(1)} %collective-permute-done.14), kind=kLoop, calls=%fused_computation | loop fusion | flops 294912 | bytes 3538944 | tf_op jit(solution)/shard_map/broadcast_in_dim | solution.py:362
  78.2 0.9 %collective-permute-done.27.refs_1_ = bf16[256,1152]{1,0:T(8,128)(2,1)S(1)} collective-permute-done((bf16[256,1152]{1,0:T(8,128)(2,1)S(1)}, bf16[256,1152]{1,0:T(8,128)(2,1)S(1)}, u32[]{:S(2)}, u32[]{:S(2)}) %collective-permute-start.27) | collective-permute-done | bytes 589856 | tf_op jit(solution)/shard_map/ppermute | solution.py:262
  79.0 3.1 %shard_map.93 = f32[1152,1152]{1,0:T(8,128)} custom-call(bf16[1152,512]{1,0:T(8,128)(2,1)S(1)} %get-tuple-element.48.x_t, f32[1152,1152]{1,0:T(8,128)S(1)} %shard_map.92.acc, bf16[256,1152]{1,0:T(8,128)(2,1)S(1)} %collective-permute-done.26.refs_0_, bf16[256,1152]{1,0:T(8,128)(2,1)S(1)} %collective-permute-done.27.refs_1_), custom_call_target="tpu_custom_call" | custom-call | flops 1358954496 | bytes 12976128 | tf_op jit(solution)/shard_map/pallas_call | solution.py:235
  (26 shorter events, 0.4 us)
Async XLA Ops:
  0.6 18.3 %copy-start = (bf16[1152,1152]{1,0:T(8,128)(2,1)S(1)}, bf16[1152,1152]{1,0:T(8,128)(2,1)}, u32[]{:S(2)}) copy-start(bf16[1152,1152]{1,0:T(8,128)(2,1)} %param.9) | copy-start | bytes 7962628
  0.6 15.4 %collective-permute-start.1 = (bf16[64,1152]{1,0:T(8,128)(2,1)}, bf16[64,1152]{1,0:T(8,128)(2,1)S(1)}, u32[]{:S(2)}, u32[]{:S(2)}) collective-permute-start(bf16[64,1152]{1,0:T(8,128)(2,1)} %bitcast.9), channel_id=1, source_target_pairs={{0,4},{1,5},{2,6},{3,7},{4,0},{5,1},{6,2},{7,3},{8,12},{9,13},{10,... | collective-permute-start | bytes 442376 | tf_op jit(solution)/shard_map/ppermute | solution.py:259
  4.7 11.3 %collective-permute-start.2 = (bf16[64,1152]{1,0:T(8,128)(2,1)}, bf16[64,1152]{1,0:T(8,128)(2,1)S(1)}, u32[]{:S(2)}, u32[]{:S(2)}) collective-permute-start(bf16[64,1152]{1,0:T(8,128)(2,1)} %bitcast.10), channel_id=1, source_target_pairs={{0,6},{1,7},{2,4},{3,5},{4,2},{5,3},{6,0},{7,1},{8,14},{9,15},{10,... | collective-permute-start | bytes 442376 | tf_op jit(solution)/shard_map/ppermute | solution.py:259
  6.1 11.8 %collective-permute-start = (bf16[64,1152]{1,0:T(8,128)(2,1)}, bf16[64,1152]{1,0:T(8,128)(2,1)S(1)}, u32[]{:S(2)}, u32[]{:S(2)}) collective-permute-start(bf16[64,1152]{1,0:T(8,128)(2,1)} %bitcast.11), channel_id=1, source_target_pairs={{0,2},{1,3},{2,0},{3,1},{4,6},{5,7},{6,4},{7,5},{8,10},{9,11},{10,... | collective-permute-start | bytes 442376 | tf_op jit(solution)/shard_map/ppermute | solution.py:259
  6.3 13.6 %collective-permute-start.4 = (bf16[256,1152]{1,0:T(8,128)(2,1)}, bf16[256,1152]{1,0:T(8,128)(2,1)}, u32[]{:S(2)}, u32[]{:S(2)}) collective-permute-start(bf16[256,1152]{1,0:T(8,128)(2,1)} %bitcast.15), channel_id=1, source_target_pairs={{0,1},{1,0},{2,3},{3,2},{4,5},{5,4},{6,7},{7,6},{8,9},{9,8},{10,11... | collective-permute-start | bytes 1769480 | tf_op jit(solution)/shard_map/ppermute | solution.py:262
  6.3 13.6 %collective-permute-start.3 = (s32[1,256]{1,0:T(1,128)}, s32[1,256]{1,0:T(1,128)S(1)}, u32[]{:S(2)}, u32[]{:S(2)}) collective-permute-start(s32[1,256]{1,0:T(1,128)} %refs_0_.1), channel_id=1, source_target_pairs={{0,1},{1,0},{2,3},{3,2},{4,5},{5,4},{6,7},{7,6},{8,9},{9,8},{10,11... | collective-permute-start | bytes 3080 | tf_op jit(solution)/shard_map/ppermute | solution.py:262
  16.0 6.8 %collective-permute-start.8 = (bf16[128,1152]{1,0:T(8,128)(2,1)S(1)}, bf16[128,1152]{1,0:T(8,128)(2,1)S(1)}, u32[]{:S(2)}, u32[]{:S(2)}) collective-permute-start(bf16[128,1152]{1,0:T(8,128)(2,1)S(1)} %pad_maximum_fusion.5), channel_id=1, source_target_pairs={{0,8},{1,17},{2,10},{3,19},{4,12},{5,21},{6,14},{7,23},{8,0},{9,25... | collective-permute-start | bytes 884744 | tf_op jit(solution)/shard_map/ppermute | solution.py:270
  17.9 0.9 %copy-start.1 = (bf16[1,64,1152]{2,1,0:T(8,128)(2,1)S(1)}, bf16[1,64,1152]{2,1,0:T(8,128)(2,1)}, u32[]{:S(2)}) copy-start(bf16[1,64,1152]{2,1,0:T(8,128)(2,1)} %param.6) | copy-start | bytes 442372
  18.9 1.1 %copy-start.3 = (bf16[1,256,1152]{2,1,0:T(8,128)(2,1)S(1)}, bf16[1,256,1152]{2,1,0:T(8,128)(2,1)}, u32[]{:S(2)}) copy-start(bf16[1,256,1152]{2,1,0:T(8,128)(2,1)} %param.7) | copy-start | bytes 1769476
  18.9 1.1 %copy-start.4 = (s32[1,256]{1,0:T(1,128)S(1)}, s32[1,256]{1,0:T(1,128)}, u32[]{:S(2)}) copy-start(s32[1,256]{1,0:T(1,128)} %refs_0_.1) | copy-start | bytes 3076
  22.3 2.7 %copy-start.2 = (bf16[1,64,1152]{2,1,0:T(8,128)(2,1)S(1)}, bf16[1,64,1152]{2,1,0:T(8,128)(2,1)}, u32[]{:S(2)}) copy-start(bf16[1,64,1152]{2,1,0:T(8,128)(2,1)} %param.6) | copy-start | bytes 442372
  22.9 18.7 %collective-permute-start.9 = (bf16[256,1152]{1,0:T(8,128)(2,1)S(1)}, bf16[256,1152]{1,0:T(8,128)(2,1)S(1)}, u32[]{:S(2)}, u32[]{:S(2)}) collective-permute-start(bf16[256,1152]{1,0:T(8,128)(2,1)S(1)} %pad_maximum_fusion.refs_0_), channel_id=1, source_target_pairs={{0,16},{1,9},{2,18},{3,11},{4,20},{5,13},{6,22},{7,15},{8,24},{9,1... | collective-permute-start | bytes 1769480 | tf_op jit(solution)/shard_map/ppermute | solution.py:270
  25.0 7.6 %collective-permute-start.15 = (bf16[128,1152]{1,0:T(8,128)(2,1)S(1)}, bf16[128,1152]{1,0:T(8,128)(2,1)S(1)}, u32[]{:S(2)}, u32[]{:S(2)}) collective-permute-start(bf16[128,1152]{1,0:T(8,128)(2,1)S(1)} %pad_maximum_fusion.8), channel_id=1, source_target_pairs={{0,8},{1,17},{2,10},{3,19},{4,12},{5,21},{6,14},{7,23},{8,0},{9,25... | collective-permute-start | bytes 884744 | tf_op jit(solution)/shard_map/ppermute | solution.py:270
  26.6 7.8 %collective-permute-start.5 = (bf16[64,1152]{1,0:T(8,128)(2,1)S(1)}, bf16[64,1152]{1,0:T(8,128)(2,1)S(1)}, u32[]{:S(2)}, u32[]{:S(2)}) collective-permute-start(bf16[64,1152]{1,0:T(8,128)(2,1)S(1)} %get-tuple-element.31), channel_id=1, source_target_pairs={{0,6},{1,7},{2,4},{3,5},{4,2},{5,3},{6,0},{7,1},{8,14},{9,15},{10,... | collective-permute-start | bytes 442376 | tf_op jit(solution)/shard_map/ppermute | solution.py:259
  28.8 12.7 %collective-permute-start.6 = (bf16[64,1152]{1,0:T(8,128)(2,1)S(1)}, bf16[64,1152]{1,0:T(8,128)(2,1)S(1)}, u32[]{:S(2)}, u32[]{:S(2)}) collective-permute-start(bf16[64,1152]{1,0:T(8,128)(2,1)S(1)} %get-tuple-element.32), channel_id=1, source_target_pairs={{0,4},{1,5},{2,6},{3,7},{4,0},{5,1},{6,2},{7,3},{8,12},{9,13},{10,... | collective-permute-start | bytes 442376 | tf_op jit(solution)/shard_map/ppermute | solution.py:259
  31.0 10.5 %collective-permute-start.7 = (bf16[64,1152]{1,0:T(8,128)(2,1)S(1)}, bf16[64,1152]{1,0:T(8,128)(2,1)S(1)}, u32[]{:S(2)}, u32[]{:S(2)}) collective-permute-start(bf16[64,1152]{1,0:T(8,128)(2,1)S(1)} %get-tuple-element.33), channel_id=1, source_target_pairs={{0,2},{1,3},{2,0},{3,1},{4,6},{5,7},{6,4},{7,5},{8,10},{9,11},{10,... | collective-permute-start | bytes 442376 | tf_op jit(solution)/shard_map/ppermute | solution.py:259
  41.7 6.8 %collective-permute-start.13 = (bf16[64,1152]{1,0:T(8,128)(2,1)S(1)}, bf16[64,1152]{1,0:T(8,128)(2,1)S(1)}, u32[]{:S(2)}, u32[]{:S(2)}) collective-permute-start(bf16[64,1152]{1,0:T(8,128)(2,1)S(1)} %shard_map.87), channel_id=1, source_target_pairs={{0,8},{1,17},{2,10},{3,19},{4,12},{5,21},{6,14},{7,23},{8,0},{9,25... | collective-permute-start | bytes 442376 | tf_op jit(solution)/shard_map/ppermute | solution.py:270
  42.4 15.9 %collective-permute-start.16 = (bf16[256,1152]{1,0:T(8,128)(2,1)S(1)}, bf16[256,1152]{1,0:T(8,128)(2,1)S(1)}, u32[]{:S(2)}, u32[]{:S(2)}) collective-permute-start(bf16[256,1152]{1,0:T(8,128)(2,1)S(1)} %pad_maximum_fusion.1.refs_0_), channel_id=1, source_target_pairs={{0,16},{1,9},{2,18},{3,11},{4,20},{5,13},{6,22},{7,15},{8,24},{9,1... | collective-permute-start | bytes 1769480 | tf_op jit(solution)/shard_map/ppermute | solution.py:270
  43.3 7.7 %collective-permute-start.12 = (bf16[64,1152]{1,0:T(8,128)(2,1)S(1)}, bf16[64,1152]{1,0:T(8,128)(2,1)S(1)}, u32[]{:S(2)}, u32[]{:S(2)}) collective-permute-start(bf16[64,1152]{1,0:T(8,128)(2,1)S(1)} %shard_map.87), channel_id=1, source_target_pairs={{0,2},{1,3},{2,0},{3,1},{4,6},{5,7},{6,4},{7,5},{8,10},{9,11},{10,... | collective-permute-start | bytes 442376 | tf_op jit(solution)/shard_map/ppermute | solution.py:259
  43.3 13.8 %collective-permute-start.10 = (bf16[64,1152]{1,0:T(8,128)(2,1)S(1)}, bf16[64,1152]{1,0:T(8,128)(2,1)S(1)}, u32[]{:S(2)}, u32[]{:S(2)}) collective-permute-start(bf16[64,1152]{1,0:T(8,128)(2,1)S(1)} %shard_map.87), channel_id=1, source_target_pairs={{0,4},{1,5},{2,6},{3,7},{4,0},{5,1},{6,2},{7,3},{8,12},{9,13},{10,... | collective-permute-start | bytes 442376 | tf_op jit(solution)/shard_map/ppermute | solution.py:259
  46.7 10.4 %collective-permute-start.11 = (bf16[64,1152]{1,0:T(8,128)(2,1)S(1)}, bf16[64,1152]{1,0:T(8,128)(2,1)S(1)}, u32[]{:S(2)}, u32[]{:S(2)}) collective-permute-start(bf16[64,1152]{1,0:T(8,128)(2,1)S(1)} %shard_map.87), channel_id=1, source_target_pairs={{0,6},{1,7},{2,4},{3,5},{4,2},{5,3},{6,0},{7,1},{8,14},{9,15},{10,... | collective-permute-start | bytes 442376 | tf_op jit(solution)/shard_map/ppermute | solution.py:259
  48.6 10.4 %collective-permute-start.19 = (bf16[128,1152]{1,0:T(8,128)(2,1)S(1)}, bf16[128,1152]{1,0:T(8,128)(2,1)S(1)}, u32[]{:S(2)}, u32[]{:S(2)}) collective-permute-start(bf16[128,1152]{1,0:T(8,128)(2,1)S(1)} %pad_maximum_fusion.7), channel_id=1, source_target_pairs={{0,16},{1,9},{2,18},{3,11},{4,20},{5,13},{6,22},{7,15},{8,24},{9,1... | collective-permute-start | bytes 884744 | tf_op jit(solution)/shard_map/ppermute | solution.py:270
  50.9 8.2 %collective-permute-start.20 = (bf16[64,1152]{1,0:T(8,128)(2,1)S(1)}, bf16[64,1152]{1,0:T(8,128)(2,1)S(1)}, u32[]{:S(2)}, u32[]{:S(2)}) collective-permute-start(bf16[64,1152]{1,0:T(8,128)(2,1)S(1)} %collective-permute-done.12), channel_id=1, source_target_pairs={{0,8},{1,17},{2,10},{3,19},{4,12},{5,21},{6,14},{7,23},{8,0},{9,25... | collective-permute-start | bytes 442376 | tf_op jit(solution)/shard_map/ppermute | solution.py:270
  57.2 8.4 %collective-permute-start.22 = (bf16[128,1152]{1,0:T(8,128)(2,1)S(1)}, bf16[128,1152]{1,0:T(8,128)(2,1)S(1)}, u32[]{:S(2)}, u32[]{:S(2)}) collective-permute-start(bf16[128,1152]{1,0:T(8,128)(2,1)S(1)} %pad_maximum_fusion.6), channel_id=1, source_target_pairs={{0,8},{1,17},{2,10},{3,19},{4,12},{5,21},{6,14},{7,23},{8,0},{9,25... | collective-permute-start | bytes 884744 | tf_op jit(solution)/shard_map/ppermute | solution.py:270
  58.3 8.8 %collective-permute-start.18 = (bf16[512,1152]{1,0:T(8,128)(2,1)S(1)}, bf16[512,1152]{1,0:T(8,128)(2,1)S(1)}, u32[]{:S(2)}, u32[]{:S(2)}) collective-permute-start(bf16[512,1152]{1,0:T(8,128)(2,1)S(1)} %shard_map.90.refs_1_), channel_id=1, source_target_pairs={{0,1},{1,0},{2,3},{3,2},{4,5},{5,4},{6,7},{7,6},{8,9},{9,8},{10,11... | collective-permute-start | bytes 3538952 | tf_op jit(solution)/shard_map/ppermute | solution.py:262
  58.4 9.8 %collective-permute-start.17 = (bf16[512,1152]{1,0:T(8,128)(2,1)S(1)}, bf16[512,1152]{1,0:T(8,128)(2,1)S(1)}, u32[]{:S(2)}, u32[]{:S(2)}) collective-permute-start(bf16[512,1152]{1,0:T(8,128)(2,1)S(1)} %shard_map.89.refs_0_), channel_id=1, source_target_pairs={{0,1},{1,0},{2,3},{3,2},{4,5},{5,4},{6,7},{7,6},{8,9},{9,8},{10,11... | collective-permute-start | bytes 3538952 | tf_op jit(solution)/shard_map/ppermute | solution.py:262
  59.0 8.0 %collective-permute-start.23 = (bf16[256,1152]{1,0:T(8,128)(2,1)S(1)}, bf16[256,1152]{1,0:T(8,128)(2,1)S(1)}, u32[]{:S(2)}, u32[]{:S(2)}) collective-permute-start(bf16[256,1152]{1,0:T(8,128)(2,1)S(1)} %pad_maximum_fusion.2.refs_0_), channel_id=1, source_target_pairs={{0,1},{1,0},{2,3},{3,2},{4,5},{5,4},{6,7},{7,6},{8,9},{9,8},{10,11... | collective-permute-start | bytes 1769480 | tf_op jit(solution)/shard_map/ppermute | solution.py:262
  59.1 6.8 %collective-permute-start.21 = (bf16[128,1152]{1,0:T(8,128)(2,1)S(1)}, bf16[128,1152]{1,0:T(8,128)(2,1)S(1)}, u32[]{:S(2)}, u32[]{:S(2)}) collective-permute-start(bf16[128,1152]{1,0:T(8,128)(2,1)S(1)} %pad_maximum_fusion.9), channel_id=1, source_target_pairs={{0,16},{1,9},{2,18},{3,11},{4,20},{5,13},{6,22},{7,15},{8,24},{9,1... | collective-permute-start | bytes 884744 | tf_op jit(solution)/shard_map/ppermute | solution.py:270
  65.5 11.5 %collective-permute-start.14 = (f32[256,1152]{1,0:T(8,128)S(1)}, f32[256,1152]{1,0:T(8,128)S(1)}, u32[]{:S(2)}, u32[]{:S(2)}) collective-permute-start(f32[256,1152]{1,0:T(8,128)S(1)} %get-tuple-element.44), channel_id=1, source_target_pairs={{0,1},{1,0},{2,3},{3,2},{4,5},{5,4},{6,7},{7,6},{8,9},{9,8},{10,11... | collective-permute-start | bytes 3538952 | tf_op jit(solution)/shard_map/ppermute | solution.py:262
  66.0 3.5 %collective-permute-start.24 = (bf16[256,1152]{1,0:T(8,128)(2,1)S(1)}, bf16[256,1152]{1,0:T(8,128)(2,1)S(1)}, u32[]{:S(2)}, u32[]{:S(2)}) collective-permute-start(bf16[256,1152]{1,0:T(8,128)(2,1)S(1)} %pad_maximum_fusion.3.refs_1_), channel_id=1, source_target_pairs={{0,1},{1,0},{2,3},{3,2},{4,5},{5,4},{6,7},{7,6},{8,9},{9,8},{10,11... | collective-permute-start | bytes 1769480 | tf_op jit(solution)/shard_map/ppermute | solution.py:262
  67.0 3.0 %collective-permute-start.25 = (bf16[256,1152]{1,0:T(8,128)(2,1)S(1)}, bf16[256,1152]{1,0:T(8,128)(2,1)S(1)}, u32[]{:S(2)}, u32[]{:S(2)}) collective-permute-start(bf16[256,1152]{1,0:T(8,128)(2,1)S(1)} %pad_maximum_fusion.4.refs_2_), channel_id=1, source_target_pairs={{0,1},{1,0},{2,3},{3,2},{4,5},{5,4},{6,7},{7,6},{8,9},{9,8},{10,11... | collective-permute-start | bytes 1769480 | tf_op jit(solution)/shard_map/ppermute | solution.py:262
  67.1 9.9 %collective-permute-start.26 = (bf16[256,1152]{1,0:T(8,128)(2,1)S(1)}, bf16[256,1152]{1,0:T(8,128)(2,1)S(1)}, u32[]{:S(2)}, u32[]{:S(2)}) collective-permute-start(bf16[256,1152]{1,0:T(8,128)(2,1)S(1)} %pad_maximum_fusion.4.refs_2_), channel_id=1, source_target_pairs={{0,16},{1,9},{2,18},{3,11},{4,20},{5,13},{6,22},{7,15},{8,24},{9,1... | collective-permute-start | bytes 1769480 | tf_op jit(solution)/shard_map/ppermute | solution.py:270
  77.0 2.0 %collective-permute-start.27 = (bf16[256,1152]{1,0:T(8,128)(2,1)S(1)}, bf16[256,1152]{1,0:T(8,128)(2,1)S(1)}, u32[]{:S(2)}, u32[]{:S(2)}) collective-permute-start(bf16[256,1152]{1,0:T(8,128)(2,1)S(1)} %collective-permute-done.26.refs_0_), channel_id=1, source_target_pairs={{0,1},{1,0},{2,3},{3,2},{4,5},{5,4},{6,7},{7,6},{8,9},{9,8},{10,11... | collective-permute-start | bytes 1769480 | tf_op jit(solution)/shard_map/ppermute | solution.py:262

commit v16 on v15

--- a/solution.py
+++ b/solution.py
@@ -221,7 +221,7 @@
 
 def weight_sum(acc, x_t, gs, factor):
     depth, images = x_t.shape
-    n = 3
+    n = 3 if acc is None else 6
     early = acc is None
     vmem = pl.BlockSpec(memory_space=pltpu.VMEM)
     scratch = [pltpu.VMEM((images, depth), BF16)]

time: 82.3 us -> 82.1 us (level)
  no operation moved by 1% of the time
where the time goes in v16:
time: 82.1 us; the launch traced here: 81.9 us
  waiting for transfers between devices  32.3 us (39%)
  starting transfers between devices  30.2 us (37%)
  Pallas kernels  12.1 us (15%)
  matrix products  2.65 us (3%)
  between operations  2.13 us (3%)
  other arithmetic  1.49 us (2%)
  local copies, waits for them, and re-layouts  1.01 us (1%)
    ppermute x9, waiting for transfers between devices, along_z(): return lax.ppermute(v, 'blk', [(i, i ^ 2 * k) for i in range(nb)])  21.6 us
    ppermute x9, starting transfers between devices, along_z(): return lax.ppermute(v, 'blk', [(i, i ^ 2 * k) for i in range(nb)])  15 us
    ppermute x10, starting transfers between devices, step_d(): return lax.ppermute(v, ('dp', 'blk'), perm)  12.9 us
    ppermute x10, waiting for transfers between devices, step_d(): return lax.ppermute(v, ('dp', 'blk'), perm)  9.22 us
    pallas_call x2, Pallas kernels, weight_sum(): pl.pallas_call(kernel, out_shape=jax.ShapeDtypeStruct((depth, depth), F32...  7.62 us
    dot_general x2, matrix products, dot(): return lax.dot_general(a, b, dims, preferred_element_type=F32)  2.65 us
    ppermute x9, starting transfers between devices, swap(): return lax.ppermute(v, 'blk', [(i, i ^ 1) for i in range(nb)])  2.32 us
    pallas_call x1, Pallas kernels, scores(): pl.pallas_call(functools.partial(score_kernel, nz), out_shape=outs, in_sp...  2.3 us
  transfers between devices with their start and end apart: 28, of which 12 were waited for; matrix products, arithmetic and copies ran while one was open for 5% of the time, Pallas kernels for 11%

profile of v16, /device:TPU:0, one launch (start us, length us, event | category | flops | bytes accessed | tf_op | source)
XLA Modules:
  0.0 81.9 jit_solution(10706286056016303295)
XLA Ops:
  0.6 0.0 copy-start
  0.6 4.1 %collective-permute-start.1 = (bf16[64,1152]{1,0:T(8,128)(2,1)}, bf16[64,1152]{1,0:T(8,128)(2,1)S(1)}, u32[]{:S(2)}, u32[]{:S(2)}) collective-permute-start(bf16[64,1152]{1,0:T(8,128)(2,1)} %bitcast.9), channel_id=1, source_target_pairs={{0,4},{1,5},{2,6},{3,7},{4,0},{5,1},{6,2},{7,3},{8,12},{9,13},{10,... | collective-permute-start | bytes 442376 | tf_op jit(solution)/shard_map/ppermute | solution.py:259
  4.7 1.3 %collective-permute-start.2 = (bf16[64,1152]{1,0:T(8,128)(2,1)}, bf16[64,1152]{1,0:T(8,128)(2,1)S(1)}, u32[]{:S(2)}, u32[]{:S(2)}) collective-permute-start(bf16[64,1152]{1,0:T(8,128)(2,1)} %bitcast.10), channel_id=1, source_target_pairs={{0,6},{1,7},{2,4},{3,5},{4,2},{5,3},{6,0},{7,1},{8,14},{9,15},{10,... | collective-permute-start | bytes 442376 | tf_op jit(solution)/shard_map/ppermute | solution.py:259
  6.1 0.2 collective-permute-start
  6.3 0.5 collective-permute-start.3
  8.1 7.9 %collective-permute-done.1.refs_2_ = bf16[64,1152]{1,0:T(8,128)(2,1)S(1)} collective-permute-done((bf16[64,1152]{1,0:T(8,128)(2,1)}, bf16[64,1152]{1,0:T(8,128)(2,1)S(1)}, u32[]{:S(2)}, u32[]{:S(2)}) %collective-permute-start.1) | collective-permute-done | bytes 147488 | tf_op jit(solution)/shard_map/ppermute | solution.py:259
  16.0 0.0 collective-permute-done.2.refs_3_
  16.0 1.9 %collective-permute-start.8 = (bf16[128,1152]{1,0:T(8,128)(2,1)S(1)}, bf16[128,1152]{1,0:T(8,128)(2,1)S(1)}, u32[]{:S(2)}, u32[]{:S(2)}) collective-permute-start(bf16[128,1152]{1,0:T(8,128)(2,1)S(1)} %pad_maximum_fusion.5), channel_id=1, source_target_pairs={{0,8},{1,17},{2,10},{3,19},{4,12},{5,21},{6,14},{7,23},{8,0},{9,25... | collective-permute-start | bytes 884744 | tf_op jit(solution)/shard_map/ppermute | solution.py:270
  17.9 0.0 collective-permute-done.refs_1_
  17.9 0.9 %copy-done.1 = bf16[1,64,1152]{2,1,0:T(8,128)(2,1)S(1)} copy-done((bf16[1,64,1152]{2,1,0:T(8,128)(2,1)S(1)}, bf16[1,64,1152]{2,1,0:T(8,128)(2,1)}, u32[]{:S(2)}) %copy-start.1) | copy-done | bytes 147480
  18.9 0.0 copy-start.3
  18.9 0.0 copy-start.4
  18.9 1.0 %fusion.embed = f32[256,1152]{1,0:T(8,128)S(1)} fusion(bf16[256,1152]{1,0:T(8,128)(2,1)S(1)} %shard_map.85, bf16[1152,1152]{1,0:T(8,128)(2,1)S(1)} %copy-done), kind=kOutput, calls=%fused_computation.12 | convolution fusion | flops 679477248 | bytes 4423680 | tf_op jit(solution)/shard_map/dot_general | solution.py:17
  19.9 0.0 collective-permute-done.3.refs_1_
  20.0 0.1 iota.7.both
  20.0 2.3 %shard_map.86 = (f32[64,1152]{1,0:T(8,128)S(1)}, f32[64,1152]{1,0:T(8,128)S(1)}, f32[64,128]{1,0:T(8,128)S(1)}, bf16[256,1152]{1,0:T(8,128)(2,1)S(1)}, bf16[256,...) custom-call(f32[16,128]{1,0:T(8,128)S(1)} %iota.7.both, ...), custom_call_target="tpu_custom_call" | custom-call | flops 603979776 | bytes 4718592 | tf_op jit(solution)/shard_map/pallas_call | solution.py:74
  22.3 0.0 copy-start.2
  22.4 0.5 collective-permute-done.8
  22.9 2.1 %collective-permute-start.9 = (bf16[256,1152]{1,0:T(8,128)(2,1)S(1)}, bf16[256,1152]{1,0:T(8,128)(2,1)S(1)}, u32[]{:S(2)}, u32[]{:S(2)}) collective-permute-start(bf16[256,1152]{1,0:T(8,128)(2,1)S(1)} %pad_maximum_fusion.refs_0_), channel_id=1, source_target_pairs={{0,16},{1,9},{2,18},{3,11},{4,20},{5,13},{6,22},{7,15},{8,24},{9,1... | collective-permute-start | bytes 1769480 | tf_op jit(solution)/shard_map/ppermute | solution.py:270
  25.0 1.6 %collective-permute-start.15 = (bf16[128,1152]{1,0:T(8,128)(2,1)S(1)}, bf16[128,1152]{1,0:T(8,128)(2,1)S(1)}, u32[]{:S(2)}, u32[]{:S(2)}) collective-permute-start(bf16[128,1152]{1,0:T(8,128)(2,1)S(1)} %pad_maximum_fusion.8), channel_id=1, source_target_pairs={{0,8},{1,17},{2,10},{3,19},{4,12},{5,21},{6,14},{7,23},{8,0},{9,25... | collective-permute-start | bytes 884744 | tf_op jit(solution)/shard_map/ppermute | solution.py:270
  26.6 2.2 %collective-permute-start.5 = (bf16[64,1152]{1,0:T(8,128)(2,1)S(1)}, bf16[64,1152]{1,0:T(8,128)(2,1)S(1)}, u32[]{:S(2)}, u32[]{:S(2)}) collective-permute-start(bf16[64,1152]{1,0:T(8,128)(2,1)S(1)} %get-tuple-element.31), channel_id=1, source_target_pairs={{0,6},{1,7},{2,4},{3,5},{4,2},{5,3},{6,0},{7,1},{8,14},{9,15},{10,... | collective-permute-start | bytes 442376 | tf_op jit(solution)/shard_map/ppermute | solution.py:259
  28.8 2.2 %collective-permute-start.6 = (bf16[64,1152]{1,0:T(8,128)(2,1)S(1)}, bf16[64,1152]{1,0:T(8,128)(2,1)S(1)}, u32[]{:S(2)}, u32[]{:S(2)}) collective-permute-start(bf16[64,1152]{1,0:T(8,128)(2,1)S(1)} %get-tuple-element.32), channel_id=1, source_target_pairs={{0,4},{1,5},{2,6},{3,7},{4,0},{5,1},{6,2},{7,3},{8,12},{9,13},{10,... | collective-permute-start | bytes 442376 | tf_op jit(solution)/shard_map/ppermute | solution.py:259
  31.0 0.6 collective-permute-start.7
  31.6 1.0 %collective-permute-done.15 = bf16[128,1152]{1,0:T(8,128)(2,1)S(1)} collective-permute-done((bf16[128,1152]{1,0:T(8,128)(2,1)S(1)}, bf16[128,1152]{1,0:T(8,128)(2,1)S(1)}, u32[]{:S(2)}, u32[]{:S(2)}) %collective-permute-start.15) | collective-permute-done | bytes 294944 | tf_op jit(solution)/shard_map/ppermute | solution.py:270
  32.6 1.8 %collective-permute-done.5.refs_0_ = bf16[64,1152]{1,0:T(8,128)(2,1)S(1)} collective-permute-done((bf16[64,1152]{1,0:T(8,128)(2,1)S(1)}, bf16[64,1152]{1,0:T(8,128)(2,1)S(1)}, u32[]{:S(2)}, u32[]{:S(2)}) %collective-permute-start.5) | collective-permute-done | bytes 147488 | tf_op jit(solution)/shard_map/ppermute | solution.py:259
  34.4 7.1 %collective-permute-done.6.refs_1_ = bf16[64,1152]{1,0:T(8,128)(2,1)S(1)} collective-permute-done((bf16[64,1152]{1,0:T(8,128)(2,1)S(1)}, bf16[64,1152]{1,0:T(8,128)(2,1)S(1)}, u32[]{:S(2)}, u32[]{:S(2)}) %collective-permute-start.6) | collective-permute-done | bytes 147488 | tf_op jit(solution)/shard_map/ppermute | solution.py:259
  41.5 0.0 collective-permute-done.7.refs_2_
  41.5 0.0 collective-permute-done.9.refs_1_
  41.5 0.2 shard_map.87
  41.7 0.6 collective-permute-start.13
  42.4 0.9 %collective-permute-start.16 = (bf16[256,1152]{1,0:T(8,128)(2,1)S(1)}, bf16[256,1152]{1,0:T(8,128)(2,1)S(1)}, u32[]{:S(2)}, u32[]{:S(2)}) collective-permute-start(bf16[256,1152]{1,0:T(8,128)(2,1)S(1)} %pad_maximum_fusion.1.refs_0_), channel_id=1, source_target_pairs={{0,16},{1,9},{2,18},{3,11},{4,20},{5,13},{6,22},{7,15},{8,24},{9,1... | collective-permute-start | bytes 1769480 | tf_op jit(solution)/shard_map/ppermute | solution.py:270
  43.3 0.0 collective-permute-start.12
  43.3 3.4 %collective-permute-start.10 = (bf16[64,1152]{1,0:T(8,128)(2,1)S(1)}, bf16[64,1152]{1,0:T(8,128)(2,1)S(1)}, u32[]{:S(2)}, u32[]{:S(2)}) collective-permute-start(bf16[64,1152]{1,0:T(8,128)(2,1)S(1)} %shard_map.87), channel_id=1, source_target_pairs={{0,4},{1,5},{2,6},{3,7},{4,0},{5,1},{6,2},{7,3},{8,12},{9,13},{10,... | collective-permute-start | bytes 442376 | tf_op jit(solution)/shard_map/ppermute | solution.py:259
  46.7 1.0 %collective-permute-start.11 = (bf16[64,1152]{1,0:T(8,128)(2,1)S(1)}, bf16[64,1152]{1,0:T(8,128)(2,1)S(1)}, u32[]{:S(2)}, u32[]{:S(2)}) collective-permute-start(bf16[64,1152]{1,0:T(8,128)(2,1)S(1)} %shard_map.87), channel_id=1, source_target_pairs={{0,6},{1,7},{2,4},{3,5},{4,2},{5,3},{6,0},{7,1},{8,14},{9,15},{10,... | collective-permute-start | bytes 442376 | tf_op jit(solution)/shard_map/ppermute | solution.py:259
  47.6 0.9 %collective-permute-done.13 = bf16[64,1152]{1,0:T(8,128)(2,1)S(1)} collective-permute-done((bf16[64,1152]{1,0:T(8,128)(2,1)S(1)}, bf16[64,1152]{1,0:T(8,128)(2,1)S(1)}, u32[]{:S(2)}, u32[]{:S(2)}) %collective-permute-start.13) | collective-permute-done | bytes 147488 | tf_op jit(solution)/shard_map/ppermute | solution.py:270
  48.6 0.6 collective-permute-start.19
  49.2 1.7 %fusion.1 = f32[64,1152]{1,0:T(8,128)} fusion(bf16[64,1152]{1,0:T(8,128)(2,1)S(1)} %shard_map.87, bf16[1152,1152]{1,0:T(8,128)(2,1)S(1)} %copy-done), kind=kOutput, calls=%fused_computation.13 | convolution fusion | flops 169869312 | bytes 3096576 | tf_op jit(solution)/shard_map/dot_general | solution.py:17
  50.8 0.1 shard_map.90.refs_1_
  50.9 0.0 collective-permute-done.12
  50.9 1.3 %collective-permute-start.20 = (bf16[64,1152]{1,0:T(8,128)(2,1)S(1)}, bf16[64,1152]{1,0:T(8,128)(2,1)S(1)}, u32[]{:S(2)}, u32[]{:S(2)}) collective-permute-start(bf16[64,1152]{1,0:T(8,128)(2,1)S(1)} %collective-permute-done.12), channel_id=1, source_target_pairs={{0,8},{1,17},{2,10},{3,19},{4,12},{5,21},{6,14},{7,23},{8,0},{9,25... | collective-permute-start | bytes 442376 | tf_op jit(solution)/shard_map/ppermute | solution.py:270
  52.3 4.9 %collective-permute-done.10 = bf16[64,1152]{1,0:T(8,128)(2,1)S(1)} collective-permute-done((bf16[64,1152]{1,0:T(8,128)(2,1)S(1)}, bf16[64,1152]{1,0:T(8,128)(2,1)S(1)}, u32[]{:S(2)}, u32[]{:S(2)}) %collective-permute-start.10) | collective-permute-done | bytes 147488 | tf_op jit(solution)/shard_map/ppermute | solution.py:259
  57.1 0.0 collective-permute-done.11
  57.2 1.2 %collective-permute-start.22 = (bf16[128,1152]{1,0:T(8,128)(2,1)S(1)}, bf16[128,1152]{1,0:T(8,128)(2,1)S(1)}, u32[]{:S(2)}, u32[]{:S(2)}) collective-permute-start(bf16[128,1152]{1,0:T(8,128)(2,1)S(1)} %pad_maximum_fusion.6), channel_id=1, source_target_pairs={{0,8},{1,17},{2,10},{3,19},{4,12},{5,21},{6,14},{7,23},{8,0},{9,25... | collective-permute-start | bytes 884744 | tf_op jit(solution)/shard_map/ppermute | solution.py:270
  58.3 0.0 collective-permute-done.16.refs_1_
  58.3 0.1 shard_map.89.refs_0_
  58.4 0.6 collective-permute-start.17
  59.0 0.0 collective-permute-done.19
  59.0 0.1 collective-permute-start.23
  59.1 1.6 %collective-permute-start.21 = (bf16[128,1152]{1,0:T(8,128)(2,1)S(1)}, bf16[128,1152]{1,0:T(8,128)(2,1)S(1)}, u32[]{:S(2)}, u32[]{:S(2)}) collective-permute-start(bf16[128,1152]{1,0:T(8,128)(2,1)S(1)} %pad_maximum_fusion.9), channel_id=1, source_target_pairs={{0,16},{1,9},{2,18},{3,11},{4,20},{5,13},{6,22},{7,15},{8,24},{9,1... | collective-permute-start | bytes 884744 | tf_op jit(solution)/shard_map/ppermute | solution.py:270
  60.7 0.5 shard_map.88
  61.3 4.2 %collective-permute-done.22 = bf16[128,1152]{1,0:T(8,128)(2,1)S(1)} collective-permute-done((bf16[128,1152]{1,0:T(8,128)(2,1)S(1)}, bf16[128,1152]{1,0:T(8,128)(2,1)S(1)}, u32[]{:S(2)}, u32[]{:S(2)}) %collective-permute-start.22) | collective-permute-done | bytes 294944 | tf_op jit(solution)/shard_map/ppermute | solution.py:270
  65.5 0.0 collective-permute-start.14
  65.6 0.4 collective-permute-done.21
  66.0 1.0 %collective-permute-start.24 = (bf16[256,1152]{1,0:T(8,128)(2,1)S(1)}, bf16[256,1152]{1,0:T(8,128)(2,1)S(1)}, u32[]{:S(2)}, u32[]{:S(2)}) collective-permute-start(bf16[256,1152]{1,0:T(8,128)(2,1)S(1)} %pad_maximum_fusion.3.refs_1_), channel_id=1, source_target_pairs={{0,1},{1,0},{2,3},{3,2},{4,5},{5,4},{6,7},{7,6},{8,9},{9,8},{10,11... | collective-permute-start | bytes 1769480 | tf_op jit(solution)/shard_map/ppermute | solution.py:262
  67.0 0.1 collective-permute-start.25
  67.1 0.0 collective-permute-done.18.refs_3_
  67.1 1.1 %collective-permute-start.26 = (bf16[256,1152]{1,0:T(8,128)(2,1)S(1)}, bf16[256,1152]{1,0:T(8,128)(2,1)S(1)}, u32[]{:S(2)}, u32[]{:S(2)}) collective-permute-start(bf16[256,1152]{1,0:T(8,128)(2,1)S(1)} %pad_maximum_fusion.4.refs_2_), channel_id=1, source_target_pairs={{0,16},{1,9},{2,18},{3,11},{4,20},{5,13},{6,22},{7,15},{8,24},{9,1... | collective-permute-start | bytes 1769480 | tf_op jit(solution)/shard_map/ppermute | solution.py:270
  68.2 1.3 %shard_map.91 = (bf16[1152,1536]{1,0:T(8,128)(2,1)S(1)}, bf16[1152,512]{1,0:T(8,128)(2,1)S(1)}) custom-call(bf16[512,1152]{1,0:T(8,128)(2,1)S(1)} %shard_map.89.refs_0_, bf16[512,1152]{1,0:T(8,128)(2,1)S(1)} %shard_map.90.refs_1_, bf16[512,1152]{1,0:T(8,128)(2,1)S(1)} %collective-permute-done.17.refs_2_, bf16[512,1152]{1,0:T(8,128)(2,1)S(1)} %collective-permute-done.18.refs_3_), custom_call_target="tpu_custom_call" | custom-call | bytes 9437184 | tf_op jit(solution)/shard_map/pallas_call | solution.py:180
  69.5 0.5 collective-permute-done.25.refs_5_
  70.1 4.8 %shard_map.92.acc = f32[1152,1152]{1,0:T(8,128)S(1)} custom-call(bf16[1152,1536]{1,0:T(8,128)(2,1)S(1)} %get-tuple-element.49.x_t, bf16[256,1152]{1,0:T(8,128)(2,1)S(1)} %pad_maximum_fusion.2.refs_0_, bf16[256,1152]{1,0:T(8,128)(2,1)S(1)} %pad_maximum_fusion.3.refs_1_, bf16[256,1152]{1,0:T(8,128)(2,1)S(1)} %pad_maximum_fusion.4.refs_2_, ...), custom_call_target="tpu_custom_call" | custom-call | flops 4076863488 | bytes 12386304 | tf_op jit(solution)/shard_map/pallas_call | solution.py:235
  74.8 2.2 %collective-permute-done.26.refs_0_ = bf16[256,1152]{1,0:T(8,128)(2,1)S(1)} collective-permute-done((bf16[256,1152]{1,0:T(8,128)(2,1)S(1)}, bf16[256,1152]{1,0:T(8,128)(2,1)S(1)}, u32[]{:S(2)}, u32[]{:S(2)}) %collective-permute-start.26) | collective-permute-done | bytes 589856 | tf_op jit(solution)/shard_map/ppermute | solution.py:270
  77.0 1.1 %add_bitcast_fusion = f32[1,256,1152]{2,1,0:T(8,128)} fusion(f32[256,1152]{1,0:T(8,128)S(1)} %get-tuple-element.43, f32[256,1152]{1,0:T(8,128)S(1)} %collective-permute-done.14), kind=kLoop, calls=%fused_computation | loop fusion | flops 294912 | bytes 3538944 | tf_op jit(solution)/shard_map/broadcast_in_dim | solution.py:362
  78.2 0.9 %collective-permute-done.27.refs_1_ = bf16[256,1152]{1,0:T(8,128)(2,1)S(1)} collective-permute-done((bf16[256,1152]{1,0:T(8,128)(2,1)S(1)}, bf16[256,1152]{1,0:T(8,128)(2,1)S(1)}, u32[]{:S(2)}, u32[]{:S(2)}) %collective-permute-start.27) | collective-permute-done | bytes 589856 | tf_op jit(solution)/shard_map/ppermute | solution.py:262
  79.0 2.9 %shard_map.93 = f32[1152,1152]{1,0:T(8,128)} custom-call(bf16[1152,512]{1,0:T(8,128)(2,1)S(1)} %get-tuple-element.48.x_t, f32[1152,1152]{1,0:T(8,128)S(1)} %shard_map.92.acc, bf16[256,1152]{1,0:T(8,128)(2,1)S(1)} %collective-permute-done.26.refs_0_, bf16[256,1152]{1,0:T(8,128)(2,1)S(1)} %collective-permute-done.27.refs_1_), custom_call_target="tpu_custom_call" | custom-call | flops 1358954496 | bytes 12976128 | tf_op jit(solution)/shard_map/pallas_call | solution.py:235
  (26 shorter events, 0.4 us)
Async XLA Ops:
  0.6 18.3 %copy-start = (bf16[1152,1152]{1,0:T(8,128)(2,1)S(1)}, bf16[1152,1152]{1,0:T(8,128)(2,1)}, u32[]{:S(2)}) copy-start(bf16[1152,1152]{1,0:T(8,128)(2,1)} %param.9) | copy-start | bytes 7962628
  0.6 15.4 %collective-permute-start.1 = (bf16[64,1152]{1,0:T(8,128)(2,1)}, bf16[64,1152]{1,0:T(8,128)(2,1)S(1)}, u32[]{:S(2)}, u32[]{:S(2)}) collective-permute-start(bf16[64,1152]{1,0:T(8,128)(2,1)} %bitcast.9), channel_id=1, source_target_pairs={{0,4},{1,5},{2,6},{3,7},{4,0},{5,1},{6,2},{7,3},{8,12},{9,13},{10,... | collective-permute-start | bytes 442376 | tf_op jit(solution)/shard_map/ppermute | solution.py:259
  4.7 11.3 %collective-permute-start.2 = (bf16[64,1152]{1,0:T(8,128)(2,1)}, bf16[64,1152]{1,0:T(8,128)(2,1)S(1)}, u32[]{:S(2)}, u32[]{:S(2)}) collective-permute-start(bf16[64,1152]{1,0:T(8,128)(2,1)} %bitcast.10), channel_id=1, source_target_pairs={{0,6},{1,7},{2,4},{3,5},{4,2},{5,3},{6,0},{7,1},{8,14},{9,15},{10,... | collective-permute-start | bytes 442376 | tf_op jit(solution)/shard_map/ppermute | solution.py:259
  6.1 11.8 %collective-permute-start = (bf16[64,1152]{1,0:T(8,128)(2,1)}, bf16[64,1152]{1,0:T(8,128)(2,1)S(1)}, u32[]{:S(2)}, u32[]{:S(2)}) collective-permute-start(bf16[64,1152]{1,0:T(8,128)(2,1)} %bitcast.11), channel_id=1, source_target_pairs={{0,2},{1,3},{2,0},{3,1},{4,6},{5,7},{6,4},{7,5},{8,10},{9,11},{10,... | collective-permute-start | bytes 442376 | tf_op jit(solution)/shard_map/ppermute | solution.py:259
  6.3 13.6 %collective-permute-start.4 = (bf16[256,1152]{1,0:T(8,128)(2,1)}, bf16[256,1152]{1,0:T(8,128)(2,1)}, u32[]{:S(2)}, u32[]{:S(2)}) collective-permute-start(bf16[256,1152]{1,0:T(8,128)(2,1)} %bitcast.15), channel_id=1, source_target_pairs={{0,1},{1,0},{2,3},{3,2},{4,5},{5,4},{6,7},{7,6},{8,9},{9,8},{10,11... | collective-permute-start | bytes 1769480 | tf_op jit(solution)/shard_map/ppermute | solution.py:262
  6.3 13.6 %collective-permute-start.3 = (s32[1,256]{1,0:T(1,128)}, s32[1,256]{1,0:T(1,128)S(1)}, u32[]{:S(2)}, u32[]{:S(2)}) collective-permute-start(s32[1,256]{1,0:T(1,128)} %refs_0_.1), channel_id=1, source_target_pairs={{0,1},{1,0},{2,3},{3,2},{4,5},{5,4},{6,7},{7,6},{8,9},{9,8},{10,11... | collective-permute-start | bytes 3080 | tf_op jit(solution)/shard_map/ppermute | solution.py:262
  16.0 6.8 %collective-permute-start.8 = (bf16[128,1152]{1,0:T(8,128)(2,1)S(1)}, bf16[128,1152]{1,0:T(8,128)(2,1)S(1)}, u32[]{:S(2)}, u32[]{:S(2)}) collective-permute-start(bf16[128,1152]{1,0:T(8,128)(2,1)S(1)} %pad_maximum_fusion.5), channel_id=1, source_target_pairs={{0,8},{1,17},{2,10},{3,19},{4,12},{5,21},{6,14},{7,23},{8,0},{9,25... | collective-permute-start | bytes 884744 | tf_op jit(solution)/shard_map/ppermute | solution.py:270
  17.9 0.9 %copy-start.1 = (bf16[1,64,1152]{2,1,0:T(8,128)(2,1)S(1)}, bf16[1,64,1152]{2,1,0:T(8,128)(2,1)}, u32[]{:S(2)}) copy-start(bf16[1,64,1152]{2,1,0:T(8,128)(2,1)} %param.6) | copy-start | bytes 442372
  18.9 1.1 %copy-start.3 = (bf16[1,256,1152]{2,1,0:T(8,128)(2,1)S(1)}, bf16[1,256,1152]{2,1,0:T(8,128)(2,1)}, u32[]{:S(2)}) copy-start(bf16[1,256,1152]{2,1,0:T(8,128)(2,1)} %param.7) | copy-start | bytes 1769476
  18.9 1.1 %copy-start.4 = (s32[1,256]{1,0:T(1,128)S(1)}, s32[1,256]{1,0:T(1,128)}, u32[]{:S(2)}) copy-start(s32[1,256]{1,0:T(1,128)} %refs_0_.1) | copy-start | bytes 3076
  22.3 2.7 %copy-start.2 = (bf16[1,64,1152]{2,1,0:T(8,128)(2,1)S(1)}, bf16[1,64,1152]{2,1,0:T(8,128)(2,1)}, u32[]{:S(2)}) copy-start(bf16[1,64,1152]{2,1,0:T(8,128)(2,1)} %param.6) | copy-start | bytes 442372
  22.9 18.7 %collective-permute-start.9 = (bf16[256,1152]{1,0:T(8,128)(2,1)S(1)}, bf16[256,1152]{1,0:T(8,128)(2,1)S(1)}, u32[]{:S(2)}, u32[]{:S(2)}) collective-permute-start(bf16[256,1152]{1,0:T(8,128)(2,1)S(1)} %pad_maximum_fusion.refs_0_), channel_id=1, source_target_pairs={{0,16},{1,9},{2,18},{3,11},{4,20},{5,13},{6,22},{7,15},{8,24},{9,1... | collective-permute-start | bytes 1769480 | tf_op jit(solution)/shard_map/ppermute | solution.py:270
  25.0 7.6 %collective-permute-start.15 = (bf16[128,1152]{1,0:T(8,128)(2,1)S(1)}, bf16[128,1152]{1,0:T(8,128)(2,1)S(1)}, u32[]{:S(2)}, u32[]{:S(2)}) collective-permute-start(bf16[128,1152]{1,0:T(8,128)(2,1)S(1)} %pad_maximum_fusion.8), channel_id=1, source_target_pairs={{0,8},{1,17},{2,10},{3,19},{4,12},{5,21},{6,14},{7,23},{8,0},{9,25... | collective-permute-start | bytes 884744 | tf_op jit(solution)/shard_map/ppermute | solution.py:270
  26.6 7.8 %collective-permute-start.5 = (bf16[64,1152]{1,0:T(8,128)(2,1)S(1)}, bf16[64,1152]{1,0:T(8,128)(2,1)S(1)}, u32[]{:S(2)}, u32[]{:S(2)}) collective-permute-start(bf16[64,1152]{1,0:T(8,128)(2,1)S(1)} %get-tuple-element.31), channel_id=1, source_target_pairs={{0,6},{1,7},{2,4},{3,5},{4,2},{5,3},{6,0},{7,1},{8,14},{9,15},{10,... | collective-permute-start | bytes 442376 | tf_op jit(solution)/shard_map/ppermute | solution.py:259
  28.8 12.7 %collective-permute-start.6 = (bf16[64,1152]{1,0:T(8,128)(2,1)S(1)}, bf16[64,1152]{1,0:T(8,128)(2,1)S(1)}, u32[]{:S(2)}, u32[]{:S(2)}) collective-permute-start(bf16[64,1152]{1,0:T(8,128)(2,1)S(1)} %get-tuple-element.32), channel_id=1, source_target_pairs={{0,4},{1,5},{2,6},{3,7},{4,0},{5,1},{6,2},{7,3},{8,12},{9,13},{10,... | collective-permute-start | bytes 442376 | tf_op jit(solution)/shard_map/ppermute | solution.py:259
  31.0 10.5 %collective-permute-start.7 = (bf16[64,1152]{1,0:T(8,128)(2,1)S(1)}, bf16[64,1152]{1,0:T(8,128)(2,1)S(1)}, u32[]{:S(2)}, u32[]{:S(2)}) collective-permute-start(bf16[64,1152]{1,0:T(8,128)(2,1)S(1)} %get-tuple-element.33), channel_id=1, source_target_pairs={{0,2},{1,3},{2,0},{3,1},{4,6},{5,7},{6,4},{7,5},{8,10},{9,11},{10,... | collective-permute-start | bytes 442376 | tf_op jit(solution)/shard_map/ppermute | solution.py:259
  41.7 6.8 %collective-permute-start.13 = (bf16[64,1152]{1,0:T(8,128)(2,1)S(1)}, bf16[64,1152]{1,0:T(8,128)(2,1)S(1)}, u32[]{:S(2)}, u32[]{:S(2)}) collective-permute-start(bf16[64,1152]{1,0:T(8,128)(2,1)S(1)} %shard_map.87), channel_id=1, source_target_pairs={{0,8},{1,17},{2,10},{3,19},{4,12},{5,21},{6,14},{7,23},{8,0},{9,25... | collective-permute-start | bytes 442376 | tf_op jit(solution)/shard_map/ppermute | solution.py:270
  42.4 15.9 %collective-permute-start.16 = (bf16[256,1152]{1,0:T(8,128)(2,1)S(1)}, bf16[256,1152]{1,0:T(8,128)(2,1)S(1)}, u32[]{:S(2)}, u32[]{:S(2)}) collective-permute-start(bf16[256,1152]{1,0:T(8,128)(2,1)S(1)} %pad_maximum_fusion.1.refs_0_), channel_id=1, source_target_pairs={{0,16},{1,9},{2,18},{3,11},{4,20},{5,13},{6,22},{7,15},{8,24},{9,1... | collective-permute-start | bytes 1769480 | tf_op jit(solution)/shard_map/ppermute | solution.py:270
  43.3 7.7 %collective-permute-start.12 = (bf16[64,1152]{1,0:T(8,128)(2,1)S(1)}, bf16[64,1152]{1,0:T(8,128)(2,1)S(1)}, u32[]{:S(2)}, u32[]{:S(2)}) collective-permute-start(bf16[64,1152]{1,0:T(8,128)(2,1)S(1)} %shard_map.87), channel_id=1, source_target_pairs={{0,2},{1,3},{2,0},{3,1},{4,6},{5,7},{6,4},{7,5},{8,10},{9,11},{10,... | collective-permute-start | bytes 442376 | tf_op jit(solution)/shard_map/ppermute | solution.py:259
  43.3 13.8 %collective-permute-start.10 = (bf16[64,1152]{1,0:T(8,128)(2,1)S(1)}, bf16[64,1152]{1,0:T(8,128)(2,1)S(1)}, u32[]{:S(2)}, u32[]{:S(2)}) collective-permute-start(bf16[64,1152]{1,0:T(8,128)(2,1)S(1)} %shard_map.87), channel_id=1, source_target_pairs={{0,4},{1,5},{2,6},{3,7},{4,0},{5,1},{6,2},{7,3},{8,12},{9,13},{10,... | collective-permute-start | bytes 442376 | tf_op jit(solution)/shard_map/ppermute | solution.py:259
  46.7 10.4 %collective-permute-start.11 = (bf16[64,1152]{1,0:T(8,128)(2,1)S(1)}, bf16[64,1152]{1,0:T(8,128)(2,1)S(1)}, u32[]{:S(2)}, u32[]{:S(2)}) collective-permute-start(bf16[64,1152]{1,0:T(8,128)(2,1)S(1)} %shard_map.87), channel_id=1, source_target_pairs={{0,6},{1,7},{2,4},{3,5},{4,2},{5,3},{6,0},{7,1},{8,14},{9,15},{10,... | collective-permute-start | bytes 442376 | tf_op jit(solution)/shard_map/ppermute | solution.py:259
  48.6 10.4 %collective-permute-start.19 = (bf16[128,1152]{1,0:T(8,128)(2,1)S(1)}, bf16[128,1152]{1,0:T(8,128)(2,1)S(1)}, u32[]{:S(2)}, u32[]{:S(2)}) collective-permute-start(bf16[128,1152]{1,0:T(8,128)(2,1)S(1)} %pad_maximum_fusion.7), channel_id=1, source_target_pairs={{0,16},{1,9},{2,18},{3,11},{4,20},{5,13},{6,22},{7,15},{8,24},{9,1... | collective-permute-start | bytes 884744 | tf_op jit(solution)/shard_map/ppermute | solution.py:270
  50.9 8.2 %collective-permute-start.20 = (bf16[64,1152]{1,0:T(8,128)(2,1)S(1)}, bf16[64,1152]{1,0:T(8,128)(2,1)S(1)}, u32[]{:S(2)}, u32[]{:S(2)}) collective-permute-start(bf16[64,1152]{1,0:T(8,128)(2,1)S(1)} %collective-permute-done.12), channel_id=1, source_target_pairs={{0,8},{1,17},{2,10},{3,19},{4,12},{5,21},{6,14},{7,23},{8,0},{9,25... | collective-permute-start | bytes 442376 | tf_op jit(solution)/shard_map/ppermute | solution.py:270
  57.2 8.4 %collective-permute-start.22 = (bf16[128,1152]{1,0:T(8,128)(2,1)S(1)}, bf16[128,1152]{1,0:T(8,128)(2,1)S(1)}, u32[]{:S(2)}, u32[]{:S(2)}) collective-permute-start(bf16[128,1152]{1,0:T(8,128)(2,1)S(1)} %pad_maximum_fusion.6), channel_id=1, source_target_pairs={{0,8},{1,17},{2,10},{3,19},{4,12},{5,21},{6,14},{7,23},{8,0},{9,25... | collective-permute-start | bytes 884744 | tf_op jit(solution)/shard_map/ppermute | solution.py:270
  58.3 8.8 %collective-permute-start.18 = (bf16[512,1152]{1,0:T(8,128)(2,1)S(1)}, bf16[512,1152]{1,0:T(8,128)(2,1)S(1)}, u32[]{:S(2)}, u32[]{:S(2)}) collective-permute-start(bf16[512,1152]{1,0:T(8,128)(2,1)S(1)} %shard_map.90.refs_1_), channel_id=1, source_target_pairs={{0,1},{1,0},{2,3},{3,2},{4,5},{5,4},{6,7},{7,6},{8,9},{9,8},{10,11... | collective-permute-start | bytes 3538952 | tf_op jit(solution)/shard_map/ppermute | solution.py:262
  58.4 9.8 %collective-permute-start.17 = (bf16[512,1152]{1,0:T(8,128)(2,1)S(1)}, bf16[512,1152]{1,0:T(8,128)(2,1)S(1)}, u32[]{:S(2)}, u32[]{:S(2)}) collective-permute-start(bf16[512,1152]{1,0:T(8,128)(2,1)S(1)} %shard_map.89.refs_0_), channel_id=1, source_target_pairs={{0,1},{1,0},{2,3},{3,2},{4,5},{5,4},{6,7},{7,6},{8,9},{9,8},{10,11... | collective-permute-start | bytes 3538952 | tf_op jit(solution)/shard_map/ppermute | solution.py:262
  59.0 8.0 %collective-permute-start.23 = (bf16[256,1152]{1,0:T(8,128)(2,1)S(1)}, bf16[256,1152]{1,0:T(8,128)(2,1)S(1)}, u32[]{:S(2)}, u32[]{:S(2)}) collective-permute-start(bf16[256,1152]{1,0:T(8,128)(2,1)S(1)} %pad_maximum_fusion.2.refs_0_), channel_id=1, source_target_pairs={{0,1},{1,0},{2,3},{3,2},{4,5},{5,4},{6,7},{7,6},{8,9},{9,8},{10,11... | collective-permute-start | bytes 1769480 | tf_op jit(solution)/shard_map/ppermute | solution.py:262
  59.1 6.8 %collective-permute-start.21 = (bf16[128,1152]{1,0:T(8,128)(2,1)S(1)}, bf16[128,1152]{1,0:T(8,128)(2,1)S(1)}, u32[]{:S(2)}, u32[]{:S(2)}) collective-permute-start(bf16[128,1152]{1,0:T(8,128)(2,1)S(1)} %pad_maximum_fusion.9), channel_id=1, source_target_pairs={{0,16},{1,9},{2,18},{3,11},{4,20},{5,13},{6,22},{7,15},{8,24},{9,1... | collective-permute-start | bytes 884744 | tf_op jit(solution)/shard_map/ppermute | solution.py:270
  65.5 11.5 %collective-permute-start.14 = (f32[256,1152]{1,0:T(8,128)S(1)}, f32[256,1152]{1,0:T(8,128)S(1)}, u32[]{:S(2)}, u32[]{:S(2)}) collective-permute-start(f32[256,1152]{1,0:T(8,128)S(1)} %get-tuple-element.44), channel_id=1, source_target_pairs={{0,1},{1,0},{2,3},{3,2},{4,5},{5,4},{6,7},{7,6},{8,9},{9,8},{10,11... | collective-permute-start | bytes 3538952 | tf_op jit(solution)/shard_map/ppermute | solution.py:262
  66.0 3.5 %collective-permute-start.24 = (bf16[256,1152]{1,0:T(8,128)(2,1)S(1)}, bf16[256,1152]{1,0:T(8,128)(2,1)S(1)}, u32[]{:S(2)}, u32[]{:S(2)}) collective-permute-start(bf16[256,1152]{1,0:T(8,128)(2,1)S(1)} %pad_maximum_fusion.3.refs_1_), channel_id=1, source_target_pairs={{0,1},{1,0},{2,3},{3,2},{4,5},{5,4},{6,7},{7,6},{8,9},{9,8},{10,11... | collective-permute-start | bytes 1769480 | tf_op jit(solution)/shard_map/ppermute | solution.py:262
  67.0 3.0 %collective-permute-start.25 = (bf16[256,1152]{1,0:T(8,128)(2,1)S(1)}, bf16[256,1152]{1,0:T(8,128)(2,1)S(1)}, u32[]{:S(2)}, u32[]{:S(2)}) collective-permute-start(bf16[256,1152]{1,0:T(8,128)(2,1)S(1)} %pad_maximum_fusion.4.refs_2_), channel_id=1, source_target_pairs={{0,1},{1,0},{2,3},{3,2},{4,5},{5,4},{6,7},{7,6},{8,9},{9,8},{10,11... | collective-permute-start | bytes 1769480 | tf_op jit(solution)/shard_map/ppermute | solution.py:262
  67.1 9.9 %collective-permute-start.26 = (bf16[256,1152]{1,0:T(8,128)(2,1)S(1)}, bf16[256,1152]{1,0:T(8,128)(2,1)S(1)}, u32[]{:S(2)}, u32[]{:S(2)}) collective-permute-start(bf16[256,1152]{1,0:T(8,128)(2,1)S(1)} %pad_maximum_fusion.4.refs_2_), channel_id=1, source_target_pairs={{0,16},{1,9},{2,18},{3,11},{4,20},{5,13},{6,22},{7,15},{8,24},{9,1... | collective-permute-start | bytes 1769480 | tf_op jit(solution)/shard_map/ppermute | solution.py:270
  77.0 2.0 %collective-permute-start.27 = (bf16[256,1152]{1,0:T(8,128)(2,1)S(1)}, bf16[256,1152]{1,0:T(8,128)(2,1)S(1)}, u32[]{:S(2)}, u32[]{:S(2)}) collective-permute-start(bf16[256,1152]{1,0:T(8,128)(2,1)S(1)} %collective-permute-done.26.refs_0_), channel_id=1, source_target_pairs={{0,1},{1,0},{2,3},{3,2},{4,5},{5,4},{6,7},{7,6},{8,9},{9,8},{10,11... | collective-permute-start | bytes 1769480 | tf_op jit(solution)/shard_map/ppermute | solution.py:262
